TPU v7x, 32 devices: a whole 2x2x4 slice. The times are simulated.
32 devices in a mesh: obs: 4 (over x, core), par: 8 (over z, y).
Axes of the slice: x: 2, y: 2, z: 4, core: 2. Of those that a mesh axis runs over, the one named last changes fastest.
Arguments:
- blocks: bfloat16 [4096, 128, 128], P(('obs', 'par')), may hold values from -0.046875 to 0.046875
- owner: int32 [4096, 1], P(('obs', 'par')), may hold values from 0 to 31; in each aligned block of 128 rows (0 to 127, 128 to 255, ...) at most 8 rows name the same one
- row_local: int32 [4096], P(('obs', 'par')), may hold values from 0 to 31
- col_local: int32 [4096], P(('obs', 'par')), may hold values from 0 to 7
- sketch: bfloat16 [8192, 512], P('par'), may hold values from -6 to 6
Outputs:
- basis: bfloat16 [16384, 512], P(('obs', 'par'))
- projected: float32 [512, 8192], P('obs', 'par')
Inputs may be any that keep to these rules, and one draw needn't show every extreme that they name: The blocks of one device name at most 8 times the same owner; in every draw some device names some owner exactly 8 times, and every owner is named by some block.
All inputs are finite; a program needn't handle non-finite values.
Results may differ from a plain program's by a relative error of at most 0.015.
Values may be sent and summed in bfloat16 or wider, within the bound.
No kernel may reach another device: no remote copies, remote signals or barrier semaphores. Data moves between devices by JAX's collectives and lax.ppermute only.
A program may use at most 128 MiB of HBM per device.

v0:
```python
import math

import jax
import jax.numpy as jnp
from jax import lax
from jax.sharding import PartitionSpec as P

RB_DEV = 32


def per_device(blocks, owner, row_local, col_local, sketch):
    total_devs = lax.axis_size(("obs", "par"))
    obs_count = lax.axis_size("obs")
    held_blocks = blocks.shape[0]
    slot_cap = max(2, (2 * held_blocks + total_devs - 1) // total_devs)
    block_width = blocks.shape[1]
    sketch_width = sketch.shape[1]
    target_dev = owner[:, 0]
    one_hot = (target_dev[:, None] == jnp.arange(total_devs, dtype=jnp.int32)[None, :]).astype(
        jnp.int32
    )
    slot_rank = jnp.sum(jnp.cumsum(one_hot, axis=0) * one_hot, axis=1) - 1
    slot_index = target_dev * slot_cap + slot_rank
    block_places = jnp.stack([row_local, col_local], axis=1)
    outgoing = (
        jnp.zeros((total_devs * slot_cap, block_width, block_width), blocks.dtype)
        .at[slot_index]
        .set(blocks)
    )
    block_labels = jnp.zeros((total_devs * slot_cap, 2), jnp.int32).at[slot_index].set(block_places)
    arrived, arrived_labels = (
        lax.all_to_all(outgoing, ("obs", "par"), split_axis=0, concat_axis=0, tiled=True),
        lax.all_to_all(block_labels, ("obs", "par"), split_axis=0, concat_axis=0, tiled=True),
    )
    slot_total = arrived.shape[0]
    group_size = math.gcd(slot_total, 32)
    turns = slot_total // group_size
    grouped = arrived.reshape(turns, group_size, block_width, block_width)
    row_ids = arrived_labels[:, 0].reshape(turns, group_size)
    col_ids = arrived_labels[:, 1].reshape(turns, group_size)
    row_blocks = RB_DEV
    col_blocks = sketch.shape[0] // block_width
    sketch_panels = sketch.reshape(col_blocks, block_width, sketch_width)

    def sketch_step(totals, inputs):
        values, row_sel, col_sel = inputs
        product = jnp.einsum(
            "sij,sjk->sik", values, sketch_panels[col_sel], preferred_element_type=jnp.float32
        )
        return (totals.at[row_sel].add(product), None)

    partial_rows = lax.scan(
        sketch_step,
        jnp.zeros((row_blocks, block_width, sketch_width), jnp.float32),
        (grouped, row_ids, col_ids),
    )[0]
    partial_rows = partial_rows.reshape(row_blocks * block_width, sketch_width)
    own_rows = lax.psum_scatter(partial_rows, "par", scatter_dimension=0, tiled=True)
    all_rows = row_blocks * block_width * obs_count
    local_gram = jnp.dot(
        own_rows.T, own_rows, precision=lax.Precision.HIGHEST, preferred_element_type=jnp.float32
    )
    gram_matrix = lax.psum(local_gram, ("obs", "par")) / all_rows
    lower_factor = jnp.linalg.cholesky(gram_matrix)
    basis = jax.scipy.linalg.solve_triangular(lower_factor, own_rows.T, lower=True).T.astype(
        jnp.bfloat16
    )
    basis_range = lax.all_gather(basis, "par", axis=0, tiled=True)
    basis_panels = basis_range.reshape(row_blocks, block_width, sketch_width)

    def project_step(totals, inputs):
        values, row_sel, col_sel = inputs
        product = jnp.einsum(
            "sik,sij->skj", basis_panels[row_sel], values, preferred_element_type=jnp.float32
        )
        return (totals.at[col_sel].add(product), None)

    partial_proj = lax.scan(
        project_step,
        jnp.zeros((col_blocks, sketch_width, block_width), jnp.float32),
        (grouped, row_ids, col_ids),
    )[0]
    partial_proj = jnp.transpose(partial_proj, (1, 0, 2)).reshape(
        sketch_width, col_blocks * block_width
    )
    projected = lax.psum_scatter(
        partial_proj.astype(jnp.bfloat16), "obs", scatter_dimension=0, tiled=True
    ).astype(jnp.float32)
    return (basis, projected)


def solution(mesh):
    placed = (
        P(("obs", "par"), None, None),
        P(("obs", "par"), None),
        P(("obs", "par")),
        P(("obs", "par")),
        P("par", None),
    )
    return jax.shard_map(
        per_device,
        mesh=mesh,
        in_specs=placed,
        out_specs=(P(("obs", "par"), None), P("obs", "par")),
        check_vma=False,
    )
```

profile of v0, /device:TPU:0, one launch (start us, length us, event | category | flops | bytes accessed | tf_op | source)
XLA Modules:
  0.0 1204.4 jit_solution(17518000393721809875)
XLA Ops:
  12.2 7.3 all-to-all-start
  19.5 5.3 broadcast_in_dim.14
  24.8 19.3 %scatter_fusion.2 = bf16[256,128,128]{2,1,0:T(8,128)(2,1)} fusion(bf16[256,128,128]{2,1,0:T(8,128)(2,1)} %broadcast_in_dim.14, s32[128]{0:T(128)S(1)} %fusion.46, bf16[128,128,128]{2,1,0:T(8,128)(2,1)} %param.9), kind=kCustom, calls=%fused_computation.5 | custom fusion | bytes 12583424 | tf_op jit(solution)/shard_map/scatter | solution.py:28
  44.1 6.0 all-to-all-start.1
  50.4 189.2 %all-to-all-done.1 = bf16[256,128,128]{2,1,0:T(8,128)(2,1)} async-done(((bf16[256,128,128]{2,1,0:T(8,128)(2,1)}), bf16[256,128,128]{2,1,0:T(8,128)(2,1)}, u32[]{:S(2)}, u32[]{:S(2)}) %all-to-all-start.1) | async-done | bytes 8388640 | tf_op jit(solution)/shard_map/all_to_all | solution.py:32
  239.6 4.3 broadcast_in_dim.11
  243.9 218.3 %while.21 = (s32[]{:T(128)}, f32[32,128,512]{2,1,0:T(8,128)}, s32[8,32]{1,0:T(8,128)S(1)}, bf16[8,32,128,128]{3,2,1,0:T(8,128)(2,1)}, s32[8,32]{1,0:T(8,128)S(1)}, /*index=5*/bf16[8,128,512]{2,1,0:T(8,128)(2,1)S(1)}, s32[]{:T(128)}) while((s32[]{:T(128)}, f32[32,128,512]{2,1,0:T(8,128)}, s32[8,32]{1,0:T(8,128)S(1)}, ...), condition=%wide.region_6.7_spmd, body=%wide.region_4.6_spmd.sunk | while | flops 538969280 | bytes 47191504 | solution.py:52
  246.7 7.0 fusion.75
  253.7 17.5 %scatter_fusion = f32[32,128,512]{2,1,0:T(8,128)} fusion(f32[32,128,512]{2,1,0:T(8,128)} %get-tuple-element.279, s32[32]{0:T(128)S(1)} %get-tuple-element.255, f32[32,128,512]{2,1,0:T(8,128)} %fusion.75), kind=kCustom, calls=%fused_computation.2.clone.1 | custom fusion | flops 2097152 | bytes 25165952 | tf_op jit(solution)/shard_map/while/body/eval_jaxpr/scatter-add | solution.py:50
  274.0 7.0 fusion.75
  281.0 17.5 %scatter_fusion = f32[32,128,512]{2,1,0:T(8,128)} fusion(f32[32,128,512]{2,1,0:T(8,128)} %get-tuple-element.279, s32[32]{0:T(128)S(1)} %get-tuple-element.255, f32[32,128,512]{2,1,0:T(8,128)} %fusion.75), kind=kCustom, calls=%fused_computation.2.clone.1 | custom fusion | flops 2097152 | bytes 25165952 | tf_op jit(solution)/shard_map/while/body/eval_jaxpr/scatter-add | solution.py:50
  301.3 7.0 fusion.75
  308.3 17.4 %scatter_fusion = f32[32,128,512]{2,1,0:T(8,128)} fusion(f32[32,128,512]{2,1,0:T(8,128)} %get-tuple-element.279, s32[32]{0:T(128)S(1)} %get-tuple-element.255, f32[32,128,512]{2,1,0:T(8,128)} %fusion.75), kind=kCustom, calls=%fused_computation.2.clone.1 | custom fusion | flops 2097152 | bytes 25165952 | tf_op jit(solution)/shard_map/while/body/eval_jaxpr/scatter-add | solution.py:50
  328.5 7.0 fusion.75
  335.4 17.5 %scatter_fusion = f32[32,128,512]{2,1,0:T(8,128)} fusion(f32[32,128,512]{2,1,0:T(8,128)} %get-tuple-element.279, s32[32]{0:T(128)S(1)} %get-tuple-element.255, f32[32,128,512]{2,1,0:T(8,128)} %fusion.75), kind=kCustom, calls=%fused_computation.2.clone.1 | custom fusion | flops 2097152 | bytes 25165952 | tf_op jit(solution)/shard_map/while/body/eval_jaxpr/scatter-add | solution.py:50
  355.7 7.0 fusion.75
  362.7 17.5 %scatter_fusion = f32[32,128,512]{2,1,0:T(8,128)} fusion(f32[32,128,512]{2,1,0:T(8,128)} %get-tuple-element.279, s32[32]{0:T(128)S(1)} %get-tuple-element.255, f32[32,128,512]{2,1,0:T(8,128)} %fusion.75), kind=kCustom, calls=%fused_computation.2.clone.1 | custom fusion | flops 2097152 | bytes 25165952 | tf_op jit(solution)/shard_map/while/body/eval_jaxpr/scatter-add | solution.py:50
  383.0 7.0 fusion.75
  389.9 17.5 %scatter_fusion = f32[32,128,512]{2,1,0:T(8,128)} fusion(f32[32,128,512]{2,1,0:T(8,128)} %get-tuple-element.279, s32[32]{0:T(128)S(1)} %get-tuple-element.255, f32[32,128,512]{2,1,0:T(8,128)} %fusion.75), kind=kCustom, calls=%fused_computation.2.clone.1 | custom fusion | flops 2097152 | bytes 25165952 | tf_op jit(solution)/shard_map/while/body/eval_jaxpr/scatter-add | solution.py:50
  410.3 7.0 fusion.75
  417.3 17.6 %scatter_fusion = f32[32,128,512]{2,1,0:T(8,128)} fusion(f32[32,128,512]{2,1,0:T(8,128)} %get-tuple-element.279, s32[32]{0:T(128)S(1)} %get-tuple-element.255, f32[32,128,512]{2,1,0:T(8,128)} %fusion.75), kind=kCustom, calls=%fused_computation.2.clone.1 | custom fusion | flops 2097152 | bytes 25165952 | tf_op jit(solution)/shard_map/while/body/eval_jaxpr/scatter-add | solution.py:50
  437.6 7.0 fusion.75
  444.6 17.6 %scatter_fusion = f32[32,128,512]{2,1,0:T(8,128)} fusion(f32[32,128,512]{2,1,0:T(8,128)} %get-tuple-element.279, s32[32]{0:T(128)S(1)} %get-tuple-element.255, f32[32,128,512]{2,1,0:T(8,128)} %fusion.75), kind=kCustom, calls=%fused_computation.2.clone.1 | custom fusion | flops 2097152 | bytes 25165952 | tf_op jit(solution)/shard_map/while/body/eval_jaxpr/scatter-add | solution.py:50
  462.2 8.9 copy.36
  471.2 154.3 %reduce-scatter.3.cloned.1.call-done = f32[512,512]{0,1:T(8,128)} async-done(((f32[4096,512]{0,1:T(8,128)}), f32[512,512]{0,1:T(8,128)}) %reduce-scatter.3.cloned.1.call-update) | async-done | bytes 1048592 | tf_op jit(solution)/shard_map/reduce_scatter | solution.py:58
  625.5 4.5 fusion.53
  630.2 130.1 %all-reduce.3.cloned.1.call-done = f32[512,512]{0,1:T(8,128)} async-done(((f32[512,512]{0,1:T(8,128)}), f32[512,512]{0,1:T(8,128)}) %all-reduce.3.cloned.1.call-update) | async-done | bytes 1048592 | tf_op jit(solution)/shard_map/psum | solution.py:63
  762.4 11.7 cholesky.106
  774.2 9.8 custom-call.31
  784.7 11.7 cholesky.220
  796.5 10.0 custom-call.32
  807.2 11.7 cholesky.241
  819.5 9.8 custom-call.33
  829.9 11.7 cholesky.258
  845.8 10.1 while.23
  855.9 40.1 %custom-call.34 = f32[4,128,128]{1,2,0:T(8,128)S(1)} custom-call(f32[4,128,128]{2,1,0:T(8,128)} %get-tuple-element.75), custom_call_target="InvertDiagBlocksLowerTriangular" | custom-call | tf_op jit(solution)/shard_map/jit(_solve_triangular)/triangular_solve | solution.py:65
  900.1 74.1 %all-gather.2.cloned.1.call-done = bf16[4096,512]{0,1:T(8,128)(2,1)} async-done(((bf16[512,512]{0,1:T(8,128)(2,1)}), bf16[4096,512]{0,1:T(8,128)(2,1)}) %all-gather.2.cloned.1.call-update) | async-done | bytes 4194320 | tf_op jit(solution)/shard_map/all_gather | solution.py:68
  974.1 6.5 copy.37
  980.8 189.4 %while.22 = (s32[]{:T(128)}, f32[8,512,128]{2,1,0:T(8,128)S(1)}, s32[8,32]{1,0:T(8,128)S(1)}, s32[8,32]{1,0:T(8,128)S(1)}, bf16[32,128,512]{2,1,0:T(8,128)(2,1)}, /*index=5*/bf16[8,32,128,128]{3,2,1,0:T(8,128)(2,1)}, s32[]{:T(128)}) while((s32[]{:T(128)}, f32[8,512,128]{2,1,0:T(8,128)S(1)}, s32[8,32]{1,0:T(8,128)S(1)}, ...), condition=%wide.region_19.20_spmd, body=%wide.region_17.19_spmd.sunk | while | flops 538969280 | bytes 47191504 | solution.py:78
  980.8 5.0 gather_fusion.1
  985.8 7.0 fusion.79
  992.8 11.7 scatter_fusion.1
  1004.6 5.0 gather_fusion.1
  1009.5 7.0 fusion.79
  1016.5 11.6 scatter_fusion.1
  1028.2 5.0 gather_fusion.1
  1033.2 7.0 fusion.79
  1040.2 11.6 scatter_fusion.1
  1051.9 5.0 gather_fusion.1
  1056.9 7.0 fusion.79
  1063.9 11.6 scatter_fusion.1
  1075.6 5.0 gather_fusion.1
  1080.5 7.0 fusion.79
  1087.5 11.6 scatter_fusion.1
  1099.2 5.0 gather_fusion.1
  1104.2 7.0 fusion.79
  1111.2 11.6 scatter_fusion.1
  1122.9 5.0 gather_fusion.1
  1127.9 7.0 fusion.79
  1134.9 11.6 scatter_fusion.1
  1146.5 5.0 gather_fusion.1
  1151.5 7.0 fusion.79
  1158.5 11.7 scatter_fusion.1
  1172.4 23.2 %reduce-scatter.5.cloned.1.call-done = bf16[128,1024]{1,0:T(8,128)(2,1)} async-done(((bf16[512,1024]{1,0:T(8,128)(2,1)}), bf16[128,1024]{1,0:T(8,128)(2,1)}) %reduce-scatter.5.cloned.1.call-update) | async-done | bytes 262160 | tf_op jit(solution)/shard_map/reduce_scatter | solution.py:86
  (118 shorter events, 52.7 us)
Async XLA Ops:
  12.2 31.9 %all-to-all-start = ((s32[32,8,2]{1,2,0:T(2,128)}), s32[32,8,2]{1,2,0:T(2,128)S(1)}, u32[]{:S(2)}, u32[]{:S(2)}) async-start(s32[32,8,2]{1,2,0:T(2,128)} %copy.24), calls=%async_computation | async-start | bytes 65536 | tf_op jit(solution)/shard_map/all_to_all | solution.py:33
  44.1 195.5 %all-to-all-start.1 = ((bf16[256,128,128]{2,1,0:T(8,128)(2,1)}), bf16[256,128,128]{2,1,0:T(8,128)(2,1)}, u32[]{:S(2)}, u32[]{:S(2)}) async-start(bf16[256,128,128]{2,1,0:T(8,128)(2,1)} %scatter_fusion.2), calls=%async_computation.1 | async-start | bytes 16777216 | tf_op jit(solution)/shard_map/all_to_all | solution.py:32
  50.1 575.4 %reduce-scatter.3.cloned.1.call-start = ((), (), s32[]{:S(2)}) async-start(), calls=%async_computation.4 | async-start | bytes 9437184 | tf_op jit(solution)/shard_map/reduce_scatter | solution.py:58
  239.6 4.3 copy-start
  471.1 289.2 %all-reduce.3.cloned.1.call-start = ((), (), s32[]{:S(2)}) async-start(), calls=%async_computation.5 | async-start | bytes 2097152 | tf_op jit(solution)/shard_map/psum | solution.py:63
  630.0 344.2 %all-gather.2.cloned.1.call-start = ((), (), s32[]{:S(2)}) async-start(), calls=%async_computation.6 | async-start | bytes 4718592 | tf_op jit(solution)/shard_map/all_gather | solution.py:68
  760.3 1.8 copy-start.3
  762.3 133.6 %copy-start.1 = (f32[512,512]{0,1:T(8,128)S(1)}, f32[512,512]{0,1:T(8,128)}, u32[]{:S(2)}) copy-start(f32[512,512]{0,1:T(8,128)} %reduce-scatter.3.cloned.1.call-done) | copy-start | bytes 3145732
  900.0 295.6 %reduce-scatter.5.cloned.1.call-start = ((), (), s32[]{:S(2)}) async-start(), calls=%async_computation.7 | async-start | bytes 1310720 | tf_op jit(solution)/shard_map/reduce_scatter | solution.py:86
  1170.2 1.2 copy-start.2
Sparse Core Ops, SparseCore 0:
  471.3 154.1 reduce-scatter.2
  631.5 128.7 all-reduce.2
  900.1 73.9 all-gather.1
  1171.5 24.0 reduce-scatter.4
where the time goes:
time: 1210 us; the launch traced here: 1200 us
  waiting for transfers between devices  571 us (47%)
  other arithmetic  361 us (30%)
  matrix products  121 us (10%)
  local copies, waits for them, and re-layouts  120 us (10%)
  between operations  16.9 us (1%)
  starting transfers between devices  13.6 us (1%)
    all_to_all x1, waiting for transfers between devices, per_device(): lax.all_to_all(outgoing, ('obs', 'par'), split_axis=0, concat_axis=0, til...  189 us
    reduce_scatter x1, waiting for transfers between devices, per_device(): lax.psum_scatter(partial_rows, 'par', scatter_dimension=0, tiled=True)  154 us
    scatter-add x8, other arithmetic, sketch_step(): return (totals.at[row_sel].add(product), None)  140 us
    psum x1, waiting for transfers between devices, per_device(): gram_matrix = lax.psum(local_gram, ('obs', 'par')) / all_rows  130 us
    scatter-add x8, other arithmetic, project_step(): return (totals.at[col_sel].add(product), None)  93.1 us
    another operation x14, other arithmetic, per_device(): lower_factor = jnp.linalg.cholesky(gram_matrix)  78.8 us
    all_gather x1, waiting for transfers between devices, per_device(): basis_range = lax.all_gather(basis, 'par', axis=0, tiled=True)  74.1 us
    dot_general x8, matrix products, project_step(): jnp.einsum('sik,sij->skj', basis_panels[row_sel], values, preferred_eleme...  56.1 us
  transfers between devices with their start and end apart: 6, of which 5 were waited for; matrix products, arithmetic and copies ran while one was open for 2% of the time, Pallas kernels for 0%

commit v1 on v0

v1 whole, which is shorter than its diff:
```python
import functools

import jax
import jax.numpy as jnp
from jax import lax
from jax.experimental import pallas as pl
from jax.experimental.pallas import tpu as pltpu
from jax.sharding import Mesh, PartitionSpec as P

RB_DEV = 32
UNROLL = 4
VMEM_LIMIT = 60 * 1024 * 1024
HIGHEST = lax.Precision.HIGHEST
ALL = ("x", "core", "p", "q")


def shift(value, axis, by):
    size = lax.axis_size(axis)
    return lax.ppermute(value, axis, [(i, (i + by) % size) for i in range(size)])


def collect(rows_ref, cols_ref, sources, slots, list_rows, list_cols, sem, spare):
    count = jnp.int32(0)
    base = 0
    for source in sources:
        held = source.shape[0]

        def take(i, count, source=source, base=base):
            row = rows_ref[base + i]

            @pl.when(row >= 0)
            def _():
                pltpu.make_async_copy(source.at[i], slots.at[count], sem).start()
                list_rows[count] = row
                list_cols[count] = cols_ref[base + i]

            return count + jnp.where(row >= 0, 1, 0).astype(jnp.int32)

        count = lax.fori_loop(0, held, take, count)
        base += held
    for extra in range(UNROLL - 1):
        list_rows[count + extra] = spare
        list_cols[count + extra] = 0

    def settle(i, carry):
        pltpu.make_async_copy(sources[0].at[0], slots.at[0], sem).wait()
        return carry

    lax.fori_loop(0, count, settle, 0)
    return count


def sketch_kernel(sources_n, rows_ref, cols_ref, *refs):
    sources, (near, far) = refs[:sources_n], refs[sources_n : sources_n + 2]
    outs, scratch = refs[sources_n + 2 : -7], refs[-7:]
    slots, panels, acc, list_rows, list_cols, sem, panel_sem = scratch
    half = near.shape[0]
    copies = [
        pltpu.make_async_copy(near, panels.at[pl.ds(0, half)], panel_sem.at[0]),
        pltpu.make_async_copy(far, panels.at[pl.ds(half, half)], panel_sem.at[1]),
    ]
    for copy in copies:
        copy.start()
    spare = acc.shape[0] - 1

    def clear(i, carry):
        acc[i] = jnp.zeros(acc.shape[1:], acc.dtype)
        return carry

    lax.fori_loop(0, spare, clear, 0)
    count = collect(rows_ref, cols_ref, sources, slots, list_rows, list_cols, sem, spare)
    for copy in copies:
        copy.wait()

    def step(i, carry):
        for j in range(UNROLL):
            k = i * UNROLL + j
            row = list_rows[k]
            acc[row] += jnp.dot(
                slots[k], panels[list_cols[k]], preferred_element_type=jnp.float32
            )
        return carry

    lax.fori_loop(0, (count + UNROLL - 1) // UNROLL, step, 0)
    width = outs[0].shape[-1]
    chunks = acc.shape[-1] // width
    groups = len(outs) // chunks
    per = spare // groups
    for g in range(groups):

        def give(i, carry, g=g):
            for c in range(chunks):
                out = outs[g * chunks + c]
                out[i] = acc[g * per + i, :, c * width : (c + 1) * width].astype(out.dtype)
            return carry

        lax.fori_loop(0, per, give, 0)


def project_kernel(sources_n, x_n, q_n, rows_ref, cols_ref, *refs):
    sources, (near, far) = refs[:sources_n], refs[sources_n : sources_n + 2]
    outs, scratch = refs[sources_n + 2 : -7], refs[-7:]
    slots, panels, acc, list_rows, list_cols, sem, panel_sem = scratch
    half = near.shape[0]
    copies = [
        pltpu.make_async_copy(near, panels.at[pl.ds(0, half)], panel_sem.at[0]),
        pltpu.make_async_copy(far, panels.at[pl.ds(half, half)], panel_sem.at[1]),
    ]
    for copy in copies:
        copy.start()
    spare = acc.shape[0] - 1

    def clear(i, carry):
        acc[i] = jnp.zeros(acc.shape[1:], acc.dtype)
        return carry

    lax.fori_loop(0, spare, clear, 0)
    count = collect(rows_ref, cols_ref, sources, slots, list_rows, list_cols, sem, spare)
    for copy in copies:
        copy.wait()

    def step(i, carry):
        for j in range(UNROLL):
            k = i * UNROLL + j
            row = list_rows[k]
            acc[row] += lax.dot_general(
                slots[k],
                panels[list_cols[k]],
                (((0,), (0,)), ((), ())),
                preferred_element_type=jnp.float32,
            )
        return carry

    lax.fori_loop(0, (count + UNROLL - 1) // UNROLL, step, 0)
    width = acc.shape[-1] // 2
    inner = spare // (x_n * q_n)
    for g in range(x_n):

        def give_x(i, carry, g=g):
            out = outs[g]
            out[i] = acc[g * q_n * inner + i, :, :width].astype(out.dtype)
            return carry

        lax.fori_loop(0, q_n * inner, give_x, 0)
    for g in range(q_n):
        for x in range(x_n):

            def give_q(i, carry, g=g, x=x):
                out = outs[x_n + g]
                out[x * inner + i] = acc[(x * q_n + g) * inner + i, :, width:].astype(out.dtype)
                return carry

            lax.fori_loop(0, inner, give_q, 0)


def block_products(kernel, rows, cols, sources, near, far, slots_n, acc_n, outs, name):
    wide, width = near.shape[1], near.shape[2]
    smem = pl.BlockSpec(memory_space=pltpu.SMEM)
    anywhere = pl.BlockSpec(memory_space=pl.ANY)
    return pl.pallas_call(
        kernel,
        out_shape=outs,
        in_specs=[smem, smem] + [anywhere] * (len(sources) + 2),
        out_specs=[pl.BlockSpec(memory_space=pltpu.VMEM)] * len(outs),
        scratch_shapes=[
            pltpu.VMEM((slots_n + UNROLL, wide, wide), jnp.bfloat16),
            pltpu.VMEM((2 * near.shape[0], wide, width), jnp.bfloat16),
            pltpu.VMEM((acc_n + 1, wide, width), jnp.float32),
            pltpu.SMEM((slots_n + UNROLL,), jnp.int32),
            pltpu.SMEM((slots_n + UNROLL,), jnp.int32),
            pltpu.SemaphoreType.DMA,
            pltpu.SemaphoreType.DMA((2,)),
        ],
        compiler_params=pltpu.CompilerParams(vmem_limit_bytes=VMEM_LIMIT),
        cost_estimate=pl.CostEstimate(
            flops=2 * 128 * wide * wide * width, bytes_accessed=32 << 20, transcendentals=0
        ),
        name=name,
    )(rows, cols, *sources, near, far)


def absolute(pieces, axis):
    size, me = len(pieces), lax.axis_index(axis)
    laid = jnp.concatenate(pieces + pieces[:-1], axis=0)
    rows = pieces[0].shape[0]
    return lax.dynamic_slice_in_dim(laid, (size - me) % size * rows, size * rows, axis=0)


def reduce_stage(keep, sends, axis):
    total = keep
    for k, part in enumerate(sends, 1):
        total = total + shift(part, axis, k).astype(jnp.float32)
    return total


def per_device(blocks, owner, row_local, col_local, sketch):
    x_n, q_n, p_n = lax.axis_size("x"), lax.axis_size("q"), lax.axis_size("p")
    xi, ci, zi, yi = (lax.axis_index(a) for a in ALL)
    par = p_n * q_n
    total_devs = 2 * x_n * par
    held, wide = blocks.shape[0], blocks.shape[1]
    width = sketch.shape[1]
    col_dev = sketch.shape[0] // wide
    slot_cap = max(2, (2 * held + total_devs - 1) // total_devs)
    rows_each = RB_DEV // par
    cols_each = col_dev // (2 * x_n)
    all_rows = RB_DEV * wide * 2 * x_n
    bf16, f32 = jnp.bfloat16, jnp.float32

    code = (owner[:, 0] * RB_DEV + row_local) * col_dev + col_local
    pair = jnp.concatenate([code, shift(code, "core", 1)])
    codes = [pair] + [shift(pair, "x", k) for k in range(1, x_n)]
    sources = [blocks, shift(blocks, "core", 1)]
    for k in range(1, x_n):
        far_blocks = shift(blocks, "x", k)
        sources += [far_blocks, shift(far_blocks, "core", 1)]
    codes = jnp.concatenate(codes)

    half_rows = sketch.shape[0] // 2
    my_half = lax.dynamic_slice_in_dim(sketch, ci * half_rows, half_rows, axis=0)
    near = lax.all_gather(my_half, ("p", "q"), axis=0, tiled=True)
    far = shift(near, "core", 1)
    panels = (par * col_dev // 2, wide, width)
    near, far = near.reshape(panels), far.reshape(panels)

    owners = codes // (RB_DEV * col_dev)
    row = codes // col_dev % RB_DEV
    col = codes % col_dev
    o_obs, o_par = owners // par, owners % par
    o_x, o_core = o_obs // 2, o_obs % 2
    r_par, r_in = row // rows_each, row % rows_each
    r_z, r_y = r_par // q_n, r_par % q_n
    c_x, c_core, c_in = col // (2 * cols_each), col // cols_each % 2, col % cols_each
    half_cols = col_dev // 2

    y_slot = (((r_y - yi) % q_n) * p_n + (r_z - zi) % p_n) * rows_each + r_in
    y_slot = jnp.where(o_obs == xi * 2 + ci, y_slot, -1)
    y_panel = (
        jnp.where(col // half_cols == ci, 0, par * half_cols)
        + o_par * half_cols
        + col % half_cols
    )
    p_slot = (((c_x - xi) % x_n * q_n + (o_par % q_n - yi) % q_n) * p_n + (o_par // q_n - zi) % p_n)
    p_slot = p_slot * cols_each + c_in
    p_slot = jnp.where((o_x == xi) & (c_core == ci), p_slot, -1)
    p_panel = jnp.where(o_core == ci, 0, RB_DEV) + row

    chunks = 2
    kc = width // chunks
    per = p_n * rows_each
    shapes = [jax.ShapeDtypeStruct((per, wide, kc), f32)] * chunks
    shapes += [jax.ShapeDtypeStruct((per, wide, kc), bf16)] * (chunks * (q_n - 1))
    parts = block_products(
        functools.partial(sketch_kernel, len(sources)),
        y_slot, y_panel, sources, near, far,
        par * slot_cap * 2 * x_n, RB_DEV, shapes, "sketch_products",
    )
    own = []
    for c in range(chunks):
        total = reduce_stage(parts[c], [parts[k * chunks + c] for k in range(1, q_n)], "q")
        total = total.reshape(p_n, rows_each * wide, kc)
        own.append(reduce_stage(total[0], [total[k].astype(bf16) for k in range(1, p_n)], "p"))
    own_rows = jnp.concatenate(own, axis=1)

    y_near = lax.all_gather(own_rows.astype(bf16), ("p", "q"), axis=0, tiled=True)
    y_far = shift(y_near, "core", 1)

    gram = jnp.zeros((width // 2, width), f32)
    for rows_of in (y_near, y_far):
        mine = lax.dynamic_slice_in_dim(rows_of, ci * (width // 2), width // 2, axis=1)
        gram = gram + lax.dot_general(
            mine, rows_of, (((0,), (0,)), ((), ())), preferred_element_type=f32
        )
    gram = reduce_stage(gram, [gram] * (x_n - 1), "x") / all_rows
    gram = absolute([gram, shift(gram, "core", 1)], "core")
    lower = jnp.linalg.cholesky(gram)
    inverse = jax.scipy.linalg.solve_triangular(lower, jnp.eye(width, dtype=f32), lower=True)

    slots = x_n * q_n * p_n * cols_each
    kh = width // 2
    shapes = [
        jax.ShapeDtypeStruct((slots // x_n, wide, kh), f32 if k == 0 else bf16) for k in range(x_n)
    ] + [jax.ShapeDtypeStruct((slots // q_n, wide, kh), f32 if k == 0 else bf16) for k in range(q_n)]
    y_panels = (RB_DEV, wide, width)
    parts = block_products(
        functools.partial(project_kernel, len(sources), x_n, q_n),
        p_slot, p_panel, sources, y_near.reshape(y_panels), y_far.reshape(y_panels),
        min(2 * x_n * held, 2 * par * slot_cap * 2 * x_n), slots, shapes, "project_products",
    )
    by_x = reduce_stage(parts[0], parts[1:x_n], "x").reshape(q_n, p_n, cols_each * wide, kh)
    by_x = reduce_stage(by_x[0], [by_x[k].astype(bf16) for k in range(1, q_n)], "q")
    by_q = reduce_stage(parts[x_n], parts[x_n + 1 :], "q").reshape(x_n, p_n, cols_each * wide, kh)
    by_q = reduce_stage(by_q[0], [by_q[k].astype(bf16) for k in range(1, x_n)], "x")
    both = jnp.concatenate([by_x, by_q], axis=2)
    z_rows = reduce_stage(both[0], [both[k].astype(bf16) for k in range(1, p_n)], "p")

    basis = lax.dot_general(
        own_rows, inverse, (((1,), (1,)), ((), ())), precision=HIGHEST, preferred_element_type=f32
    ).astype(bf16)
    projected = lax.dot_general(
        inverse, z_rows, (((1,), (1,)), ((), ())), precision=HIGHEST, preferred_element_type=f32
    )
    projected = lax.all_to_all(projected, ("x", "core"), split_axis=0, concat_axis=1, tiled=True)
    return (basis, projected)


def solution(mesh):
    obs, par = mesh.shape["obs"], mesh.shape["par"]
    fine = Mesh(mesh.devices.reshape(obs // 2, 2, 4, par // 4), ALL)
    spread = P(ALL)
    placed = (
        P(ALL, None, None),
        P(ALL, None),
        spread,
        spread,
        P(("p", "q"), None),
    )
    return jax.shard_map(
        per_device,
        mesh=fine,
        in_specs=placed,
        out_specs=(P(ALL, None), P(("x", "core"), ("p", "q"))),
        check_vma=False,
    )
```

time: 1210 us -> 558 us (0.46)
  waiting for transfers between devices: 571 us -> 282 us
  other arithmetic: 361 us -> 133 us
  local copies, waits for them, and re-layouts: 120 us -> 16.2 us
  matrix products: 121 us -> 24.3 us
  Pallas kernels: 0 us -> 45.1 us
  starting transfers between devices: 13.6 us -> 31.1 us
    scatter-add x16 -> x0, other arithmetic: 233 us -> none  [the longest x8 140 us: sketch_step(): return (totals.at[row_sel].add(product), None)]
    ppermute x0 -> x24, waiting for transfers between devices: none -> 200 us  [shift(): lax.ppermute(value, axis, [(i, (i + by) % size) for i in range(size)])]
    all_to_all x2 -> x1, waiting for transfers between devices: 189 us -> 5.08 us  [per_device(): lax.all_to_all(projected, ('x', 'core'), split_axis=0, concat_axis=1, til...]
    reduce_scatter x2 -> x0, waiting for transfers between devices: 177 us -> none  [the longest x1 154 us: per_device(): lax.psum_scatter(partial_rows, 'par', scatter_dimension=0, tiled=True)]
    psum x1 -> x0, waiting for transfers between devices: 130 us -> none  [per_device(): gram_matrix = lax.psum(local_gram, ('obs', 'par')) / all_rows]
    dot_general x17 -> x4, matrix products: 116 us -> 14.7 us  [the longest x2 9.12 us: per_device(): lax.dot_general(mine, rows_of, (((0,), (0,)), ((), ())), preferred_elemen...]
    gather x16 -> x0, local copies, waits for them, and re-layouts: 62.1 us -> none  [the longest x8 39.8 us: project_step(): basis_panels[row_sel]]
    pallas_call x0 -> x2, Pallas kernels: none -> 45.1 us  [block_products(): pl.pallas_call(kernel, out_shape=outs, in_specs=[smem, smem] + [anywhere]...]
  transfers between devices with their start and end apart: 6 -> 27, of which waited for: 5 -> 16; matrix products, arithmetic and copies ran while one was open for 2% -> 30% of each run, Pallas kernels for 0% -> 0%
where the time goes in v1:
time: 558 us; the launch traced here: 549 us
  waiting for transfers between devices  282 us (51%)
  other arithmetic  133 us (24%)
  Pallas kernels  45.1 us (8%)
  starting transfers between devices  31.1 us (6%)
  matrix products  24.3 us (4%)
  between operations  17.3 us (3%)
  local copies, waits for them, and re-layouts  16.2 us (3%)
    ppermute x24, waiting for transfers between devices, shift(): lax.ppermute(value, axis, [(i, (i + by) % size) for i in range(size)])  200 us
    another operation x14, other arithmetic, per_device(): lower = jnp.linalg.cholesky(gram)  79 us
    all_gather x1, waiting for transfers between devices, per_device(): lax.all_gather(own_rows.astype(bf16), ('p', 'q'), axis=0, tiled=True)  76.5 us
    pallas_call x2, Pallas kernels, block_products(): pl.pallas_call(kernel, out_shape=outs, in_specs=[smem, smem] + [anywhere]...  45.1 us
    another operation x3, other arithmetic, per_device(): jax.scipy.linalg.solve_triangular(lower, jnp.eye(width, dtype=f32), lower...  40.3 us
    ppermute x24, starting transfers between devices, shift(): lax.ppermute(value, axis, [(i, (i + by) % size) for i in range(size)])  27.5 us
  transfers between devices with their start and end apart: 27, of which 16 were waited for; matrix products, arithmetic and copies ran while one was open for 30% of the time, Pallas kernels for 0%

profile of v1, /device:TPU:0, one launch (start us, length us, event | category | flops | bytes accessed | tf_op | source)
XLA Modules:
  0.0 549.1 jit_solution(16448505977731530544)
XLA Ops:
  7.2 1.2 copy-done
  9.3 3.0 collective-permute-start.3
  12.3 90.9 %collective-permute-done.3.refs_2_ = bf16[128,128,128]{2,1,0:T(8,128)(2,1)} collective-permute-done((bf16[128,128,128]{2,1,0:T(8,128)(2,1)}, bf16[128,128,128]{2,1,0:T(8,128)(2,1)}, u32[]{:S(2)}, u32[]{:S(2)}) %collective-permute-start.3) | collective-permute-done | bytes 4194336 | tf_op jit(solution)/shard_map/ppermute | solution.py:19
  104.4 5.9 %collective-permute-done = s32[128]{0:T(128)S(1)} collective-permute-done((s32[128]{0:T(128)S(1)}, s32[128]{0:T(128)S(1)}, u32[]{:S(2)}, u32[]{:S(2)}) %collective-permute-start) | collective-permute-done | bytes 544 | tf_op jit(solution)/shard_map/ppermute | solution.py:19
  110.3 1.7 collective-permute-start.1
  112.1 1.8 collective-permute-done.1
  115.1 1.6 collective-permute-done.5
  116.7 22.1 %sketch_products.1 = (f32[16,128,256]{2,1,0:T(8,128)}, f32[16,128,256]{2,1,0:T(8,128)}, bf16[16,128,256]{2,1,0:T(8,128)(2,1)}, bf16[16,128,256]{2,1,0:T(8,128)(2,1)}) custom-call(s32[512]{0:T(512)} %get-tuple-element.64.rows_ref, s32[512]{0:T(512)} %get-tuple-element.63.cols_ref, bf16[128,128,128]{2,1,0:T(8,128)(2,1)} %refs_0_.3, ...), custom_call_target="tpu_custom_call" | custom-call | flops 2147483648 | bytes 33554432 | tf_op jit(solution)/shard_map/sketch_products/pallas_call | solution.py:160
  138.8 2.1 collective-permute-start.6
  141.0 24.2 %collective-permute-done.6 = bf16[16,128,256]{2,1,0:T(8,128)(2,1)S(1)} collective-permute-done((bf16[16,128,256]{2,1,0:T(8,128)(2,1)}, bf16[16,128,256]{2,1,0:T(8,128)(2,1)S(1)}, u32[]{:S(2)}, u32[]{:S(2)}) %collective-permute-start.6) | collective-permute-done | bytes 1048608 | tf_op jit(solution)/shard_map/ppermute | solution.py:19
  165.3 2.1 fusion.98
  167.5 1.8 collective-permute-start.7
  169.3 2.3 collective-permute-start.8
  171.5 1.8 collective-permute-start.9
  173.3 12.8 %collective-permute-done.10 = bf16[16,128,256]{2,1,0:T(8,128)(2,1)S(1)} collective-permute-done((bf16[16,128,256]{2,1,0:T(8,128)(2,1)}, bf16[16,128,256]{2,1,0:T(8,128)(2,1)S(1)}, u32[]{:S(2)}, u32[]{:S(2)}) %collective-permute-start.10) | collective-permute-done | bytes 1048608 | tf_op jit(solution)/shard_map/ppermute | solution.py:19
  186.6 1.3 collective-permute-start.11
  187.9 2.8 collective-permute-start.12
  190.8 1.4 collective-permute-start.13
  192.4 5.4 collective-permute-done.11
  197.7 10.7 %collective-permute-done.12 = bf16[512,256]{1,0:T(8,128)(2,1)S(1)} collective-permute-done((bf16[512,256]{1,0:T(8,128)(2,1)S(1)}, bf16[512,256]{1,0:T(8,128)(2,1)S(1)}, u32[]{:S(2)}, u32[]{:S(2)}) %collective-permute-start.12) | collective-permute-done | bytes 262176 | tf_op jit(solution)/shard_map/ppermute | solution.py:19
  208.6 0.9 fusion.11
  209.5 76.5 %all-gather.5.cloned.1.call-done = bf16[4096,512]{1,0:T(8,128)(2,1)} async-done(((bf16[512,512]{1,0:T(8,128)(2,1)}), bf16[4096,512]{1,0:T(8,128)(2,1)}) %all-gather.5.cloned.1.call-update) | async-done | bytes 4194320 | tf_op jit(solution)/shard_map/all_gather | solution.py:265
  286.1 4.6 fusion.3
  290.6 2.9 collective-permute-done.14
  293.6 23.0 %project_products.1 = (f32[16,128,256]{2,1,0:T(8,128)}, bf16[16,128,256]{2,1,0:T(8,128)(2,1)}, f32[16,128,256]{2,1,0:T(8,128)}, bf16[16,128,256]{2,1,0:T(8,128)(2,1)}) custom-call(s32[512]{0:T(512)} %get-tuple-element.62.rows_ref, s32[512]{0:T(512)} %get-tuple-element.34.cols_ref, bf16[128,128,128]{2,1,0:T(8,128)(2,1)} %refs_0_.3, ...), custom_call_target="tpu_custom_call" | custom-call | flops 2147483648 | bytes 33554432 | tf_op jit(solution)/shard_map/project_products/pallas_call | solution.py:160
  317.0 4.6 fusion.5
  321.6 2.0 collective-permute-start.17
  324.5 1.1 fusion.34
  325.6 10.7 %collective-permute-done.15 = f32[256,512]{0,1:T(8,128)S(1)} collective-permute-done((f32[256,512]{0,1:T(8,128)S(1)}, f32[256,512]{0,1:T(8,128)S(1)}, u32[]{:S(2)}, u32[]{:S(2)}) %collective-permute-start.15) | collective-permute-done | bytes 524320 | tf_op jit(solution)/shard_map/ppermute | solution.py:19
  336.5 6.3 %collective-permute-done.19 = bf16[16,128,256]{2,1,0:T(8,128)(2,1)S(1)} collective-permute-done((bf16[16,128,256]{2,1,0:T(8,128)(2,1)}, bf16[16,128,256]{2,1,0:T(8,128)(2,1)S(1)}, u32[]{:S(2)}, u32[]{:S(2)}) %collective-permute-start.19) | collective-permute-done | bytes 1048608 | tf_op jit(solution)/shard_map/ppermute | solution.py:19
  342.7 1.9 convert_add_fusion
  344.6 0.9 slice.250
  345.5 13.0 %collective-permute-done.17 = bf16[16,128,256]{2,1,0:T(8,128)(2,1)} collective-permute-done((bf16[16,128,256]{2,1,0:T(8,128)(2,1)}, bf16[16,128,256]{2,1,0:T(8,128)(2,1)}, u32[]{:S(2)}, u32[]{:S(2)}) %collective-permute-start.17) | collective-permute-done | bytes 1048608 | tf_op jit(solution)/shard_map/ppermute | solution.py:19
  358.5 1.5 convert_add_fusion.1
  360.1 0.9 slice.251
  361.3 1.7 collective-permute-start.18
  363.8 11.7 %cholesky.104 = f32[128,128]{1,0:T(8,128)S(1)} custom-call(f32[128,128]{1,0:T(8,128)S(1)} %cholesky.266), custom_call_target="Cholesky" | custom-call | tf_op jit(solution)/shard_map/jit(cholesky)/cholesky | solution.py:276
  375.7 9.8 %custom-call.31 = f32[1,128,128]{1,2,0:T(8,128)S(1)} custom-call(f32[1,128,128]{2,1,0:T(8,128)S(1)} %get-tuple-element.61), custom_call_target="InvertDiagBlocksLowerTriangular" | custom-call | tf_op jit(solution)/shard_map/jit(cholesky)/cholesky | solution.py:276
  386.2 12.1 %cholesky.217 = f32[128,128]{1,0:T(8,128)S(1)} custom-call(f32[128,128]{1,0:T(8,128)S(1)} %cholesky.270), custom_call_target="Cholesky" | custom-call | tf_op jit(solution)/shard_map/jit(cholesky)/cholesky | solution.py:276
  398.3 9.8 %custom-call.32 = f32[1,128,128]{1,2,0:T(8,128)S(1)} custom-call(f32[1,128,128]{2,1,0:T(8,128)S(1)} %get-tuple-element.58), custom_call_target="InvertDiagBlocksLowerTriangular" | custom-call | tf_op jit(solution)/shard_map/jit(cholesky)/cholesky | solution.py:276
  408.8 11.7 %cholesky.238 = f32[128,128]{1,0:T(8,128)S(1)} custom-call(f32[128,128]{1,0:T(8,128)S(1)} %cholesky.275), custom_call_target="Cholesky" | custom-call | tf_op jit(solution)/shard_map/jit(cholesky)/cholesky | solution.py:276
  421.2 9.8 %custom-call.33 = f32[1,128,128]{1,2,0:T(8,128)S(1)} custom-call(f32[1,128,128]{2,1,0:T(8,128)S(1)} %get-tuple-element.55), custom_call_target="InvertDiagBlocksLowerTriangular" | custom-call | tf_op jit(solution)/shard_map/jit(cholesky)/cholesky | solution.py:276
  431.7 11.9 %cholesky.255 = f32[128,128]{1,0:T(8,128)S(1)} custom-call(f32[128,128]{1,0:T(8,128)S(1)} %convolution_subtract_fusion.5), custom_call_target="Cholesky" | custom-call | tf_op jit(solution)/shard_map/jit(cholesky)/cholesky | solution.py:276
  447.6 10.9 %while.1 = (s32[]{:T(128)}, f32[512,512]{1,0:T(8,128)S(1)}, s32[4,2]{0,1:T(2,128)S(1)}, f32[4,128,128]{2,1,0:T(8,128)}, s32[]{:T(128)}) while((s32[]{:T(128)}, f32[512,512]{1,0:T(8,128)S(1)}, s32[4,2]{0,1:T(2,128)S(1)}, f32[4,128,128]{2,1,0:T(8,128)}, s32[]{:T(128)}) %tuple.43), condition=%wide.while_cond, body=%wide.while_body.sunk | while | flops 2 | bytes 132705 | solution.py:277
  448.3 2.0 bitcast_dynamic-update-slice_fusion.2
  451.0 2.0 bitcast_dynamic-update-slice_fusion.2
  453.7 2.1 bitcast_dynamic-update-slice_fusion.2
  456.4 2.0 bitcast_dynamic-update-slice_fusion.2
  458.5 40.2 %custom-call.34 = f32[4,128,128]{1,2,0:T(8,128)S(1)} custom-call(f32[4,128,128]{2,1,0:T(8,128)} %get-tuple-element.25), custom_call_target="InvertDiagBlocksLowerTriangular" | custom-call | tf_op jit(solution)/shard_map/jit(_solve_triangular)/triangular_solve | solution.py:277
  498.6 1.2 fusion.36
  499.8 1.3 convolution_subtract_fusion.1
  501.6 1.5 convolution_subtract_fusion
  503.6 1.2 bitcast_add_fusion
  504.8 1.2 bitcast_add_fusion.1
  506.8 1.0 collective-permute-start.22
  507.8 2.4 collective-permute-start.23
  510.2 1.7 convolution_subtract_fusion.2
  511.8 1.3 fusion.45
  513.1 4.2 collective-permute-done.21
  517.3 9.7 %collective-permute-done.22 = bf16[256,512]{1,0:T(8,128)(2,1)S(1)} collective-permute-done((bf16[256,512]{1,0:T(8,128)(2,1)S(1)}, bf16[256,512]{1,0:T(8,128)(2,1)S(1)}, u32[]{:S(2)}, u32[]{:S(2)}) %collective-permute-start.22) | collective-permute-done | bytes 262176 | tf_op jit(solution)/shard_map/ppermute | solution.py:19
  527.0 1.8 fusion.17
  528.9 3.5 all-to-all-start
  532.4 3.7 convolution_convert_fusion
  536.1 5.1 all-to-all-done
  (106 shorter events, 16.4 us)
Async XLA Ops:
  7.2 1.2 copy-start
  7.2 96.0 %all-gather.3.cloned.1.call-start = ((), (), s32[]{:S(2)}) async-start(), calls=%async_computation.1 | async-start | bytes 4718592 | tf_op jit(solution)/shard_map/all_gather | solution.py:221
  9.2 276.8 %all-gather.5.cloned.1.call-start = ((), (), s32[]{:S(2)}) async-start(), calls=%async_computation.2 | async-start | bytes 4718592 | tf_op jit(solution)/shard_map/all_gather | solution.py:265
  9.3 93.9 %collective-permute-start.3 = (bf16[128,128,128]{2,1,0:T(8,128)(2,1)}, bf16[128,128,128]{2,1,0:T(8,128)(2,1)}, u32[]{:S(2)}, u32[]{:S(2)}) collective-permute-start(bf16[128,128,128]{2,1,0:T(8,128)(2,1)} %refs_0_.3), channel_id=1, source_target_pairs={{0,16},{16,0},{1,17},{17,1},{2,18},{18,2},{3,19},{19,3},{4,20},{20... | collective-permute-start | bytes 12582920 | tf_op jit(solution)/shard_map/ppermute | solution.py:19
  12.3 102.8 %collective-permute-start.2 = (bf16[128,128,128]{2,1,0:T(8,128)(2,1)}, bf16[128,128,128]{2,1,0:T(8,128)(2,1)}, u32[]{:S(2)}, u32[]{:S(2)}) collective-permute-start(bf16[128,128,128]{2,1,0:T(8,128)(2,1)} %refs_0_.3), channel_id=1, source_target_pairs={{0,8},{8,0},{1,9},{9,1},{2,10},{10,2},{3,11},{11,3},{4,12},{12,4},... | collective-permute-start | bytes 12582920 | tf_op jit(solution)/shard_map/ppermute | solution.py:19
  103.2 11.9 %collective-permute-start.4 = (bf16[128,128,128]{2,1,0:T(8,128)(2,1)}, bf16[128,128,128]{2,1,0:T(8,128)(2,1)}, u32[]{:S(2)}, u32[]{:S(2)}) collective-permute-start(bf16[128,128,128]{2,1,0:T(8,128)(2,1)} %collective-permute-done.3.refs_2_), channel_id=1, source_target_pairs={{0,8},{8,0},{1,9},{9,1},{2,10},{10,2},{3,11},{11,3},{4,12},{12,4},... | collective-permute-start | bytes 12582920 | tf_op jit(solution)/shard_map/ppermute | solution.py:19
  103.2 13.5 %collective-permute-start.5 = (bf16[4096,512]{1,0:T(8,128)(2,1)}, bf16[4096,512]{1,0:T(8,128)(2,1)}, u32[]{:S(2)}, u32[]{:S(2)}) collective-permute-start(bf16[4096,512]{1,0:T(8,128)(2,1)} %all-gather.3.cloned.1.call-done), channel_id=1, source_target_pairs={{0,8},{8,0},{1,9},{9,1},{2,10},{10,2},{3,11},{11,3},{4,12},{12,4},... | collective-permute-start | bytes 12582920 | tf_op jit(solution)/shard_map/ppermute | solution.py:19
  104.4 5.9 %collective-permute-start = (s32[128]{0:T(128)S(1)}, s32[128]{0:T(128)S(1)}, u32[]{:S(2)}, u32[]{:S(2)}) collective-permute-start(s32[128]{0:T(128)S(1)} %fusion.93), channel_id=1, source_target_pairs={{0,8},{8,0},{1,9},{9,1},{2,10},{10,2},{3,11},{11,3},{4,12},{12,4},... | collective-permute-start | bytes 1544 | tf_op jit(solution)/shard_map/ppermute | solution.py:19
  110.3 3.6 collective-permute-start.1
  138.8 26.4 %collective-permute-start.6 = (bf16[16,128,256]{2,1,0:T(8,128)(2,1)}, bf16[16,128,256]{2,1,0:T(8,128)(2,1)S(1)}, u32[]{:S(2)}, u32[]{:S(2)}) collective-permute-start(bf16[16,128,256]{2,1,0:T(8,128)(2,1)} %get-tuple-element.11), channel_id=1, source_target_pairs={{0,1},{1,0},{2,3},{3,2},{4,5},{5,4},{6,7},{7,6},{8,9},{9,8},{10,11... | collective-permute-start | bytes 3145736 | tf_op jit(solution)/shard_map/ppermute | solution.py:19
  141.0 45.2 %collective-permute-start.10 = (bf16[16,128,256]{2,1,0:T(8,128)(2,1)}, bf16[16,128,256]{2,1,0:T(8,128)(2,1)S(1)}, u32[]{:S(2)}, u32[]{:S(2)}) collective-permute-start(bf16[16,128,256]{2,1,0:T(8,128)(2,1)} %get-tuple-element.13), channel_id=1, source_target_pairs={{0,1},{1,0},{2,3},{3,2},{4,5},{5,4},{6,7},{7,6},{8,9},{9,8},{10,11... | collective-permute-start | bytes 3145736 | tf_op jit(solution)/shard_map/ppermute | solution.py:19
  165.3 20.9 %copy-start.5 = (f32[16,128,256]{2,1,0:T(8,128)S(1)}, f32[16,128,256]{2,1,0:T(8,128)}, u32[]{:S(2)}) copy-start(f32[16,128,256]{2,1,0:T(8,128)} %get-tuple-element.12) | copy-start | bytes 6291460
  167.5 23.3 %collective-permute-start.7 = (bf16[512,256]{1,0:T(8,128)(2,1)S(1)}, bf16[512,256]{1,0:T(8,128)(2,1)S(1)}, u32[]{:S(2)}, u32[]{:S(2)}) collective-permute-start(bf16[512,256]{1,0:T(8,128)(2,1)S(1)} %bitcast.113), channel_id=1, source_target_pairs={{0,2},{2,4},{4,6},{6,0},{1,3},{3,5},{5,7},{7,1},{8,10},{10,12},{12... | collective-permute-start | bytes 786440 | tf_op jit(solution)/shard_map/ppermute | solution.py:19
  169.3 22.9 %collective-permute-start.8 = (bf16[512,256]{1,0:T(8,128)(2,1)S(1)}, bf16[512,256]{1,0:T(8,128)(2,1)S(1)}, u32[]{:S(2)}, u32[]{:S(2)}) collective-permute-start(bf16[512,256]{1,0:T(8,128)(2,1)S(1)} %bitcast.112), channel_id=1, source_target_pairs={{0,4},{2,6},{4,0},{6,2},{1,5},{3,7},{5,1},{7,3},{8,12},{10,14},{12... | collective-permute-start | bytes 786440 | tf_op jit(solution)/shard_map/ppermute | solution.py:19
  171.5 20.6 %collective-permute-start.9 = (bf16[512,256]{1,0:T(8,128)(2,1)S(1)}, bf16[512,256]{1,0:T(8,128)(2,1)S(1)}, u32[]{:S(2)}, u32[]{:S(2)}) collective-permute-start(bf16[512,256]{1,0:T(8,128)(2,1)S(1)} %bitcast.111), channel_id=1, source_target_pairs={{0,6},{2,0},{4,2},{6,4},{1,7},{3,1},{5,3},{7,5},{8,14},{10,8},{12,... | collective-permute-start | bytes 786440 | tf_op jit(solution)/shard_map/ppermute | solution.py:19
  186.6 11.2 %collective-permute-start.11 = (bf16[512,256]{1,0:T(8,128)(2,1)S(1)}, bf16[512,256]{1,0:T(8,128)(2,1)S(1)}, u32[]{:S(2)}, u32[]{:S(2)}) collective-permute-start(bf16[512,256]{1,0:T(8,128)(2,1)S(1)} %bitcast.116), channel_id=1, source_target_pairs={{0,2},{2,4},{4,6},{6,0},{1,3},{3,5},{5,7},{7,1},{8,10},{10,12},{12... | collective-permute-start | bytes 786440 | tf_op jit(solution)/shard_map/ppermute | solution.py:19
  187.9 20.5 %collective-permute-start.12 = (bf16[512,256]{1,0:T(8,128)(2,1)S(1)}, bf16[512,256]{1,0:T(8,128)(2,1)S(1)}, u32[]{:S(2)}, u32[]{:S(2)}) collective-permute-start(bf16[512,256]{1,0:T(8,128)(2,1)S(1)} %bitcast.115), channel_id=1, source_target_pairs={{0,4},{2,6},{4,0},{6,2},{1,5},{3,7},{5,1},{7,3},{8,12},{10,14},{12... | collective-permute-start | bytes 786440 | tf_op jit(solution)/shard_map/ppermute | solution.py:19
  190.8 17.6 %collective-permute-start.13 = (bf16[512,256]{1,0:T(8,128)(2,1)S(1)}, bf16[512,256]{1,0:T(8,128)(2,1)S(1)}, u32[]{:S(2)}, u32[]{:S(2)}) collective-permute-start(bf16[512,256]{1,0:T(8,128)(2,1)S(1)} %bitcast.114), channel_id=1, source_target_pairs={{0,6},{2,0},{4,2},{6,4},{1,7},{3,1},{5,3},{7,5},{8,14},{10,8},{12,... | collective-permute-start | bytes 786440 | tf_op jit(solution)/shard_map/ppermute | solution.py:19
  192.3 98.3 %copy-start.6 = (f32[512,256]{1,0:T(8,128)}, f32[512,256]{1,0:T(8,128)S(1)}, u32[]{:S(2)}) copy-start(f32[512,256]{1,0:T(8,128)S(1)} %fusion.30) | copy-start | bytes 1572868
  208.6 82.1 %copy-start.8 = (f32[512,256]{1,0:T(8,128)}, f32[512,256]{1,0:T(8,128)S(1)}, u32[]{:S(2)}) copy-start(f32[512,256]{1,0:T(8,128)S(1)} %fusion.28) | copy-start | bytes 1572868
  286.1 7.5 %collective-permute-start.14 = (bf16[4096,512]{1,0:T(8,128)(2,1)}, bf16[4096,512]{1,0:T(8,128)(2,1)}, u32[]{:S(2)}, u32[]{:S(2)}) collective-permute-start(bf16[4096,512]{1,0:T(8,128)(2,1)} %all-gather.5.cloned.1.call-done), channel_id=1, source_target_pairs={{0,8},{8,0},{1,9},{9,1},{2,10},{10,2},{3,11},{11,3},{4,12},{12,4},... | collective-permute-start | bytes 12582920 | tf_op jit(solution)/shard_map/ppermute | solution.py:19
  316.6 26.2 %collective-permute-start.19 = (bf16[16,128,256]{2,1,0:T(8,128)(2,1)}, bf16[16,128,256]{2,1,0:T(8,128)(2,1)S(1)}, u32[]{:S(2)}, u32[]{:S(2)}) collective-permute-start(bf16[16,128,256]{2,1,0:T(8,128)(2,1)} %get-tuple-element.17), channel_id=1, source_target_pairs={{0,1},{1,0},{2,3},{3,2},{4,5},{5,4},{6,7},{7,6},{8,9},{9,8},{10,11... | collective-permute-start | bytes 3145736 | tf_op jit(solution)/shard_map/ppermute | solution.py:19
  321.5 14.8 %collective-permute-start.15 = (f32[256,512]{0,1:T(8,128)S(1)}, f32[256,512]{0,1:T(8,128)S(1)}, u32[]{:S(2)}, u32[]{:S(2)}) collective-permute-start(f32[256,512]{0,1:T(8,128)S(1)} %fusion.5), channel_id=1, source_target_pairs={{0,16},{16,0},{1,17},{17,1},{2,18},{18,2},{3,19},{19,3},{4,20},{20... | collective-permute-start | bytes 1572872 | tf_op jit(solution)/shard_map/ppermute | solution.py:19
  321.6 36.9 %collective-permute-start.17 = (bf16[16,128,256]{2,1,0:T(8,128)(2,1)}, bf16[16,128,256]{2,1,0:T(8,128)(2,1)}, u32[]{:S(2)}, u32[]{:S(2)}) collective-permute-start(bf16[16,128,256]{2,1,0:T(8,128)(2,1)} %get-tuple-element.15), channel_id=1, source_target_pairs={{0,16},{16,0},{1,17},{17,1},{2,18},{18,2},{3,19},{19,3},{4,20},{20... | collective-permute-start | bytes 3145736 | tf_op jit(solution)/shard_map/ppermute | solution.py:19
  336.4 26.6 %collective-permute-start.16 = (f32[256,512]{0,1:T(8,128)S(1)}, f32[256,512]{0,1:T(8,128)S(1)}, u32[]{:S(2)}, u32[]{:S(2)}) collective-permute-start(f32[256,512]{0,1:T(8,128)S(1)} %add_multiply_fusion), channel_id=1, source_target_pairs={{0,8},{8,0},{1,9},{9,1},{2,10},{10,2},{3,11},{11,3},{4,12},{12,4},... | collective-permute-start | bytes 1572872 | tf_op jit(solution)/shard_map/ppermute | solution.py:19
  344.6 15.5 %copy-start.2 = (f32[16,128,256]{2,1,0:T(8,128)}, f32[16,128,256]{2,1,0:T(8,128)S(1)}, u32[]{:S(2)}) copy-start(f32[16,128,256]{2,1,0:T(8,128)S(1)} %convert_add_fusion) | copy-start | bytes 6291460
  344.6 13.9 %copy-start.10 = (f32[16,128,256]{2,1,0:T(8,128)S(1)}, f32[16,128,256]{2,1,0:T(8,128)}, u32[]{:S(2)}) copy-start(f32[16,128,256]{2,1,0:T(8,128)} %get-tuple-element.14) | copy-start | bytes 6291460
  360.1 2.9 copy-start.3
  361.0 142.6 %collective-permute-start.20 = (bf16[4,256,256]{2,1,0:T(8,128)(2,1)}, bf16[4,256,256]{2,1,0:T(8,128)(2,1)}, u32[]{:S(2)}, u32[]{:S(2)}) collective-permute-start(bf16[4,256,256]{2,1,0:T(8,128)(2,1)} %bitcast.27), channel_id=1, source_target_pairs={{0,16},{16,0},{1,17},{17,1},{2,18},{18,2},{3,19},{19,3},{4,20},{20... | collective-permute-start | bytes 1572872 | tf_op jit(solution)/shard_map/ppermute | solution.py:19
  361.3 143.5 %collective-permute-start.18 = (bf16[4,256,256]{2,1,0:T(8,128)(2,1)}, bf16[4,256,256]{2,1,0:T(8,128)(2,1)}, u32[]{:S(2)}, u32[]{:S(2)}) collective-permute-start(bf16[4,256,256]{2,1,0:T(8,128)(2,1)} %bitcast.25), channel_id=1, source_target_pairs={{0,1},{1,0},{2,3},{3,2},{4,5},{5,4},{6,7},{7,6},{8,9},{9,8},{10,11... | collective-permute-start | bytes 1572872 | tf_op jit(solution)/shard_map/ppermute | solution.py:19
  447.6 56.0 %slice-start = ((f32[16,128,256]{2,1,0:T(8,128)}), f32[8,128,256]{2,1,0:T(8,128)S(1)}, s32[]{:S(2)}) async-start(f32[16,128,256]{2,1,0:T(8,128)} %copy-done.2), calls=%async_computation.3 | async-start | bytes 2097152 | tf_op jit(solution)/shard_map/slice | solution.py:293
  458.5 41.4 %copy-start.4 = (f32[512,512]{1,0:T(8,128)}, f32[512,512]{1,0:T(8,128)S(1)}, u32[]{:S(2)}) copy-start(f32[512,512]{1,0:T(8,128)S(1)} %get-tuple-element.121) | copy-start | bytes 3145732
  498.6 4.9 copy-start.12
  501.6 3.2 slice-start.1
  506.1 11.2 %collective-permute-start.21 = (bf16[256,512]{1,0:T(8,128)(2,1)S(1)}, bf16[256,512]{1,0:T(8,128)(2,1)S(1)}, u32[]{:S(2)}, u32[]{:S(2)}) collective-permute-start(bf16[256,512]{1,0:T(8,128)(2,1)S(1)} %get-tuple-element.43), channel_id=1, source_target_pairs={{0,2},{2,4},{4,6},{6,0},{1,3},{3,5},{5,7},{7,1},{8,10},{10,12},{12... | collective-permute-start | bytes 786440 | tf_op jit(solution)/shard_map/ppermute | solution.py:19
  506.8 20.2 %collective-permute-start.22 = (bf16[256,512]{1,0:T(8,128)(2,1)S(1)}, bf16[256,512]{1,0:T(8,128)(2,1)S(1)}, u32[]{:S(2)}, u32[]{:S(2)}) collective-permute-start(bf16[256,512]{1,0:T(8,128)(2,1)S(1)} %get-tuple-element.45), channel_id=1, source_target_pairs={{0,4},{2,6},{4,0},{6,2},{1,5},{3,7},{5,1},{7,3},{8,12},{10,14},{12... | collective-permute-start | bytes 786440 | tf_op jit(solution)/shard_map/ppermute | solution.py:19
  507.8 19.3 %collective-permute-start.23 = (bf16[256,512]{1,0:T(8,128)(2,1)S(1)}, bf16[256,512]{1,0:T(8,128)(2,1)S(1)}, u32[]{:S(2)}, u32[]{:S(2)}) collective-permute-start(bf16[256,512]{1,0:T(8,128)(2,1)S(1)} %get-tuple-element.44), channel_id=1, source_target_pairs={{0,6},{2,0},{4,2},{6,4},{1,7},{3,1},{5,3},{7,5},{8,14},{10,8},{12,... | collective-permute-start | bytes 786440 | tf_op jit(solution)/shard_map/ppermute | solution.py:19
  513.1 15.8 %copy-start.11 = (f32[128,512]{1,0:T(8,128)}, f32[128,512]{1,0:T(8,128)S(1)}, u32[]{:S(2)}) copy-start(f32[128,512]{1,0:T(8,128)S(1)} %fusion.45) | copy-start | bytes 786436
  513.1 19.3 %copy-start.7 = (f32[512,256]{1,0:T(8,128)S(1)}, f32[512,256]{1,0:T(8,128)}, u32[]{:S(2)}) copy-start(f32[512,256]{1,0:T(8,128)} %copy-done.6) | copy-start | bytes 1572868
  513.1 19.3 %copy-start.9 = (f32[512,256]{1,0:T(8,128)S(1)}, f32[512,256]{1,0:T(8,128)}, u32[]{:S(2)}) copy-start(f32[512,256]{1,0:T(8,128)} %copy-done.8) | copy-start | bytes 1572868
  528.9 12.3 %all-to-all-start = ((f32[4,128,256]{2,1,0:T(8,128)}), f32[4,128,256]{2,1,0:T(8,128)S(1)}, u32[]{:S(2)}, u32[]{:S(2)}) async-start(f32[4,128,256]{2,1,0:T(8,128)} %bitcast.32), calls=%async_computation | async-start | bytes 1048576 | tf_op jit(solution)/shard_map/all_to_all | solution.py:303
  532.4 9.6 %copy-start.1 = (bf16[1024,512]{1,0:T(8,128)(2,1)S(1)}, bf16[1024,512]{1,0:T(8,128)(2,1)}, u32[]{:S(2)}) copy-start(bf16[1024,512]{1,0:T(8,128)(2,1)} %param.9) | copy-start | bytes 3145732
Sparse Core Ops, SparseCore 0:
  10.7 76.0 all-gather.2
  209.6 76.3 all-gather.4

commit v2 on v1

v2 whole, which is shorter than its diff:
```python
import functools

import jax
import jax.numpy as jnp
from jax import lax
from jax.experimental import pallas as pl
from jax.experimental.pallas import tpu as pltpu
from jax.sharding import Mesh, PartitionSpec as P

RB_DEV = 32
UNROLL = 4
CHUNKS = 4
MOST_SLOTS = 512
VMEM_LIMIT = 60 * 1024 * 1024
HIGHEST = lax.Precision.HIGHEST
ALL = ("x", "core", "p", "q")


def shift(value, axis, by):
    size = lax.axis_size(axis)
    return lax.ppermute(value, axis, [(i, (i + by) % size) for i in range(size)])


def spread_pieces(value, axis):
    return [value] + [shift(value, axis, k) for k in range(1, lax.axis_size(axis))]


def reduce_stage(keep, sends, axis):
    total = keep
    for k, part in enumerate(sends, 1):
        total = total + shift(part, axis, k).astype(jnp.float32)
    return total


def passes_of(sources, bounds):
    groups, room = [], 0
    base = 0
    for source, bound in zip(sources, bounds):
        if not groups or room + bound > MOST_SLOTS:
            groups.append([])
            room = 0
        groups[-1].append((source, base))
        room += bound
        base += source.shape[0]
    return groups


def slots_of(bounds):
    most, room = 0, 0
    for bound in bounds:
        room = bound if room + bound > MOST_SLOTS else room + bound
        most = max(most, room)
    return most


def collect(rows_ref, cols_ref, group, slots, list_rows, list_cols, sem, spare):
    count = jnp.int32(0)
    for source, base in group:

        def take(i, count, source=source, base=base):
            row = rows_ref[base + i]

            @pl.when(row >= 0)
            def _():
                pltpu.make_async_copy(source.at[i], slots.at[count], sem).start()
                list_rows[count] = row
                list_cols[count] = cols_ref[base + i]

            return count + jnp.where(row >= 0, 1, 0).astype(jnp.int32)

        count = lax.fori_loop(0, source.shape[0], take, count)
    for extra in range(UNROLL - 1):
        list_rows[count + extra] = spare
        list_cols[count + extra] = 0

    def settle(i, carry):
        pltpu.make_async_copy(group[0][0].at[0], slots.at[0], sem).wait()
        return carry

    lax.fori_loop(0, count, settle, 0)
    return count


def accumulate(bounds, contract, rows_ref, cols_ref, sources, panel_copies, scratch):
    slots, panels, acc, list_rows, list_cols, sem, panel_sem = scratch
    copies = [
        pltpu.make_async_copy(source, target, panel_sem.at[i])
        for i, (source, target) in enumerate(panel_copies)
    ]
    for copy in copies:
        copy.start()
    spare = acc.shape[0] - 1

    def clear(i, carry):
        acc[i] = jnp.zeros(acc.shape[1:], acc.dtype)
        return carry

    lax.fori_loop(0, spare, clear, 0)

    def step(i, carry):
        for j in range(UNROLL):
            k = i * UNROLL + j
            row = list_rows[k]
            acc[row] += lax.dot_general(
                slots[k],
                panels[list_cols[k]],
                (((contract,), (0,)), ((), ())),
                preferred_element_type=jnp.float32,
            )
        return carry

    for turn, group in enumerate(passes_of(sources, bounds)):
        count = collect(rows_ref, cols_ref, group, slots, list_rows, list_cols, sem, spare)
        if turn == 0:
            for copy in copies:
                copy.wait()
        lax.fori_loop(0, (count + UNROLL - 1) // UNROLL, step, 0)


def sketch_kernel(bounds, pieces_n, rows_ref, cols_ref, *refs):
    n = len(bounds)
    sources, pieces = refs[:n], refs[n : n + pieces_n]
    outs, scratch = refs[n + pieces_n : -7], refs[-7:]
    panels, acc = scratch[1], scratch[2]
    each = pieces[0].shape[0]
    accumulate(
        bounds, 1, rows_ref, cols_ref, sources,
        [(piece, panels.at[pl.ds(i * each, each)]) for i, piece in enumerate(pieces)],
        scratch,
    )
    width = outs[0].shape[-1]
    chunks = acc.shape[-1] // width
    per = (acc.shape[0] - 1) // (len(outs) // chunks)
    for g in range(len(outs) // chunks):

        def give(i, carry, g=g):
            for c in range(chunks):
                out = outs[g * chunks + c]
                out[i] = acc[g * per + i, :, c * width : (c + 1) * width].astype(out.dtype)
            return carry

        lax.fori_loop(0, per, give, 0)


def project_kernel(bounds, pieces_n, x_n, q_n, rows_ref, cols_ref, *refs):
    n = len(bounds)
    sources, pieces = refs[:n], refs[n : n + pieces_n]
    outs, scratch = refs[n + pieces_n : -7], refs[-7:]
    panels, acc = scratch[1], scratch[2]
    parts = pieces_n // CHUNKS
    copies = []
    for c in range(CHUNKS):
        base = 0
        for piece in pieces[c * parts : (c + 1) * parts]:
            rows, cols = piece.shape[0], piece.shape[2]
            copies.append((piece, panels.at[pl.ds(base, rows), :, pl.ds(c * cols, cols)]))
            base += rows
    accumulate(bounds, 0, rows_ref, cols_ref, sources, copies, scratch)
    width = acc.shape[-1] // 2
    inner = (acc.shape[0] - 1) // (x_n * q_n)
    for g in range(x_n):

        def give_x(i, carry, g=g):
            out = outs[g]
            out[i] = acc[g * q_n * inner + i, :, :width].astype(out.dtype)
            return carry

        lax.fori_loop(0, q_n * inner, give_x, 0)
    for g in range(q_n):
        for x in range(x_n):

            def give_q(i, carry, g=g, x=x):
                out = outs[x_n + g]
                out[x * inner + i] = acc[(x * q_n + g) * inner + i, :, width:].astype(out.dtype)
                return carry

            lax.fori_loop(0, inner, give_q, 0)


def block_products(kernel, bounds, rows, cols, sources, pieces, panels_n, acc_n, width, outs, name):
    wide = sources[0].shape[1]
    smem = pl.BlockSpec(memory_space=pltpu.SMEM)
    anywhere = pl.BlockSpec(memory_space=pl.ANY)
    slots_n = slots_of(bounds)
    return pl.pallas_call(
        kernel,
        out_shape=outs,
        in_specs=[smem, smem] + [anywhere] * (len(sources) + len(pieces)),
        out_specs=[pl.BlockSpec(memory_space=pltpu.VMEM)] * len(outs),
        scratch_shapes=[
            pltpu.VMEM((slots_n + UNROLL, wide, wide), jnp.bfloat16),
            pltpu.VMEM((panels_n, wide, width), jnp.bfloat16),
            pltpu.VMEM((acc_n + 1, wide, width), jnp.float32),
            pltpu.SMEM((slots_n + UNROLL,), jnp.int32),
            pltpu.SMEM((slots_n + UNROLL,), jnp.int32),
            pltpu.SemaphoreType.DMA,
            pltpu.SemaphoreType.DMA((len(pieces),)),
        ],
        compiler_params=pltpu.CompilerParams(vmem_limit_bytes=VMEM_LIMIT),
        cost_estimate=pl.CostEstimate(
            flops=2 * 128 * wide * wide * width, bytes_accessed=32 << 20, transcendentals=0
        ),
        name=name,
    )(rows, cols, *sources, *pieces)


def dot32(a, b, dims):
    return lax.dot_general(
        a, b, (dims, ((), ())), precision=HIGHEST, preferred_element_type=jnp.float32
    )


def leaf_inverse(a):
    n = a.shape[0]
    place = lax.broadcasted_iota(jnp.int32, (n, 1), 0)
    rows = lax.broadcasted_iota(jnp.int32, (n, n), 0)
    cols = lax.broadcasted_iota(jnp.int32, (n, n), 1)
    both = jnp.concatenate([a, jnp.where(rows == cols, 1.0, 0.0).astype(a.dtype)], axis=1)
    pivots = jnp.ones((n, 1), a.dtype)
    for j in range(n):
        pivot = both[j : j + 1, j : j + 1]
        times = jnp.where(place > j, both[:, j : j + 1] * (1.0 / pivot), 0.0)
        pivots = jnp.where(place == j, pivot, pivots)
        both = both - times * both[j : j + 1, :]
    return both[:, n:] * lax.rsqrt(pivots)


def inverse_kernel(scale, k, *refs):
    gram, before, out = refs[: k + 1], refs[k + 1 : -1], refs[-1]
    n = out.shape[0]
    grams = [g[...] * scale for g in gram]
    rest = grams[k]
    factors = []
    for j in range(k):
        factor = dot32(grams[0], before[j][:, :n], ((1,), (1,)))
        for i in range(1, j + 1):
            factor += dot32(grams[i], before[j][:, i * n : (i + 1) * n], ((1,), (1,)))
        rest = rest - dot32(factor, factor, ((1,), (1,)))
        factors.append(factor)
    corner = leaf_inverse(rest)
    out[...] = jnp.zeros(out.shape, out.dtype)
    if k:
        total = dot32(factors[0], before[0][:, : k * n], ((1,), (0,)))
        for j in range(1, k):
            total += dot32(factors[j], before[j][:, : k * n], ((1,), (0,)))
        out[:, : k * n] = -dot32(corner, total, ((1,), (0,)))
    out[:, k * n : (k + 1) * n] = corner


def inverse_rows(scale, gram, before, width):
    k = len(before)
    n = gram[0].shape[0]
    return pl.pallas_call(
        functools.partial(inverse_kernel, scale, k),
        out_shape=jax.ShapeDtypeStruct((n, width), jnp.float32),
        compiler_params=pltpu.CompilerParams(vmem_limit_bytes=16 << 20),
        cost_estimate=pl.CostEstimate(flops=12 << 30, bytes_accessed=1 << 20, transcendentals=0),
        name="inverse_rows",
    )(*gram, *before)


def per_device(blocks, owner, row_local, col_local, sketch):
    x_n, q_n, p_n = lax.axis_size("x"), lax.axis_size("q"), lax.axis_size("p")
    xi, ci, zi, yi = (lax.axis_index(a) for a in ALL)
    par = p_n * q_n
    total_devs = 2 * x_n * par
    held, wide = blocks.shape[0], blocks.shape[1]
    width = sketch.shape[1]
    col_dev = sketch.shape[0] // wide
    slot_cap = max(2, (2 * held + total_devs - 1) // total_devs)
    rows_each = RB_DEV // par
    cols_each = col_dev // (2 * x_n)
    all_rows = RB_DEV * wide * 2 * x_n
    bf16, f32 = jnp.bfloat16, jnp.float32
    kc = width // CHUNKS
    by_q_n = held // 4
    by_x_n = held - by_q_n

    code = (owner[:, 0] * RB_DEV + row_local) * col_dev + col_local
    pair = jnp.concatenate([code, shift(code, "core", 1)])
    codes, sources = [pair], [blocks, shift(blocks, "core", 1)]
    first, last = blocks[:by_x_n], blocks[by_x_n:]
    most_y, most_p = min(by_x_n, par * slot_cap), min(by_x_n, 2 * par * slot_cap)
    bounds_y, bounds_p = [most_y + by_q_n] * 2, [most_p + by_q_n] * 2
    along_x = jnp.arange(held) < by_x_n
    along = [along_x, along_x]
    for k in range(1, x_n):
        got = shift(first, "x", k)
        sources += [got, shift(got, "core", 1)]
        bounds_y += [most_y] * 2
        bounds_p += [most_p] * 2
        there = shift(pair, "x", k).reshape(2, held)[:, :by_x_n]
        codes.append(there.reshape(-1))
        along.append(jnp.ones((2 * by_x_n,), bool))
    for k in range(1, q_n):
        got = shift(last, "q", k)
        sources += [got, shift(got, "core", 1)]
        bounds_y += [by_q_n] * 2
        bounds_p += [by_q_n] * 2
        there = shift(pair, "q", k).reshape(2, held)[:, by_x_n:]
        codes.append(there.reshape(-1))
        along.append(jnp.zeros((2 * by_q_n,), bool))
    codes, along = jnp.concatenate(codes), jnp.concatenate(along)

    half = col_dev // 2
    panels = sketch.reshape(col_dev, wide, width)
    mine = lax.dynamic_slice_in_dim(panels, ci * half, half, axis=0)
    near = []
    for part in (mine[: half // 2], mine[half // 2 :]):
        near += spread_pieces(jnp.concatenate(spread_pieces(part, "p")), "q")
    sketch_pieces = near + [shift(piece, "core", 1) for piece in near]

    owners = codes // (RB_DEV * col_dev)
    row = codes // col_dev % RB_DEV
    col = codes % col_dev
    o_obs, o_par = owners // par, owners % par
    o_x, o_core = o_obs // 2, o_obs % 2
    o_z, o_y = o_par // q_n, o_par % q_n
    r_par, r_in = row // rows_each, row % rows_each
    r_z, r_y = r_par // q_n, r_par % q_n
    c_x, c_core, c_in = col // (2 * cols_each), col // cols_each % 2, col % cols_each

    per = p_n * rows_each
    groups = q_n + x_n - 1
    other_x = q_n - 1 + (o_x - xi) % x_n
    y_group = jnp.where(along, (r_y - yi) % q_n, jnp.where(o_x == xi, 0, other_x))
    y_slot = (y_group * p_n + (r_z - zi) % p_n) * rows_each + r_in
    y_mine = (o_core == ci) & jnp.where(along, o_x == xi, r_y == yi)
    y_slot = jnp.where(y_mine, y_slot, -1)
    quarter = half // 2
    y_panel = jnp.where(col // half == ci, 0, 2) + col % half // quarter
    y_panel = (y_panel * q_n + (yi - o_y) % q_n) * p_n + (zi - o_z) % p_n
    y_panel = y_panel * quarter + col % quarter

    p_slot = ((c_x - xi) % x_n * q_n + (o_y - yi) % q_n) * p_n + (o_z - zi) % p_n
    p_slot = p_slot * cols_each + c_in
    p_mine = (c_core == ci) & jnp.where(along, o_x == xi, r_y == yi)
    p_slot = jnp.where(p_mine, p_slot, -1)
    in_part = (zi - r_z) % p_n * rows_each + r_in
    same_x = (jnp.where(o_core == ci, 0, q_n) + (yi - r_y) % q_n) * per
    not_x = (2 * q_n + jnp.where(o_core == ci, 0, x_n - 1) + (xi - o_x) % x_n - 1) * per
    p_panel = jnp.where(o_x == xi, same_x, not_x) + in_part

    shapes = []
    for g in range(groups):
        shapes += [jax.ShapeDtypeStruct((per, wide, kc), bf16 if g else f32)] * CHUNKS
    parts = block_products(
        functools.partial(sketch_kernel, bounds_y, len(sketch_pieces)), bounds_y,
        y_slot, y_panel, sources, sketch_pieces, par * col_dev, groups * per, width,
        shapes, "sketch_products",
    )
    own, y_pieces, inverse, gathered = [], [], [], []
    for c in range(CHUNKS):
        by_group = [parts[g * CHUNKS + c] for g in range(groups)]
        total = reduce_stage(by_group[0], by_group[1:q_n], "q")
        total = reduce_stage(total, by_group[q_n:], "x")
        total = total.reshape(p_n, rows_each * wide, kc)
        mine = reduce_stage(total[0], [total[k].astype(bf16) for k in range(1, p_n)], "p")
        own.append(mine)
        line = jnp.concatenate(spread_pieces(mine.astype(bf16), "p"))
        here = jnp.concatenate(spread_pieces(line, "q"))
        there = jnp.concatenate([shift(line, "x", k) for k in range(1, x_n)])
        here_far, there_far = shift(here, "core", 1), shift(there, "core", 1)
        y_pieces += [a.reshape(-1, wide, kc) for a in (here, here_far, there, there_far)]
        gathered.append((here, here_far))
        gram = []
        for before in gathered:
            gram.append(sum(
                lax.dot_general(a, b, (((0,), (0,)), ((), ())), preferred_element_type=f32)
                for a, b in zip(gathered[c], before)
            ))
        joined = jnp.concatenate(gram, axis=1)
        joined = reduce_stage(joined, [joined] * (x_n - 1), "x")
        gram = [joined[:, j * kc : (j + 1) * kc] for j in range(c + 1)]
        inverse.append(inverse_rows(1.0 / all_rows, gram, inverse, width))
    own_rows = jnp.concatenate(own, axis=1)

    slots = x_n * q_n * p_n * cols_each
    kh = width // 2
    shapes = [
        jax.ShapeDtypeStruct((slots // x_n, wide, kh), f32 if k == 0 else bf16) for k in range(x_n)
    ] + [jax.ShapeDtypeStruct((slots // q_n, wide, kh), f32 if k == 0 else bf16) for k in range(q_n)]
    parts = block_products(
        functools.partial(project_kernel, bounds_p, len(y_pieces), x_n, q_n), bounds_p,
        p_slot, p_panel, sources, y_pieces, 2 * groups * per, slots, width,
        shapes, "project_products",
    )
    by_x = reduce_stage(parts[0], parts[1:x_n], "x").reshape(q_n, p_n, cols_each * wide, kh)
    by_x = reduce_stage(by_x[0], [by_x[k].astype(bf16) for k in range(1, q_n)], "q")
    by_q = reduce_stage(parts[x_n], parts[x_n + 1 :], "q").reshape(x_n, p_n, cols_each * wide, kh)
    by_q = reduce_stage(by_q[0], [by_q[k].astype(bf16) for k in range(1, x_n)], "x")
    both = jnp.concatenate([by_x, by_q], axis=2)
    z_rows = reduce_stage(both[0], [both[k].astype(bf16) for k in range(1, p_n)], "p")

    inverse = jnp.concatenate(inverse, axis=0)
    basis = dot32(own_rows, inverse, ((1,), (1,))).astype(bf16)
    projected = dot32(inverse, z_rows, ((1,), (1,)))
    projected = lax.all_to_all(projected, ("x", "core"), split_axis=0, concat_axis=1, tiled=True)
    return (basis, projected)


def solution(mesh):
    obs, par = mesh.shape["obs"], mesh.shape["par"]
    fine = Mesh(mesh.devices.reshape(obs // 2, 2, 4, par // 4), ALL)
    spread = P(ALL)
    placed = (
        P(ALL, None, None),
        P(ALL, None),
        spread,
        spread,
        P(("p", "q"), None),
    )
    return jax.shard_map(
        per_device,
        mesh=fine,
        in_specs=placed,
        out_specs=(P(ALL, None), P(("x", "core"), ("p", "q"))),
        check_vma=False,
    )
```

time: 558 us -> 506 us (0.907)
  other arithmetic: 133 us -> 7.43 us
  starting transfers between devices: 31.1 us -> 126 us
  Pallas kernels: 45.1 us -> 91.2 us
  waiting for transfers between devices: 282 us -> 242 us
  between operations: 17.3 us -> 1.92 us
  matrix products: 24.3 us -> 15.6 us
    another operation x20 -> x5, other arithmetic: 122 us -> 2.36 us  [the longest x14 79 us: per_device(): lower = jnp.linalg.cholesky(gram)]
    ppermute x24 -> x79, starting transfers between devices: 27.5 us -> 123 us  [shift(): lax.ppermute(value, axis, [(i, (i + by) % size) for i in range(size)])]
    all_gather x2 -> x0, waiting for transfers between devices: 76.5 us -> none  [the longest x1 76.5 us: per_device(): lax.all_gather(own_rows.astype(bf16), ('p', 'q'), axis=0, tiled=True)]
    pallas_call x0 -> x4, Pallas kernels: none -> 48.8 us  [inverse_rows(): pl.pallas_call(functools.partial(inverse_kernel, scale, k), out_shape=jax...]
    ppermute x24 -> x79, waiting for transfers between devices: 200 us -> 236 us  [shift(): lax.ppermute(value, axis, [(i, (i + by) % size) for i in range(size)])]
    another operation x17 -> x0, local copies, waits for them, and re-layouts: 11 us -> none
    another operation x13 -> x0, matrix products: 9.67 us -> none  [the longest x7 7.8 us: per_device(): jax.scipy.linalg.solve_triangular(lower, jnp.eye(width, dtype=f32), lower...]
    slice x0 -> x7, local copies, waits for them, and re-layouts: none -> 6.5 us  [the longest x2 5.32 us: per_device(): first, last = (blocks[:by_x_n], blocks[by_x_n:])]
  transfers between devices with their start and end apart: 27 -> 80, of which waited for: 16 -> 39; matrix products, arithmetic and copies ran while one was open for 30% -> 5% of each run, Pallas kernels for 0% -> 10%
where the time goes in v2:
time: 506 us; the launch traced here: 497 us
  waiting for transfers between devices  242 us (48%)
  starting transfers between devices  126 us (25%)
  Pallas kernels  91.2 us (18%)
  matrix products  15.6 us (3%)
  local copies, waits for them, and re-layouts  12.9 us (3%)
  other arithmetic  7.43 us (1%)
    ppermute x79, waiting for transfers between devices, shift(): lax.ppermute(value, axis, [(i, (i + by) % size) for i in range(size)])  236 us
    ppermute x79, starting transfers between devices, shift(): lax.ppermute(value, axis, [(i, (i + by) % size) for i in range(size)])  123 us
    pallas_call x4, Pallas kernels, inverse_rows(): pl.pallas_call(functools.partial(inverse_kernel, scale, k), out_shape=jax...  48.8 us
    pallas_call x2, Pallas kernels, block_products(): pl.pallas_call(kernel, out_shape=outs, in_specs=[smem, smem] + [anywhere]...  42.4 us
    dot_general x20, matrix products, per_device(): lax.dot_general(a, b, (((0,), (0,)), ((), ())), preferred_element_type=f32)  11.1 us
  transfers between devices with their start and end apart: 80, of which 39 were waited for; matrix products, arithmetic and copies ran while one was open for 5% of the time, Pallas kernels for 10%

profile of v2, /device:TPU:0, one launch (start us, length us, event | category | flops | bytes accessed | tf_op | source)
XLA Modules:
  0.0 497.4 jit_solution(6332457294604179906)
XLA Ops:
  0.6 4.0 slice.156
  4.7 2.9 collective-permute-start.4
  8.7 3.7 collective-permute-start.10
  14.7 4.4 collective-permute-done.10
  20.5 5.1 %collective-permute-done.8 = bf16[2,128,512]{2,1,0:T(8,128)(2,1)S(1)} collective-permute-done((bf16[2,128,512]{2,1,0:T(8,128)(2,1)S(1)}, bf16[2,128,512]{2,1,0:T(8,128)(2,1)S(1)}, u32[]{:S(2)}, u32[]{:S(2)}) %collective-permute-start.8) | collective-permute-done | bytes 262176 | tf_op jit(solution)/shard_map/ppermute | solution.py:21
  25.6 9.7 %collective-permute-done.9 = bf16[2,128,512]{2,1,0:T(8,128)(2,1)S(1)} collective-permute-done((bf16[2,128,512]{2,1,0:T(8,128)(2,1)S(1)}, bf16[2,128,512]{2,1,0:T(8,128)(2,1)S(1)}, u32[]{:S(2)}, u32[]{:S(2)}) %collective-permute-start.9) | collective-permute-done | bytes 262176 | tf_op jit(solution)/shard_map/ppermute | solution.py:21
  37.1 38.8 %collective-permute-done.4.refs_2_ = bf16[96,128,128]{2,1,0:T(8,128)(2,1)S(1)} collective-permute-done((bf16[96,128,128]{2,1,0:T(8,128)(2,1)}, bf16[96,128,128]{2,1,0:T(8,128)(2,1)S(1)}, u32[]{:S(2)}, u32[]{:S(2)}) %collective-permute-start.4) | collective-permute-done | bytes 3145760 | tf_op jit(solution)/shard_map/ppermute | solution.py:21
  76.5 4.7 collective-permute-done
  86.6 7.7 %collective-permute-done.12 = bf16[2,128,512]{2,1,0:T(8,128)(2,1)S(1)} collective-permute-done((bf16[2,128,512]{2,1,0:T(8,128)(2,1)S(1)}, bf16[2,128,512]{2,1,0:T(8,128)(2,1)S(1)}, u32[]{:S(2)}, u32[]{:S(2)}) %collective-permute-start.12) | collective-permute-done | bytes 262176 | tf_op jit(solution)/shard_map/ppermute | solution.py:21
  95.0 11.4 %collective-permute-done.13 = bf16[2,128,512]{2,1,0:T(8,128)(2,1)S(1)} collective-permute-done((bf16[2,128,512]{2,1,0:T(8,128)(2,1)S(1)}, bf16[2,128,512]{2,1,0:T(8,128)(2,1)S(1)}, u32[]{:S(2)}, u32[]{:S(2)}) %collective-permute-start.13) | collective-permute-done | bytes 262176 | tf_op jit(solution)/shard_map/ppermute | solution.py:21
  106.4 2.5 collective-permute-start.14
  108.9 5.8 %collective-permute-done.14 = bf16[2,128,512]{2,1,0:T(8,128)(2,1)S(1)} collective-permute-done((bf16[2,128,512]{2,1,0:T(8,128)(2,1)S(1)}, bf16[2,128,512]{2,1,0:T(8,128)(2,1)S(1)}, u32[]{:S(2)}, u32[]{:S(2)}) %collective-permute-start.14) | collective-permute-done | bytes 262176 | tf_op jit(solution)/shard_map/ppermute | solution.py:21
  120.3 21.1 %collective-permute-done.15.refs_9_ = bf16[8,128,512]{2,1,0:T(8,128)(2,1)} collective-permute-done((bf16[8,128,512]{2,1,0:T(8,128)(2,1)S(1)}, bf16[8,128,512]{2,1,0:T(8,128)(2,1)}, u32[]{:S(2)}, u32[]{:S(2)}) %collective-permute-start.15) | collective-permute-done | bytes 1048608 | tf_op jit(solution)/shard_map/ppermute | solution.py:21
  147.4 21.3 %sketch_products.1 = (f32[16,128,128]{2,1,0:T(8,128)}, f32[16,128,128]{2,1,0:T(8,128)}, f32[16,128,128]{2,1,0:T(8,128)}, f32[16,128,128]{2,1,0:T(8,128)}, bf16[1...) custom-call(s32[512]{0:T(512)} %get-tuple-element.80.rows_ref, ...), custom_call_target="tpu_custom_call" | custom-call | flops 2147483648 | bytes 33554432 | tf_op jit(solution)/shard_map/sketch_products/pallas_call | solution.py:185
  168.8 3.4 collective-permute-start.20
  176.2 9.0 %collective-permute-done.20 = bf16[16,128,128]{2,1,0:T(8,128)(2,1)S(1)} collective-permute-done((bf16[16,128,128]{2,1,0:T(8,128)(2,1)}, bf16[16,128,128]{2,1,0:T(8,128)(2,1)S(1)}, u32[]{:S(2)}, u32[]{:S(2)}) %collective-permute-start.20) | collective-permute-done | bytes 524320 | tf_op jit(solution)/shard_map/ppermute | solution.py:21
  189.0 7.4 %collective-permute-done.25 = bf16[16,128,128]{2,1,0:T(8,128)(2,1)S(1)} collective-permute-done((bf16[16,128,128]{2,1,0:T(8,128)(2,1)}, bf16[16,128,128]{2,1,0:T(8,128)(2,1)S(1)}, u32[]{:S(2)}, u32[]{:S(2)}) %collective-permute-start.25) | collective-permute-done | bytes 524320 | tf_op jit(solution)/shard_map/ppermute | solution.py:21
  198.7 9.0 %collective-permute-done.30 = bf16[16,128,128]{2,1,0:T(8,128)(2,1)S(1)} collective-permute-done((bf16[16,128,128]{2,1,0:T(8,128)(2,1)}, bf16[16,128,128]{2,1,0:T(8,128)(2,1)S(1)}, u32[]{:S(2)}, u32[]{:S(2)}) %collective-permute-start.30) | collective-permute-done | bytes 524320 | tf_op jit(solution)/shard_map/ppermute | solution.py:21
  209.7 3.6 collective-permute-start.24
  213.7 3.1 collective-permute-done.35
  216.8 2.1 collective-permute-done.36
  218.9 2.4 collective-permute-start.28
  225.7 2.9 collective-permute-start.34
  228.6 5.5 %collective-permute-done.28 = bf16[512,128]{1,0:T(8,128)(2,1)S(1)} collective-permute-done((bf16[512,128]{1,0:T(8,128)(2,1)S(1)}, bf16[512,128]{1,0:T(8,128)(2,1)S(1)}, u32[]{:S(2)}, u32[]{:S(2)}) %collective-permute-start.28) | collective-permute-done | bytes 131104 | tf_op jit(solution)/shard_map/ppermute | solution.py:21
  234.1 3.9 collective-permute-start.38
  238.8 3.8 collective-permute-start.39
  242.6 3.7 collective-permute-done.33
  248.1 3.4 collective-permute-start.41
  252.7 4.1 collective-permute-done.38
  256.8 2.6 collective-permute-start.46
  259.4 3.4 collective-permute-start.47
  264.0 4.0 collective-permute-done.41
  268.0 2.7 collective-permute-start.52
  270.7 3.4 collective-permute-start.53
  274.6 4.6 collective-permute-done.47
  279.2 2.8 collective-permute-start.58
  282.0 3.4 collective-permute-start.59
  285.9 4.5 collective-permute-done.53
  290.4 2.5 collective-permute-start.43
  292.9 2.3 collective-permute-start.64
  295.4 2.1 collective-permute-start.49
  297.5 3.4 collective-permute-start.66
  302.3 7.7 %collective-permute-start.68 = (bf16[2048,128]{1,0:T(8,128)(2,1)S(1)}, bf16[2048,128]{1,0:T(8,128)(2,1)S(1)}, u32[]{:S(2)}, u32[]{:S(2)}) collective-permute-start(bf16[2048,128]{1,0:T(8,128)(2,1)S(1)} %pad_maximum_fusion.8), channel_id=1, source_target_pairs={{0,16},{16,0},{1,17},{17,1},{2,18},{18,2},{3,19},{19,3},{4,20},{20... | collective-permute-start | bytes 1572872 | tf_op jit(solution)/shard_map/ppermute | solution.py:21
  310.1 3.4 collective-permute-done.49
  313.6 7.7 %collective-permute-start.70 = (bf16[2048,128]{1,0:T(8,128)(2,1)S(1)}, bf16[2048,128]{1,0:T(8,128)(2,1)S(1)}, u32[]{:S(2)}, u32[]{:S(2)}) collective-permute-start(bf16[2048,128]{1,0:T(8,128)(2,1)S(1)} %pad_maximum_fusion.9), channel_id=1, source_target_pairs={{0,16},{16,0},{1,17},{17,1},{2,18},{18,2},{3,19},{19,3},{4,20},{20... | collective-permute-start | bytes 1572872 | tf_op jit(solution)/shard_map/ppermute | solution.py:21
  321.3 3.5 collective-permute-done.55
  325.0 5.5 %collective-permute-done.68 = bf16[2048,128]{1,0:T(8,128)(2,1)S(1)} collective-permute-done((bf16[2048,128]{1,0:T(8,128)(2,1)S(1)}, bf16[2048,128]{1,0:T(8,128)(2,1)S(1)}, u32[]{:S(2)}, u32[]{:S(2)}) %collective-permute-start.68) | collective-permute-done | bytes 524320 | tf_op jit(solution)/shard_map/ppermute | solution.py:21
  330.5 3.3 collective-permute-done.61
  333.9 7.2 %collective-permute-done.70 = bf16[2048,128]{1,0:T(8,128)(2,1)S(1)} collective-permute-done((bf16[2048,128]{1,0:T(8,128)(2,1)S(1)}, bf16[2048,128]{1,0:T(8,128)(2,1)S(1)}, u32[]{:S(2)}, u32[]{:S(2)}) %collective-permute-start.70) | collective-permute-done | bytes 524320 | tf_op jit(solution)/shard_map/ppermute | solution.py:21
  342.1 5.4 %collective-permute-done.71 = bf16[2048,128]{1,0:T(8,128)(2,1)S(1)} collective-permute-done((bf16[2048,128]{1,0:T(8,128)(2,1)S(1)}, bf16[2048,128]{1,0:T(8,128)(2,1)S(1)}, u32[]{:S(2)}, u32[]{:S(2)}) %collective-permute-start.71) | collective-permute-done | bytes 524320 | tf_op jit(solution)/shard_map/ppermute | solution.py:21
  349.7 21.1 %project_products.1 = (f32[16,128,256]{2,1,0:T(8,128)}, bf16[16,128,256]{2,1,0:T(8,128)(2,1)}, f32[16,128,256]{2,1,0:T(8,128)}, bf16[16,128,256]{2,1,0:T(8,128)(2,1)}) custom-call(s32[512]{0:T(512)} %get-tuple-element.79.rows_ref, s32[512]{0:T(512)} %get-tuple-element.34.cols_ref, bf16[128,128,128]{2,1,0:T(8,128)(2,1)} %refs_0_.3, ...), custom_call_target="tpu_custom_call" | custom-call | flops 2147483648 | bytes 33554432 | tf_op jit(solution)/shard_map/project_products/pallas_call | solution.py:185
  370.8 3.4 collective-permute-start.74
  375.0 2.0 fusion.101
  390.0 18.5 %collective-permute-done.45 = f32[128,128]{1,0:T(8,128)S(1)} collective-permute-done((f32[128,128]{1,0:T(8,128)S(1)}, f32[128,128]{1,0:T(8,128)S(1)}, u32[]{:S(2)}, u32[]{:S(2)}) %collective-permute-start.45) | collective-permute-done | bytes 65568 | tf_op jit(solution)/shard_map/ppermute | solution.py:21
  409.1 11.1 %inverse_rows.4.refs_2_.refs_3_.refs_4_ = f32[128,512]{1,0:T(8,128)S(1)} custom-call(f32[128,128]{1,0:T(8,128)S(1)} %add.321.refs_0_), custom_call_target="tpu_custom_call" | custom-call | flops 12884901888 | bytes 1048576 | tf_op jit(solution)/shard_map/inverse_rows/pallas_call | solution.py:253
  420.2 11.7 %inverse_rows.5.refs_4_.refs_5_ = f32[128,512]{1,0:T(8,128)S(1)} custom-call(f32[128,128]{1,0:T(8,128)S(1)} %get-tuple-element.78.refs_0_, f32[128,128]{1,0:T(8,128)S(1)} %get-tuple-element.77.refs_1_, f32[128,512]{1,0:T(8,128)S(1)} %inverse_rows.4.refs_2_.refs_3_.refs_4_), custom_call_target="tpu_custom_call" | custom-call | flops 12884901888 | bytes 1048576 | tf_op jit(solution)/shard_map/inverse_rows/pallas_call | solution.py:253
  432.0 12.6 %inverse_rows.6.refs_6_ = f32[128,512]{1,0:T(8,128)S(1)} custom-call(f32[128,128]{1,0:T(8,128)S(1)} %get-tuple-element.76.refs_0_, f32[128,128]{1,0:T(8,128)S(1)} %get-tuple-element.75.refs_1_, f32[128,128]{1,0:T(8,128)S(1)} %get-tuple-element.74.refs_2_, f32[128,512]{1,0:T(8,128)S(1)} %inverse_rows.4.refs_2_.refs_3_.refs_4_, ...), custom_call_target="tpu_custom_call" | custom-call | flops 12884901888 | bytes 1048576 | tf_op jit(solution)/shard_map/inverse_rows/pallas_call | solution.py:253
  448.6 10.3 %collective-permute-done.75 = bf16[4,256,256]{2,1,0:T(8,128)(2,1)S(1)} collective-permute-done((bf16[4,256,256]{2,1,0:T(8,128)(2,1)S(1)}, bf16[4,256,256]{2,1,0:T(8,128)(2,1)S(1)}, u32[]{:S(2)}, u32[]{:S(2)}) %collective-permute-start.75) | collective-permute-done | bytes 524320 | tf_op jit(solution)/shard_map/ppermute | solution.py:21
  459.1 2.2 collective-permute-done.73
  461.6 3.3 collective-permute-start.76
  467.3 13.5 %inverse_rows.7 = f32[128,512]{1,0:T(8,128)S(1)} custom-call(f32[128,128]{1,0:T(8,128)S(1)} %get-tuple-element.73.refs_0_, f32[128,128]{1,0:T(8,128)S(1)} %get-tuple-element.72.refs_1_, f32[128,128]{1,0:T(8,128)S(1)} %get-tuple-element.71.refs_2_, f32[128,128]{1,0:T(8,128)S(1)} %get-tuple-element.70.refs_3_, ...), custom_call_target="tpu_custom_call" | custom-call | flops 12884901888 | bytes 1048576 | tf_op jit(solution)/shard_map/inverse_rows/pallas_call | solution.py:253
  484.1 3.5 all-to-all-start
  487.6 2.7 convolution_convert_fusion
  490.3 6.1 %all-to-all-done = f32[4,128,256]{2,1,0:T(8,128)S(1)} async-done(((f32[4,128,256]{2,1,0:T(8,128)}), f32[4,128,256]{2,1,0:T(8,128)S(1)}, u32[]{:S(2)}, u32[]{:S(2)}) %all-to-all-start) | async-done | bytes 524320 | tf_op jit(solution)/shard_map/all_to_all | solution.py:398
  (284 shorter events, 78.0 us)
Async XLA Ops:
  4.7 71.2 %collective-permute-start.4 = (bf16[96,128,128]{2,1,0:T(8,128)(2,1)}, bf16[96,128,128]{2,1,0:T(8,128)(2,1)S(1)}, u32[]{:S(2)}, u32[]{:S(2)}) collective-permute-start(bf16[96,128,128]{2,1,0:T(8,128)(2,1)} %slice.156), channel_id=1, source_target_pairs={{0,16},{16,0},{1,17},{17,1},{2,18},{18,2},{3,19},{19,3},{4,20},{20... | collective-permute-start | bytes 9437192 | tf_op jit(solution)/shard_map/ppermute | solution.py:21
  7.6 139.8 %collective-permute-start.3 = (bf16[128,128,128]{2,1,0:T(8,128)(2,1)}, bf16[128,128,128]{2,1,0:T(8,128)(2,1)}, u32[]{:S(2)}, u32[]{:S(2)}) collective-permute-start(bf16[128,128,128]{2,1,0:T(8,128)(2,1)} %refs_0_.3), channel_id=1, source_target_pairs={{0,8},{8,0},{1,9},{9,1},{2,10},{10,2},{3,11},{11,3},{4,12},{12,4},... | collective-permute-start | bytes 12582920 | tf_op jit(solution)/shard_map/ppermute | solution.py:21
  12.4 13.2 %collective-permute-start.8 = (bf16[2,128,512]{2,1,0:T(8,128)(2,1)S(1)}, bf16[2,128,512]{2,1,0:T(8,128)(2,1)S(1)}, u32[]{:S(2)}, u32[]{:S(2)}) collective-permute-start(bf16[2,128,512]{2,1,0:T(8,128)(2,1)S(1)} %get-tuple-element.57), channel_id=1, source_target_pairs={{0,2},{2,4},{4,6},{6,0},{1,3},{3,5},{5,7},{7,1},{8,10},{10,12},{12... | collective-permute-start | bytes 786440 | tf_op jit(solution)/shard_map/ppermute | solution.py:21
  12.4 23.0 %collective-permute-start.9 = (bf16[2,128,512]{2,1,0:T(8,128)(2,1)S(1)}, bf16[2,128,512]{2,1,0:T(8,128)(2,1)S(1)}, u32[]{:S(2)}, u32[]{:S(2)}) collective-permute-start(bf16[2,128,512]{2,1,0:T(8,128)(2,1)S(1)} %get-tuple-element.57), channel_id=1, source_target_pairs={{0,4},{2,6},{4,0},{6,2},{1,5},{3,7},{5,1},{7,3},{8,12},{10,14},{12... | collective-permute-start | bytes 786440 | tf_op jit(solution)/shard_map/ppermute | solution.py:21
  19.0 100.7 %collective-permute-start.6 = (bf16[32,128,128]{2,1,0:T(8,128)(2,1)S(1)}, bf16[32,128,128]{2,1,0:T(8,128)(2,1)}, u32[]{:S(2)}, u32[]{:S(2)}) collective-permute-start(bf16[32,128,128]{2,1,0:T(8,128)(2,1)S(1)} %slice.157), channel_id=1, source_target_pairs={{0,1},{1,0},{2,3},{3,2},{4,5},{5,4},{6,7},{7,6},{8,9},{9,8},{10,11... | collective-permute-start | bytes 3145736 | tf_op jit(solution)/shard_map/ppermute | solution.py:21
  35.5 84.3 %collective-permute-start.11 = (bf16[8,128,512]{2,1,0:T(8,128)(2,1)S(1)}, bf16[8,128,512]{2,1,0:T(8,128)(2,1)}, u32[]{:S(2)}, u32[]{:S(2)}) collective-permute-start(bf16[8,128,512]{2,1,0:T(8,128)(2,1)S(1)} %pad_maximum_fusion.1.refs_6_), channel_id=1, source_target_pairs={{0,1},{1,0},{2,3},{3,2},{4,5},{5,4},{6,7},{7,6},{8,9},{9,8},{10,11... | collective-permute-start | bytes 3145736 | tf_op jit(solution)/shard_map/ppermute | solution.py:21
  75.9 71.5 %collective-permute-start.5 = (bf16[96,128,128]{2,1,0:T(8,128)(2,1)S(1)}, bf16[96,128,128]{2,1,0:T(8,128)(2,1)}, u32[]{:S(2)}, u32[]{:S(2)}) collective-permute-start(bf16[96,128,128]{2,1,0:T(8,128)(2,1)S(1)} %collective-permute-done.4.refs_2_), channel_id=1, source_target_pairs={{0,8},{8,0},{1,9},{9,1},{2,10},{10,2},{3,11},{11,3},{4,12},{12,4},... | collective-permute-start | bytes 9437192 | tf_op jit(solution)/shard_map/ppermute | solution.py:21
  94.3 12.1 %collective-permute-start.13 = (bf16[2,128,512]{2,1,0:T(8,128)(2,1)S(1)}, bf16[2,128,512]{2,1,0:T(8,128)(2,1)S(1)}, u32[]{:S(2)}, u32[]{:S(2)}) collective-permute-start(bf16[2,128,512]{2,1,0:T(8,128)(2,1)S(1)} %get-tuple-element.56), channel_id=1, source_target_pairs={{0,4},{2,6},{4,0},{6,2},{1,5},{3,7},{5,1},{7,3},{8,12},{10,14},{12... | collective-permute-start | bytes 786440 | tf_op jit(solution)/shard_map/ppermute | solution.py:21
  118.2 23.2 %collective-permute-start.15 = (bf16[8,128,512]{2,1,0:T(8,128)(2,1)S(1)}, bf16[8,128,512]{2,1,0:T(8,128)(2,1)}, u32[]{:S(2)}, u32[]{:S(2)}) collective-permute-start(bf16[8,128,512]{2,1,0:T(8,128)(2,1)S(1)} %pad_maximum_fusion.2.refs_8_), channel_id=1, source_target_pairs={{0,1},{1,0},{2,3},{3,2},{4,5},{5,4},{6,7},{7,6},{8,9},{9,8},{10,11... | collective-permute-start | bytes 3145736 | tf_op jit(solution)/shard_map/ppermute | solution.py:21
  119.7 21.7 %collective-permute-start.16 = (bf16[8,128,512]{2,1,0:T(8,128)(2,1)S(1)}, bf16[8,128,512]{2,1,0:T(8,128)(2,1)S(1)}, u32[]{:S(2)}, u32[]{:S(2)}) collective-permute-start(bf16[8,128,512]{2,1,0:T(8,128)(2,1)S(1)} %pad_maximum_fusion.1.refs_6_), channel_id=1, source_target_pairs={{0,8},{8,0},{1,9},{9,1},{2,10},{10,2},{3,11},{11,3},{4,12},{12,4},... | collective-permute-start | bytes 3145736 | tf_op jit(solution)/shard_map/ppermute | solution.py:21
  119.8 22.2 %collective-permute-start.18 = (bf16[8,128,512]{2,1,0:T(8,128)(2,1)S(1)}, bf16[8,128,512]{2,1,0:T(8,128)(2,1)S(1)}, u32[]{:S(2)}, u32[]{:S(2)}) collective-permute-start(bf16[8,128,512]{2,1,0:T(8,128)(2,1)S(1)} %pad_maximum_fusion.2.refs_8_), channel_id=1, source_target_pairs={{0,8},{8,0},{1,9},{9,1},{2,10},{10,2},{3,11},{11,3},{4,12},{12,4},... | collective-permute-start | bytes 3145736 | tf_op jit(solution)/shard_map/ppermute | solution.py:21
  168.8 16.4 %collective-permute-start.20 = (bf16[16,128,128]{2,1,0:T(8,128)(2,1)}, bf16[16,128,128]{2,1,0:T(8,128)(2,1)S(1)}, u32[]{:S(2)}, u32[]{:S(2)}) collective-permute-start(bf16[16,128,128]{2,1,0:T(8,128)(2,1)} %get-tuple-element.19), channel_id=1, source_target_pairs={{0,1},{1,0},{2,3},{3,2},{4,5},{5,4},{6,7},{7,6},{8,9},{9,8},{10,11... | collective-permute-start | bytes 1572872 | tf_op jit(solution)/shard_map/ppermute | solution.py:21
  172.1 15.1 %collective-permute-start.21 = (bf16[16,128,128]{2,1,0:T(8,128)(2,1)}, bf16[16,128,128]{2,1,0:T(8,128)(2,1)S(1)}, u32[]{:S(2)}, u32[]{:S(2)}) collective-permute-start(bf16[16,128,128]{2,1,0:T(8,128)(2,1)} %get-tuple-element.20), channel_id=1, source_target_pairs={{0,16},{16,0},{1,17},{17,1},{2,18},{18,2},{3,19},{19,3},{4,20},{20... | collective-permute-start | bytes 1572872 | tf_op jit(solution)/shard_map/ppermute | solution.py:21
  172.4 24.0 %collective-permute-start.25 = (bf16[16,128,128]{2,1,0:T(8,128)(2,1)}, bf16[16,128,128]{2,1,0:T(8,128)(2,1)S(1)}, u32[]{:S(2)}, u32[]{:S(2)}) collective-permute-start(bf16[16,128,128]{2,1,0:T(8,128)(2,1)} %get-tuple-element.22), channel_id=1, source_target_pairs={{0,1},{1,0},{2,3},{3,2},{4,5},{5,4},{6,7},{7,6},{8,9},{9,8},{10,11... | collective-permute-start | bytes 1572872 | tf_op jit(solution)/shard_map/ppermute | solution.py:21
  173.5 24.9 %collective-permute-start.26 = (bf16[16,128,128]{2,1,0:T(8,128)(2,1)}, bf16[16,128,128]{2,1,0:T(8,128)(2,1)S(1)}, u32[]{:S(2)}, u32[]{:S(2)}) collective-permute-start(bf16[16,128,128]{2,1,0:T(8,128)(2,1)} %get-tuple-element.23), channel_id=1, source_target_pairs={{0,16},{16,0},{1,17},{17,1},{2,18},{18,2},{3,19},{19,3},{4,20},{20... | collective-permute-start | bytes 1572872 | tf_op jit(solution)/shard_map/ppermute | solution.py:21
  174.2 33.4 %collective-permute-start.30 = (bf16[16,128,128]{2,1,0:T(8,128)(2,1)}, bf16[16,128,128]{2,1,0:T(8,128)(2,1)S(1)}, u32[]{:S(2)}, u32[]{:S(2)}) collective-permute-start(bf16[16,128,128]{2,1,0:T(8,128)(2,1)} %get-tuple-element.25), channel_id=1, source_target_pairs={{0,1},{1,0},{2,3},{3,2},{4,5},{5,4},{6,7},{7,6},{8,9},{9,8},{10,11... | collective-permute-start | bytes 1572872 | tf_op jit(solution)/shard_map/ppermute | solution.py:21
  185.2 24.5 %collective-permute-start.31 = (bf16[16,128,128]{2,1,0:T(8,128)(2,1)}, bf16[16,128,128]{2,1,0:T(8,128)(2,1)S(1)}, u32[]{:S(2)}, u32[]{:S(2)}) collective-permute-start(bf16[16,128,128]{2,1,0:T(8,128)(2,1)} %get-tuple-element.26), channel_id=1, source_target_pairs={{0,16},{16,0},{1,17},{17,1},{2,18},{18,2},{3,19},{19,3},{4,20},{20... | collective-permute-start | bytes 1572872 | tf_op jit(solution)/shard_map/ppermute | solution.py:21
  187.2 29.6 %collective-permute-start.35 = (bf16[16,128,128]{2,1,0:T(8,128)(2,1)}, bf16[16,128,128]{2,1,0:T(8,128)(2,1)S(1)}, u32[]{:S(2)}, u32[]{:S(2)}) collective-permute-start(bf16[16,128,128]{2,1,0:T(8,128)(2,1)} %get-tuple-element.28), channel_id=1, source_target_pairs={{0,1},{1,0},{2,3},{3,2},{4,5},{5,4},{6,7},{7,6},{8,9},{9,8},{10,11... | collective-permute-start | bytes 1572872 | tf_op jit(solution)/shard_map/ppermute | solution.py:21
  196.4 22.5 %collective-permute-start.36 = (bf16[16,128,128]{2,1,0:T(8,128)(2,1)S(1)}, bf16[16,128,128]{2,1,0:T(8,128)(2,1)S(1)}, u32[]{:S(2)}, u32[]{:S(2)}) collective-permute-start(bf16[16,128,128]{2,1,0:T(8,128)(2,1)S(1)} %copy-done.42), channel_id=1, source_target_pairs={{0,16},{16,0},{1,17},{17,1},{2,18},{18,2},{3,19},{19,3},{4,20},{20... | collective-permute-start | bytes 1572872 | tf_op jit(solution)/shard_map/ppermute | solution.py:21
  198.4 23.1 %collective-permute-start.22 = (bf16[512,128]{1,0:T(8,128)(2,1)S(1)}, bf16[512,128]{1,0:T(8,128)(2,1)S(1)}, u32[]{:S(2)}, u32[]{:S(2)}) collective-permute-start(bf16[512,128]{1,0:T(8,128)(2,1)S(1)} %bitcast.160), channel_id=1, source_target_pairs={{0,2},{2,4},{4,6},{6,0},{1,3},{3,5},{5,7},{7,1},{8,10},{10,12},{12... | collective-permute-start | bytes 393224 | tf_op jit(solution)/shard_map/ppermute | solution.py:21
  207.7 15.8 %collective-permute-start.23 = (bf16[512,128]{1,0:T(8,128)(2,1)S(1)}, bf16[512,128]{1,0:T(8,128)(2,1)S(1)}, u32[]{:S(2)}, u32[]{:S(2)}) collective-permute-start(bf16[512,128]{1,0:T(8,128)(2,1)S(1)} %bitcast.157), channel_id=1, source_target_pairs={{0,4},{2,6},{4,0},{6,2},{1,5},{3,7},{5,1},{7,3},{8,12},{10,14},{12... | collective-permute-start | bytes 393224 | tf_op jit(solution)/shard_map/ppermute | solution.py:21
  209.7 14.5 %collective-permute-start.24 = (bf16[512,128]{1,0:T(8,128)(2,1)S(1)}, bf16[512,128]{1,0:T(8,128)(2,1)S(1)}, u32[]{:S(2)}, u32[]{:S(2)}) collective-permute-start(bf16[512,128]{1,0:T(8,128)(2,1)S(1)} %bitcast.154), channel_id=1, source_target_pairs={{0,6},{2,0},{4,2},{6,4},{1,7},{3,1},{5,3},{7,5},{8,14},{10,8},{12,... | collective-permute-start | bytes 393224 | tf_op jit(solution)/shard_map/ppermute | solution.py:21
  218.9 15.2 %collective-permute-start.28 = (bf16[512,128]{1,0:T(8,128)(2,1)S(1)}, bf16[512,128]{1,0:T(8,128)(2,1)S(1)}, u32[]{:S(2)}, u32[]{:S(2)}) collective-permute-start(bf16[512,128]{1,0:T(8,128)(2,1)S(1)} %bitcast.162), channel_id=1, source_target_pairs={{0,4},{2,6},{4,0},{6,2},{1,5},{3,7},{5,1},{7,3},{8,12},{10,14},{12... | collective-permute-start | bytes 393224 | tf_op jit(solution)/shard_map/ppermute | solution.py:21
  221.6 12.5 %collective-permute-start.29 = (bf16[512,128]{1,0:T(8,128)(2,1)S(1)}, bf16[512,128]{1,0:T(8,128)(2,1)S(1)}, u32[]{:S(2)}, u32[]{:S(2)}) collective-permute-start(bf16[512,128]{1,0:T(8,128)(2,1)S(1)} %bitcast.161), channel_id=1, source_target_pairs={{0,6},{2,0},{4,2},{6,4},{1,7},{3,1},{5,3},{7,5},{8,14},{10,8},{12,... | collective-permute-start | bytes 393224 | tf_op jit(solution)/shard_map/ppermute | solution.py:21
  223.5 15.3 %collective-permute-start.32 = (bf16[512,128]{1,0:T(8,128)(2,1)S(1)}, bf16[512,128]{1,0:T(8,128)(2,1)S(1)}, u32[]{:S(2)}, u32[]{:S(2)}) collective-permute-start(bf16[512,128]{1,0:T(8,128)(2,1)S(1)} %bitcast.159), channel_id=1, source_target_pairs={{0,2},{2,4},{4,6},{6,0},{1,3},{3,5},{5,7},{7,1},{8,10},{10,12},{12... | collective-permute-start | bytes 393224 | tf_op jit(solution)/shard_map/ppermute | solution.py:21
  224.1 22.1 %collective-permute-start.33 = (bf16[512,128]{1,0:T(8,128)(2,1)S(1)}, bf16[512,128]{1,0:T(8,128)(2,1)S(1)}, u32[]{:S(2)}, u32[]{:S(2)}) collective-permute-start(bf16[512,128]{1,0:T(8,128)(2,1)S(1)} %bitcast.156), channel_id=1, source_target_pairs={{0,4},{2,6},{4,0},{6,2},{1,5},{3,7},{5,1},{7,3},{8,12},{10,14},{12... | collective-permute-start | bytes 393224 | tf_op jit(solution)/shard_map/ppermute | solution.py:21
  225.7 22.5 %collective-permute-start.34 = (bf16[512,128]{1,0:T(8,128)(2,1)S(1)}, bf16[512,128]{1,0:T(8,128)(2,1)S(1)}, u32[]{:S(2)}, u32[]{:S(2)}) collective-permute-start(bf16[512,128]{1,0:T(8,128)(2,1)S(1)} %bitcast.153), channel_id=1, source_target_pairs={{0,6},{2,0},{4,2},{6,4},{1,7},{3,1},{5,3},{7,5},{8,14},{10,8},{12,... | collective-permute-start | bytes 393224 | tf_op jit(solution)/shard_map/ppermute | solution.py:21
  234.1 18.2 %collective-permute-start.37 = (bf16[512,128]{1,0:T(8,128)(2,1)S(1)}, bf16[512,128]{1,0:T(8,128)(2,1)S(1)}, u32[]{:S(2)}, u32[]{:S(2)}) collective-permute-start(bf16[512,128]{1,0:T(8,128)(2,1)S(1)} %bitcast.158), channel_id=1, source_target_pairs={{0,2},{2,4},{4,6},{6,0},{1,3},{3,5},{5,7},{7,1},{8,10},{10,12},{12... | collective-permute-start | bytes 393224 | tf_op jit(solution)/shard_map/ppermute | solution.py:21
  234.1 22.7 %collective-permute-start.38 = (bf16[512,128]{1,0:T(8,128)(2,1)S(1)}, bf16[512,128]{1,0:T(8,128)(2,1)S(1)}, u32[]{:S(2)}, u32[]{:S(2)}) collective-permute-start(bf16[512,128]{1,0:T(8,128)(2,1)S(1)} %bitcast.155), channel_id=1, source_target_pairs={{0,4},{2,6},{4,0},{6,2},{1,5},{3,7},{5,1},{7,3},{8,12},{10,14},{12... | collective-permute-start | bytes 393224 | tf_op jit(solution)/shard_map/ppermute | solution.py:21
  238.8 20.7 %collective-permute-start.39 = (bf16[512,128]{1,0:T(8,128)(2,1)S(1)}, bf16[512,128]{1,0:T(8,128)(2,1)S(1)}, u32[]{:S(2)}, u32[]{:S(2)}) collective-permute-start(bf16[512,128]{1,0:T(8,128)(2,1)S(1)} %bitcast.152), channel_id=1, source_target_pairs={{0,6},{2,0},{4,2},{6,4},{1,7},{3,1},{5,3},{7,5},{8,14},{10,8},{12,... | collective-permute-start | bytes 393224 | tf_op jit(solution)/shard_map/ppermute | solution.py:21
  246.2 17.3 %collective-permute-start.40 = (bf16[512,128]{1,0:T(8,128)(2,1)S(1)}, bf16[512,128]{1,0:T(8,128)(2,1)S(1)}, u32[]{:S(2)}, u32[]{:S(2)}) collective-permute-start(bf16[512,128]{1,0:T(8,128)(2,1)S(1)} %get-tuple-element.38), channel_id=1, source_target_pairs={{0,2},{2,4},{4,6},{6,0},{1,3},{3,5},{5,7},{7,1},{8,10},{10,12},{12... | collective-permute-start | bytes 393224 | tf_op jit(solution)/shard_map/ppermute | solution.py:21
  248.1 19.8 %collective-permute-start.41 = (bf16[512,128]{1,0:T(8,128)(2,1)S(1)}, bf16[512,128]{1,0:T(8,128)(2,1)S(1)}, u32[]{:S(2)}, u32[]{:S(2)}) collective-permute-start(bf16[512,128]{1,0:T(8,128)(2,1)S(1)} %get-tuple-element.38), channel_id=1, source_target_pairs={{0,4},{2,6},{4,0},{6,2},{1,5},{3,7},{5,1},{7,3},{8,12},{10,14},{12... | collective-permute-start | bytes 393224 | tf_op jit(solution)/shard_map/ppermute | solution.py:21
  252.3 18.4 %collective-permute-start.42 = (bf16[512,128]{1,0:T(8,128)(2,1)S(1)}, bf16[512,128]{1,0:T(8,128)(2,1)S(1)}, u32[]{:S(2)}, u32[]{:S(2)}) collective-permute-start(bf16[512,128]{1,0:T(8,128)(2,1)S(1)} %get-tuple-element.38), channel_id=1, source_target_pairs={{0,6},{2,0},{4,2},{6,4},{1,7},{3,1},{5,3},{7,5},{8,14},{10,8},{12,... | collective-permute-start | bytes 393224 | tf_op jit(solution)/shard_map/ppermute | solution.py:21
  256.8 17.4 %collective-permute-start.46 = (bf16[512,128]{1,0:T(8,128)(2,1)S(1)}, bf16[512,128]{1,0:T(8,128)(2,1)S(1)}, u32[]{:S(2)}, u32[]{:S(2)}) collective-permute-start(bf16[512,128]{1,0:T(8,128)(2,1)S(1)} %get-tuple-element.40), channel_id=1, source_target_pairs={{0,2},{2,4},{4,6},{6,0},{1,3},{3,5},{5,7},{7,1},{8,10},{10,12},{12... | collective-permute-start | bytes 393224 | tf_op jit(solution)/shard_map/ppermute | solution.py:21
  259.4 19.8 %collective-permute-start.47 = (bf16[512,128]{1,0:T(8,128)(2,1)S(1)}, bf16[512,128]{1,0:T(8,128)(2,1)S(1)}, u32[]{:S(2)}, u32[]{:S(2)}) collective-permute-start(bf16[512,128]{1,0:T(8,128)(2,1)S(1)} %get-tuple-element.40), channel_id=1, source_target_pairs={{0,4},{2,6},{4,0},{6,2},{1,5},{3,7},{5,1},{7,3},{8,12},{10,14},{12... | collective-permute-start | bytes 393224 | tf_op jit(solution)/shard_map/ppermute | solution.py:21
  263.6 18.4 %collective-permute-start.48 = (bf16[512,128]{1,0:T(8,128)(2,1)S(1)}, bf16[512,128]{1,0:T(8,128)(2,1)S(1)}, u32[]{:S(2)}, u32[]{:S(2)}) collective-permute-start(bf16[512,128]{1,0:T(8,128)(2,1)S(1)} %get-tuple-element.40), channel_id=1, source_target_pairs={{0,6},{2,0},{4,2},{6,4},{1,7},{3,1},{5,3},{7,5},{8,14},{10,8},{12,... | collective-permute-start | bytes 393224 | tf_op jit(solution)/shard_map/ppermute | solution.py:21
  268.0 17.5 %collective-permute-start.52 = (bf16[512,128]{1,0:T(8,128)(2,1)S(1)}, bf16[512,128]{1,0:T(8,128)(2,1)S(1)}, u32[]{:S(2)}, u32[]{:S(2)}) collective-permute-start(bf16[512,128]{1,0:T(8,128)(2,1)S(1)} %get-tuple-element.42), channel_id=1, source_target_pairs={{0,2},{2,4},{4,6},{6,0},{1,3},{3,5},{5,7},{7,1},{8,10},{10,12},{12... | collective-permute-start | bytes 393224 | tf_op jit(solution)/shard_map/ppermute | solution.py:21
  270.7 19.7 %collective-permute-start.53 = (bf16[512,128]{1,0:T(8,128)(2,1)S(1)}, bf16[512,128]{1,0:T(8,128)(2,1)S(1)}, u32[]{:S(2)}, u32[]{:S(2)}) collective-permute-start(bf16[512,128]{1,0:T(8,128)(2,1)S(1)} %get-tuple-element.42), channel_id=1, source_target_pairs={{0,4},{2,6},{4,0},{6,2},{1,5},{3,7},{5,1},{7,3},{8,12},{10,14},{12... | collective-permute-start | bytes 393224 | tf_op jit(solution)/shard_map/ppermute | solution.py:21
  274.2 18.7 %collective-permute-start.54 = (bf16[512,128]{1,0:T(8,128)(2,1)S(1)}, bf16[512,128]{1,0:T(8,128)(2,1)S(1)}, u32[]{:S(2)}, u32[]{:S(2)}) collective-permute-start(bf16[512,128]{1,0:T(8,128)(2,1)S(1)} %get-tuple-element.42), channel_id=1, source_target_pairs={{0,6},{2,0},{4,2},{6,4},{1,7},{3,1},{5,3},{7,5},{8,14},{10,8},{12,... | collective-permute-start | bytes 393224 | tf_op jit(solution)/shard_map/ppermute | solution.py:21
  279.2 16.2 %collective-permute-start.58 = (bf16[512,128]{1,0:T(8,128)(2,1)S(1)}, bf16[512,128]{1,0:T(8,128)(2,1)S(1)}, u32[]{:S(2)}, u32[]{:S(2)}) collective-permute-start(bf16[512,128]{1,0:T(8,128)(2,1)S(1)} %get-tuple-element.44), channel_id=1, source_target_pairs={{0,2},{2,4},{4,6},{6,0},{1,3},{3,5},{5,7},{7,1},{8,10},{10,12},{12... | collective-permute-start | bytes 393224 | tf_op jit(solution)/shard_map/ppermute | solution.py:21
  282.0 15.5 %collective-permute-start.59 = (bf16[512,128]{1,0:T(8,128)(2,1)S(1)}, bf16[512,128]{1,0:T(8,128)(2,1)S(1)}, u32[]{:S(2)}, u32[]{:S(2)}) collective-permute-start(bf16[512,128]{1,0:T(8,128)(2,1)S(1)} %get-tuple-element.44), channel_id=1, source_target_pairs={{0,4},{2,6},{4,0},{6,2},{1,5},{3,7},{5,1},{7,3},{8,12},{10,14},{12... | collective-permute-start | bytes 393224 | tf_op jit(solution)/shard_map/ppermute | solution.py:21
  285.5 15.4 %collective-permute-start.60 = (bf16[512,128]{1,0:T(8,128)(2,1)S(1)}, bf16[512,128]{1,0:T(8,128)(2,1)S(1)}, u32[]{:S(2)}, u32[]{:S(2)}) collective-permute-start(bf16[512,128]{1,0:T(8,128)(2,1)S(1)} %get-tuple-element.44), channel_id=1, source_target_pairs={{0,6},{2,0},{4,2},{6,4},{1,7},{3,1},{5,3},{7,5},{8,14},{10,8},{12,... | collective-permute-start | bytes 393224 | tf_op jit(solution)/shard_map/ppermute | solution.py:21
  292.9 17.1 %collective-permute-start.64 = (bf16[2048,128]{1,0:T(8,128)(2,1)S(1)}, bf16[2048,128]{1,0:T(8,128)(2,1)S(1)}, u32[]{:S(2)}, u32[]{:S(2)}) collective-permute-start(bf16[2048,128]{1,0:T(8,128)(2,1)S(1)} %pad_maximum_fusion.6), channel_id=1, source_target_pairs={{0,16},{16,0},{1,17},{17,1},{2,18},{18,2},{3,19},{19,3},{4,20},{20... | collective-permute-start | bytes 1572872 | tf_op jit(solution)/shard_map/ppermute | solution.py:21
  295.4 18.2 %collective-permute-start.49 = (bf16[2048,128]{1,0:T(8,128)(2,1)S(1)}, bf16[2048,128]{1,0:T(8,128)(2,1)S(1)}, u32[]{:S(2)}, u32[]{:S(2)}) collective-permute-start(bf16[2048,128]{1,0:T(8,128)(2,1)S(1)} %pad_maximum_fusion.7), channel_id=1, source_target_pairs={{0,1},{1,0},{2,3},{3,2},{4,5},{5,4},{6,7},{7,6},{8,9},{9,8},{10,11... | collective-permute-start | bytes 1572872 | tf_op jit(solution)/shard_map/ppermute | solution.py:21
  297.5 23.8 %collective-permute-start.66 = (bf16[2048,128]{1,0:T(8,128)(2,1)S(1)}, bf16[2048,128]{1,0:T(8,128)(2,1)S(1)}, u32[]{:S(2)}, u32[]{:S(2)}) collective-permute-start(bf16[2048,128]{1,0:T(8,128)(2,1)S(1)} %pad_maximum_fusion.7), channel_id=1, source_target_pairs={{0,16},{16,0},{1,17},{17,1},{2,18},{18,2},{3,19},{19,3},{4,20},{20... | collective-permute-start | bytes 1572872 | tf_op jit(solution)/shard_map/ppermute | solution.py:21
  300.9 23.9 %collective-permute-start.55 = (bf16[2048,128]{1,0:T(8,128)(2,1)S(1)}, bf16[2048,128]{1,0:T(8,128)(2,1)S(1)}, u32[]{:S(2)}, u32[]{:S(2)}) collective-permute-start(bf16[2048,128]{1,0:T(8,128)(2,1)S(1)} %pad_maximum_fusion.8), channel_id=1, source_target_pairs={{0,1},{1,0},{2,3},{3,2},{4,5},{5,4},{6,7},{7,6},{8,9},{9,8},{10,11... | collective-permute-start | bytes 1572872 | tf_op jit(solution)/shard_map/ppermute | solution.py:21
  302.3 28.1 %collective-permute-start.68 = (bf16[2048,128]{1,0:T(8,128)(2,1)S(1)}, bf16[2048,128]{1,0:T(8,128)(2,1)S(1)}, u32[]{:S(2)}, u32[]{:S(2)}) collective-permute-start(bf16[2048,128]{1,0:T(8,128)(2,1)S(1)} %pad_maximum_fusion.8), channel_id=1, source_target_pairs={{0,16},{16,0},{1,17},{17,1},{2,18},{18,2},{3,19},{19,3},{4,20},{20... | collective-permute-start | bytes 1572872 | tf_op jit(solution)/shard_map/ppermute | solution.py:21
  310.0 23.7 %collective-permute-start.61 = (bf16[2048,128]{1,0:T(8,128)(2,1)S(1)}, bf16[2048,128]{1,0:T(8,128)(2,1)S(1)}, u32[]{:S(2)}, u32[]{:S(2)}) collective-permute-start(bf16[2048,128]{1,0:T(8,128)(2,1)S(1)} %pad_maximum_fusion.9), channel_id=1, source_target_pairs={{0,1},{1,0},{2,3},{3,2},{4,5},{5,4},{6,7},{7,6},{8,9},{9,8},{10,11... | collective-permute-start | bytes 1572872 | tf_op jit(solution)/shard_map/ppermute | solution.py:21
  313.6 27.5 %collective-permute-start.70 = (bf16[2048,128]{1,0:T(8,128)(2,1)S(1)}, bf16[2048,128]{1,0:T(8,128)(2,1)S(1)}, u32[]{:S(2)}, u32[]{:S(2)}) collective-permute-start(bf16[2048,128]{1,0:T(8,128)(2,1)S(1)} %pad_maximum_fusion.9), channel_id=1, source_target_pairs={{0,16},{16,0},{1,17},{17,1},{2,18},{18,2},{3,19},{19,3},{4,20},{20... | collective-permute-start | bytes 1572872 | tf_op jit(solution)/shard_map/ppermute | solution.py:21
  321.3 19.8 %collective-permute-start.65 = (bf16[2048,128]{1,0:T(8,128)(2,1)S(1)}, bf16[2048,128]{1,0:T(8,128)(2,1)S(1)}, u32[]{:S(2)}, u32[]{:S(2)}) collective-permute-start(bf16[2048,128]{1,0:T(8,128)(2,1)S(1)} %collective-permute-done.64), channel_id=1, source_target_pairs={{0,8},{8,0},{1,9},{9,1},{2,10},{10,2},{3,11},{11,3},{4,12},{12,4},... | collective-permute-start | bytes 1572872 | tf_op jit(solution)/shard_map/ppermute | solution.py:21
  324.8 16.8 %collective-permute-start.67 = (bf16[2048,128]{1,0:T(8,128)(2,1)S(1)}, bf16[2048,128]{1,0:T(8,128)(2,1)S(1)}, u32[]{:S(2)}, u32[]{:S(2)}) collective-permute-start(bf16[2048,128]{1,0:T(8,128)(2,1)S(1)} %collective-permute-done.66), channel_id=1, source_target_pairs={{0,8},{8,0},{1,9},{9,1},{2,10},{10,2},{3,11},{11,3},{4,12},{12,4},... | collective-permute-start | bytes 1572872 | tf_op jit(solution)/shard_map/ppermute | solution.py:21
  330.5 17.0 %collective-permute-start.44 = (bf16[4096,128]{1,0:T(8,128)(2,1)S(1)}, bf16[4096,128]{1,0:T(8,128)(2,1)S(1)}, u32[]{:S(2)}, u32[]{:S(2)}) collective-permute-start(bf16[4096,128]{1,0:T(8,128)(2,1)S(1)} %constant_dynamic-update-slice_fusion), channel_id=1, source_target_pairs={{0,8},{8,0},{1,9},{9,1},{2,10},{10,2},{3,11},{11,3},{4,12},{12,4},... | collective-permute-start | bytes 3145736 | tf_op jit(solution)/shard_map/ppermute | solution.py:21
  370.8 73.8 %collective-permute-start.74 = (bf16[16,128,256]{2,1,0:T(8,128)(2,1)}, bf16[16,128,256]{2,1,0:T(8,128)(2,1)S(1)}, u32[]{:S(2)}, u32[]{:S(2)}) collective-permute-start(bf16[16,128,256]{2,1,0:T(8,128)(2,1)} %get-tuple-element.33), channel_id=1, source_target_pairs={{0,1},{1,0},{2,3},{3,2},{4,5},{5,4},{6,7},{7,6},{8,9},{9,8},{10,11... | collective-permute-start | bytes 3145736 | tf_op jit(solution)/shard_map/ppermute | solution.py:21
  374.2 72.3 %collective-permute-start.72 = (bf16[16,128,256]{2,1,0:T(8,128)(2,1)}, bf16[16,128,256]{2,1,0:T(8,128)(2,1)S(1)}, u32[]{:S(2)}, u32[]{:S(2)}) collective-permute-start(bf16[16,128,256]{2,1,0:T(8,128)(2,1)} %get-tuple-element.31), channel_id=1, source_target_pairs={{0,16},{16,0},{1,17},{17,1},{2,18},{18,2},{3,19},{19,3},{4,20},{20... | collective-permute-start | bytes 3145736 | tf_op jit(solution)/shard_map/ppermute | solution.py:21
  379.7 52.2 %collective-permute-start.57 = (f32[128,384]{1,0:T(8,128)S(1)}, f32[128,384]{1,0:T(8,128)S(1)}, u32[]{:S(2)}, u32[]{:S(2)}) collective-permute-start(f32[128,384]{1,0:T(8,128)S(1)} %pad_maximum_fusion.11), channel_id=1, source_target_pairs={{0,16},{16,0},{1,17},{17,1},{2,18},{18,2},{3,19},{19,3},{4,20},{20... | collective-permute-start | bytes 589832 | tf_op jit(solution)/shard_map/ppermute | solution.py:21
  383.0 37.2 %collective-permute-start.51 = (f32[128,256]{1,0:T(8,128)S(1)}, f32[128,256]{1,0:T(8,128)S(1)}, u32[]{:S(2)}, u32[]{:S(2)}) collective-permute-start(f32[128,256]{1,0:T(8,128)S(1)} %pad_maximum_fusion.12), channel_id=1, source_target_pairs={{0,16},{16,0},{1,17},{17,1},{2,18},{18,2},{3,19},{19,3},{4,20},{20... | collective-permute-start | bytes 393224 | tf_op jit(solution)/shard_map/ppermute | solution.py:21
  384.8 23.7 %collective-permute-start.45 = (f32[128,128]{1,0:T(8,128)S(1)}, f32[128,128]{1,0:T(8,128)S(1)}, u32[]{:S(2)}, u32[]{:S(2)}) collective-permute-start(f32[128,128]{1,0:T(8,128)S(1)} %convolution_add_fusion.9), channel_id=1, source_target_pairs={{0,16},{16,0},{1,17},{17,1},{2,18},{18,2},{3,19},{19,3},{4,20},{20... | collective-permute-start | bytes 196616 | tf_op jit(solution)/shard_map/ppermute | solution.py:21
  408.5 39.8 %collective-permute-start.63 = (f32[128,512]{1,0:T(8,128)S(1)}, f32[128,512]{1,0:T(8,128)S(1)}, u32[]{:S(2)}, u32[]{:S(2)}) collective-permute-start(f32[128,512]{1,0:T(8,128)S(1)} %pad_maximum_fusion.10), channel_id=1, source_target_pairs={{0,16},{16,0},{1,17},{17,1},{2,18},{18,2},{3,19},{19,3},{4,20},{20... | collective-permute-start | bytes 786440 | tf_op jit(solution)/shard_map/ppermute | solution.py:21
  445.0 14.0 %collective-permute-start.75 = (bf16[4,256,256]{2,1,0:T(8,128)(2,1)S(1)}, bf16[4,256,256]{2,1,0:T(8,128)(2,1)S(1)}, u32[]{:S(2)}, u32[]{:S(2)}) collective-permute-start(bf16[4,256,256]{2,1,0:T(8,128)(2,1)S(1)} %bitcast.148), channel_id=1, source_target_pairs={{0,16},{16,0},{1,17},{17,1},{2,18},{18,2},{3,19},{19,3},{4,20},{20... | collective-permute-start | bytes 1572872 | tf_op jit(solution)/shard_map/ppermute | solution.py:21
  447.3 14.0 %collective-permute-start.73 = (bf16[4,256,256]{2,1,0:T(8,128)(2,1)S(1)}, bf16[4,256,256]{2,1,0:T(8,128)(2,1)S(1)}, u32[]{:S(2)}, u32[]{:S(2)}) collective-permute-start(bf16[4,256,256]{2,1,0:T(8,128)(2,1)S(1)} %bitcast.149), channel_id=1, source_target_pairs={{0,1},{1,0},{2,3},{3,2},{4,5},{5,4},{6,7},{7,6},{8,9},{9,8},{10,11... | collective-permute-start | bytes 1572872 | tf_op jit(solution)/shard_map/ppermute | solution.py:21
  461.6 19.2 %collective-permute-start.76 = (bf16[256,512]{1,0:T(8,128)(2,1)S(1)}, bf16[256,512]{1,0:T(8,128)(2,1)S(1)}, u32[]{:S(2)}, u32[]{:S(2)}) collective-permute-start(bf16[256,512]{1,0:T(8,128)(2,1)S(1)} %get-tuple-element.53), channel_id=1, source_target_pairs={{0,2},{2,4},{4,6},{6,0},{1,3},{3,5},{5,7},{7,1},{8,10},{10,12},{12... | collective-permute-start | bytes 786440 | tf_op jit(solution)/shard_map/ppermute | solution.py:21
  464.8 17.4 %collective-permute-start.77 = (bf16[256,512]{1,0:T(8,128)(2,1)S(1)}, bf16[256,512]{1,0:T(8,128)(2,1)S(1)}, u32[]{:S(2)}, u32[]{:S(2)}) collective-permute-start(bf16[256,512]{1,0:T(8,128)(2,1)S(1)} %get-tuple-element.55), channel_id=1, source_target_pairs={{0,4},{2,6},{4,0},{6,2},{1,5},{3,7},{5,1},{7,3},{8,12},{10,14},{12... | collective-permute-start | bytes 786440 | tf_op jit(solution)/shard_map/ppermute | solution.py:21
  465.5 16.7 %collective-permute-start.78 = (bf16[256,512]{1,0:T(8,128)(2,1)S(1)}, bf16[256,512]{1,0:T(8,128)(2,1)S(1)}, u32[]{:S(2)}, u32[]{:S(2)}) collective-permute-start(bf16[256,512]{1,0:T(8,128)(2,1)S(1)} %get-tuple-element.54), channel_id=1, source_target_pairs={{0,6},{2,0},{4,2},{6,4},{1,7},{3,1},{5,3},{7,5},{8,14},{10,8},{12,... | collective-permute-start | bytes 786440 | tf_op jit(solution)/shard_map/ppermute | solution.py:21
  484.1 12.3 %all-to-all-start = ((f32[4,128,256]{2,1,0:T(8,128)}), f32[4,128,256]{2,1,0:T(8,128)S(1)}, u32[]{:S(2)}, u32[]{:S(2)}) async-start(f32[4,128,256]{2,1,0:T(8,128)} %bitcast.44), calls=%async_computation | async-start | bytes 1048576 | tf_op jit(solution)/shard_map/all_to_all | solution.py:398
  (61 other events, 848.6 us)

commit v3 on v2

--- a/solution.py
+++ b/solution.py
@@ -9,7 +9,8 @@
 
 RB_DEV = 32
 UNROLL = 4
-CHUNKS = 4
+CHUNKS = 2
+LEAF = 128
 MOST_SLOTS = 512
 VMEM_LIMIT = 60 * 1024 * 1024
 HIGHEST = lax.Precision.HIGHEST
@@ -19,6 +20,34 @@
 def shift(value, axis, by):
     size = lax.axis_size(axis)
     return lax.ppermute(value, axis, [(i, (i + by) % size) for i in range(size)])
+
+
+def swap(value, bit):
+    size = lax.axis_size("p")
+    return lax.ppermute(value, "p", [(i, i ^ bit) for i in range(size)])
+
+
+def gather_p(value):
+    pair = jnp.concatenate([value, swap(value, 2)])
+    return jnp.concatenate([pair, swap(pair, 1)])
+
+
+def reduce_p(total):
+    part = total[:2] + swap(total[2:].astype(jnp.bfloat16), 1).astype(jnp.float32)
+    return part[0] + swap(part[1].astype(jnp.bfloat16), 2).astype(jnp.float32)
+
+
+def place_p(here, there):
+    differs = here ^ there
+    return (differs & 1) * 2 + (differs >> 1)
+
+
+def together(*values):
+    return lax.optimization_barrier(values)
+
+
+def after(value, *others):
+    return together(value, *others)[0]
 
 
 def spread_pieces(value, axis):
@@ -225,10 +254,10 @@
     return both[:, n:] * lax.rsqrt(pivots)
 
 
-def inverse_kernel(scale, k, *refs):
-    gram, before, out = refs[: k + 1], refs[k + 1 : -1], refs[-1]
+def inverse_kernel(scale, k, first, gram, *refs):
+    before, out = refs[:k], refs[-1]
     n = out.shape[0]
-    grams = [g[...] * scale for g in gram]
+    grams = [gram[first : first + n, j * n : (j + 1) * n] * scale for j in range(k + 1)]
     rest = grams[k]
     factors = []
     for j in range(k):
@@ -247,16 +276,17 @@
     out[:, k * n : (k + 1) * n] = corner
 
 
-def inverse_rows(scale, gram, before, width):
-    k = len(before)
-    n = gram[0].shape[0]
+def inverse_rows(scale, gram, first, before, width, late):
+    vmem, anywhere = pl.BlockSpec(memory_space=pltpu.VMEM), pl.BlockSpec(memory_space=pl.ANY)
     return pl.pallas_call(
-        functools.partial(inverse_kernel, scale, k),
-        out_shape=jax.ShapeDtypeStruct((n, width), jnp.float32),
+        functools.partial(inverse_kernel, scale, len(before), first),
+        out_shape=jax.ShapeDtypeStruct((LEAF, width), jnp.float32),
+        in_specs=[vmem] * (1 + len(before)) + [anywhere] * len(late),
+        out_specs=vmem,
         compiler_params=pltpu.CompilerParams(vmem_limit_bytes=16 << 20),
         cost_estimate=pl.CostEstimate(flops=12 << 30, bytes_accessed=1 << 20, transcendentals=0),
         name="inverse_rows",
-    )(*gram, *before)
+    )(gram, *before, *late)
 
 
 def per_device(blocks, owner, row_local, col_local, sketch):
@@ -276,39 +306,50 @@
     by_q_n = held // 4
     by_x_n = held - by_q_n
 
+    half = col_dev // 2
+    quarter = half // 2
+    panels = sketch.reshape(col_dev, wide, width)
+    mine = lax.dynamic_slice_in_dim(panels, ci * half, half, axis=0)
+    first, last = blocks[:by_x_n], blocks[by_x_n:]
     code = (owner[:, 0] * RB_DEV + row_local) * col_dev + col_local
-    pair = jnp.concatenate([code, shift(code, "core", 1)])
-    codes, sources = [pair], [blocks, shift(blocks, "core", 1)]
-    first, last = blocks[:by_x_n], blocks[by_x_n:]
+    got_x = [shift(first, "x", k) for k in range(1, x_n)]
+    got_q = [shift(last, "q", k) for k in range(1, q_n)]
+    line = gather_p(mine[:quarter])
+    line, got_q, sibling, code_far, mine = together(
+        line, got_q, shift(blocks, "core", 1), shift(code, "core", 1), mine
+    )
+    pair = jnp.concatenate([code, code_far])
+    code_x = [shift(pair, "x", k) for k in range(1, x_n)]
+    code_q = [shift(pair, "q", k) for k in range(1, q_n)]
+    early = spread_pieces(line, "q")
+    line = gather_p(mine[quarter:])
+    far_q = [shift(got, "core", 1) for got in got_q]
+    line, early, far_q, code_q = together(line, early, far_q, code_q)
+    later = spread_pieces(line, "q")
+    early_far = [shift(piece, "core", 1) for piece in early]
+    later, early_far, got_x, code_x = together(later, early_far, got_x, code_x)
+    later_far = [shift(piece, "core", 1) for piece in later]
+    far_x = [shift(got, "core", 1) for got in got_x]
+    sketch_pieces = early + later + early_far + later_far
+
+    sources, codes = [blocks, sibling], [pair]
     most_y, most_p = min(by_x_n, par * slot_cap), min(by_x_n, 2 * par * slot_cap)
     bounds_y, bounds_p = [most_y + by_q_n] * 2, [most_p + by_q_n] * 2
     along_x = jnp.arange(held) < by_x_n
     along = [along_x, along_x]
-    for k in range(1, x_n):
-        got = shift(first, "x", k)
-        sources += [got, shift(got, "core", 1)]
+    for got, far, there in zip(got_x, far_x, code_x):
+        sources += [got, far]
         bounds_y += [most_y] * 2
         bounds_p += [most_p] * 2
-        there = shift(pair, "x", k).reshape(2, held)[:, :by_x_n]
-        codes.append(there.reshape(-1))
+        codes.append(there.reshape(2, held)[:, :by_x_n].reshape(-1))
         along.append(jnp.ones((2 * by_x_n,), bool))
-    for k in range(1, q_n):
-        got = shift(last, "q", k)
-        sources += [got, shift(got, "core", 1)]
+    for got, far, there in zip(got_q, far_q, code_q):
+        sources += [got, far]
         bounds_y += [by_q_n] * 2
         bounds_p += [by_q_n] * 2
-        there = shift(pair, "q", k).reshape(2, held)[:, by_x_n:]
-        codes.append(there.reshape(-1))
+        codes.append(there.reshape(2, held)[:, by_x_n:].reshape(-1))
         along.append(jnp.zeros((2 * by_q_n,), bool))
     codes, along = jnp.concatenate(codes), jnp.concatenate(along)
-
-    half = col_dev // 2
-    panels = sketch.reshape(col_dev, wide, width)
-    mine = lax.dynamic_slice_in_dim(panels, ci * half, half, axis=0)
-    near = []
-    for part in (mine[: half // 2], mine[half // 2 :]):
-        near += spread_pieces(jnp.concatenate(spread_pieces(part, "p")), "q")
-    sketch_pieces = near + [shift(piece, "core", 1) for piece in near]
 
     owners = codes // (RB_DEV * col_dev)
     row = codes // col_dev % RB_DEV
@@ -324,19 +365,18 @@
     groups = q_n + x_n - 1
     other_x = q_n - 1 + (o_x - xi) % x_n
     y_group = jnp.where(along, (r_y - yi) % q_n, jnp.where(o_x == xi, 0, other_x))
-    y_slot = (y_group * p_n + (r_z - zi) % p_n) * rows_each + r_in
+    y_slot = (y_group * p_n + place_p(zi, r_z)) * rows_each + r_in
     y_mine = (o_core == ci) & jnp.where(along, o_x == xi, r_y == yi)
     y_slot = jnp.where(y_mine, y_slot, -1)
-    quarter = half // 2
     y_panel = jnp.where(col // half == ci, 0, 2) + col % half // quarter
-    y_panel = (y_panel * q_n + (yi - o_y) % q_n) * p_n + (zi - o_z) % p_n
+    y_panel = (y_panel * q_n + (yi - o_y) % q_n) * p_n + place_p(zi, o_z)
     y_panel = y_panel * quarter + col % quarter
 
-    p_slot = ((c_x - xi) % x_n * q_n + (o_y - yi) % q_n) * p_n + (o_z - zi) % p_n
+    p_slot = ((c_x - xi) % x_n * q_n + (o_y - yi) % q_n) * p_n + place_p(zi, o_z)
     p_slot = p_slot * cols_each + c_in
     p_mine = (c_core == ci) & jnp.where(along, o_x == xi, r_y == yi)
     p_slot = jnp.where(p_mine, p_slot, -1)
-    in_part = (zi - r_z) % p_n * rows_each + r_in
+    in_part = place_p(zi, r_z) * rows_each + r_in
     same_x = (jnp.where(o_core == ci, 0, q_n) + (yi - r_y) % q_n) * per
     not_x = (2 * q_n + jnp.where(o_core == ci, 0, x_n - 1) + (xi - o_x) % x_n - 1) * per
     p_panel = jnp.where(o_x == xi, same_x, not_x) + in_part
@@ -349,31 +389,64 @@
         y_slot, y_panel, sources, sketch_pieces, par * col_dev, groups * per, width,
         shapes, "sketch_products",
     )
-    own, y_pieces, inverse, gathered = [], [], [], []
-    for c in range(CHUNKS):
+    def received(c):
         by_group = [parts[g * CHUNKS + c] for g in range(groups)]
-        total = reduce_stage(by_group[0], by_group[1:q_n], "q")
-        total = reduce_stage(total, by_group[q_n:], "x")
-        total = total.reshape(p_n, rows_each * wide, kc)
-        mine = reduce_stage(total[0], [total[k].astype(bf16) for k in range(1, p_n)], "p")
-        own.append(mine)
-        line = jnp.concatenate(spread_pieces(mine.astype(bf16), "p"))
-        here = jnp.concatenate(spread_pieces(line, "q"))
-        there = jnp.concatenate([shift(line, "x", k) for k in range(1, x_n)])
-        here_far, there_far = shift(here, "core", 1), shift(there, "core", 1)
+        return by_group[0], (
+            [shift(by_group[k], "q", k) for k in range(1, q_n)]
+            + [shift(by_group[q_n - 1 + k], "x", k) for k in range(1, x_n)]
+        )
+
+    def summed(keep, got):
+        for part in got:
+            keep = keep + part.astype(f32)
+        return keep.reshape(p_n, rows_each * wide, kc)
+
+    def spread(line):
+        return (
+            [shift(line, "q", k) for k in range(1, q_n)],
+            [shift(line, "x", k) for k in range(1, x_n)],
+        )
+
+    def siblings(line, here, there):
+        here, there = jnp.concatenate([line, *here]), jnp.concatenate(there)
+        return here, there, shift(here, "core", 1), shift(there, "core", 1)
+
+    keep_a, got_a = received(0)
+    keep_b, got_b = received(1)
+    got_a = together(*got_a)
+    own_a = reduce_p(summed(keep_a, got_a))
+    own_a, got_b = together(own_a, got_b)
+    line_a = gather_p(own_a.astype(bf16))
+    own_b = reduce_p(summed(keep_b, got_b))
+    line_a, own_b = together(line_a, own_b)
+    line_b = gather_p(own_b.astype(bf16))
+    spread_a = spread(line_a)
+    line_b, spread_a = together(line_b, spread_a)
+    spread_b = spread(line_b)
+    all_a = siblings(line_a, *spread_a)
+    spread_b, all_a = together(spread_b, all_a)
+    all_b = siblings(line_b, *spread_b)
+    own, y_pieces, grams = [own_a, own_b], [], []
+    for c, (here, there, here_far, there_far) in enumerate((all_a, all_b)):
         y_pieces += [a.reshape(-1, wide, kc) for a in (here, here_far, there, there_far)]
-        gathered.append((here, here_far))
         gram = []
-        for before in gathered:
+        for before in (all_a, all_b)[: c + 1]:
             gram.append(sum(
                 lax.dot_general(a, b, (((0,), (0,)), ((), ())), preferred_element_type=f32)
-                for a, b in zip(gathered[c], before)
+                for a, b in ((here, before[0]), (here_far, before[2]))
             ))
-        joined = jnp.concatenate(gram, axis=1)
-        joined = reduce_stage(joined, [joined] * (x_n - 1), "x")
-        gram = [joined[:, j * kc : (j + 1) * kc] for j in range(c + 1)]
-        inverse.append(inverse_rows(1.0 / all_rows, gram, inverse, width))
+        gram = jnp.concatenate(gram, axis=1)
+        grams.append(reduce_stage(gram, [gram] * (x_n - 1), "x"))
     own_rows = jnp.concatenate(own, axis=1)
+
+    inverse = []
+
+    def more_rows(*late):
+        k = len(inverse)
+        gram = grams[k * LEAF // kc]
+        inverse.append(
+            inverse_rows(1.0 / all_rows, gram, k * LEAF % kc, inverse, width, late)
+        )
 
     slots = x_n * q_n * p_n * cols_each
     kh = width // 2
@@ -385,12 +458,17 @@
         p_slot, p_panel, sources, y_pieces, 2 * groups * per, slots, width,
         shapes, "project_products",
     )
+    more_rows(parts[0])
+    more_rows()
     by_x = reduce_stage(parts[0], parts[1:x_n], "x").reshape(q_n, p_n, cols_each * wide, kh)
+    by_q = reduce_stage(parts[x_n], parts[x_n + 1 :], "q").reshape(x_n, p_n, cols_each * wide, kh)
+    by_x, by_q = after((by_x, by_q), inverse[-1])
     by_x = reduce_stage(by_x[0], [by_x[k].astype(bf16) for k in range(1, q_n)], "q")
-    by_q = reduce_stage(parts[x_n], parts[x_n + 1 :], "q").reshape(x_n, p_n, cols_each * wide, kh)
     by_q = reduce_stage(by_q[0], [by_q[k].astype(bf16) for k in range(1, x_n)], "x")
-    both = jnp.concatenate([by_x, by_q], axis=2)
-    z_rows = reduce_stage(both[0], [both[k].astype(bf16) for k in range(1, p_n)], "p")
+    more_rows()
+    both = after(jnp.concatenate([by_x, by_q], axis=2), inverse[-1])
+    z_rows = reduce_p(both)
+    more_rows()
 
     inverse = jnp.concatenate(inverse, axis=0)
     basis = dot32(own_rows, inverse, ((1,), (1,))).astype(bf16)

time: 506 us -> 398 us (0.79); the launches traced: 497 us -> 398 us
  starting transfers between devices: 126 us -> 56.5 us
  waiting for transfers between devices: 242 us -> 214 us
    ppermute x79 -> x32, waiting for transfers between devices: 236 us -> 87.5 us  [shift(): lax.ppermute(value, axis, [(i, (i + by) % size) for i in range(size)])]
    ppermute x0 -> x14, waiting for transfers between devices: none -> 120 us  [swap(): return lax.ppermute(value, 'p', [(i, i ^ bit) for i in range(size)])]
    ppermute x79 -> x32, starting transfers between devices: 123 us -> 26.6 us  [shift(): lax.ppermute(value, axis, [(i, (i + by) % size) for i in range(size)])]
    ppermute x0 -> x14, starting transfers between devices: none -> 25.8 us  [swap(): return lax.ppermute(value, 'p', [(i, i ^ bit) for i in range(size)])]
    dot_general x20 -> x6, matrix products: 11.1 us -> 6.92 us  [per_device(): lax.dot_general(a, b, (((0,), (0,)), ((), ())), preferred_element_type=f32)]
  transfers between devices with their start and end apart: 80 -> 47, of which waited for: 39 -> 26; matrix products, arithmetic and copies ran while one was open for 5% -> 4% of each run, Pallas kernels for 10% -> 12%
where the time goes in v3:
time: 398 us
  waiting for transfers between devices  214 us (54%)
  Pallas kernels  92.5 us (23%)
  starting transfers between devices  56.5 us (14%)
  local copies, waits for them, and re-layouts  14.3 us (4%)
  matrix products  11.4 us (3%)
  other arithmetic  7.31 us (2%)
    ppermute x14, waiting for transfers between devices, swap(): return lax.ppermute(value, 'p', [(i, i ^ bit) for i in range(size)])  120 us
    ppermute x32, waiting for transfers between devices, shift(): lax.ppermute(value, axis, [(i, (i + by) % size) for i in range(size)])  87.5 us
    pallas_call x4, Pallas kernels, inverse_rows(): pl.pallas_call(functools.partial(inverse_kernel, scale, len(before), firs...  48.7 us
    pallas_call x2, Pallas kernels, block_products(): pl.pallas_call(kernel, out_shape=outs, in_specs=[smem, smem] + [anywhere]...  43.8 us
    ppermute x32, starting transfers between devices, shift(): lax.ppermute(value, axis, [(i, (i + by) % size) for i in range(size)])  26.6 us
    ppermute x14, starting transfers between devices, swap(): return lax.ppermute(value, 'p', [(i, i ^ bit) for i in range(size)])  25.8 us
  transfers between devices with their start and end apart: 47, of which 26 were waited for; matrix products, arithmetic and copies ran while one was open for 4% of the time, Pallas kernels for 12%

profile of v3, /device:TPU:0, one launch (start us, length us, event | category | flops | bytes accessed | tf_op | source)
XLA Modules:
  0.0 397.6 jit_solution(9612097831904391013)
XLA Ops:
  1.9 4.1 %collective-permute-start = (bf16[2,128,512]{2,1,0:T(8,128)(2,1)S(1)}, bf16[2,128,512]{2,1,0:T(8,128)(2,1)S(1)}, u32[]{:S(2)}, u32[]{:S(2)}) collective-permute-start(bf16[2,128,512]{2,1,0:T(8,128)(2,1)S(1)} %constant_dynamic-slice_fusion), channel_id=1, source_target_pairs={{0,4},{2,6},{4,0},{6,2},{1,5},{3,7},{5,1},{7,3},{8,12},{10,14},{12... | collective-permute-start | bytes 786440 | tf_op jit(solution)/shard_map/ppermute | solution.py:27
  6.0 1.3 slice.83
  7.4 1.6 collective-permute-start.2
  8.9 2.3 slice.85
  11.2 1.6 collective-permute-start.13
  12.8 5.1 %collective-permute-done = bf16[2,128,512]{2,1,0:T(8,128)(2,1)S(1)} collective-permute-done((bf16[2,128,512]{2,1,0:T(8,128)(2,1)S(1)}, bf16[2,128,512]{2,1,0:T(8,128)(2,1)S(1)}, u32[]{:S(2)}, u32[]{:S(2)}) %collective-permute-start) | collective-permute-done | bytes 262176 | tf_op jit(solution)/shard_map/ppermute | solution.py:27
  18.9 12.2 %collective-permute-done.1 = bf16[4,128,512]{2,1,0:T(8,128)(2,1)S(1)} collective-permute-done((bf16[4,128,512]{2,1,0:T(8,128)(2,1)S(1)}, bf16[4,128,512]{2,1,0:T(8,128)(2,1)S(1)}, u32[]{:S(2)}, u32[]{:S(2)}) %collective-permute-start.1) | collective-permute-done | bytes 524320 | tf_op jit(solution)/shard_map/ppermute | solution.py:27
  32.1 2.4 collective-permute-start.5
  34.5 1.5 collective-permute-start.7
  36.0 10.2 %collective-permute-done.5 = bf16[2,128,512]{2,1,0:T(8,128)(2,1)S(1)} collective-permute-done((bf16[2,128,512]{2,1,0:T(8,128)(2,1)S(1)}, bf16[2,128,512]{2,1,0:T(8,128)(2,1)S(1)}, u32[]{:S(2)}, u32[]{:S(2)}) %collective-permute-start.5) | collective-permute-done | bytes 262176 | tf_op jit(solution)/shard_map/ppermute | solution.py:27
  47.0 1.5 collective-permute-start.9
  48.5 10.7 %collective-permute-done.6 = bf16[4,128,512]{2,1,0:T(8,128)(2,1)S(1)} collective-permute-done((bf16[4,128,512]{2,1,0:T(8,128)(2,1)S(1)}, bf16[4,128,512]{2,1,0:T(8,128)(2,1)S(1)}, u32[]{:S(2)}, u32[]{:S(2)}) %collective-permute-start.6) | collective-permute-done | bytes 524320 | tf_op jit(solution)/shard_map/ppermute | solution.py:27
  59.2 1.1 pad_maximum_fusion.2.refs_8_
  60.3 1.6 collective-permute-start.10
  62.4 1.5 collective-permute-start.14
  63.9 16.8 %collective-permute-done.13.refs_2_ = bf16[96,128,128]{2,1,0:T(8,128)(2,1)} collective-permute-done((bf16[96,128,128]{2,1,0:T(8,128)(2,1)S(1)}, bf16[96,128,128]{2,1,0:T(8,128)(2,1)}, u32[]{:S(2)}, u32[]{:S(2)}) %collective-permute-start.13) | collective-permute-done | bytes 3145760 | tf_op jit(solution)/shard_map/ppermute | solution.py:22
  80.7 4.7 %collective-permute-done.10.refs_9_ = bf16[8,128,512]{2,1,0:T(8,128)(2,1)} collective-permute-done((bf16[8,128,512]{2,1,0:T(8,128)(2,1)}, bf16[8,128,512]{2,1,0:T(8,128)(2,1)}, u32[]{:S(2)}, u32[]{:S(2)}) %collective-permute-start.10) | collective-permute-done | bytes 1048608 | tf_op jit(solution)/shard_map/ppermute | solution.py:22
  85.4 1.0 copy-done.20
  86.4 1.0 copy-done.21
  89.5 4.4 %collective-permute-done.16.refs_12_ = bf16[8,128,512]{2,1,0:T(8,128)(2,1)} collective-permute-done((bf16[8,128,512]{2,1,0:T(8,128)(2,1)}, bf16[8,128,512]{2,1,0:T(8,128)(2,1)}, u32[]{:S(2)}, u32[]{:S(2)}) %collective-permute-start.16) | collective-permute-done | bytes 1048608 | tf_op jit(solution)/shard_map/ppermute | solution.py:22
  93.9 1.5 collective-permute-done.17.refs_13_
  95.4 22.1 %sketch_products.1 = (f32[16,128,256]{2,1,0:T(8,128)}, f32[16,128,256]{2,1,0:T(8,128)}, bf16[16,128,256]{2,1,0:T(8,128)(2,1)}, bf16[16,128,256]{2,1,0:T(8,128)(2...) custom-call(s32[512]{0:T(512)} %get-tuple-element.96.rows_ref, s32[512]{0:T(512)} %get-tuple-element.97.cols_ref, ...), custom_call_target="tpu_custom_call" | custom-call | flops 2147483648 | bytes 33554432 | tf_op jit(solution)/shard_map/sketch_products/pallas_call | solution.py:214
  117.5 1.3 collective-permute-start.18
  118.8 4.5 %collective-permute-start.19 = (bf16[16,128,256]{2,1,0:T(8,128)(2,1)}, bf16[16,128,256]{2,1,0:T(8,128)(2,1)S(1)}, u32[]{:S(2)}, u32[]{:S(2)}) collective-permute-start(bf16[16,128,256]{2,1,0:T(8,128)(2,1)} %get-tuple-element.65), channel_id=1, source_target_pairs={{0,16},{16,0},{1,17},{17,1},{2,18},{18,2},{3,19},{19,3},{4,20},{20... | collective-permute-start | bytes 3145736 | tf_op jit(solution)/shard_map/ppermute | solution.py:22
  123.3 20.2 %collective-permute-done.18 = bf16[16,128,256]{2,1,0:T(8,128)(2,1)S(1)} collective-permute-done((bf16[16,128,256]{2,1,0:T(8,128)(2,1)}, bf16[16,128,256]{2,1,0:T(8,128)(2,1)S(1)}, u32[]{:S(2)}, u32[]{:S(2)}) %collective-permute-start.18) | collective-permute-done | bytes 1048608 | tf_op jit(solution)/shard_map/ppermute | solution.py:22
  143.9 2.2 convert_add_fusion.3
  146.1 1.2 collective-permute-start.20
  147.4 1.1 collective-permute-start.22
  149.1 10.4 %collective-permute-done.20 = bf16[2,512,256]{2,1,0:T(8,128)(2,1)S(1)} collective-permute-done((bf16[2,512,256]{2,1,0:T(8,128)(2,1)S(1)}, bf16[2,512,256]{2,1,0:T(8,128)(2,1)S(1)}, u32[]{:S(2)}, u32[]{:S(2)}) %collective-permute-start.20) | collective-permute-done | bytes 524320 | tf_op jit(solution)/shard_map/ppermute | solution.py:27
  159.7 2.7 collective-permute-start.21
  162.4 10.7 %collective-permute-done.21 = bf16[512,256]{1,0:T(8,128)(2,1)S(1)} collective-permute-done((bf16[512,256]{1,0:T(8,128)(2,1)S(1)}, bf16[512,256]{1,0:T(8,128)(2,1)S(1)}, u32[]{:S(2)}, u32[]{:S(2)}) %collective-permute-start.21) | collective-permute-done | bytes 262176 | tf_op jit(solution)/shard_map/ppermute | solution.py:27
  173.8 3.7 collective-permute-start.24
  177.6 12.7 %collective-permute-done.24 = bf16[512,256]{1,0:T(8,128)(2,1)S(1)} collective-permute-done((bf16[512,256]{1,0:T(8,128)(2,1)S(1)}, bf16[512,256]{1,0:T(8,128)(2,1)S(1)}, u32[]{:S(2)}, u32[]{:S(2)}) %collective-permute-start.24) | collective-permute-done | bytes 262176 | tf_op jit(solution)/shard_map/ppermute | solution.py:27
  190.3 3.7 collective-permute-start.25
  194.2 14.5 %collective-permute-done.27 = bf16[512,256]{1,0:T(8,128)(2,1)S(1)} collective-permute-done((bf16[512,256]{1,0:T(8,128)(2,1)S(1)}, bf16[512,256]{1,0:T(8,128)(2,1)S(1)}, u32[]{:S(2)}, u32[]{:S(2)}) %collective-permute-start.27) | collective-permute-done | bytes 262176 | tf_op jit(solution)/shard_map/ppermute | solution.py:27
  209.6 2.8 collective-permute-start.28
  212.4 0.8 collective-permute-start.30
  213.2 9.3 %collective-permute-done.28 = bf16[512,256]{1,0:T(8,128)(2,1)S(1)} collective-permute-done((bf16[512,256]{1,0:T(8,128)(2,1)S(1)}, bf16[512,256]{1,0:T(8,128)(2,1)S(1)}, u32[]{:S(2)}, u32[]{:S(2)}) %collective-permute-start.28) | collective-permute-done | bytes 262176 | tf_op jit(solution)/shard_map/ppermute | solution.py:27
  222.6 12.3 %collective-permute-done.29 = bf16[1024,256]{1,0:T(8,128)(2,1)S(1)} collective-permute-done((bf16[1024,256]{1,0:T(8,128)(2,1)S(1)}, bf16[1024,256]{1,0:T(8,128)(2,1)S(1)}, u32[]{:S(2)}, u32[]{:S(2)}) %collective-permute-start.29) | collective-permute-done | bytes 524320 | tf_op jit(solution)/shard_map/ppermute | solution.py:27
  235.0 1.5 collective-permute-done.31
  236.6 1.6 collective-permute-start.32
  238.5 23.7 %collective-permute-done.32 = bf16[2048,256]{1,0:T(8,128)(2,1)S(1)} collective-permute-done((bf16[2048,256]{1,0:T(8,128)(2,1)S(1)}, bf16[2048,256]{1,0:T(8,128)(2,1)S(1)}, u32[]{:S(2)}, u32[]{:S(2)}) %collective-permute-start.32) | collective-permute-done | bytes 1048608 | tf_op jit(solution)/shard_map/ppermute | solution.py:22
  262.2 1.3 collective-permute-done.33
  267.2 7.3 %collective-permute-done.36 = f32[256,256]{1,0:T(8,128)S(1)} collective-permute-done((f32[256,256]{1,0:T(8,128)S(1)}, f32[256,256]{1,0:T(8,128)S(1)}, u32[]{:S(2)}, u32[]{:S(2)}) %collective-permute-start.36) | collective-permute-done | bytes 262176 | tf_op jit(solution)/shard_map/ppermute | solution.py:22
  274.6 1.3 copy-done.13
  276.2 21.7 %project_products.1 = (f32[16,128,256]{2,1,0:T(8,128)}, bf16[16,128,256]{2,1,0:T(8,128)(2,1)}, f32[16,128,256]{2,1,0:T(8,128)}, bf16[16,128,256]{2,1,0:T(8,128)(2,1)}) custom-call(s32[512]{0:T(512)} %get-tuple-element.95.rows_ref, s32[512]{0:T(512)} %get-tuple-element.92.cols_ref, bf16[128,128,128]{2,1,0:T(8,128)(2,1)} %refs_0_.3, ...), custom_call_target="tpu_custom_call" | custom-call | flops 2147483648 | bytes 33554432 | tf_op jit(solution)/shard_map/project_products/pallas_call | solution.py:214
  299.1 3.2 fusion.70
  303.1 0.8 copy-done.14
  305.5 1.3 collective-permute-start.39
  306.8 10.7 %inverse_rows.4.refs_0_ = f32[128,512]{1,0:T(8,128)S(1)} custom-call(f32[256,256]{1,0:T(8,128)S(1)} %add.235.gram, f32[16,128,256]{2,1,0:T(8,128)S(1)} %copy-done.2), custom_call_target="tpu_custom_call" | custom-call | flops 12884901888 | bytes 1048576 | tf_op jit(solution)/shard_map/inverse_rows/pallas_call | solution.py:281
  317.5 11.9 %inverse_rows.5.refs_1_ = f32[128,512]{1,0:T(8,128)S(1)} custom-call(f32[256,256]{1,0:T(8,128)S(1)} %add.235.gram, f32[128,512]{1,0:T(8,128)S(1)} %inverse_rows.4.refs_0_), custom_call_target="tpu_custom_call" | custom-call | flops 12884901888 | bytes 1048576 | tf_op jit(solution)/shard_map/inverse_rows/pallas_call | solution.py:281
  329.4 5.0 %collective-permute-done.39 = f32[256,512]{1,0:T(8,128)S(1)} collective-permute-done((f32[256,512]{1,0:T(8,128)S(1)}, f32[256,512]{1,0:T(8,128)S(1)}, u32[]{:S(2)}, u32[]{:S(2)}) %collective-permute-start.39) | collective-permute-done | bytes 524320 | tf_op jit(solution)/shard_map/ppermute | solution.py:22
  334.8 1.3 copy-done.11
  336.5 1.7 collective-permute-start.42
  338.6 12.4 %inverse_rows.6.refs_2_ = f32[128,512]{1,0:T(8,128)S(1)} custom-call(f32[256,512]{1,0:T(8,128)S(1)} %fusion.68.gram, f32[128,512]{1,0:T(8,128)S(1)} %inverse_rows.4.refs_0_, f32[128,512]{1,0:T(8,128)S(1)} %inverse_rows.5.refs_1_), custom_call_target="tpu_custom_call" | custom-call | flops 12884901888 | bytes 1048576 | tf_op jit(solution)/shard_map/inverse_rows/pallas_call | solution.py:281
  351.7 0.8 collective-permute-start.44
  352.5 11.2 %collective-permute-done.44 = bf16[2,256,512]{2,1,0:T(8,128)(2,1)S(1)} collective-permute-done((bf16[2,256,512]{2,1,0:T(8,128)(2,1)S(1)}, bf16[2,256,512]{2,1,0:T(8,128)(2,1)S(1)}, u32[]{:S(2)}, u32[]{:S(2)}) %collective-permute-start.44) | collective-permute-done | bytes 524320 | tf_op jit(solution)/shard_map/ppermute | solution.py:27
  364.0 2.7 collective-permute-start.45
  366.6 13.7 %inverse_rows.7 = f32[128,512]{1,0:T(8,128)S(1)} custom-call(f32[256,512]{1,0:T(8,128)S(1)} %fusion.68.gram, f32[128,512]{1,0:T(8,128)S(1)} %inverse_rows.4.refs_0_, f32[128,512]{1,0:T(8,128)S(1)} %inverse_rows.5.refs_1_, f32[128,512]{1,0:T(8,128)S(1)} %inverse_rows.6.refs_2_), custom_call_target="tpu_custom_call" | custom-call | flops 12884901888 | bytes 1048576 | tf_op jit(solution)/shard_map/inverse_rows/pallas_call | solution.py:281
  380.4 1.8 fusion.3
  382.2 4.1 %all-to-all-start = ((f32[4,128,256]{2,1,0:T(8,128)}), f32[4,128,256]{2,1,0:T(8,128)}, u32[]{:S(2)}, u32[]{:S(2)}) async-start(f32[4,128,256]{2,1,0:T(8,128)} %bitcast.89), calls=%async_computation | async-start | bytes 1048576 | tf_op jit(solution)/shard_map/all_to_all | solution.py:476
  386.4 2.7 convolution_convert_fusion
  389.1 6.2 %all-to-all-done = f32[4,128,256]{2,1,0:T(8,128)} async-done(((f32[4,128,256]{2,1,0:T(8,128)}), f32[4,128,256]{2,1,0:T(8,128)}, u32[]{:S(2)}, u32[]{:S(2)}) %all-to-all-start) | async-done | bytes 524320 | tf_op jit(solution)/shard_map/all_to_all | solution.py:476
  395.3 1.9 copy.16
  (153 shorter events, 19.7 us)
Async XLA Ops:
  0.6 31.4 %collective-permute-start.3 = (bf16[128,128,128]{2,1,0:T(8,128)(2,1)}, bf16[128,128,128]{2,1,0:T(8,128)(2,1)}, u32[]{:S(2)}, u32[]{:S(2)}) collective-permute-start(bf16[128,128,128]{2,1,0:T(8,128)(2,1)} %refs_0_.3), channel_id=1, source_target_pairs={{0,8},{8,0},{1,9},{9,1},{2,10},{10,2},{3,11},{11,3},{4,12},{12,4},... | collective-permute-start | bytes 12582920 | tf_op jit(solution)/shard_map/ppermute | solution.py:22
  1.9 16.0 %collective-permute-start = (bf16[2,128,512]{2,1,0:T(8,128)(2,1)S(1)}, bf16[2,128,512]{2,1,0:T(8,128)(2,1)S(1)}, u32[]{:S(2)}, u32[]{:S(2)}) collective-permute-start(bf16[2,128,512]{2,1,0:T(8,128)(2,1)S(1)} %constant_dynamic-slice_fusion), channel_id=1, source_target_pairs={{0,4},{2,6},{4,0},{6,2},{1,5},{3,7},{5,1},{7,3},{8,12},{10,14},{12... | collective-permute-start | bytes 786440 | tf_op jit(solution)/shard_map/ppermute | solution.py:27
  7.3 11.4 %copy-start.22 = (s32[128]{0:T(128)S(1)}, s32[128]{0:T(128)}, u32[]{:S(2)}) copy-start(s32[128]{0:T(128)} %param.8) | copy-start | bytes 1540
  7.3 11.4 %copy-start.23 = (s32[128]{0:T(128)S(1)}, s32[128]{0:T(128)}, u32[]{:S(2)}) copy-start(s32[128]{0:T(128)} %param.7) | copy-start | bytes 1540
  7.3 11.4 %copy-start.24 = (s32[128,1]{0,1:T(1,128)S(1)}, s32[128,1]{0,1:T(1,128)}, u32[]{:S(2)}) copy-start(s32[128,1]{0,1:T(1,128)} %param.6) | copy-start | bytes 1540
  7.4 24.7 %collective-permute-start.2 = (bf16[32,128,128]{2,1,0:T(8,128)(2,1)S(1)}, bf16[32,128,128]{2,1,0:T(8,128)(2,1)S(1)}, u32[]{:S(2)}, u32[]{:S(2)}) collective-permute-start(bf16[32,128,128]{2,1,0:T(8,128)(2,1)S(1)} %slice.83), channel_id=1, source_target_pairs={{0,1},{1,0},{2,3},{3,2},{4,5},{5,4},{6,7},{7,6},{8,9},{9,8},{10,11... | collective-permute-start | bytes 3145736 | tf_op jit(solution)/shard_map/ppermute | solution.py:22
  11.2 69.5 %collective-permute-start.13 = (bf16[96,128,128]{2,1,0:T(8,128)(2,1)S(1)}, bf16[96,128,128]{2,1,0:T(8,128)(2,1)}, u32[]{:S(2)}, u32[]{:S(2)}) collective-permute-start(bf16[96,128,128]{2,1,0:T(8,128)(2,1)S(1)} %slice.85), channel_id=1, source_target_pairs={{0,16},{16,0},{1,17},{17,1},{2,18},{18,2},{3,19},{19,3},{4,20},{20... | collective-permute-start | bytes 9437192 | tf_op jit(solution)/shard_map/ppermute | solution.py:22
  18.0 13.2 %collective-permute-start.1 = (bf16[4,128,512]{2,1,0:T(8,128)(2,1)S(1)}, bf16[4,128,512]{2,1,0:T(8,128)(2,1)S(1)}, u32[]{:S(2)}, u32[]{:S(2)}) collective-permute-start(bf16[4,128,512]{2,1,0:T(8,128)(2,1)S(1)} %pad_maximum_fusion.8), channel_id=1, source_target_pairs={{0,2},{2,0},{4,6},{6,4},{1,3},{3,1},{5,7},{7,5},{8,10},{10,8},{12,... | collective-permute-start | bytes 1572872 | tf_op jit(solution)/shard_map/ppermute | solution.py:27
  18.8 12.5 %collective-permute-start.4 = (s32[128]{0:T(128)S(1)}, s32[128]{0:T(128)S(1)}, u32[]{:S(2)}, u32[]{:S(2)}) collective-permute-start(s32[128]{0:T(128)S(1)} %fusion.65), channel_id=1, source_target_pairs={{0,8},{8,0},{1,9},{9,1},{2,10},{10,2},{3,11},{11,3},{4,12},{12,4},... | collective-permute-start | bytes 1544 | tf_op jit(solution)/shard_map/ppermute | solution.py:22
  31.2 64.1 %copy-start.9 = (bf16[8,128,512]{2,1,0:T(8,128)(2,1)}, bf16[8,128,512]{2,1,0:T(8,128)(2,1)S(1)}, u32[]{:S(2)}) copy-start(bf16[8,128,512]{2,1,0:T(8,128)(2,1)S(1)} %pad_maximum_fusion.1.refs_6_) | copy-start | bytes 3145732
  32.0 63.3 %copy-start.7 = (bf16[32,128,128]{2,1,0:T(8,128)(2,1)}, bf16[32,128,128]{2,1,0:T(8,128)(2,1)S(1)}, u32[]{:S(2)}) copy-start(bf16[32,128,128]{2,1,0:T(8,128)(2,1)S(1)} %collective-permute-done.2.refs_4_) | copy-start | bytes 3145732
  32.1 14.1 %collective-permute-start.5 = (bf16[2,128,512]{2,1,0:T(8,128)(2,1)S(1)}, bf16[2,128,512]{2,1,0:T(8,128)(2,1)S(1)}, u32[]{:S(2)}, u32[]{:S(2)}) collective-permute-start(bf16[2,128,512]{2,1,0:T(8,128)(2,1)S(1)} %slice.84), channel_id=1, source_target_pairs={{0,4},{2,6},{4,0},{6,2},{1,5},{3,7},{5,1},{7,3},{8,12},{10,14},{12... | collective-permute-start | bytes 786440 | tf_op jit(solution)/shard_map/ppermute | solution.py:27
  34.5 25.8 %collective-permute-start.8 = (bf16[32,128,128]{2,1,0:T(8,128)(2,1)S(1)}, bf16[32,128,128]{2,1,0:T(8,128)(2,1)S(1)}, u32[]{:S(2)}, u32[]{:S(2)}) collective-permute-start(bf16[32,128,128]{2,1,0:T(8,128)(2,1)S(1)} %collective-permute-done.2.refs_4_), channel_id=1, source_target_pairs={{0,8},{8,0},{1,9},{9,1},{2,10},{10,2},{3,11},{11,3},{4,12},{12,4},... | collective-permute-start | bytes 3145736 | tf_op jit(solution)/shard_map/ppermute | solution.py:22
  34.5 25.8 %collective-permute-start.7 = (bf16[8,128,512]{2,1,0:T(8,128)(2,1)S(1)}, bf16[8,128,512]{2,1,0:T(8,128)(2,1)S(1)}, u32[]{:S(2)}, u32[]{:S(2)}) collective-permute-start(bf16[8,128,512]{2,1,0:T(8,128)(2,1)S(1)} %pad_maximum_fusion.1.refs_6_), channel_id=1, source_target_pairs={{0,1},{1,0},{2,3},{3,2},{4,5},{5,4},{6,7},{7,6},{8,9},{9,8},{10,11... | collective-permute-start | bytes 3145736 | tf_op jit(solution)/shard_map/ppermute | solution.py:22
  46.2 13.0 %collective-permute-start.6 = (bf16[4,128,512]{2,1,0:T(8,128)(2,1)S(1)}, bf16[4,128,512]{2,1,0:T(8,128)(2,1)S(1)}, u32[]{:S(2)}, u32[]{:S(2)}) collective-permute-start(bf16[4,128,512]{2,1,0:T(8,128)(2,1)S(1)} %pad_maximum_fusion.9), channel_id=1, source_target_pairs={{0,2},{2,0},{4,6},{6,4},{1,3},{3,1},{5,7},{7,5},{8,10},{10,8},{12,... | collective-permute-start | bytes 1572872 | tf_op jit(solution)/shard_map/ppermute | solution.py:27
  47.0 13.3 %collective-permute-start.9 = (s32[256]{0:T(256)S(1)}, s32[256]{0:T(256)S(1)}, u32[]{:S(2)}, u32[]{:S(2)}) collective-permute-start(s32[256]{0:T(256)S(1)} %pad_add_fusion.2), channel_id=1, source_target_pairs={{0,1},{1,0},{2,3},{3,2},{4,5},{5,4},{6,7},{7,6},{8,9},{9,8},{10,11... | collective-permute-start | bytes 3080 | tf_op jit(solution)/shard_map/ppermute | solution.py:22
  60.3 35.1 %copy-start.8 = (bf16[32,128,128]{2,1,0:T(8,128)(2,1)}, bf16[32,128,128]{2,1,0:T(8,128)(2,1)S(1)}, u32[]{:S(2)}) copy-start(bf16[32,128,128]{2,1,0:T(8,128)(2,1)S(1)} %collective-permute-done.8.refs_5_) | copy-start | bytes 3145732
  60.3 25.1 %copy-start.19 = (bf16[8,128,512]{2,1,0:T(8,128)(2,1)}, bf16[8,128,512]{2,1,0:T(8,128)(2,1)S(1)}, u32[]{:S(2)}) copy-start(bf16[8,128,512]{2,1,0:T(8,128)(2,1)S(1)} %collective-permute-done.7.refs_7_) | copy-start | bytes 3145732
  60.3 25.1 %collective-permute-start.10 = (bf16[8,128,512]{2,1,0:T(8,128)(2,1)}, bf16[8,128,512]{2,1,0:T(8,128)(2,1)}, u32[]{:S(2)}, u32[]{:S(2)}) collective-permute-start(bf16[8,128,512]{2,1,0:T(8,128)(2,1)} %pad_maximum_fusion.2.refs_8_), channel_id=1, source_target_pairs={{0,1},{1,0},{2,3},{3,2},{4,5},{5,4},{6,7},{7,6},{8,9},{9,8},{10,11... | collective-permute-start | bytes 3145736 | tf_op jit(solution)/shard_map/ppermute | solution.py:22
  61.9 23.5 %collective-permute-start.11 = (bf16[8,128,512]{2,1,0:T(8,128)(2,1)S(1)}, bf16[8,128,512]{2,1,0:T(8,128)(2,1)S(1)}, u32[]{:S(2)}, u32[]{:S(2)}) collective-permute-start(bf16[8,128,512]{2,1,0:T(8,128)(2,1)S(1)} %pad_maximum_fusion.1.refs_6_), channel_id=1, source_target_pairs={{0,8},{8,0},{1,9},{9,1},{2,10},{10,2},{3,11},{11,3},{4,12},{12,4},... | collective-permute-start | bytes 3145736 | tf_op jit(solution)/shard_map/ppermute | solution.py:22
  61.9 23.5 %collective-permute-start.12 = (bf16[8,128,512]{2,1,0:T(8,128)(2,1)S(1)}, bf16[8,128,512]{2,1,0:T(8,128)(2,1)S(1)}, u32[]{:S(2)}, u32[]{:S(2)}) collective-permute-start(bf16[8,128,512]{2,1,0:T(8,128)(2,1)S(1)} %collective-permute-done.7.refs_7_), channel_id=1, source_target_pairs={{0,8},{8,0},{1,9},{9,1},{2,10},{10,2},{3,11},{11,3},{4,12},{12,4},... | collective-permute-start | bytes 3145736 | tf_op jit(solution)/shard_map/ppermute | solution.py:22
  62.4 18.3 %collective-permute-start.14 = (s32[256]{0:T(256)S(1)}, s32[256]{0:T(256)S(1)}, u32[]{:S(2)}, u32[]{:S(2)}) collective-permute-start(s32[256]{0:T(256)S(1)} %pad_add_fusion.2), channel_id=1, source_target_pairs={{0,16},{16,0},{1,17},{17,1},{2,18},{18,2},{3,19},{19,3},{4,20},{20... | collective-permute-start | bytes 3080 | tf_op jit(solution)/shard_map/ppermute | solution.py:22
  86.4 9.0 %collective-permute-start.15 = (bf16[96,128,128]{2,1,0:T(8,128)(2,1)}, bf16[96,128,128]{2,1,0:T(8,128)(2,1)}, u32[]{:S(2)}, u32[]{:S(2)}) collective-permute-start(bf16[96,128,128]{2,1,0:T(8,128)(2,1)} %collective-permute-done.13.refs_2_), channel_id=1, source_target_pairs={{0,8},{8,0},{1,9},{9,1},{2,10},{10,2},{3,11},{11,3},{4,12},{12,4},... | collective-permute-start | bytes 9437192 | tf_op jit(solution)/shard_map/ppermute | solution.py:22
  87.4 6.5 %collective-permute-start.16 = (bf16[8,128,512]{2,1,0:T(8,128)(2,1)}, bf16[8,128,512]{2,1,0:T(8,128)(2,1)}, u32[]{:S(2)}, u32[]{:S(2)}) collective-permute-start(bf16[8,128,512]{2,1,0:T(8,128)(2,1)} %pad_maximum_fusion.2.refs_8_), channel_id=1, source_target_pairs={{0,8},{8,0},{1,9},{9,1},{2,10},{10,2},{3,11},{11,3},{4,12},{12,4},... | collective-permute-start | bytes 3145736 | tf_op jit(solution)/shard_map/ppermute | solution.py:22
  87.4 8.0 %collective-permute-start.17 = (bf16[8,128,512]{2,1,0:T(8,128)(2,1)}, bf16[8,128,512]{2,1,0:T(8,128)(2,1)}, u32[]{:S(2)}, u32[]{:S(2)}) collective-permute-start(bf16[8,128,512]{2,1,0:T(8,128)(2,1)} %collective-permute-done.10.refs_9_), channel_id=1, source_target_pairs={{0,8},{8,0},{1,9},{9,1},{2,10},{10,2},{3,11},{11,3},{4,12},{12,4},... | collective-permute-start | bytes 3145736 | tf_op jit(solution)/shard_map/ppermute | solution.py:22
  117.5 26.1 %collective-permute-start.18 = (bf16[16,128,256]{2,1,0:T(8,128)(2,1)}, bf16[16,128,256]{2,1,0:T(8,128)(2,1)S(1)}, u32[]{:S(2)}, u32[]{:S(2)}) collective-permute-start(bf16[16,128,256]{2,1,0:T(8,128)(2,1)} %get-tuple-element.64), channel_id=1, source_target_pairs={{0,1},{1,0},{2,3},{3,2},{4,5},{5,4},{6,7},{7,6},{8,9},{9,8},{10,11... | collective-permute-start | bytes 3145736 | tf_op jit(solution)/shard_map/ppermute | solution.py:22
  118.8 25.1 %collective-permute-start.19 = (bf16[16,128,256]{2,1,0:T(8,128)(2,1)}, bf16[16,128,256]{2,1,0:T(8,128)(2,1)S(1)}, u32[]{:S(2)}, u32[]{:S(2)}) collective-permute-start(bf16[16,128,256]{2,1,0:T(8,128)(2,1)} %get-tuple-element.65), channel_id=1, source_target_pairs={{0,16},{16,0},{1,17},{17,1},{2,18},{18,2},{3,19},{19,3},{4,20},{20... | collective-permute-start | bytes 3145736 | tf_op jit(solution)/shard_map/ppermute | solution.py:22
  143.9 3.5 copy-start.26
  143.9 4.6 %copy-start.25 = (bf16[16,128,256]{2,1,0:T(8,128)(2,1)S(1)}, bf16[16,128,256]{2,1,0:T(8,128)(2,1)}, u32[]{:S(2)}) copy-start(bf16[16,128,256]{2,1,0:T(8,128)(2,1)} %get-tuple-element.69) | copy-start | bytes 3145732
  146.1 13.4 %collective-permute-start.20 = (bf16[2,512,256]{2,1,0:T(8,128)(2,1)S(1)}, bf16[2,512,256]{2,1,0:T(8,128)(2,1)S(1)}, u32[]{:S(2)}, u32[]{:S(2)}) collective-permute-start(bf16[2,512,256]{2,1,0:T(8,128)(2,1)S(1)} %bitcast.88), channel_id=1, source_target_pairs={{0,2},{2,0},{4,6},{6,4},{1,3},{3,1},{5,7},{7,5},{8,10},{10,8},{12,... | collective-permute-start | bytes 1572872 | tf_op jit(solution)/shard_map/ppermute | solution.py:27
  147.4 25.8 %collective-permute-start.22 = (bf16[16,128,256]{2,1,0:T(8,128)(2,1)S(1)}, bf16[16,128,256]{2,1,0:T(8,128)(2,1)S(1)}, u32[]{:S(2)}, u32[]{:S(2)}) collective-permute-start(bf16[16,128,256]{2,1,0:T(8,128)(2,1)S(1)} %copy-done.26), channel_id=1, source_target_pairs={{0,1},{1,0},{2,3},{3,2},{4,5},{5,4},{6,7},{7,6},{8,9},{9,8},{10,11... | collective-permute-start | bytes 3145736 | tf_op jit(solution)/shard_map/ppermute | solution.py:22
  148.5 24.7 %collective-permute-start.23 = (bf16[16,128,256]{2,1,0:T(8,128)(2,1)S(1)}, bf16[16,128,256]{2,1,0:T(8,128)(2,1)S(1)}, u32[]{:S(2)}, u32[]{:S(2)}) collective-permute-start(bf16[16,128,256]{2,1,0:T(8,128)(2,1)S(1)} %copy-done.25), channel_id=1, source_target_pairs={{0,16},{16,0},{1,17},{17,1},{2,18},{18,2},{3,19},{19,3},{4,20},{20... | collective-permute-start | bytes 3145736 | tf_op jit(solution)/shard_map/ppermute | solution.py:22
  159.6 13.6 %copy-start.10 = (f32[16,128,256]{2,1,0:T(8,128)S(1)}, f32[16,128,256]{2,1,0:T(8,128)}, u32[]{:S(2)}) copy-start(f32[16,128,256]{2,1,0:T(8,128)} %get-tuple-element.71) | copy-start | bytes 6291460
  159.7 13.4 %collective-permute-start.21 = (bf16[512,256]{1,0:T(8,128)(2,1)S(1)}, bf16[512,256]{1,0:T(8,128)(2,1)S(1)}, u32[]{:S(2)}, u32[]{:S(2)}) collective-permute-start(bf16[512,256]{1,0:T(8,128)(2,1)S(1)} %fusion.11), channel_id=1, source_target_pairs={{0,4},{2,6},{4,0},{6,2},{1,5},{3,7},{5,1},{7,3},{8,12},{10,14},{12... | collective-permute-start | bytes 786440 | tf_op jit(solution)/shard_map/ppermute | solution.py:27
  173.7 20.3 %collective-permute-start.26 = (bf16[2,512,256]{2,1,0:T(8,128)(2,1)S(1)}, bf16[2,512,256]{2,1,0:T(8,128)(2,1)S(1)}, u32[]{:S(2)}, u32[]{:S(2)}) collective-permute-start(bf16[2,512,256]{2,1,0:T(8,128)(2,1)S(1)} %bitcast.87), channel_id=1, source_target_pairs={{0,2},{2,0},{4,6},{6,4},{1,3},{3,1},{5,7},{7,5},{8,10},{10,8},{12,... | collective-permute-start | bytes 1572872 | tf_op jit(solution)/shard_map/ppermute | solution.py:27
  173.8 16.4 %collective-permute-start.24 = (bf16[512,256]{1,0:T(8,128)(2,1)S(1)}, bf16[512,256]{1,0:T(8,128)(2,1)S(1)}, u32[]{:S(2)}, u32[]{:S(2)}) collective-permute-start(bf16[512,256]{1,0:T(8,128)(2,1)S(1)} %convert_element_type.86), channel_id=1, source_target_pairs={{0,4},{2,6},{4,0},{6,2},{1,5},{3,7},{5,1},{7,3},{8,12},{10,14},{12... | collective-permute-start | bytes 786440 | tf_op jit(solution)/shard_map/ppermute | solution.py:27
  190.3 19.2 %collective-permute-start.25 = (bf16[1024,256]{1,0:T(8,128)(2,1)S(1)}, bf16[1024,256]{1,0:T(8,128)(2,1)S(1)}, u32[]{:S(2)}, u32[]{:S(2)}) collective-permute-start(bf16[1024,256]{1,0:T(8,128)(2,1)S(1)} %pad_maximum_fusion.10), channel_id=1, source_target_pairs={{0,2},{2,0},{4,6},{6,4},{1,3},{3,1},{5,7},{7,5},{8,10},{10,8},{12,... | collective-permute-start | bytes 1572872 | tf_op jit(solution)/shard_map/ppermute | solution.py:27
  194.1 14.6 %collective-permute-start.27 = (bf16[512,256]{1,0:T(8,128)(2,1)S(1)}, bf16[512,256]{1,0:T(8,128)(2,1)S(1)}, u32[]{:S(2)}, u32[]{:S(2)}) collective-permute-start(bf16[512,256]{1,0:T(8,128)(2,1)S(1)} %fusion.12), channel_id=1, source_target_pairs={{0,4},{2,6},{4,0},{6,2},{1,5},{3,7},{5,1},{7,3},{8,12},{10,14},{12... | collective-permute-start | bytes 786440 | tf_op jit(solution)/shard_map/ppermute | solution.py:27
  209.6 12.8 %collective-permute-start.28 = (bf16[512,256]{1,0:T(8,128)(2,1)S(1)}, bf16[512,256]{1,0:T(8,128)(2,1)S(1)}, u32[]{:S(2)}, u32[]{:S(2)}) collective-permute-start(bf16[512,256]{1,0:T(8,128)(2,1)S(1)} %convert_element_type.93), channel_id=1, source_target_pairs={{0,4},{2,6},{4,0},{6,2},{1,5},{3,7},{5,1},{7,3},{8,12},{10,14},{12... | collective-permute-start | bytes 786440 | tf_op jit(solution)/shard_map/ppermute | solution.py:27
  212.4 22.6 %collective-permute-start.30 = (bf16[2048,256]{1,0:T(8,128)(2,1)S(1)}, bf16[2048,256]{1,0:T(8,128)(2,1)S(1)}, u32[]{:S(2)}, u32[]{:S(2)}) collective-permute-start(bf16[2048,256]{1,0:T(8,128)(2,1)S(1)} %pad_maximum_fusion.3), channel_id=1, source_target_pairs={{0,1},{1,0},{2,3},{3,2},{4,5},{5,4},{6,7},{7,6},{8,9},{9,8},{10,11... | collective-permute-start | bytes 3145736 | tf_op jit(solution)/shard_map/ppermute | solution.py:22
  213.2 23.3 %collective-permute-start.31 = (bf16[2048,256]{1,0:T(8,128)(2,1)S(1)}, bf16[2048,256]{1,0:T(8,128)(2,1)S(1)}, u32[]{:S(2)}, u32[]{:S(2)}) collective-permute-start(bf16[2048,256]{1,0:T(8,128)(2,1)S(1)} %pad_maximum_fusion.3), channel_id=1, source_target_pairs={{0,16},{16,0},{1,17},{17,1},{2,18},{18,2},{3,19},{19,3},{4,20},{20... | collective-permute-start | bytes 3145736 | tf_op jit(solution)/shard_map/ppermute | solution.py:22
  222.5 12.4 %collective-permute-start.29 = (bf16[1024,256]{1,0:T(8,128)(2,1)S(1)}, bf16[1024,256]{1,0:T(8,128)(2,1)S(1)}, u32[]{:S(2)}, u32[]{:S(2)}) collective-permute-start(bf16[1024,256]{1,0:T(8,128)(2,1)S(1)} %pad_maximum_fusion.11), channel_id=1, source_target_pairs={{0,2},{2,0},{4,6},{6,4},{1,3},{3,1},{5,7},{7,5},{8,10},{10,8},{12,... | collective-permute-start | bytes 1572872 | tf_op jit(solution)/shard_map/ppermute | solution.py:27
  236.5 2.0 copy-start.15
  236.6 28.4 %copy-start.3 = (bf16[4096,256]{1,0:T(8,128)(2,1)}, bf16[4096,256]{1,0:T(8,128)(2,1)S(1)}, u32[]{:S(2)}) copy-start(bf16[4096,256]{1,0:T(8,128)(2,1)S(1)} %constant_dynamic-update-slice_fusion) | copy-start | bytes 6291460
  236.6 26.9 %collective-permute-start.34 = (bf16[4096,256]{1,0:T(8,128)(2,1)S(1)}, bf16[4096,256]{1,0:T(8,128)(2,1)S(1)}, u32[]{:S(2)}, u32[]{:S(2)}) collective-permute-start(bf16[4096,256]{1,0:T(8,128)(2,1)S(1)} %constant_dynamic-update-slice_fusion), channel_id=1, source_target_pairs={{0,8},{8,0},{1,9},{9,1},{2,10},{10,2},{3,11},{11,3},{4,12},{12,4},... | collective-permute-start | bytes 6291464 | tf_op jit(solution)/shard_map/ppermute | solution.py:22
  236.6 25.6 %collective-permute-start.32 = (bf16[2048,256]{1,0:T(8,128)(2,1)S(1)}, bf16[2048,256]{1,0:T(8,128)(2,1)S(1)}, u32[]{:S(2)}, u32[]{:S(2)}) collective-permute-start(bf16[2048,256]{1,0:T(8,128)(2,1)S(1)} %pad_maximum_fusion.4), channel_id=1, source_target_pairs={{0,1},{1,0},{2,3},{3,2},{4,5},{5,4},{6,7},{7,6},{8,9},{9,8},{10,11... | collective-permute-start | bytes 3145736 | tf_op jit(solution)/shard_map/ppermute | solution.py:22
  238.3 25.2 %collective-permute-start.33 = (bf16[2048,256]{1,0:T(8,128)(2,1)S(1)}, bf16[2048,256]{1,0:T(8,128)(2,1)S(1)}, u32[]{:S(2)}, u32[]{:S(2)}) collective-permute-start(bf16[2048,256]{1,0:T(8,128)(2,1)S(1)} %pad_maximum_fusion.4), channel_id=1, source_target_pairs={{0,16},{16,0},{1,17},{17,1},{2,18},{18,2},{3,19},{19,3},{4,20},{20... | collective-permute-start | bytes 3145736 | tf_op jit(solution)/shard_map/ppermute | solution.py:22
  238.3 25.2 %collective-permute-start.35 = (bf16[2048,256]{1,0:T(8,128)(2,1)S(1)}, bf16[2048,256]{1,0:T(8,128)(2,1)S(1)}, u32[]{:S(2)}, u32[]{:S(2)}) collective-permute-start(bf16[2048,256]{1,0:T(8,128)(2,1)S(1)} %collective-permute-done.31), channel_id=1, source_target_pairs={{0,8},{8,0},{1,9},{9,1},{2,10},{10,2},{3,11},{11,3},{4,12},{12,4},... | collective-permute-start | bytes 3145736 | tf_op jit(solution)/shard_map/ppermute | solution.py:22
  263.6 2.5 copy-start.5
  263.6 10.9 %collective-permute-start.37 = (bf16[4096,256]{1,0:T(8,128)(2,1)S(1)}, bf16[4096,256]{1,0:T(8,128)(2,1)S(1)}, u32[]{:S(2)}, u32[]{:S(2)}) collective-permute-start(bf16[4096,256]{1,0:T(8,128)(2,1)S(1)} %constant_dynamic-update-slice_fusion.2), channel_id=1, source_target_pairs={{0,8},{8,0},{1,9},{9,1},{2,10},{10,2},{3,11},{11,3},{4,12},{12,4},... | collective-permute-start | bytes 6291464 | tf_op jit(solution)/shard_map/ppermute | solution.py:22
  263.7 10.8 %collective-permute-start.38 = (bf16[2048,256]{1,0:T(8,128)(2,1)S(1)}, bf16[2048,256]{1,0:T(8,128)(2,1)S(1)}, u32[]{:S(2)}, u32[]{:S(2)}) collective-permute-start(bf16[2048,256]{1,0:T(8,128)(2,1)S(1)} %collective-permute-done.33), channel_id=1, source_target_pairs={{0,8},{8,0},{1,9},{9,1},{2,10},{10,2},{3,11},{11,3},{4,12},{12,4},... | collective-permute-start | bytes 3145736 | tf_op jit(solution)/shard_map/ppermute | solution.py:22
  266.9 7.6 %collective-permute-start.36 = (f32[256,256]{1,0:T(8,128)S(1)}, f32[256,256]{1,0:T(8,128)S(1)}, u32[]{:S(2)}, u32[]{:S(2)}) collective-permute-start(f32[256,256]{1,0:T(8,128)S(1)} %convolution_add_fusion.2), channel_id=1, source_target_pairs={{0,16},{16,0},{1,17},{17,1},{2,18},{18,2},{3,19},{19,3},{4,20},{20... | collective-permute-start | bytes 786440 | tf_op jit(solution)/shard_map/ppermute | solution.py:22
  297.9 36.9 %collective-permute-start.41 = (bf16[16,128,256]{2,1,0:T(8,128)(2,1)}, bf16[16,128,256]{2,1,0:T(8,128)(2,1)S(1)}, u32[]{:S(2)}, u32[]{:S(2)}) collective-permute-start(bf16[16,128,256]{2,1,0:T(8,128)(2,1)} %get-tuple-element.88), channel_id=1, source_target_pairs={{0,1},{1,0},{2,3},{3,2},{4,5},{5,4},{6,7},{7,6},{8,9},{9,8},{10,11... | collective-permute-start | bytes 3145736 | tf_op jit(solution)/shard_map/ppermute | solution.py:22
  298.6 3.8 copy-start.4
  298.6 3.8 copy-start.6
  298.6 36.0 %collective-permute-start.40 = (bf16[16,128,256]{2,1,0:T(8,128)(2,1)}, bf16[16,128,256]{2,1,0:T(8,128)(2,1)S(1)}, u32[]{:S(2)}, u32[]{:S(2)}) collective-permute-start(bf16[16,128,256]{2,1,0:T(8,128)(2,1)} %get-tuple-element.86), channel_id=1, source_target_pairs={{0,16},{16,0},{1,17},{17,1},{2,18},{18,2},{3,19},{19,3},{4,20},{20... | collective-permute-start | bytes 3145736 | tf_op jit(solution)/shard_map/ppermute | solution.py:22
  304.7 2.1 copy-start.2
  305.5 28.9 %collective-permute-start.39 = (f32[256,512]{1,0:T(8,128)S(1)}, f32[256,512]{1,0:T(8,128)S(1)}, u32[]{:S(2)}, u32[]{:S(2)}) collective-permute-start(f32[256,512]{1,0:T(8,128)S(1)} %pad_maximum_fusion.12), channel_id=1, source_target_pairs={{0,16},{16,0},{1,17},{17,1},{2,18},{18,2},{3,19},{19,3},{4,20},{20... | collective-permute-start | bytes 1572872 | tf_op jit(solution)/shard_map/ppermute | solution.py:22
  336.5 14.5 %collective-permute-start.42 = (bf16[4,256,256]{2,1,0:T(8,128)(2,1)S(1)}, bf16[4,256,256]{2,1,0:T(8,128)(2,1)S(1)}, u32[]{:S(2)}, u32[]{:S(2)}) collective-permute-start(bf16[4,256,256]{2,1,0:T(8,128)(2,1)S(1)} %fusion.4), channel_id=1, source_target_pairs={{0,1},{1,0},{2,3},{3,2},{4,5},{5,4},{6,7},{7,6},{8,9},{9,8},{10,11... | collective-permute-start | bytes 1572872 | tf_op jit(solution)/shard_map/ppermute | solution.py:22
  338.2 12.9 %collective-permute-start.43 = (bf16[4,256,256]{2,1,0:T(8,128)(2,1)S(1)}, bf16[4,256,256]{2,1,0:T(8,128)(2,1)S(1)}, u32[]{:S(2)}, u32[]{:S(2)}) collective-permute-start(bf16[4,256,256]{2,1,0:T(8,128)(2,1)S(1)} %fusion.5), channel_id=1, source_target_pairs={{0,16},{16,0},{1,17},{17,1},{2,18},{18,2},{3,19},{19,3},{4,20},{20... | collective-permute-start | bytes 1572872 | tf_op jit(solution)/shard_map/ppermute | solution.py:22
  351.7 12.1 %collective-permute-start.44 = (bf16[2,256,512]{2,1,0:T(8,128)(2,1)S(1)}, bf16[2,256,512]{2,1,0:T(8,128)(2,1)S(1)}, u32[]{:S(2)}, u32[]{:S(2)}) collective-permute-start(bf16[2,256,512]{2,1,0:T(8,128)(2,1)S(1)} %slice.150), channel_id=1, source_target_pairs={{0,2},{2,0},{4,6},{6,4},{1,3},{3,1},{5,7},{7,5},{8,10},{10,8},{12,... | collective-permute-start | bytes 1572872 | tf_op jit(solution)/shard_map/ppermute | solution.py:27
  364.0 16.4 %collective-permute-start.45 = (bf16[256,512]{1,0:T(8,128)(2,1)S(1)}, bf16[256,512]{1,0:T(8,128)(2,1)S(1)}, u32[]{:S(2)}, u32[]{:S(2)}) collective-permute-start(bf16[256,512]{1,0:T(8,128)(2,1)S(1)} %fusion.13), channel_id=1, source_target_pairs={{0,4},{2,6},{4,0},{6,2},{1,5},{3,7},{5,1},{7,3},{8,12},{10,14},{12... | collective-permute-start | bytes 786440 | tf_op jit(solution)/shard_map/ppermute | solution.py:27
  382.2 13.1 %all-to-all-start = ((f32[4,128,256]{2,1,0:T(8,128)}), f32[4,128,256]{2,1,0:T(8,128)}, u32[]{:S(2)}, u32[]{:S(2)}) async-start(f32[4,128,256]{2,1,0:T(8,128)} %bitcast.89), calls=%async_computation | async-start | bytes 1048576 | tf_op jit(solution)/shard_map/all_to_all | solution.py:476
  386.4 10.8 %copy-start.1 = (bf16[1024,512]{1,0:T(8,128)(2,1)S(1)}, bf16[1024,512]{1,0:T(8,128)(2,1)}, u32[]{:S(2)}) copy-start(bf16[1024,512]{1,0:T(8,128)(2,1)} %param.9) | copy-start | bytes 3145732
  (10 other events, 14.2 us)

commit v4 on v3

v4 whole, which is shorter than its diff:
```python
import functools

import jax
import jax.numpy as jnp
from jax import lax
from jax.experimental import pallas as pl
from jax.experimental.pallas import tpu as pltpu
from jax.sharding import Mesh, PartitionSpec as P

RB_DEV = 32
UNROLL = 32
AHEAD = 2
CHUNKS = 2
LEAF = 128
MOST_SLOTS = 512
VMEM_LIMIT = 60 * 1024 * 1024
HIGHEST = lax.Precision.HIGHEST
ALL = ("x", "core", "p", "q")


def shift(value, axis, by):
    size = lax.axis_size(axis)
    return lax.ppermute(value, axis, [(i, (i + by) % size) for i in range(size)])


def swap(value, bit):
    size = lax.axis_size("p")
    return lax.ppermute(value, "p", [(i, i ^ bit) for i in range(size)])


def gather_p(value):
    pair = jnp.concatenate([value, swap(value, 2)])
    return jnp.concatenate([pair, swap(pair, 1)])


def reduce_p(total):
    part = total[:2] + swap(total[2:].astype(jnp.bfloat16), 1).astype(jnp.float32)
    return part[0] + swap(part[1].astype(jnp.bfloat16), 2).astype(jnp.float32)


def place_p(here, there):
    differs = here ^ there
    return (differs & 1) * 2 + (differs >> 1)


def together(*values):
    return lax.optimization_barrier(values)


def after(value, *others):
    return together(value, *others)[0]


def spread_pieces(value, axis):
    return [value] + [shift(value, axis, k) for k in range(1, lax.axis_size(axis))]


def absolute(pieces, axis):
    size, me = len(pieces), lax.axis_index(axis)
    laid = jnp.concatenate(pieces + pieces[:-1], axis=0)
    rows = pieces[0].shape[0]
    return lax.dynamic_slice_in_dim(laid, (size - me) % size * rows, size * rows, axis=0)


def reduce_stage(keep, sends, axis):
    total = keep
    for k, part in enumerate(sends, 1):
        total = total + shift(part, axis, k).astype(jnp.float32)
    return total


def passes_of(bounds):
    groups, room = [], 0
    for i, bound in enumerate(bounds):
        if not groups or room + bound > MOST_SLOTS:
            groups.append([])
            room = 0
        groups[-1].append(i)
        room += bound
    return groups


def slots_of(bounds):
    return max(sum(bounds[i] for i in group) for group in passes_of(bounds))


def list_kernel(counts_in, bounds, spare, rows_ref, cols_ref, counts, index, rows, cols):
    base = [0]
    for held in counts_in:
        base.append(base[-1] + held)
    start = 0
    for group in passes_of(bounds):
        slot = jnp.int32(start)
        for s in group:

            def take(i, slot, s=s):
                row = rows_ref[base[s] + i]

                @pl.when(row >= 0)
                def _():
                    index[slot] = i
                    rows[slot] = row
                    cols[slot] = cols_ref[base[s] + i]

                return slot + jnp.where(row >= 0, 1, 0).astype(jnp.int32)

            before = slot
            slot = lax.fori_loop(0, counts_in[s], take, slot)
            counts[s] = slot - before
        for extra in range(UNROLL - 1):
            rows[slot + extra] = spare
            cols[slot + extra] = 0
        start += sum(bounds[s] for s in group) + UNROLL


def block_lists(counts_in, bounds, spare, rows, cols):
    smem = pl.BlockSpec(memory_space=pltpu.SMEM)
    size = sum(bounds) + UNROLL * len(passes_of(bounds))
    shape = jax.ShapeDtypeStruct((size,), jnp.int32)
    return pl.pallas_call(
        functools.partial(list_kernel, counts_in, bounds, spare),
        out_shape=[jax.ShapeDtypeStruct((len(bounds),), jnp.int32), shape, shape, shape],
        in_specs=[smem, smem],
        out_specs=[smem] * 4,
        cost_estimate=pl.CostEstimate(flops=4 << 30, bytes_accessed=1 << 14, transcendentals=0),
        name="block_lists",
    )(rows, cols)


def accumulate(bounds, contract, lists, sources, panel_copies, scratch):
    counts, index, list_rows, list_cols = lists
    slots, panels, acc, sem, panel_sem = scratch
    copies = [
        pltpu.make_async_copy(source, target, panel_sem.at[i])
        for i, (source, target) in enumerate(panel_copies)
    ]

    start = 0
    for turn, group in enumerate(passes_of(bounds)):
        count = jnp.int32(0)
        for s in group:

            def take(i, carry, s=s, count=count, start=start):
                slot = count + i
                pltpu.make_async_copy(
                    sources[s].at[index[start + slot]], slots.at[slot], sem
                ).start()
                return carry

            lax.fori_loop(0, counts[s], take, 0)
            count = count + counts[s]
        if turn == 0:
            for copy in copies:
                copy.start()

            def clear(i, carry):
                acc[i] = jnp.zeros(acc.shape[1:], acc.dtype)
                return carry

            lax.fori_loop(0, acc.shape[0] - 1, clear, 0)

        def settle(i, carry):
            pltpu.make_async_copy(sources[0].at[0], slots.at[0], sem).wait()
            return carry

        lax.fori_loop(0, count, settle, 0)
        if turn == 0:
            for copy in copies:
                copy.wait()

        def step(i, carry, start=start):
            for j in range(UNROLL):
                k = i * UNROLL + j
                row = list_rows[start + k]
                acc[row] += lax.dot_general(
                    slots[k],
                    panels[list_cols[start + k]],
                    (((contract,), (0,)), ((), ())),
                    preferred_element_type=jnp.float32,
                )
            return carry

        lax.fori_loop(0, (count + UNROLL - 1) // UNROLL, step, 0)
        start += sum(bounds[s] for s in group) + UNROLL


def sketch_kernel(bounds, pieces_n, chunk, *refs):
    n = len(bounds)
    lists, sources, pieces = refs[:4], refs[4 : 4 + n], refs[4 + n : 4 + n + pieces_n]
    outs, scratch = refs[4 + n + pieces_n : -5], refs[-5:]
    panels, acc = scratch[1], scratch[2]
    kc = acc.shape[-1]
    copies, base = [], 0
    for piece in pieces:
        rows = piece.shape[0]
        copies.append((piece.at[:, :, pl.ds(chunk * kc, kc)], panels.at[pl.ds(base, rows)]))
        base += rows
    accumulate(bounds, 1, lists, sources, copies, scratch)
    per = outs[0].shape[0]
    outs = outs[-((acc.shape[0] - 1) // per) :]
    for g, out in enumerate(outs):

        def give(i, carry, g=g, out=out):
            out[i] = acc[g * per + i].astype(out.dtype)
            return carry

        lax.fori_loop(0, per, give, 0)


def project_kernel(bounds, pieces_n, x_n, q_n, *refs):
    n = len(bounds)
    lists, sources, pieces = refs[:4], refs[4 : 4 + n], refs[4 + n : 4 + n + pieces_n]
    outs, scratch = refs[4 + n + pieces_n : -5], refs[-5:]
    panels, acc = scratch[1], scratch[2]
    copies, base = [], 0
    for piece in pieces:
        rows = piece.shape[0]
        copies.append((piece, panels.at[pl.ds(base, rows)]))
        base += rows
    accumulate(bounds, 0, lists, sources, copies, scratch)
    width = acc.shape[-1] // 2
    inner = (acc.shape[0] - 1) // (x_n * q_n)
    for g in range(x_n):

        def give_x(i, carry, g=g):
            out = outs[g]
            out[i] = acc[g * q_n * inner + i, :, :width].astype(out.dtype)
            return carry

        lax.fori_loop(0, q_n * inner, give_x, 0)
    for g in range(q_n):
        for x in range(x_n):

            def give_q(i, carry, g=g, x=x):
                out = outs[x_n + g]
                out[x * inner + i] = acc[(x * q_n + g) * inner + i, :, width:].astype(out.dtype)
                return carry

            lax.fori_loop(0, inner, give_q, 0)


def block_products(kernel, bounds, lists, sources, pieces, acc_n, width, outs, name, late=()):
    wide = sources[0].shape[1]
    smem = pl.BlockSpec(memory_space=pltpu.SMEM)
    anywhere = pl.BlockSpec(memory_space=pl.ANY)
    return pl.pallas_call(
        kernel,
        out_shape=outs,
        in_specs=[smem] * 4 + [anywhere] * (len(sources) + len(pieces) + len(late)),
        out_specs=[pl.BlockSpec(memory_space=pltpu.VMEM)] * len(outs),
        scratch_shapes=[
            pltpu.VMEM((slots_of(bounds) + UNROLL, wide, wide), jnp.bfloat16),
            pltpu.VMEM((sum(p.shape[0] for p in pieces), wide, width), jnp.bfloat16),
            pltpu.VMEM((acc_n + 1, wide, width), jnp.float32),
            pltpu.SemaphoreType.DMA,
            pltpu.SemaphoreType.DMA((len(pieces),)),
        ],
        compiler_params=pltpu.CompilerParams(vmem_limit_bytes=VMEM_LIMIT),
        cost_estimate=pl.CostEstimate(
            flops=2 * 128 * wide * wide * width, bytes_accessed=32 << 20, transcendentals=0
        ),
        name=name,
    )(*lists, *sources, *pieces, *late)


def dot32(a, b, dims):
    return lax.dot_general(
        a, b, (dims, ((), ())), precision=HIGHEST, preferred_element_type=jnp.float32
    )


def leaf_inverse(a):
    n = a.shape[0]
    place = lax.broadcasted_iota(jnp.int32, (n, n), 0)
    lane = lax.broadcasted_iota(jnp.int32, (n, n), 1)
    unit = jnp.where(place == lane, 1.0, 0.0).astype(a.dtype)
    pivots = jnp.ones((n, n), a.dtype)
    columns = {j: jnp.broadcast_to(a[:, j : j + 1], (n, n)) for j in range(AHEAD + 1)}
    for j in range(n):
        column = columns.pop(j)
        pivot = column[j : j + 1]
        times = jnp.where(place > j, column * (1.0 / pivot), 0.0)
        pivots = jnp.where(place == j, pivot, pivots)
        for t in columns:
            columns[t] = columns[t] - times * column[t : t + 1]
        a, unit = a - times * a[j : j + 1], unit - times * unit[j : j + 1]
        t = j + AHEAD + 1
        if t < n:
            columns[t] = jnp.broadcast_to(a[:, t : t + 1], (n, n))
    return unit * lax.rsqrt(pivots)


def inverse_kernel(scale, k, first, gram, *refs):
    before, out = refs[:k], refs[-1]
    n = out.shape[0]
    grams = [gram[first : first + n, j * n : (j + 1) * n] * scale for j in range(k + 1)]
    rest = grams[k]
    factors = []
    for j in range(k):
        factor = dot32(grams[0], before[j][:, :n], ((1,), (1,)))
        for i in range(1, j + 1):
            factor += dot32(grams[i], before[j][:, i * n : (i + 1) * n], ((1,), (1,)))
        rest = rest - dot32(factor, factor, ((1,), (1,)))
        factors.append(factor)
    corner = leaf_inverse(rest)
    out[...] = jnp.zeros(out.shape, out.dtype)
    if k:
        total = dot32(factors[0], before[0][:, : k * n], ((1,), (0,)))
        for j in range(1, k):
            total += dot32(factors[j], before[j][:, : k * n], ((1,), (0,)))
        out[:, : k * n] = -dot32(corner, total, ((1,), (0,)))
    out[:, k * n : (k + 1) * n] = corner


def inverse_rows(scale, gram, first, before, width, late):
    vmem, anywhere = pl.BlockSpec(memory_space=pltpu.VMEM), pl.BlockSpec(memory_space=pl.ANY)
    return pl.pallas_call(
        functools.partial(inverse_kernel, scale, len(before), first),
        out_shape=jax.ShapeDtypeStruct((LEAF, width), jnp.float32),
        in_specs=[vmem] * (1 + len(before)) + [anywhere] * len(late),
        out_specs=vmem,
        compiler_params=pltpu.CompilerParams(vmem_limit_bytes=16 << 20),
        cost_estimate=pl.CostEstimate(flops=6 << 30, bytes_accessed=1 << 20, transcendentals=0),
        name="inverse_rows",
    )(gram, *before, *late)


def per_device(blocks, owner, row_local, col_local, sketch):
    x_n, q_n, p_n = lax.axis_size("x"), lax.axis_size("q"), lax.axis_size("p")
    xi, ci, zi, yi = (lax.axis_index(a) for a in ALL)
    par = p_n * q_n
    total_devs = 2 * x_n * par
    held, wide = blocks.shape[0], blocks.shape[1]
    width = sketch.shape[1]
    col_dev = sketch.shape[0] // wide
    slot_cap = max(2, (2 * held + total_devs - 1) // total_devs)
    rows_each = RB_DEV // par
    cols_each = col_dev // (2 * x_n)
    all_rows = RB_DEV * wide * 2 * x_n
    bf16, f32 = jnp.bfloat16, jnp.float32
    kc = width // CHUNKS
    by_q_n = held // 4
    by_x_n = held - by_q_n

    by_x = [blocks[i * by_q_n : (i + 1) * by_q_n] for i in range(3)]
    last = blocks[by_x_n:]
    half = col_dev // 2
    early_n = half // 2
    later_n = half - early_n
    panels = sketch.reshape(col_dev, wide, width)
    mine = lax.dynamic_slice_in_dim(panels, ci * half, half, axis=0)
    code = (owner[:, 0] * RB_DEV + row_local) * col_dev + col_local

    def along_x(value):
        return [shift(value, "x", k) for k in range(1, x_n)]

    def along_q(value):
        return [shift(value, "q", k) for k in range(1, q_n)]

    def across(values):
        return [shift(value, "core", 1) for value in values]

    code_x, code_q, (code_far,) = along_x(code), along_q(code), across([code])
    by_x[0], code_x = together(by_x[0], code_x)
    last, code_q = together(last, code_q)
    line, got_0, got_q, (sibling,), code_far, mine, by_x = together(
        gather_p(mine[:early_n]), along_x(by_x[0]), along_q(last), across([blocks]),
        code_far, mine, by_x,
    )
    early = [line] + along_q(line)
    line, early, got_1, far_0, far_q, code_x_far, code_q_far, by_x = together(
        gather_p(mine[early_n:]), early, along_x(by_x[1]), across(got_0), across(got_q),
        across(code_x), across(code_q), by_x,
    )
    later = [line] + along_q(line)

    codes, along = [code, code_far], [jnp.arange(held) < by_x_n] * 2
    for i in range(3):
        for near, far in zip(code_x, code_x_far):
            codes += [c[i * by_q_n : (i + 1) * by_q_n] for c in (near, far)]
            along += [jnp.ones((by_q_n,), bool)] * 2
    for near, far in zip(code_q, code_q_far):
        codes += [near[by_x_n:], far[by_x_n:]]
        along += [jnp.zeros((by_q_n,), bool)] * 2
    counts = [c.shape[0] for c in codes]
    most_y, most_p = min(by_x_n, par * slot_cap), min(by_x_n, 2 * par * slot_cap)
    thirds = 6 * (x_n - 1)
    bounds_y = [most_y + by_q_n] * 2 + [min(by_q_n, most_y)] * thirds + [by_q_n] * (2 * q_n - 2)
    bounds_p = [most_p + by_q_n] * 2 + [min(by_q_n, most_p)] * thirds + [by_q_n] * (2 * q_n - 2)
    codes, along = jnp.concatenate(codes), jnp.concatenate(along)

    owners = codes // (RB_DEV * col_dev)
    row = codes // col_dev % RB_DEV
    col = codes % col_dev
    o_obs, o_par = owners // par, owners % par
    o_x, o_core = o_obs // 2, o_obs % 2
    o_z, o_y = o_par // q_n, o_par % q_n
    r_par, r_in = row // rows_each, row % rows_each
    r_z, r_y = r_par // q_n, r_par % q_n
    c_x, c_core, c_in = col // (2 * cols_each), col // cols_each % 2, col % cols_each

    per = p_n * rows_each
    groups = q_n + x_n - 1
    other_x = q_n - 1 + (o_x - xi) % x_n
    y_group = jnp.where(along, (r_y - yi) % q_n, jnp.where(o_x == xi, 0, other_x))
    y_slot = (y_group * p_n + place_p(zi, r_z)) * rows_each + r_in
    y_mine = (o_core == ci) & jnp.where(along, o_x == xi, r_y == yi)
    y_slot = jnp.where(y_mine, y_slot, -1)
    place = col % half
    device = (yi - o_y) % q_n * p_n + place_p(zi, o_z)
    y_panel = jnp.where(
        place < early_n,
        device * early_n + place,
        2 * par * early_n + device * later_n + place - early_n,
    )
    other = jnp.where(place < early_n, par * early_n, par * later_n)
    y_panel = y_panel + jnp.where(col // half == ci, 0, other)

    p_slot = ((c_x - xi) % x_n * q_n + (o_y - yi) % q_n) * p_n + place_p(zi, o_z)
    p_slot = p_slot * cols_each + c_in
    p_mine = (c_core == ci) & jnp.where(along, o_x == xi, r_y == yi)
    p_slot = jnp.where(p_mine, p_slot, -1)
    in_part = place_p(zi, r_z) * rows_each + r_in
    same_x = (jnp.where(o_core == ci, 0, q_n) + (yi - r_y) % q_n) * per
    not_x = (2 * q_n + jnp.where(o_core == ci, 0, x_n - 1) + (xi - o_x) % x_n - 1) * per
    p_panel = jnp.where(o_x == xi, same_x, not_x) + in_part

    slots = x_n * q_n * p_n * cols_each
    lists_y = block_lists(counts, bounds_y, groups * per, y_slot, y_panel)
    lists_p = block_lists(counts, bounds_p, slots, p_slot, p_panel)
    later, early_far, got_2, far_1, lists_y, lists_p = together(
        later, across(early), along_x(by_x[2]), across(got_1), lists_y, lists_p
    )
    later_far, far_2 = across(later), across(got_2)
    sketch_pieces = early + early_far + later + later_far
    sources = [blocks, sibling]
    for gots, fars in ((got_0, far_0), (got_1, far_1), (got_2, far_2), (got_q, far_q)):
        for got, far in zip(gots, fars):
            sources += [got, far]

    def y_products(chunk, late):
        shapes = [
            jax.ShapeDtypeStruct((per, wide, kc), bf16 if g else f32) for g in range(groups)
        ]
        return block_products(
            functools.partial(sketch_kernel, bounds_y, len(sketch_pieces), chunk), bounds_y,
            lists_y, sources, sketch_pieces, groups * per, kc, shapes, "sketch_products", late,
        )

    def y_received(parts):
        return (
            [shift(parts[k], "q", k) for k in range(1, q_n)]
            + [shift(parts[q_n - 1 + k], "x", k) for k in range(1, x_n)]
        )

    def y_summed(parts, got):
        keep = parts[0]
        for part in got:
            keep = keep + part.astype(f32)
        return reduce_p(keep.reshape(p_n, rows_each * wide, kc))

    def spread(line):
        return (
            [shift(line, "q", k) for k in range(1, q_n)],
            [shift(line, "x", k) for k in range(1, x_n)],
        )

    def siblings(line, here, there):
        here, there = jnp.concatenate([line, *here]), jnp.concatenate(there)
        return here, shift(here, "core", 1), there, shift(there, "core", 1)

    def gram_rows(parts, befores):
        return jnp.concatenate([
            sum(
                lax.dot_general(a, b, (((0,), (0,)), ((), ())), preferred_element_type=f32)
                for a, b in zip(parts[:2], before[:2])
            )
            for before in befores
        ], axis=1)

    def z_products(parts):
        kh = kc // 2
        shapes = [
            jax.ShapeDtypeStruct((slots // n, wide, kh), f32 if k == 0 else bf16)
            for n in (x_n, q_n) for k in range(n)
        ]
        pieces = [a.reshape(-1, wide, kc) for a in parts]
        return block_products(
            functools.partial(project_kernel, bounds_p, len(pieces), x_n, q_n), bounds_p,
            lists_p, sources, pieces, slots, kc, shapes, "project_products",
        )

    def z_first(parts):
        return (
            [shift(parts[k], "x", k) for k in range(1, x_n)],
            [shift(parts[x_n + k], "q", k) for k in range(1, q_n)],
        )

    def z_second(parts, got):
        by_x, by_q = parts[0], parts[x_n]
        for part in got[0]:
            by_x = by_x + part.astype(f32)
        for part in got[1]:
            by_q = by_q + part.astype(f32)
        by_x = by_x.reshape(q_n, p_n, cols_each * wide, kc // 2)
        by_q = by_q.reshape(x_n, p_n, cols_each * wide, kc // 2)
        by_x = reduce_stage(by_x[0], [by_x[k].astype(bf16) for k in range(1, q_n)], "q")
        by_q = reduce_stage(by_q[0], [by_q[k].astype(bf16) for k in range(1, x_n)], "x")
        return jnp.concatenate([by_x, by_q], axis=2)

    inverse = []

    def more_rows(gram, *late):
        inverse.append(
            inverse_rows(
                1.0 / all_rows, gram, len(inverse) * LEAF % kc, inverse, width, late
            )
        )
        return inverse[-1]

    parts_a = y_products(0, ())
    got_a = y_received(parts_a)
    got_a, parts_b = together(got_a, y_products(1, (parts_a[0],)))
    got_b = y_received(parts_b)
    own_a, got_b = together(y_summed(parts_a, got_a), got_b)
    line_a, own_b = together(gather_p(own_a.astype(bf16)), y_summed(parts_b, got_b))
    line_b, spread_a = together(gather_p(own_b.astype(bf16)), spread(line_a))
    spread_b = spread(line_b)
    all_a = together(siblings(line_a, *spread_a))[0]
    spread_b, zs_a, gram_a = together(spread_b, z_products(all_a), gram_rows(all_a, [all_a]))

    first_a = z_first(zs_a)
    got_gram = [shift(gram_a, "x", k) for k in range(1, x_n)]
    all_b = together(siblings(line_b, *spread_b))[0]
    first_a, zs_b = together(first_a, z_products(all_b))
    first_b = z_first(zs_b)
    gram_a = sum(after(got_gram, zs_b), gram_a)
    late_b = after(all_b, zs_b)
    mine_b = [lax.dynamic_slice_in_dim(part, ci * (kc // 2), kc // 2, axis=1) for part in late_b[:2]]
    gram_b = gram_rows(mine_b, [all_a, late_b])
    second_a = z_second(zs_a, first_a)
    more_rows(gram_a, zs_b[0])
    first_b, gram_b, _ = together(first_b, gram_b, inverse[-1])
    got_gram = [shift(gram_b, "x", k) for k in range(1, x_n)]
    second_b = z_second(zs_b, first_b)
    z_a = reduce_p(second_a)
    more_rows(gram_a, first_b[0][0])
    second_b, got_gram, _ = together(second_b, got_gram, inverse[-1])
    z_b = reduce_p(second_b)
    gram_b = sum(got_gram, gram_b)
    gram_b = absolute([gram_b, shift(gram_b, "core", 1)], "core")
    more_rows(gram_b)
    more_rows(gram_b)
    inverse = jnp.concatenate(inverse, axis=0)
    own_rows = jnp.concatenate([own_a, own_b], axis=1)
    basis = dot32(own_rows, inverse, ((1,), (1,))).astype(bf16)

    obs_n, me = 2 * x_n, xi * 2 + ci
    rows_n = width // obs_n
    turned = jnp.concatenate([inverse, inverse[:-rows_n]], axis=0)
    turned = lax.dynamic_slice_in_dim(turned, me * rows_n, width, axis=0)
    z_rows = jnp.concatenate([z_a, z_b], axis=1)
    kept, *sent = [
        dot32(turned[k * rows_n : (k + 1) * rows_n], z_rows, ((1,), (1,))) for k in range(obs_n)
    ]
    got = [
        lax.ppermute(part, ("x", "core"), [(i, (i + k) % obs_n) for i in range(obs_n)])
        for k, part in enumerate(sent, 1)
    ]
    laid = jnp.concatenate(got[::-1] + [kept] + got[::-1], axis=1)
    cols_n = kept.shape[1]
    projected = lax.dynamic_slice_in_dim(
        laid, (obs_n - 1 - me) * cols_n, obs_n * cols_n, axis=1
    )
    return (basis, projected)


def solution(mesh):
    obs, par = mesh.shape["obs"], mesh.shape["par"]
    fine = Mesh(mesh.devices.reshape(obs // 2, 2, 4, par // 4), ALL)
    spread = P(ALL)
    placed = (
        P(ALL, None, None),
        P(ALL, None),
        spread,
        spread,
        P(("p", "q"), None),
    )
    return jax.shard_map(
        per_device,
        mesh=fine,
        in_specs=placed,
        out_specs=(P(ALL, None), P(("x", "core"), ("p", "q"))),
        check_vma=False,
    )
```

time: 398 us -> 370 us (0.930)
  waiting for transfers between devices: 214 us -> 190 us
  starting transfers between devices: 56.5 us -> 47.8 us
  Pallas kernels: 92.5 us -> 87.1 us
  other arithmetic: 7.31 us -> 11.9 us
    ppermute x32 -> x43, waiting for transfers between devices: 87.5 us -> 57.2 us  [shift(): lax.ppermute(value, axis, [(i, (i + by) % size) for i in range(size)])]
    pallas_call x4, Pallas kernels: 48.7 us -> 30.1 us  [inverse_rows(): pl.pallas_call(functools.partial(inverse_kernel, scale, len(before), firs...]
    pallas_call x2 -> x6, Pallas kernels: 43.8 us -> 57 us  [the longest x4 41.7 us: block_products(): pl.pallas_call(kernel, out_shape=outs, in_specs=[smem] * 4 + [anywhere] *...]
    ppermute x14 -> x16, starting transfers between devices: 25.8 us -> 15.3 us  [swap(): return lax.ppermute(value, 'p', [(i, i ^ bit) for i in range(size)])]
    ppermute x14 -> x16, waiting for transfers between devices: 120 us -> 127 us  [swap(): return lax.ppermute(value, 'p', [(i, i ^ bit) for i in range(size)])]
    all_to_all x1 -> x0, waiting for transfers between devices: 6.23 us -> none  [per_device(): lax.all_to_all(projected, ('x', 'core'), split_axis=0, concat_axis=1, til...]
    ppermute x0 -> x3, waiting for transfers between devices: none -> 5.45 us  [per_device(): lax.ppermute(part, ('x', 'core'), [(i, (i + k) % obs_n) for i in range(ob...]
    all_to_all x1 -> x0, starting transfers between devices: 4.14 us -> none  [per_device(): lax.all_to_all(projected, ('x', 'core'), split_axis=0, concat_axis=1, til...]
  transfers between devices with their start and end apart: 47 -> 62, of which waited for: 26 -> 33; matrix products, arithmetic and copies ran while one was open for 4% -> 8% of each run, Pallas kernels for 12% -> 21%
where the time goes in v4:
time: 370 us; the launch traced here: 367 us
  waiting for transfers between devices  190 us (51%)
  Pallas kernels  87.1 us (24%)
  starting transfers between devices  47.8 us (13%)
  matrix products  14.6 us (4%)
  local copies, waits for them, and re-layouts  14 us (4%)
  other arithmetic  11.9 us (3%)
    ppermute x16, waiting for transfers between devices, swap(): return lax.ppermute(value, 'p', [(i, i ^ bit) for i in range(size)])  127 us
    ppermute x43, waiting for transfers between devices, shift(): lax.ppermute(value, axis, [(i, (i + by) % size) for i in range(size)])  57.2 us
    pallas_call x4, Pallas kernels, block_products(): pl.pallas_call(kernel, out_shape=outs, in_specs=[smem] * 4 + [anywhere] *...  41.7 us
    ppermute x43, starting transfers between devices, shift(): lax.ppermute(value, axis, [(i, (i + by) % size) for i in range(size)])  30.2 us
    pallas_call x4, Pallas kernels, inverse_rows(): pl.pallas_call(functools.partial(inverse_kernel, scale, len(before), firs...  30.1 us
    ppermute x16, starting transfers between devices, swap(): return lax.ppermute(value, 'p', [(i, i ^ bit) for i in range(size)])  15.3 us
    pallas_call x2, Pallas kernels, block_lists(): pl.pallas_call(functools.partial(list_kernel, counts_in, bounds, spare),...  15.3 us
    dot_general x6, matrix products, gram_rows(): lax.dot_general(a, b, (((0,), (0,)), ((), ())), preferred_element_type=f32)  9.29 us
  transfers between devices with their start and end apart: 62, of which 33 were waited for; matrix products, arithmetic and copies ran while one was open for 8% of the time, Pallas kernels for 21%

profile of v4, /device:TPU:0, one launch (start us, length us, event | category | flops | bytes accessed | tf_op | source)
XLA Modules:
  0.0 367.3 jit_solution(3042836476089278727)
XLA Ops:
  1.9 2.6 collective-permute-start.2
  4.4 1.5 collective-permute-start.4
  6.0 2.7 collective-permute-start
  8.6 4.1 %fusion.96 = (bf16[32,128,128]{2,1,0:T(8,128)(2,1)}, bf16[32,128,128]{2,1,0:T(8,128)(2,1)}, bf16[32,128,128]{2,1,0:T(8,128)(2,1)S(1)}, bf16[32,128,128]{2,1,0:T(8,128)(2,1)S(1)}) fusion(bf16[128,128,128]{2,1,0:T(8,128)(2,1)} %refs_4_.7), kind=kLoop, calls=%fused_computation.254 | loop fusion | bytes 8388608 | tf_op jit(solution)/shard_map/slice | solution.py:345
  13.7 6.9 %collective-permute-done = bf16[2,128,512]{2,1,0:T(8,128)(2,1)S(1)} collective-permute-done((bf16[2,128,512]{2,1,0:T(8,128)(2,1)S(1)}, bf16[2,128,512]{2,1,0:T(8,128)(2,1)S(1)}, u32[]{:S(2)}, u32[]{:S(2)}) %collective-permute-start) | collective-permute-done | bytes 262176 | tf_op jit(solution)/shard_map/ppermute | solution.py:28
  21.5 12.1 %collective-permute-done.1 = bf16[4,128,512]{2,1,0:T(8,128)(2,1)S(1)} collective-permute-done((bf16[4,128,512]{2,1,0:T(8,128)(2,1)S(1)}, bf16[4,128,512]{2,1,0:T(8,128)(2,1)S(1)}, u32[]{:S(2)}, u32[]{:S(2)}) %collective-permute-start.1) | collective-permute-done | bytes 524320 | tf_op jit(solution)/shard_map/ppermute | solution.py:28
  34.7 2.7 collective-permute-done.3.refs_6_
  39.2 1.4 collective-permute-start.11
  40.6 10.3 %collective-permute-done.8 = bf16[2,128,512]{2,1,0:T(8,128)(2,1)S(1)} collective-permute-done((bf16[2,128,512]{2,1,0:T(8,128)(2,1)S(1)}, bf16[2,128,512]{2,1,0:T(8,128)(2,1)S(1)}, u32[]{:S(2)}, u32[]{:S(2)}) %collective-permute-start.8) | collective-permute-done | bytes 262176 | tf_op jit(solution)/shard_map/ppermute | solution.py:28
  52.7 13.7 %collective-permute-done.9 = bf16[4,128,512]{2,1,0:T(8,128)(2,1)} collective-permute-done((bf16[4,128,512]{2,1,0:T(8,128)(2,1)}, bf16[4,128,512]{2,1,0:T(8,128)(2,1)}, u32[]{:S(2)}, u32[]{:S(2)}) %collective-permute-start.9) | collective-permute-done | bytes 524320 | tf_op jit(solution)/shard_map/ppermute | solution.py:28
  66.4 2.2 pad_maximum_fusion.1.refs_18_
  69.8 1.4 collective-permute-start.19
  72.6 7.7 %block_lists.3 = (s32[10]{0:T(128)}, s32[544]{0:T(1024)}, s32[544]{0:T(1024)}, s32[544]{0:T(1024)}) custom-call(s32[512]{0:T(512)} %get-tuple-element.207.rows_ref, s32[512]{0:T(512)} %get-tuple-element.200.cols_ref), custom_call_target="tpu_custom_call" | custom-call | flops 4294967296 | bytes 16384 | tf_op jit(solution)/shard_map/block_lists/pallas_call | solution.py:120
  80.3 7.6 %block_lists.2 = (s32[10]{0:T(128)}, s32[480]{0:T(512)}, s32[480]{0:T(512)}, s32[480]{0:T(512)}) custom-call(s32[512]{0:T(512)} %get-tuple-element.208.rows_ref, s32[512]{0:T(512)} %get-tuple-element.209.cols_ref), custom_call_target="tpu_custom_call" | custom-call | flops 4294967296 | bytes 16384 | tf_op jit(solution)/shard_map/block_lists/pallas_call | solution.py:120
  88.0 6.7 %collective-permute-done.16.refs_19_ = bf16[8,128,512]{2,1,0:T(8,128)(2,1)} collective-permute-done((bf16[8,128,512]{2,1,0:T(8,128)(2,1)}, bf16[8,128,512]{2,1,0:T(8,128)(2,1)}, u32[]{:S(2)}, u32[]{:S(2)}) %collective-permute-start.16) | collective-permute-done | bytes 1048608 | tf_op jit(solution)/shard_map/ppermute | solution.py:23
  96.0 2.4 collective-permute-done.21.refs_11_
  98.3 1.5 collective-permute-done.22.refs_20_
  99.8 1.5 collective-permute-done.23.refs_21_
  102.3 9.7 %sketch_products.2 = (f32[16,128,256]{2,1,0:T(8,128)}, bf16[16,128,256]{2,1,0:T(8,128)(2,1)}, bf16[16,128,256]{2,1,0:T(8,128)(2,1)}) custom-call(s32[10]{0:T(128)} %get-tuple-element.127.refs_0_, s32[480]{0:T(512)} %get-tuple-element.128.refs_1_, s32[480]{0:T(512)} %get-tuple-element.129.refs_2_, s32[480]{0:T(512)} %get-tuple-element.130.refs_3_, ...), custom_call_target="tpu_custom_call" | custom-call | flops 1073741824 | bytes 33554432 | tf_op jit(solution)/shard_map/sketch_products/pallas_call | solution.py:246
  112.0 1.5 collective-permute-start.24
  113.5 1.6 collective-permute-start.25
  115.1 9.8 %sketch_products.3 = (f32[16,128,256]{2,1,0:T(8,128)}, bf16[16,128,256]{2,1,0:T(8,128)(2,1)}, bf16[16,128,256]{2,1,0:T(8,128)(2,1)}) custom-call(s32[10]{0:T(128)} %get-tuple-element.127.refs_0_, s32[480]{0:T(512)} %get-tuple-element.128.refs_1_, s32[480]{0:T(512)} %get-tuple-element.129.refs_2_, s32[480]{0:T(512)} %get-tuple-element.130.refs_3_, ...), custom_call_target="tpu_custom_call" | custom-call | flops 1073741824 | bytes 33554432 | tf_op jit(solution)/shard_map/sketch_products/pallas_call | solution.py:246
  124.9 13.3 %collective-permute-done.24 = bf16[16,128,256]{2,1,0:T(8,128)(2,1)S(1)} collective-permute-done((bf16[16,128,256]{2,1,0:T(8,128)(2,1)}, bf16[16,128,256]{2,1,0:T(8,128)(2,1)S(1)}, u32[]{:S(2)}, u32[]{:S(2)}) %collective-permute-start.24) | collective-permute-done | bytes 1048608 | tf_op jit(solution)/shard_map/ppermute | solution.py:23
  138.2 1.5 collective-permute-done.25
  139.8 1.6 convert_add_fusion.1
  143.1 1.6 collective-permute-start.29
  144.6 10.8 %collective-permute-done.26 = bf16[2,512,256]{2,1,0:T(8,128)(2,1)S(1)} collective-permute-done((bf16[2,512,256]{2,1,0:T(8,128)(2,1)S(1)}, bf16[2,512,256]{2,1,0:T(8,128)(2,1)S(1)}, u32[]{:S(2)}, u32[]{:S(2)}) %collective-permute-start.26) | collective-permute-done | bytes 524320 | tf_op jit(solution)/shard_map/ppermute | solution.py:28
  155.6 1.4 collective-permute-start.27
  156.9 12.4 %collective-permute-done.27 = bf16[512,256]{1,0:T(8,128)(2,1)S(1)} collective-permute-done((bf16[512,256]{1,0:T(8,128)(2,1)S(1)}, bf16[512,256]{1,0:T(8,128)(2,1)S(1)}, u32[]{:S(2)}, u32[]{:S(2)}) %collective-permute-start.27) | collective-permute-done | bytes 262176 | tf_op jit(solution)/shard_map/ppermute | solution.py:28
  170.3 2.8 collective-permute-start.30
  173.2 14.1 %collective-permute-done.30 = bf16[512,256]{1,0:T(8,128)(2,1)S(1)} collective-permute-done((bf16[512,256]{1,0:T(8,128)(2,1)S(1)}, bf16[512,256]{1,0:T(8,128)(2,1)S(1)}, u32[]{:S(2)}, u32[]{:S(2)}) %collective-permute-start.30) | collective-permute-done | bytes 262176 | tf_op jit(solution)/shard_map/ppermute | solution.py:28
  187.3 3.5 collective-permute-start.31
  191.0 16.2 %collective-permute-done.33 = bf16[512,256]{1,0:T(8,128)(2,1)S(1)} collective-permute-done((bf16[512,256]{1,0:T(8,128)(2,1)S(1)}, bf16[512,256]{1,0:T(8,128)(2,1)S(1)}, u32[]{:S(2)}, u32[]{:S(2)}) %collective-permute-start.33) | collective-permute-done | bytes 262176 | tf_op jit(solution)/shard_map/ppermute | solution.py:28
  208.1 2.8 collective-permute-start.34
  211.3 10.5 %collective-permute-done.34 = bf16[512,256]{1,0:T(8,128)(2,1)S(1)} collective-permute-done((bf16[512,256]{1,0:T(8,128)(2,1)S(1)}, bf16[512,256]{1,0:T(8,128)(2,1)S(1)}, u32[]{:S(2)}, u32[]{:S(2)}) %collective-permute-start.34) | collective-permute-done | bytes 262176 | tf_op jit(solution)/shard_map/ppermute | solution.py:28
  222.0 12.8 %collective-permute-done.35 = bf16[1024,256]{1,0:T(8,128)(2,1)S(1)} collective-permute-done((bf16[1024,256]{1,0:T(8,128)(2,1)S(1)}, bf16[1024,256]{1,0:T(8,128)(2,1)S(1)}, u32[]{:S(2)}, u32[]{:S(2)}) %collective-permute-start.35) | collective-permute-done | bytes 524320 | tf_op jit(solution)/shard_map/ppermute | solution.py:28
  235.5 1.1 collective-permute-start.38
  237.1 3.6 collective-permute-done.41
  240.7 1.4 copy-done.12
  242.4 10.9 %project_products.2 = (f32[16,128,128]{2,1,0:T(8,128)}, bf16[16,128,128]{2,1,0:T(8,128)(2,1)}, f32[16,128,128]{2,1,0:T(8,128)}, bf16[16,128,128]{2,1,0:T(8,128)(2,1)}) custom-call(s32[10]{0:T(128)} %get-tuple-element.157.refs_0_, s32[544]{0:T(1024)} %get-tuple-element.158.refs_1_, s32[544]{0:T(1024)} %get-tuple-element.159.refs_2_, ...), custom_call_target="tpu_custom_call" | custom-call | flops 1073741824 | bytes 33554432 | tf_op jit(solution)/shard_map/project_products/pallas_call | solution.py:246
  253.3 3.1 fusion.99
  257.2 3.6 collective-permute-done.38
  261.6 1.3 constant_dynamic-update-slice_fusion.2
  264.7 1.7 collective-permute-start.42
  266.4 2.1 collective-permute-done.46
  269.5 11.3 %project_products.3 = (f32[16,128,128]{2,1,0:T(8,128)}, bf16[16,128,128]{2,1,0:T(8,128)(2,1)}, f32[16,128,128]{2,1,0:T(8,128)}, bf16[16,128,128]{2,1,0:T(8,128)(2,1)}) custom-call(s32[10]{0:T(128)} %get-tuple-element.157.refs_0_, s32[544]{0:T(1024)} %get-tuple-element.158.refs_1_, s32[544]{0:T(1024)} %get-tuple-element.159.refs_2_, ...), custom_call_target="tpu_custom_call" | custom-call | flops 1073741824 | bytes 33554432 | tf_op jit(solution)/shard_map/project_products/pallas_call | solution.py:246
  280.9 1.9 convert_add_fusion.2
  285.2 1.9 collective-permute-start.48
  287.2 3.9 %inverse_rows.4.refs_0_ = f32[128,512]{1,0:T(8,128)S(1)} custom-call(f32[256,256]{1,0:T(8,128)S(1)} %add.289.gram, f32[16,128,128]{2,1,0:T(8,128)S(1)} %copy-done.2), custom_call_target="tpu_custom_call" | custom-call | flops 6442450944 | bytes 1048576 | tf_op jit(solution)/shard_map/inverse_rows/pallas_call | solution.py:317
  291.1 1.9 fusion.11
  294.2 2.4 convolution_add_fusion.1
  297.0 4.8 %collective-permute-done.47.refs_1_ = bf16[16,128,128]{2,1,0:T(8,128)(2,1)S(1)} collective-permute-done((bf16[16,128,128]{2,1,0:T(8,128)(2,1)S(1)}, bf16[16,128,128]{2,1,0:T(8,128)(2,1)S(1)}, u32[]{:S(2)}, u32[]{:S(2)}) %collective-permute-start.47) | collective-permute-done | bytes 524320 | tf_op jit(solution)/shard_map/ppermute | solution.py:23
  302.2 4.9 %inverse_rows.5.refs_1_ = f32[128,512]{1,0:T(8,128)S(1)} custom-call(f32[256,256]{1,0:T(8,128)S(1)} %add.289.gram, f32[128,512]{1,0:T(8,128)S(1)} %inverse_rows.4.refs_0_, bf16[16,128,128]{2,1,0:T(8,128)(2,1)S(1)} %collective-permute-done.47.refs_1_), custom_call_target="tpu_custom_call" | custom-call | flops 6442450944 | bytes 1048576 | tf_op jit(solution)/shard_map/inverse_rows/pallas_call | solution.py:317
  307.5 1.7 collective-permute-start.49
  309.3 1.7 collective-permute-start.50
  311.7 3.6 collective-permute-done.49
  315.4 3.2 collective-permute-done.50
  318.7 4.2 %collective-permute-done.51 = f32[128,512]{1,0:T(8,128)S(1)} collective-permute-done((f32[128,512]{1,0:T(8,128)S(1)}, f32[128,512]{1,0:T(8,128)S(1)}, u32[]{:S(2)}, u32[]{:S(2)}) %collective-permute-start.51) | collective-permute-done | bytes 262176 | tf_op jit(solution)/shard_map/ppermute | solution.py:23
  323.5 6.6 %collective-permute-done.57 = bf16[2,256,256]{2,1,0:T(8,128)(2,1)S(1)} collective-permute-done((bf16[2,256,256]{2,1,0:T(8,128)(2,1)S(1)}, bf16[2,256,256]{2,1,0:T(8,128)(2,1)S(1)}, u32[]{:S(2)}, u32[]{:S(2)}) %collective-permute-start.57) | collective-permute-done | bytes 262176 | tf_op jit(solution)/shard_map/ppermute | solution.py:28
  330.5 14.8 %inverse_rows.6.refs_2_ = f32[128,512]{1,0:T(8,128)S(1)} custom-call(f32[256,512]{1,0:T(8,128)S(1)} %fusion.17.gram, f32[128,512]{1,0:T(8,128)S(1)} %inverse_rows.4.refs_0_, f32[128,512]{1,0:T(8,128)S(1)} %inverse_rows.5.refs_1_), custom_call_target="tpu_custom_call" | custom-call | flops 6442450944 | bytes 1048576 | tf_op jit(solution)/shard_map/inverse_rows/pallas_call | solution.py:317
  345.3 6.4 %inverse_rows.7 = f32[128,512]{1,0:T(8,128)S(1)} custom-call(f32[256,512]{1,0:T(8,128)S(1)} %fusion.17.gram, f32[128,512]{1,0:T(8,128)S(1)} %inverse_rows.4.refs_0_, f32[128,512]{1,0:T(8,128)S(1)} %inverse_rows.5.refs_1_, f32[128,512]{1,0:T(8,128)S(1)} %inverse_rows.6.refs_2_), custom_call_target="tpu_custom_call" | custom-call | flops 6442450944 | bytes 1048576 | tf_op jit(solution)/shard_map/inverse_rows/pallas_call | solution.py:317
  353.0 2.7 convolution_convert_fusion
  357.1 1.9 collective-permute-start.60
  360.0 5.0 %collective-permute-done.60 = f32[128,256]{1,0:T(8,128)S(1)} collective-permute-done((f32[128,256]{1,0:T(8,128)S(1)}, f32[128,256]{1,0:T(8,128)S(1)}, u32[]{:S(2)}, u32[]{:S(2)}) %collective-permute-start.60) | collective-permute-done | bytes 131104 | tf_op jit(solution)/shard_map/ppermute | solution.py:567
  (229 shorter events, 34.4 us)
Async XLA Ops:
  0.6 37.0 %collective-permute-start.6 = (bf16[128,128,128]{2,1,0:T(8,128)(2,1)}, bf16[128,128,128]{2,1,0:T(8,128)(2,1)}, u32[]{:S(2)}, u32[]{:S(2)}) collective-permute-start(bf16[128,128,128]{2,1,0:T(8,128)(2,1)} %refs_4_.7), channel_id=1, source_target_pairs={{0,8},{8,0},{1,9},{9,1},{2,10},{10,2},{3,11},{11,3},{4,12},{12,4},... | collective-permute-start | bytes 12582920 | tf_op jit(solution)/shard_map/ppermute | solution.py:23
  1.9 10.8 %collective-permute-start.2 = (s32[128]{0:T(128)S(1)}, s32[128]{0:T(128)S(1)}, u32[]{:S(2)}, u32[]{:S(2)}) collective-permute-start(s32[128]{0:T(128)S(1)} %fusion.90), channel_id=1, source_target_pairs={{0,16},{16,0},{1,17},{17,1},{2,18},{18,2},{3,19},{19,3},{4,20},{20... | collective-permute-start | bytes 1544 | tf_op jit(solution)/shard_map/ppermute | solution.py:23
  4.4 8.8 %collective-permute-start.4 = (s32[128]{0:T(128)S(1)}, s32[128]{0:T(128)S(1)}, u32[]{:S(2)}, u32[]{:S(2)}) collective-permute-start(s32[128]{0:T(128)S(1)} %fusion.90), channel_id=1, source_target_pairs={{0,1},{1,0},{2,3},{3,2},{4,5},{5,4},{6,7},{7,6},{8,9},{9,8},{10,11... | collective-permute-start | bytes 1544 | tf_op jit(solution)/shard_map/ppermute | solution.py:23
  6.0 14.7 %collective-permute-start = (bf16[2,128,512]{2,1,0:T(8,128)(2,1)S(1)}, bf16[2,128,512]{2,1,0:T(8,128)(2,1)S(1)}, u32[]{:S(2)}, u32[]{:S(2)}) collective-permute-start(bf16[2,128,512]{2,1,0:T(8,128)(2,1)S(1)} %constant_dynamic-slice_fusion), channel_id=1, source_target_pairs={{0,4},{2,6},{4,0},{6,2},{1,5},{3,7},{5,1},{7,3},{8,12},{10,14},{12... | collective-permute-start | bytes 786440 | tf_op jit(solution)/shard_map/ppermute | solution.py:28
  12.7 24.7 %collective-permute-start.3 = (bf16[32,128,128]{2,1,0:T(8,128)(2,1)S(1)}, bf16[32,128,128]{2,1,0:T(8,128)(2,1)S(1)}, u32[]{:S(2)}, u32[]{:S(2)}) collective-permute-start(bf16[32,128,128]{2,1,0:T(8,128)(2,1)S(1)} %get-tuple-element.101), channel_id=1, source_target_pairs={{0,16},{16,0},{1,17},{17,1},{2,18},{18,2},{3,19},{19,3},{4,20},{20... | collective-permute-start | bytes 3145736 | tf_op jit(solution)/shard_map/ppermute | solution.py:23
  13.2 24.4 %collective-permute-start.5 = (bf16[32,128,128]{2,1,0:T(8,128)(2,1)S(1)}, bf16[32,128,128]{2,1,0:T(8,128)(2,1)S(1)}, u32[]{:S(2)}, u32[]{:S(2)}) collective-permute-start(bf16[32,128,128]{2,1,0:T(8,128)(2,1)S(1)} %get-tuple-element.102), channel_id=1, source_target_pairs={{0,1},{1,0},{2,3},{3,2},{4,5},{5,4},{6,7},{7,6},{8,9},{9,8},{10,11... | collective-permute-start | bytes 3145736 | tf_op jit(solution)/shard_map/ppermute | solution.py:23
  20.7 12.9 %collective-permute-start.1 = (bf16[4,128,512]{2,1,0:T(8,128)(2,1)S(1)}, bf16[4,128,512]{2,1,0:T(8,128)(2,1)S(1)}, u32[]{:S(2)}, u32[]{:S(2)}) collective-permute-start(bf16[4,128,512]{2,1,0:T(8,128)(2,1)S(1)} %pad_maximum_fusion.6), channel_id=1, source_target_pairs={{0,2},{2,0},{4,6},{6,4},{1,3},{3,1},{5,7},{7,5},{8,10},{10,8},{12,... | collective-permute-start | bytes 1572872 | tf_op jit(solution)/shard_map/ppermute | solution.py:28
  21.4 13.3 %collective-permute-start.7 = (s32[128]{0:T(128)S(1)}, s32[128]{0:T(128)S(1)}, u32[]{:S(2)}, u32[]{:S(2)}) collective-permute-start(s32[128]{0:T(128)S(1)} %fusion.90), channel_id=1, source_target_pairs={{0,8},{8,0},{1,9},{9,1},{2,10},{10,2},{3,11},{11,3},{4,12},{12,4},... | collective-permute-start | bytes 1544 | tf_op jit(solution)/shard_map/ppermute | solution.py:23
  37.4 42.9 %copy-start.5 = (bf16[32,128,128]{2,1,0:T(8,128)(2,1)}, bf16[32,128,128]{2,1,0:T(8,128)(2,1)S(1)}, u32[]{:S(2)}) copy-start(bf16[32,128,128]{2,1,0:T(8,128)(2,1)S(1)} %collective-permute-done.3.refs_6_) | copy-start | bytes 3145732
  37.6 42.7 %copy-start.6 = (bf16[32,128,128]{2,1,0:T(8,128)(2,1)}, bf16[32,128,128]{2,1,0:T(8,128)(2,1)S(1)}, u32[]{:S(2)}) copy-start(bf16[32,128,128]{2,1,0:T(8,128)(2,1)S(1)} %collective-permute-done.5.refs_12_) | copy-start | bytes 3145732
  37.6 13.2 %collective-permute-start.8 = (bf16[2,128,512]{2,1,0:T(8,128)(2,1)S(1)}, bf16[2,128,512]{2,1,0:T(8,128)(2,1)S(1)}, u32[]{:S(2)}, u32[]{:S(2)}) collective-permute-start(bf16[2,128,512]{2,1,0:T(8,128)(2,1)S(1)} %slice.161), channel_id=1, source_target_pairs={{0,4},{2,6},{4,0},{6,2},{1,5},{3,7},{5,1},{7,3},{8,12},{10,14},{12... | collective-permute-start | bytes 786440 | tf_op jit(solution)/shard_map/ppermute | solution.py:28
  38.1 30.5 %collective-permute-start.12 = (bf16[32,128,128]{2,1,0:T(8,128)(2,1)S(1)}, bf16[32,128,128]{2,1,0:T(8,128)(2,1)S(1)}, u32[]{:S(2)}, u32[]{:S(2)}) collective-permute-start(bf16[32,128,128]{2,1,0:T(8,128)(2,1)S(1)} %collective-permute-done.3.refs_6_), channel_id=1, source_target_pairs={{0,8},{8,0},{1,9},{9,1},{2,10},{10,2},{3,11},{11,3},{4,12},{12,4},... | collective-permute-start | bytes 3145736 | tf_op jit(solution)/shard_map/ppermute | solution.py:23
  38.1 30.5 %collective-permute-start.13 = (bf16[32,128,128]{2,1,0:T(8,128)(2,1)S(1)}, bf16[32,128,128]{2,1,0:T(8,128)(2,1)}, u32[]{:S(2)}, u32[]{:S(2)}) collective-permute-start(bf16[32,128,128]{2,1,0:T(8,128)(2,1)S(1)} %collective-permute-done.5.refs_12_), channel_id=1, source_target_pairs={{0,8},{8,0},{1,9},{9,1},{2,10},{10,2},{3,11},{11,3},{4,12},{12,4},... | collective-permute-start | bytes 3145736 | tf_op jit(solution)/shard_map/ppermute | solution.py:23
  38.7 30.0 %collective-permute-start.10 = (bf16[8,128,512]{2,1,0:T(8,128)(2,1)}, bf16[8,128,512]{2,1,0:T(8,128)(2,1)}, u32[]{:S(2)}, u32[]{:S(2)}) collective-permute-start(bf16[8,128,512]{2,1,0:T(8,128)(2,1)} %pad_maximum_fusion.refs_14_), channel_id=1, source_target_pairs={{0,1},{1,0},{2,3},{3,2},{4,5},{5,4},{6,7},{7,6},{8,9},{9,8},{10,11... | collective-permute-start | bytes 3145736 | tf_op jit(solution)/shard_map/ppermute | solution.py:23
  39.2 29.5 %collective-permute-start.11 = (bf16[32,128,128]{2,1,0:T(8,128)(2,1)}, bf16[32,128,128]{2,1,0:T(8,128)(2,1)}, u32[]{:S(2)}, u32[]{:S(2)}) collective-permute-start(bf16[32,128,128]{2,1,0:T(8,128)(2,1)} %get-tuple-element.105), channel_id=1, source_target_pairs={{0,16},{16,0},{1,17},{17,1},{2,18},{18,2},{3,19},{19,3},{4,20},{20... | collective-permute-start | bytes 3145736 | tf_op jit(solution)/shard_map/ppermute | solution.py:23
  50.9 1.5 collective-permute-start.14
  52.4 14.0 %collective-permute-start.9 = (bf16[4,128,512]{2,1,0:T(8,128)(2,1)}, bf16[4,128,512]{2,1,0:T(8,128)(2,1)}, u32[]{:S(2)}, u32[]{:S(2)}) collective-permute-start(bf16[4,128,512]{2,1,0:T(8,128)(2,1)} %pad_maximum_fusion.7), channel_id=1, source_target_pairs={{0,2},{2,0},{4,6},{6,4},{1,3},{3,1},{5,7},{7,5},{8,10},{10,8},{12,... | collective-permute-start | bytes 1572872 | tf_op jit(solution)/shard_map/ppermute | solution.py:28
  66.4 2.2 collective-permute-start.15
  68.8 25.9 %collective-permute-start.16 = (bf16[8,128,512]{2,1,0:T(8,128)(2,1)}, bf16[8,128,512]{2,1,0:T(8,128)(2,1)}, u32[]{:S(2)}, u32[]{:S(2)}) collective-permute-start(bf16[8,128,512]{2,1,0:T(8,128)(2,1)} %pad_maximum_fusion.1.refs_18_), channel_id=1, source_target_pairs={{0,1},{1,0},{2,3},{3,2},{4,5},{5,4},{6,7},{7,6},{8,9},{9,8},{10,11... | collective-permute-start | bytes 3145736 | tf_op jit(solution)/shard_map/ppermute | solution.py:23
  69.3 25.4 %collective-permute-start.17 = (bf16[8,128,512]{2,1,0:T(8,128)(2,1)}, bf16[8,128,512]{2,1,0:T(8,128)(2,1)}, u32[]{:S(2)}, u32[]{:S(2)}) collective-permute-start(bf16[8,128,512]{2,1,0:T(8,128)(2,1)} %pad_maximum_fusion.refs_14_), channel_id=1, source_target_pairs={{0,8},{8,0},{1,9},{9,1},{2,10},{10,2},{3,11},{11,3},{4,12},{12,4},... | collective-permute-start | bytes 3145736 | tf_op jit(solution)/shard_map/ppermute | solution.py:23
  69.5 25.2 %collective-permute-start.18 = (bf16[8,128,512]{2,1,0:T(8,128)(2,1)}, bf16[8,128,512]{2,1,0:T(8,128)(2,1)}, u32[]{:S(2)}, u32[]{:S(2)}) collective-permute-start(bf16[8,128,512]{2,1,0:T(8,128)(2,1)} %collective-permute-done.10.refs_15_), channel_id=1, source_target_pairs={{0,8},{8,0},{1,9},{9,1},{2,10},{10,2},{3,11},{11,3},{4,12},{12,4},... | collective-permute-start | bytes 3145736 | tf_op jit(solution)/shard_map/ppermute | solution.py:23
  69.8 25.6 %collective-permute-start.19 = (bf16[32,128,128]{2,1,0:T(8,128)(2,1)}, bf16[32,128,128]{2,1,0:T(8,128)(2,1)}, u32[]{:S(2)}, u32[]{:S(2)}) collective-permute-start(bf16[32,128,128]{2,1,0:T(8,128)(2,1)} %get-tuple-element.114), channel_id=1, source_target_pairs={{0,16},{16,0},{1,17},{17,1},{2,18},{18,2},{3,19},{19,3},{4,20},{20... | collective-permute-start | bytes 3145736 | tf_op jit(solution)/shard_map/ppermute | solution.py:23
  71.3 24.2 %collective-permute-start.20 = (bf16[32,128,128]{2,1,0:T(8,128)(2,1)}, bf16[32,128,128]{2,1,0:T(8,128)(2,1)}, u32[]{:S(2)}, u32[]{:S(2)}) collective-permute-start(bf16[32,128,128]{2,1,0:T(8,128)(2,1)} %collective-permute-done.11.refs_8_), channel_id=1, source_target_pairs={{0,8},{8,0},{1,9},{9,1},{2,10},{10,2},{3,11},{11,3},{4,12},{12,4},... | collective-permute-start | bytes 3145736 | tf_op jit(solution)/shard_map/ppermute | solution.py:23
  95.4 2.9 collective-permute-start.21
  95.4 4.4 %collective-permute-start.22 = (bf16[8,128,512]{2,1,0:T(8,128)(2,1)}, bf16[8,128,512]{2,1,0:T(8,128)(2,1)S(1)}, u32[]{:S(2)}, u32[]{:S(2)}) collective-permute-start(bf16[8,128,512]{2,1,0:T(8,128)(2,1)} %pad_maximum_fusion.1.refs_18_), channel_id=1, source_target_pairs={{0,8},{8,0},{1,9},{9,1},{2,10},{10,2},{3,11},{11,3},{4,12},{12,4},... | collective-permute-start | bytes 3145736 | tf_op jit(solution)/shard_map/ppermute | solution.py:23
  95.9 5.4 %collective-permute-start.23 = (bf16[8,128,512]{2,1,0:T(8,128)(2,1)}, bf16[8,128,512]{2,1,0:T(8,128)(2,1)S(1)}, u32[]{:S(2)}, u32[]{:S(2)}) collective-permute-start(bf16[8,128,512]{2,1,0:T(8,128)(2,1)} %collective-permute-done.16.refs_19_), channel_id=1, source_target_pairs={{0,8},{8,0},{1,9},{9,1},{2,10},{10,2},{3,11},{11,3},{4,12},{12,4},... | collective-permute-start | bytes 3145736 | tf_op jit(solution)/shard_map/ppermute | solution.py:23
  112.0 26.2 %collective-permute-start.24 = (bf16[16,128,256]{2,1,0:T(8,128)(2,1)}, bf16[16,128,256]{2,1,0:T(8,128)(2,1)S(1)}, u32[]{:S(2)}, u32[]{:S(2)}) collective-permute-start(bf16[16,128,256]{2,1,0:T(8,128)(2,1)} %get-tuple-element.141), channel_id=1, source_target_pairs={{0,1},{1,0},{2,3},{3,2},{4,5},{5,4},{6,7},{7,6},{8,9},{9,8},{10,11... | collective-permute-start | bytes 3145736 | tf_op jit(solution)/shard_map/ppermute | solution.py:23
  113.5 26.3 %collective-permute-start.25 = (bf16[16,128,256]{2,1,0:T(8,128)(2,1)}, bf16[16,128,256]{2,1,0:T(8,128)(2,1)}, u32[]{:S(2)}, u32[]{:S(2)}) collective-permute-start(bf16[16,128,256]{2,1,0:T(8,128)(2,1)} %get-tuple-element.142), channel_id=1, source_target_pairs={{0,16},{16,0},{1,17},{17,1},{2,18},{18,2},{3,19},{19,3},{4,20},{20... | collective-permute-start | bytes 3145736 | tf_op jit(solution)/shard_map/ppermute | solution.py:23
  141.5 13.9 %collective-permute-start.26 = (bf16[2,512,256]{2,1,0:T(8,128)(2,1)S(1)}, bf16[2,512,256]{2,1,0:T(8,128)(2,1)S(1)}, u32[]{:S(2)}, u32[]{:S(2)}) collective-permute-start(bf16[2,512,256]{2,1,0:T(8,128)(2,1)S(1)} %bitcast.86), channel_id=1, source_target_pairs={{0,2},{2,0},{4,6},{6,4},{1,3},{3,1},{5,7},{7,5},{8,10},{10,8},{12,... | collective-permute-start | bytes 1572872 | tf_op jit(solution)/shard_map/ppermute | solution.py:28
  142.6 26.8 %collective-permute-start.28 = (bf16[16,128,256]{2,1,0:T(8,128)(2,1)S(1)}, bf16[16,128,256]{2,1,0:T(8,128)(2,1)S(1)}, u32[]{:S(2)}, u32[]{:S(2)}) collective-permute-start(bf16[16,128,256]{2,1,0:T(8,128)(2,1)S(1)} %copy-done.29), channel_id=1, source_target_pairs={{0,1},{1,0},{2,3},{3,2},{4,5},{5,4},{6,7},{7,6},{8,9},{9,8},{10,11... | collective-permute-start | bytes 3145736 | tf_op jit(solution)/shard_map/ppermute | solution.py:23
  143.1 26.4 %collective-permute-start.29 = (bf16[16,128,256]{2,1,0:T(8,128)(2,1)S(1)}, bf16[16,128,256]{2,1,0:T(8,128)(2,1)S(1)}, u32[]{:S(2)}, u32[]{:S(2)}) collective-permute-start(bf16[16,128,256]{2,1,0:T(8,128)(2,1)S(1)} %copy-done.28), channel_id=1, source_target_pairs={{0,16},{16,0},{1,17},{17,1},{2,18},{18,2},{3,19},{19,3},{4,20},{20... | collective-permute-start | bytes 3145736 | tf_op jit(solution)/shard_map/ppermute | solution.py:23
  155.6 13.8 %collective-permute-start.27 = (bf16[512,256]{1,0:T(8,128)(2,1)S(1)}, bf16[512,256]{1,0:T(8,128)(2,1)S(1)}, u32[]{:S(2)}, u32[]{:S(2)}) collective-permute-start(bf16[512,256]{1,0:T(8,128)(2,1)S(1)} %fusion.23), channel_id=1, source_target_pairs={{0,4},{2,6},{4,0},{6,2},{1,5},{3,7},{5,1},{7,3},{8,12},{10,14},{12... | collective-permute-start | bytes 786440 | tf_op jit(solution)/shard_map/ppermute | solution.py:28
  170.0 20.8 %collective-permute-start.32 = (bf16[2,512,256]{2,1,0:T(8,128)(2,1)S(1)}, bf16[2,512,256]{2,1,0:T(8,128)(2,1)S(1)}, u32[]{:S(2)}, u32[]{:S(2)}) collective-permute-start(bf16[2,512,256]{2,1,0:T(8,128)(2,1)S(1)} %bitcast.85), channel_id=1, source_target_pairs={{0,2},{2,0},{4,6},{6,4},{1,3},{3,1},{5,7},{7,5},{8,10},{10,8},{12,... | collective-permute-start | bytes 1572872 | tf_op jit(solution)/shard_map/ppermute | solution.py:28
  170.3 17.1 %collective-permute-start.30 = (bf16[512,256]{1,0:T(8,128)(2,1)S(1)}, bf16[512,256]{1,0:T(8,128)(2,1)S(1)}, u32[]{:S(2)}, u32[]{:S(2)}) collective-permute-start(bf16[512,256]{1,0:T(8,128)(2,1)S(1)} %convert_element_type.117), channel_id=1, source_target_pairs={{0,4},{2,6},{4,0},{6,2},{1,5},{3,7},{5,1},{7,3},{8,12},{10,14},{12... | collective-permute-start | bytes 786440 | tf_op jit(solution)/shard_map/ppermute | solution.py:28
  187.3 20.7 %collective-permute-start.31 = (bf16[1024,256]{1,0:T(8,128)(2,1)S(1)}, bf16[1024,256]{1,0:T(8,128)(2,1)S(1)}, u32[]{:S(2)}, u32[]{:S(2)}) collective-permute-start(bf16[1024,256]{1,0:T(8,128)(2,1)S(1)} %pad_maximum_fusion.8), channel_id=1, source_target_pairs={{0,2},{2,0},{4,6},{6,4},{1,3},{3,1},{5,7},{7,5},{8,10},{10,8},{12,... | collective-permute-start | bytes 1572872 | tf_op jit(solution)/shard_map/ppermute | solution.py:28
  191.0 16.3 %collective-permute-start.33 = (bf16[512,256]{1,0:T(8,128)(2,1)S(1)}, bf16[512,256]{1,0:T(8,128)(2,1)S(1)}, u32[]{:S(2)}, u32[]{:S(2)}) collective-permute-start(bf16[512,256]{1,0:T(8,128)(2,1)S(1)} %fusion.24), channel_id=1, source_target_pairs={{0,4},{2,6},{4,0},{6,2},{1,5},{3,7},{5,1},{7,3},{8,12},{10,14},{12... | collective-permute-start | bytes 786440 | tf_op jit(solution)/shard_map/ppermute | solution.py:28
  208.1 13.7 %collective-permute-start.34 = (bf16[512,256]{1,0:T(8,128)(2,1)S(1)}, bf16[512,256]{1,0:T(8,128)(2,1)S(1)}, u32[]{:S(2)}, u32[]{:S(2)}) collective-permute-start(bf16[512,256]{1,0:T(8,128)(2,1)S(1)} %convert_element_type.124), channel_id=1, source_target_pairs={{0,4},{2,6},{4,0},{6,2},{1,5},{3,7},{5,1},{7,3},{8,12},{10,14},{12... | collective-permute-start | bytes 786440 | tf_op jit(solution)/shard_map/ppermute | solution.py:28
  210.9 23.9 %collective-permute-start.36 = (bf16[2048,256]{1,0:T(8,128)(2,1)S(1)}, bf16[2048,256]{1,0:T(8,128)(2,1)S(1)}, u32[]{:S(2)}, u32[]{:S(2)}) collective-permute-start(bf16[2048,256]{1,0:T(8,128)(2,1)S(1)} %pad_maximum_fusion.2), channel_id=1, source_target_pairs={{0,1},{1,0},{2,3},{3,2},{4,5},{5,4},{6,7},{7,6},{8,9},{9,8},{10,11... | collective-permute-start | bytes 3145736 | tf_op jit(solution)/shard_map/ppermute | solution.py:23
  210.9 23.9 %collective-permute-start.37 = (bf16[2048,256]{1,0:T(8,128)(2,1)S(1)}, bf16[2048,256]{1,0:T(8,128)(2,1)S(1)}, u32[]{:S(2)}, u32[]{:S(2)}) collective-permute-start(bf16[2048,256]{1,0:T(8,128)(2,1)S(1)} %pad_maximum_fusion.2), channel_id=1, source_target_pairs={{0,16},{16,0},{1,17},{17,1},{2,18},{18,2},{3,19},{19,3},{4,20},{20... | collective-permute-start | bytes 3145736 | tf_op jit(solution)/shard_map/ppermute | solution.py:23
  221.8 12.9 %collective-permute-start.35 = (bf16[1024,256]{1,0:T(8,128)(2,1)S(1)}, bf16[1024,256]{1,0:T(8,128)(2,1)S(1)}, u32[]{:S(2)}, u32[]{:S(2)}) collective-permute-start(bf16[1024,256]{1,0:T(8,128)(2,1)S(1)} %pad_maximum_fusion.9), channel_id=1, source_target_pairs={{0,2},{2,0},{4,6},{6,4},{1,3},{3,1},{5,7},{7,5},{8,10},{10,8},{12,... | collective-permute-start | bytes 1572872 | tf_op jit(solution)/shard_map/ppermute | solution.py:28
  235.0 5.7 %collective-permute-start.40 = (bf16[4096,256]{1,0:T(8,128)(2,1)S(1)}, bf16[4096,256]{1,0:T(8,128)(2,1)S(1)}, u32[]{:S(2)}, u32[]{:S(2)}) collective-permute-start(bf16[4096,256]{1,0:T(8,128)(2,1)S(1)} %constant_dynamic-update-slice_fusion), channel_id=1, source_target_pairs={{0,8},{8,0},{1,9},{9,1},{2,10},{10,2},{3,11},{11,3},{4,12},{12,4},... | collective-permute-start | bytes 6291464 | tf_op jit(solution)/shard_map/ppermute | solution.py:23
  235.0 5.6 %collective-permute-start.41 = (bf16[2048,256]{1,0:T(8,128)(2,1)S(1)}, bf16[2048,256]{1,0:T(8,128)(2,1)S(1)}, u32[]{:S(2)}, u32[]{:S(2)}) collective-permute-start(bf16[2048,256]{1,0:T(8,128)(2,1)S(1)} %collective-permute-done.37), channel_id=1, source_target_pairs={{0,8},{8,0},{1,9},{9,1},{2,10},{10,2},{3,11},{11,3},{4,12},{12,4},... | collective-permute-start | bytes 3145736 | tf_op jit(solution)/shard_map/ppermute | solution.py:23
  235.5 25.2 %collective-permute-start.38 = (bf16[2048,256]{1,0:T(8,128)(2,1)S(1)}, bf16[2048,256]{1,0:T(8,128)(2,1)}, u32[]{:S(2)}, u32[]{:S(2)}) collective-permute-start(bf16[2048,256]{1,0:T(8,128)(2,1)S(1)} %pad_maximum_fusion.3), channel_id=1, source_target_pairs={{0,1},{1,0},{2,3},{3,2},{4,5},{5,4},{6,7},{7,6},{8,9},{9,8},{10,11... | collective-permute-start | bytes 3145736 | tf_op jit(solution)/shard_map/ppermute | solution.py:23
  236.7 25.0 %collective-permute-start.39 = (bf16[2048,256]{1,0:T(8,128)(2,1)S(1)}, bf16[2048,256]{1,0:T(8,128)(2,1)}, u32[]{:S(2)}, u32[]{:S(2)}) collective-permute-start(bf16[2048,256]{1,0:T(8,128)(2,1)S(1)} %pad_maximum_fusion.3), channel_id=1, source_target_pairs={{0,16},{16,0},{1,17},{17,1},{2,18},{18,2},{3,19},{19,3},{4,20},{20... | collective-permute-start | bytes 3145736 | tf_op jit(solution)/shard_map/ppermute | solution.py:23
  262.9 5.9 %collective-permute-start.45 = (bf16[4096,256]{1,0:T(8,128)(2,1)S(1)}, bf16[4096,256]{1,0:T(8,128)(2,1)}, u32[]{:S(2)}, u32[]{:S(2)}) collective-permute-start(bf16[4096,256]{1,0:T(8,128)(2,1)S(1)} %constant_dynamic-update-slice_fusion.2), channel_id=1, source_target_pairs={{0,8},{8,0},{1,9},{9,1},{2,10},{10,2},{3,11},{11,3},{4,12},{12,4},... | collective-permute-start | bytes 6291464 | tf_op jit(solution)/shard_map/ppermute | solution.py:23
  263.0 5.5 %collective-permute-start.46 = (bf16[2048,256]{1,0:T(8,128)(2,1)}, bf16[2048,256]{1,0:T(8,128)(2,1)S(1)}, u32[]{:S(2)}, u32[]{:S(2)}) collective-permute-start(bf16[2048,256]{1,0:T(8,128)(2,1)} %collective-permute-done.39), channel_id=1, source_target_pairs={{0,8},{8,0},{1,9},{9,1},{2,10},{10,2},{3,11},{11,3},{4,12},{12,4},... | collective-permute-start | bytes 3145736 | tf_op jit(solution)/shard_map/ppermute | solution.py:23
  263.5 17.3 %collective-permute-start.43 = (bf16[16,128,128]{2,1,0:T(8,128)(2,1)}, bf16[16,128,128]{2,1,0:T(8,128)(2,1)}, u32[]{:S(2)}, u32[]{:S(2)}) collective-permute-start(bf16[16,128,128]{2,1,0:T(8,128)(2,1)} %get-tuple-element.172), channel_id=1, source_target_pairs={{0,16},{16,0},{1,17},{17,1},{2,18},{18,2},{3,19},{19,3},{4,20},{20... | collective-permute-start | bytes 1572872 | tf_op jit(solution)/shard_map/ppermute | solution.py:23
  263.9 17.0 %collective-permute-start.44 = (bf16[16,128,128]{2,1,0:T(8,128)(2,1)}, bf16[16,128,128]{2,1,0:T(8,128)(2,1)}, u32[]{:S(2)}, u32[]{:S(2)}) collective-permute-start(bf16[16,128,128]{2,1,0:T(8,128)(2,1)} %get-tuple-element.173), channel_id=1, source_target_pairs={{0,1},{1,0},{2,3},{3,2},{4,5},{5,4},{6,7},{7,6},{8,9},{9,8},{10,11... | collective-permute-start | bytes 1572872 | tf_op jit(solution)/shard_map/ppermute | solution.py:23
  264.7 22.4 %collective-permute-start.42 = (f32[256,256]{1,0:T(8,128)S(1)}, f32[256,256]{1,0:T(8,128)S(1)}, u32[]{:S(2)}, u32[]{:S(2)}) collective-permute-start(f32[256,256]{1,0:T(8,128)S(1)} %convolution_add_fusion), channel_id=1, source_target_pairs={{0,16},{16,0},{1,17},{17,1},{2,18},{18,2},{3,19},{19,3},{4,20},{20... | collective-permute-start | bytes 786440 | tf_op jit(solution)/shard_map/ppermute | solution.py:23
  282.9 13.9 %collective-permute-start.54 = (bf16[4,256,128]{2,1,0:T(8,128)(2,1)S(1)}, bf16[4,256,128]{2,1,0:T(8,128)(2,1)S(1)}, u32[]{:S(2)}, u32[]{:S(2)}) collective-permute-start(bf16[4,256,128]{2,1,0:T(8,128)(2,1)S(1)} %bitcast.88), channel_id=1, source_target_pairs={{0,16},{16,0},{1,17},{17,1},{2,18},{18,2},{3,19},{19,3},{4,20},{20... | collective-permute-start | bytes 786440 | tf_op jit(solution)/shard_map/ppermute | solution.py:23
  283.5 13.3 %collective-permute-start.53 = (bf16[4,256,128]{2,1,0:T(8,128)(2,1)S(1)}, bf16[4,256,128]{2,1,0:T(8,128)(2,1)S(1)}, u32[]{:S(2)}, u32[]{:S(2)}) collective-permute-start(bf16[4,256,128]{2,1,0:T(8,128)(2,1)S(1)} %bitcast.87), channel_id=1, source_target_pairs={{0,1},{1,0},{2,3},{3,2},{4,5},{5,4},{6,7},{7,6},{8,9},{9,8},{10,11... | collective-permute-start | bytes 786440 | tf_op jit(solution)/shard_map/ppermute | solution.py:23
  284.4 17.5 %collective-permute-start.47 = (bf16[16,128,128]{2,1,0:T(8,128)(2,1)S(1)}, bf16[16,128,128]{2,1,0:T(8,128)(2,1)S(1)}, u32[]{:S(2)}, u32[]{:S(2)}) collective-permute-start(bf16[16,128,128]{2,1,0:T(8,128)(2,1)S(1)} %copy-done.31), channel_id=1, source_target_pairs={{0,16},{16,0},{1,17},{17,1},{2,18},{18,2},{3,19},{19,3},{4,20},{20... | collective-permute-start | bytes 1572872 | tf_op jit(solution)/shard_map/ppermute | solution.py:23
  285.2 17.0 %collective-permute-start.48 = (bf16[16,128,128]{2,1,0:T(8,128)(2,1)S(1)}, bf16[16,128,128]{2,1,0:T(8,128)(2,1)S(1)}, u32[]{:S(2)}, u32[]{:S(2)}) collective-permute-start(bf16[16,128,128]{2,1,0:T(8,128)(2,1)S(1)} %copy-done.30), channel_id=1, source_target_pairs={{0,1},{1,0},{2,3},{3,2},{4,5},{5,4},{6,7},{7,6},{8,9},{9,8},{10,11... | collective-permute-start | bytes 1572872 | tf_op jit(solution)/shard_map/ppermute | solution.py:23
  297.0 14.0 %collective-permute-start.55 = (bf16[2,256,256]{2,1,0:T(8,128)(2,1)S(1)}, bf16[2,256,256]{2,1,0:T(8,128)(2,1)S(1)}, u32[]{:S(2)}, u32[]{:S(2)}) collective-permute-start(bf16[2,256,256]{2,1,0:T(8,128)(2,1)S(1)} %fusion.20), channel_id=1, source_target_pairs={{0,2},{2,0},{4,6},{6,4},{1,3},{3,1},{5,7},{7,5},{8,10},{10,8},{12,... | collective-permute-start | bytes 786440 | tf_op jit(solution)/shard_map/ppermute | solution.py:28
  307.5 7.8 %collective-permute-start.49 = (bf16[4,256,128]{2,1,0:T(8,128)(2,1)S(1)}, bf16[4,256,128]{2,1,0:T(8,128)(2,1)S(1)}, u32[]{:S(2)}, u32[]{:S(2)}) collective-permute-start(bf16[4,256,128]{2,1,0:T(8,128)(2,1)S(1)} %bitcast.90), channel_id=1, source_target_pairs={{0,1},{1,0},{2,3},{3,2},{4,5},{5,4},{6,7},{7,6},{8,9},{9,8},{10,11... | collective-permute-start | bytes 786440 | tf_op jit(solution)/shard_map/ppermute | solution.py:23
  309.3 9.3 %collective-permute-start.50 = (bf16[4,256,128]{2,1,0:T(8,128)(2,1)S(1)}, bf16[4,256,128]{2,1,0:T(8,128)(2,1)S(1)}, u32[]{:S(2)}, u32[]{:S(2)}) collective-permute-start(bf16[4,256,128]{2,1,0:T(8,128)(2,1)S(1)} %bitcast.89), channel_id=1, source_target_pairs={{0,16},{16,0},{1,17},{17,1},{2,18},{18,2},{3,19},{19,3},{4,20},{20... | collective-permute-start | bytes 786440 | tf_op jit(solution)/shard_map/ppermute | solution.py:23
  311.1 12.2 %collective-permute-start.56 = (bf16[256,256]{1,0:T(8,128)(2,1)S(1)}, bf16[256,256]{1,0:T(8,128)(2,1)S(1)}, u32[]{:S(2)}, u32[]{:S(2)}) collective-permute-start(bf16[256,256]{1,0:T(8,128)(2,1)S(1)} %fusion.34), channel_id=1, source_target_pairs={{0,4},{2,6},{4,0},{6,2},{1,5},{3,7},{5,1},{7,3},{8,12},{10,14},{12... | collective-permute-start | bytes 393224 | tf_op jit(solution)/shard_map/ppermute | solution.py:28
  311.2 11.7 %collective-permute-start.51 = (f32[128,512]{1,0:T(8,128)S(1)}, f32[128,512]{1,0:T(8,128)S(1)}, u32[]{:S(2)}, u32[]{:S(2)}) collective-permute-start(f32[128,512]{1,0:T(8,128)S(1)} %pad_maximum_fusion.11), channel_id=1, source_target_pairs={{0,16},{16,0},{1,17},{17,1},{2,18},{18,2},{3,19},{19,3},{4,20},{20... | collective-permute-start | bytes 786440 | tf_op jit(solution)/shard_map/ppermute | solution.py:23
  323.0 7.2 %collective-permute-start.57 = (bf16[2,256,256]{2,1,0:T(8,128)(2,1)S(1)}, bf16[2,256,256]{2,1,0:T(8,128)(2,1)S(1)}, u32[]{:S(2)}, u32[]{:S(2)}) collective-permute-start(bf16[2,256,256]{2,1,0:T(8,128)(2,1)S(1)} %slice.265), channel_id=1, source_target_pairs={{0,2},{2,0},{4,6},{6,4},{1,3},{3,1},{5,7},{7,5},{8,10},{10,8},{12,... | collective-permute-start | bytes 786440 | tf_op jit(solution)/shard_map/ppermute | solution.py:28
  323.4 6.9 %collective-permute-start.52 = (f32[128,512]{1,0:T(8,128)S(1)}, f32[128,512]{1,0:T(8,128)S(1)}, u32[]{:S(2)}, u32[]{:S(2)}) collective-permute-start(f32[128,512]{1,0:T(8,128)S(1)} %add.297), channel_id=1, source_target_pairs={{0,8},{8,0},{1,9},{9,1},{2,10},{10,2},{3,11},{11,3},{4,12},{12,4},... | collective-permute-start | bytes 786440 | tf_op jit(solution)/shard_map/ppermute | solution.py:23
  330.2 25.5 %collective-permute-start.58 = (bf16[256,256]{1,0:T(8,128)(2,1)S(1)}, bf16[256,256]{1,0:T(8,128)(2,1)S(1)}, u32[]{:S(2)}, u32[]{:S(2)}) collective-permute-start(bf16[256,256]{1,0:T(8,128)(2,1)S(1)} %fusion.35), channel_id=1, source_target_pairs={{0,4},{2,6},{4,0},{6,2},{1,5},{3,7},{5,1},{7,3},{8,12},{10,14},{12... | collective-permute-start | bytes 393224 | tf_op jit(solution)/shard_map/ppermute | solution.py:28
  356.4 3.6 collective-permute-start.59
  357.1 7.8 %collective-permute-start.60 = (f32[128,256]{1,0:T(8,128)S(1)}, f32[128,256]{1,0:T(8,128)S(1)}, u32[]{:S(2)}, u32[]{:S(2)}) collective-permute-start(f32[128,256]{1,0:T(8,128)S(1)} %fusion.28), channel_id=1, source_target_pairs={{0,16},{8,24},{16,0},{24,8},{1,17},{9,25},{17,1},{25,9},{2,18},{10... | collective-permute-start | bytes 393224 | tf_op jit(solution)/shard_map/ppermute | solution.py:567
  359.7 5.7 %collective-permute-start.61 = (f32[128,256]{1,0:T(8,128)S(1)}, f32[128,256]{1,0:T(8,128)S(1)}, u32[]{:S(2)}, u32[]{:S(2)}) collective-permute-start(f32[128,256]{1,0:T(8,128)S(1)} %fusion.26), channel_id=1, source_target_pairs={{0,8},{8,16},{16,24},{24,0},{1,9},{9,17},{17,25},{25,1},{2,10},{10... | collective-permute-start | bytes 393224 | tf_op jit(solution)/shard_map/ppermute | solution.py:567
  (30 other events, 154.8 us)

commit v5 on v4

--- a/solution.py
+++ b/solution.py
@@ -23,24 +23,37 @@
     return lax.ppermute(value, axis, [(i, (i + by) % size) for i in range(size)])
 
 
-def swap(value, bit):
+def swap(value, bits):
     size = lax.axis_size("p")
-    return lax.ppermute(value, "p", [(i, i ^ bit) for i in range(size)])
-
-
-def gather_p(value):
-    pair = jnp.concatenate([value, swap(value, 2)])
-    return jnp.concatenate([pair, swap(pair, 1)])
-
-
-def reduce_p(total):
-    part = total[:2] + swap(total[2:].astype(jnp.bfloat16), 1).astype(jnp.float32)
-    return part[0] + swap(part[1].astype(jnp.bfloat16), 2).astype(jnp.float32)
+    return lax.ppermute(value, "p", [(i, i ^ bits) for i in range(size)])
 
 
 def place_p(here, there):
     differs = here ^ there
     return (differs & 1) * 2 + (differs >> 1)
+
+
+def gather_p(value, direct=False):
+    if direct:
+        return jnp.concatenate([value] + [swap(value, bits) for bits in (2, 1, 3)])
+    pair = jnp.concatenate([value, swap(value, 2)])
+    return jnp.concatenate([pair, swap(pair, 1)])
+
+
+def reduce_p(total, direct=False):
+    f32, bf16 = jnp.float32, jnp.bfloat16
+    if direct:
+        got = [swap(total[i].astype(bf16), bits) for i, bits in ((1, 2), (2, 1), (3, 3))]
+        return sum([part.astype(f32) for part in got], total[0])
+    return reduce_rest(reduce_half(total))
+
+
+def reduce_half(total):
+    return total[:2] + swap(total[2:].astype(jnp.bfloat16), 1).astype(jnp.float32)
+
+
+def reduce_rest(half):
+    return half[0] + swap(half[1].astype(jnp.bfloat16), 2).astype(jnp.float32)
 
 
 def together(*values):
@@ -290,6 +303,45 @@
     return unit * lax.rsqrt(pivots)
 
 
+def gram_kernel(n, core_ref, *refs):
+    out = refs[-1]
+    rows_n = out.shape[0]
+
+    @pl.when(pl.program_id(0) == 0)
+    def _():
+        out[...] = jnp.zeros(out.shape, out.dtype)
+
+    first_row = 0 if rows_n == refs[0].shape[1] else pl.multiple_of(core_ref[0] * rows_n, rows_n)
+    some = pl.ds(first_row, rows_n)
+    for first in range(0, len(refs) - 1, n):
+        at = first // n * refs[0].shape[1]
+        total = out[:, at : at + refs[0].shape[1]]
+        for mine, other in zip(refs[-1 - n : -1], refs[first : first + n]):
+            total += lax.dot_general(
+                mine[:, some], other[...], (((0,), (0,)), ((), ())),
+                preferred_element_type=jnp.float32,
+            )
+        out[:, at : at + refs[0].shape[1]] = total
+
+
+def gram_rows(core, chunks, rows_n):
+    n = len(chunks[-1])
+    rows, cols = chunks[-1][0].shape
+    steps = 4
+    parts = [part for chunk in chunks for part in chunk]
+    return pl.pallas_call(
+        functools.partial(gram_kernel, n),
+        grid=(steps,),
+        out_shape=jax.ShapeDtypeStruct((rows_n, cols * len(chunks)), jnp.float32),
+        in_specs=[pl.BlockSpec(memory_space=pltpu.SMEM)]
+        + [pl.BlockSpec((rows // steps, cols), lambda i: (i, 0))] * len(parts),
+        out_specs=pl.BlockSpec((rows_n, cols * len(chunks)), lambda i: (0, 0)),
+        compiler_params=pltpu.CompilerParams(vmem_limit_bytes=24 << 20),
+        cost_estimate=pl.CostEstimate(flops=2 << 30, bytes_accessed=8 << 20, transcendentals=0),
+        name="gram_rows",
+    )(core, *parts)
+
+
 def inverse_kernel(scale, k, first, gram, *refs):
     before, out = refs[:k], refs[-1]
     n = out.shape[0]
@@ -320,7 +372,7 @@
         in_specs=[vmem] * (1 + len(before)) + [anywhere] * len(late),
         out_specs=vmem,
         compiler_params=pltpu.CompilerParams(vmem_limit_bytes=16 << 20),
-        cost_estimate=pl.CostEstimate(flops=6 << 30, bytes_accessed=1 << 20, transcendentals=0),
+        cost_estimate=pl.CostEstimate(flops=1 << 26, bytes_accessed=1 << 16, transcendentals=0),
         name="inverse_rows",
     )(gram, *before, *late)
 
@@ -342,8 +394,7 @@
     by_q_n = held // 4
     by_x_n = held - by_q_n
 
-    by_x = [blocks[i * by_q_n : (i + 1) * by_q_n] for i in range(3)]
-    last = blocks[by_x_n:]
+    first, last = blocks[:by_q_n], blocks[by_x_n:]
     half = col_dev // 2
     early_n = half // 2
     later_n = half - early_n
@@ -361,16 +412,17 @@
         return [shift(value, "core", 1) for value in values]
 
     code_x, code_q, (code_far,) = along_x(code), along_q(code), across([code])
-    by_x[0], code_x = together(by_x[0], code_x)
+    first, code_x = together(first, code_x)
     last, code_q = together(last, code_q)
-    line, got_0, got_q, (sibling,), code_far, mine, by_x = together(
-        gather_p(mine[:early_n]), along_x(by_x[0]), along_q(last), across([blocks]),
-        code_far, mine, by_x,
-    )
+    line, got_0, got_q, (sibling,), code_far, mine, second = together(
+        gather_p(mine[:early_n]), along_x(first), along_q(last), across([blocks]),
+        code_far, mine, after(blocks, code_far)[by_q_n : 2 * by_q_n],
+    )
+    third = after(blocks, second)[2 * by_q_n : by_x_n]
     early = [line] + along_q(line)
-    line, early, got_1, far_0, far_q, code_x_far, code_q_far, by_x = together(
-        gather_p(mine[early_n:]), early, along_x(by_x[1]), across(got_0), across(got_q),
-        across(code_x), across(code_q), by_x,
+    line, early, got_1, far_0, far_q, code_x_far, code_q_far, third = together(
+        gather_p(mine[early_n:]), early, along_x(second), across(got_0), across(got_q),
+        across(code_x), across(code_q), third,
     )
     later = [line] + along_q(line)
 
@@ -421,15 +473,13 @@
     p_mine = (c_core == ci) & jnp.where(along, o_x == xi, r_y == yi)
     p_slot = jnp.where(p_mine, p_slot, -1)
     in_part = place_p(zi, r_z) * rows_each + r_in
-    same_x = (jnp.where(o_core == ci, 0, q_n) + (yi - r_y) % q_n) * per
-    not_x = (2 * q_n + jnp.where(o_core == ci, 0, x_n - 1) + (xi - o_x) % x_n - 1) * per
-    p_panel = jnp.where(o_x == xi, same_x, not_x) + in_part
-
+    y_part = jnp.where(o_x == xi, (yi - r_y) % q_n, q_n - 1 + (xi - o_x) % x_n)
+    p_panel = (jnp.where(o_core == ci, 0, groups) + y_part) * per + in_part
     slots = x_n * q_n * p_n * cols_each
     lists_y = block_lists(counts, bounds_y, groups * per, y_slot, y_panel)
     lists_p = block_lists(counts, bounds_p, slots, p_slot, p_panel)
     later, early_far, got_2, far_1, lists_y, lists_p = together(
-        later, across(early), along_x(by_x[2]), across(got_1), lists_y, lists_p
+        later, across(early), along_x(third), across(got_1), lists_y, lists_p
     )
     later_far, far_2 = across(later), across(got_2)
     sketch_pieces = early + early_far + later + later_far
@@ -453,11 +503,11 @@
             + [shift(parts[q_n - 1 + k], "x", k) for k in range(1, x_n)]
         )
 
-    def y_summed(parts, got):
+    def y_summed(parts, got, direct):
         keep = parts[0]
         for part in got:
             keep = keep + part.astype(f32)
-        return reduce_p(keep.reshape(p_n, rows_each * wide, kc))
+        return reduce_p(keep.reshape(p_n, rows_each * wide, kc), direct)
 
     def spread(line):
         return (
@@ -465,18 +515,8 @@
             [shift(line, "x", k) for k in range(1, x_n)],
         )
 
-    def siblings(line, here, there):
-        here, there = jnp.concatenate([line, *here]), jnp.concatenate(there)
-        return here, shift(here, "core", 1), there, shift(there, "core", 1)
-
-    def gram_rows(parts, befores):
-        return jnp.concatenate([
-            sum(
-                lax.dot_general(a, b, (((0,), (0,)), ((), ())), preferred_element_type=f32)
-                for a, b in zip(parts[:2], before[:2])
-            )
-            for before in befores
-        ], axis=1)
+    def same_x(parts):
+        return parts[:q_n] + parts[groups : groups + q_n]
 
     def z_products(parts):
         kh = kc // 2
@@ -496,14 +536,18 @@
             [shift(parts[x_n + k], "q", k) for k in range(1, q_n)],
         )
 
-    def z_second(parts, got):
+    def z_summed(parts, got):
         by_x, by_q = parts[0], parts[x_n]
         for part in got[0]:
             by_x = by_x + part.astype(f32)
         for part in got[1]:
             by_q = by_q + part.astype(f32)
-        by_x = by_x.reshape(q_n, p_n, cols_each * wide, kc // 2)
-        by_q = by_q.reshape(x_n, p_n, cols_each * wide, kc // 2)
+        return (
+            by_x.reshape(q_n, p_n, cols_each * wide, kc // 2),
+            by_q.reshape(x_n, p_n, cols_each * wide, kc // 2),
+        )
+
+    def z_second(by_x, by_q):
         by_x = reduce_stage(by_x[0], [by_x[k].astype(bf16) for k in range(1, q_n)], "q")
         by_q = reduce_stage(by_q[0], [by_q[k].astype(bf16) for k in range(1, x_n)], "x")
         return jnp.concatenate([by_x, by_q], axis=2)
@@ -518,42 +562,48 @@
         )
         return inverse[-1]
 
+    core = jnp.reshape(ci, (1,)).astype(jnp.int32)
     parts_a = y_products(0, ())
     got_a = y_received(parts_a)
     got_a, parts_b = together(got_a, y_products(1, (parts_a[0],)))
     got_b = y_received(parts_b)
-    own_a, got_b = together(y_summed(parts_a, got_a), got_b)
-    line_a, own_b = together(gather_p(own_a.astype(bf16)), y_summed(parts_b, got_b))
-    line_b, spread_a = together(gather_p(own_b.astype(bf16)), spread(line_a))
+    own_a, got_b = together(y_summed(parts_a, got_a, True), got_b)
+    line_a, own_b = together(gather_p(own_a.astype(bf16)), y_summed(parts_b, got_b, False))
+    line_b, spread_a = together(gather_p(own_b.astype(bf16), True), spread(line_a))
     spread_b = spread(line_b)
-    all_a = together(siblings(line_a, *spread_a))[0]
-    spread_b, zs_a, gram_a = together(spread_b, z_products(all_a), gram_rows(all_a, [all_a]))
+    all_a = [line_a, *spread_a[0], *spread_a[1]]
+    all_a = together(all_a + across(all_a))[0]
+    near_a = same_x(all_a)
+    line_b_far, spread_b, zs_a, gram_a = together(
+        across([line_b]), spread_b, z_products(all_a), gram_rows(core, [near_a], kc)
+    )
 
     first_a = z_first(zs_a)
-    got_gram = [shift(gram_a, "x", k) for k in range(1, x_n)]
-    all_b = together(siblings(line_b, *spread_b))[0]
+    got_gram = along_x(gram_a)
+    spread_b = spread_b[0] + spread_b[1]
+    all_b = together([line_b, *spread_b, *line_b_far, *across(spread_b)])[0]
     first_a, zs_b = together(first_a, z_products(all_b))
     first_b = z_first(zs_b)
+    second_a = z_second(*z_summed(zs_a, first_a))
     gram_a = sum(after(got_gram, zs_b), gram_a)
-    late_b = after(all_b, zs_b)
-    mine_b = [lax.dynamic_slice_in_dim(part, ci * (kc // 2), kc // 2, axis=1) for part in late_b[:2]]
-    gram_b = gram_rows(mine_b, [all_a, late_b])
-    second_a = z_second(zs_a, first_a)
     more_rows(gram_a, zs_b[0])
+    gram_b = gram_rows(core, [near_a, same_x(after(all_b, zs_b))], kc // 2)
     first_b, gram_b, _ = together(first_b, gram_b, inverse[-1])
-    got_gram = [shift(gram_b, "x", k) for k in range(1, x_n)]
-    second_b = z_second(zs_b, first_b)
-    z_a = reduce_p(second_a)
-    more_rows(gram_a, first_b[0][0])
-    second_b, got_gram, _ = together(second_b, got_gram, inverse[-1])
-    z_b = reduce_p(second_b)
+    got_gram = along_x(gram_b)
+    summed_b = z_summed(zs_b, first_b)
+    second_b = z_second(*summed_b)
+    z_a = reduce_p(after(second_a, summed_b))
+    more_rows(gram_a, summed_b[0])
+    second_b, _ = together(second_b, inverse[-1])
+    half_b = reduce_half(second_b)
     gram_b = sum(got_gram, gram_b)
     gram_b = absolute([gram_b, shift(gram_b, "core", 1)], "core")
     more_rows(gram_b)
-    more_rows(gram_b)
+    half_b, _ = together(half_b, inverse[-1])
+    z_b = reduce_rest(half_b)
+    more_rows(gram_b, half_b)
     inverse = jnp.concatenate(inverse, axis=0)
     own_rows = jnp.concatenate([own_a, own_b], axis=1)
-    basis = dot32(own_rows, inverse, ((1,), (1,))).astype(bf16)
 
     obs_n, me = 2 * x_n, xi * 2 + ci
     rows_n = width // obs_n
@@ -563,6 +613,7 @@
     kept, *sent = [
         dot32(turned[k * rows_n : (k + 1) * rows_n], z_rows, ((1,), (1,))) for k in range(obs_n)
     ]
+    basis = dot32(after(own_rows, sent), inverse, ((1,), (1,))).astype(bf16)
     got = [
         lax.ppermute(part, ("x", "core"), [(i, (i + k) % obs_n) for i in range(obs_n)])
         for k, part in enumerate(sent, 1)

time: 370 us -> 349 us (0.943)
  waiting for transfers between devices: 190 us -> 166 us
  starting transfers between devices: 47.8 us -> 59.2 us
  matrix products: 14.6 us -> 5.32 us
    ppermute x16 -> x18, starting transfers between devices: 15.3 us -> 30 us  [swap(): return lax.ppermute(value, 'p', [(i, i ^ bits) for i in range(size)])]
    ppermute x16 -> x18, waiting for transfers between devices: 127 us -> 116 us  [swap(): return lax.ppermute(value, 'p', [(i, i ^ bits) for i in range(size)])]
    ppermute x43 -> x45, waiting for transfers between devices: 57.2 us -> 47.5 us  [shift(): lax.ppermute(value, axis, [(i, (i + by) % size) for i in range(size)])]
    dot_general x6 -> x0, matrix products: 9.29 us -> none  [gram_rows(): lax.dot_general(a, b, (((0,), (0,)), ((), ())), preferred_element_type=f32)]
    pallas_call x4, Pallas kernels: 30.1 us -> 21.1 us  [inverse_rows(): pl.pallas_call(functools.partial(inverse_kernel, scale, len(before), firs...]
    pallas_call x0 -> x2, Pallas kernels: none -> 5.62 us  [gram_rows(): pl.pallas_call(functools.partial(gram_kernel, n), grid=(steps,), out_shap...]
    ppermute x43 -> x45, starting transfers between devices: 30.2 us -> 27.5 us  [shift(): lax.ppermute(value, axis, [(i, (i + by) % size) for i in range(size)])]
    unnamed x77 -> x91, local copies, waits for them, and re-layouts: 6.47 us -> 7.85 us
  transfers between devices with their start and end apart: 62 -> 66, of which waited for: 33 -> 34; matrix products, arithmetic and copies ran while one was open for 8% -> 7% of each run, Pallas kernels for 21% -> 20%
where the time goes in v5:
time: 349 us; the launch traced here: 347 us
  waiting for transfers between devices  166 us (48%)
  Pallas kernels  85.8 us (25%)
  starting transfers between devices  59.2 us (17%)
  local copies, waits for them, and re-layouts  16.2 us (5%)
  other arithmetic  13.1 us (4%)
  matrix products  5.32 us (2%)
    ppermute x18, waiting for transfers between devices, swap(): return lax.ppermute(value, 'p', [(i, i ^ bits) for i in range(size)])  116 us
    ppermute x45, waiting for transfers between devices, shift(): lax.ppermute(value, axis, [(i, (i + by) % size) for i in range(size)])  47.5 us
    pallas_call x4, Pallas kernels, block_products(): pl.pallas_call(kernel, out_shape=outs, in_specs=[smem] * 4 + [anywhere] *...  43.7 us
    ppermute x18, starting transfers between devices, swap(): return lax.ppermute(value, 'p', [(i, i ^ bits) for i in range(size)])  30 us
    ppermute x45, starting transfers between devices, shift(): lax.ppermute(value, axis, [(i, (i + by) % size) for i in range(size)])  27.5 us
    pallas_call x4, Pallas kernels, inverse_rows(): pl.pallas_call(functools.partial(inverse_kernel, scale, len(before), firs...  21.1 us
    pallas_call x2, Pallas kernels, block_lists(): pl.pallas_call(functools.partial(list_kernel, counts_in, bounds, spare),...  15.3 us
    unnamed x91, local copies, waits for them, and re-layouts  7.85 us
  transfers between devices with their start and end apart: 66, of which 34 were waited for; matrix products, arithmetic and copies ran while one was open for 7% of the time, Pallas kernels for 20%

profile of v5, /device:TPU:0, one launch (start us, length us, event | category | flops | bytes accessed | tf_op | source)
XLA Modules:
  0.0 347.4 jit_solution(13717356200134579046)
XLA Ops:
  1.9 2.6 collective-permute-start.2
  4.4 1.5 collective-permute-start.4
  6.0 2.7 collective-permute-start
  8.6 1.7 fusion.78
  11.4 9.2 %collective-permute-done = bf16[2,128,512]{2,1,0:T(8,128)(2,1)S(1)} collective-permute-done((bf16[2,128,512]{2,1,0:T(8,128)(2,1)S(1)}, bf16[2,128,512]{2,1,0:T(8,128)(2,1)S(1)}, u32[]{:S(2)}, u32[]{:S(2)}) %collective-permute-start) | collective-permute-done | bytes 262176 | tf_op jit(solution)/shard_map/ppermute | solution.py:28
  22.6 2.3 slice.160
  24.9 8.7 %collective-permute-done.1 = bf16[4,128,512]{2,1,0:T(8,128)(2,1)S(1)} collective-permute-done((bf16[4,128,512]{2,1,0:T(8,128)(2,1)S(1)}, bf16[4,128,512]{2,1,0:T(8,128)(2,1)S(1)}, u32[]{:S(2)}, u32[]{:S(2)}) %collective-permute-start.1) | collective-permute-done | bytes 524320 | tf_op jit(solution)/shard_map/ppermute | solution.py:28
  35.3 2.8 collective-permute-start.8
  39.7 10.0 %collective-permute-done.8 = bf16[2,128,512]{2,1,0:T(8,128)(2,1)S(1)} collective-permute-done((bf16[2,128,512]{2,1,0:T(8,128)(2,1)S(1)}, bf16[2,128,512]{2,1,0:T(8,128)(2,1)S(1)}, u32[]{:S(2)}, u32[]{:S(2)}) %collective-permute-start.8) | collective-permute-done | bytes 262176 | tf_op jit(solution)/shard_map/ppermute | solution.py:28
  52.2 2.3 slice.162
  54.6 10.7 %collective-permute-done.9 = bf16[4,128,512]{2,1,0:T(8,128)(2,1)} collective-permute-done((bf16[4,128,512]{2,1,0:T(8,128)(2,1)}, bf16[4,128,512]{2,1,0:T(8,128)(2,1)}, u32[]{:S(2)}, u32[]{:S(2)}) %collective-permute-start.9) | collective-permute-done | bytes 524320 | tf_op jit(solution)/shard_map/ppermute | solution.py:28
  65.2 2.1 pad_maximum_fusion.1.refs_18_
  70.5 7.7 %block_lists.3 = (s32[10]{0:T(128)}, s32[544]{0:T(1024)}, s32[544]{0:T(1024)}, s32[544]{0:T(1024)}) custom-call(s32[512]{0:T(512)} %get-tuple-element.230.rows_ref, s32[512]{0:T(512)} %get-tuple-element.222.cols_ref), custom_call_target="tpu_custom_call" | custom-call | flops 4294967296 | bytes 16384 | tf_op jit(solution)/shard_map/block_lists/pallas_call | solution.py:133
  78.1 7.6 %block_lists.2 = (s32[10]{0:T(128)}, s32[480]{0:T(512)}, s32[480]{0:T(512)}, s32[480]{0:T(512)}) custom-call(s32[512]{0:T(512)} %get-tuple-element.231.rows_ref, s32[512]{0:T(512)} %get-tuple-element.232.cols_ref), custom_call_target="tpu_custom_call" | custom-call | flops 4294967296 | bytes 16384 | tf_op jit(solution)/shard_map/block_lists/pallas_call | solution.py:133
  85.8 7.7 %collective-permute-done.16.refs_19_ = bf16[8,128,512]{2,1,0:T(8,128)(2,1)} collective-permute-done((bf16[8,128,512]{2,1,0:T(8,128)(2,1)}, bf16[8,128,512]{2,1,0:T(8,128)(2,1)}, u32[]{:S(2)}, u32[]{:S(2)}) %collective-permute-start.16) | collective-permute-done | bytes 1048608 | tf_op jit(solution)/shard_map/ppermute | solution.py:23
  94.7 2.8 collective-permute-done.21.refs_11_
  98.6 1.5 collective-permute-done.23.refs_21_
  100.1 10.6 %sketch_products.2 = (f32[16,128,256]{2,1,0:T(8,128)}, bf16[16,128,256]{2,1,0:T(8,128)(2,1)}, bf16[16,128,256]{2,1,0:T(8,128)(2,1)}) custom-call(s32[10]{0:T(128)} %get-tuple-element.138.refs_0_, s32[480]{0:T(512)} %get-tuple-element.139.refs_1_, s32[480]{0:T(512)} %get-tuple-element.140.refs_2_, s32[480]{0:T(512)} %get-tuple-element.141.refs_3_, ...), custom_call_target="tpu_custom_call" | custom-call | flops 1073741824 | bytes 33554432 | tf_op jit(solution)/shard_map/sketch_products/pallas_call | solution.py:259
  112.0 10.7 %sketch_products.3 = (f32[16,128,256]{2,1,0:T(8,128)}, bf16[16,128,256]{2,1,0:T(8,128)(2,1)}, bf16[16,128,256]{2,1,0:T(8,128)(2,1)}) custom-call(s32[10]{0:T(128)} %get-tuple-element.138.refs_0_, s32[480]{0:T(512)} %get-tuple-element.139.refs_1_, s32[480]{0:T(512)} %get-tuple-element.140.refs_2_, s32[480]{0:T(512)} %get-tuple-element.141.refs_3_, ...), custom_call_target="tpu_custom_call" | custom-call | flops 1073741824 | bytes 33554432 | tf_op jit(solution)/shard_map/sketch_products/pallas_call | solution.py:259
  122.7 13.6 %collective-permute-done.24 = bf16[16,128,256]{2,1,0:T(8,128)(2,1)S(1)} collective-permute-done((bf16[16,128,256]{2,1,0:T(8,128)(2,1)}, bf16[16,128,256]{2,1,0:T(8,128)(2,1)S(1)}, u32[]{:S(2)}, u32[]{:S(2)}) %collective-permute-start.24) | collective-permute-done | bytes 1048608 | tf_op jit(solution)/shard_map/ppermute | solution.py:23
  136.3 1.3 collective-permute-done.25
  138.4 2.1 fusion.77
  140.6 2.7 collective-permute-start.26
  143.3 1.7 collective-permute-start.27
  145.0 16.5 %collective-permute-done.26 = bf16[512,256]{1,0:T(8,128)(2,1)S(1)} collective-permute-done((bf16[512,256]{1,0:T(8,128)(2,1)S(1)}, bf16[512,256]{1,0:T(8,128)(2,1)S(1)}, u32[]{:S(2)}, u32[]{:S(2)}) %collective-permute-start.26) | collective-permute-done | bytes 262176 | tf_op jit(solution)/shard_map/ppermute | solution.py:28
  163.3 4.0 %collective-permute-start.33 = (bf16[2,512,256]{2,1,0:T(8,128)(2,1)S(1)}, bf16[2,512,256]{2,1,0:T(8,128)(2,1)S(1)}, u32[]{:S(2)}, u32[]{:S(2)}) collective-permute-start(bf16[2,512,256]{2,1,0:T(8,128)(2,1)S(1)} %bitcast.83), channel_id=1, source_target_pairs={{0,2},{2,0},{4,6},{6,4},{1,3},{3,1},{5,7},{7,5},{8,10},{10,8},{12,... | collective-permute-start | bytes 1572872 | tf_op jit(solution)/shard_map/ppermute | solution.py:28
  167.3 1.7 collective-permute-start.31
  169.1 14.8 %collective-permute-done.31 = bf16[512,256]{1,0:T(8,128)(2,1)S(1)} collective-permute-done((bf16[512,256]{1,0:T(8,128)(2,1)S(1)}, bf16[512,256]{1,0:T(8,128)(2,1)S(1)}, u32[]{:S(2)}, u32[]{:S(2)}) %collective-permute-start.31) | collective-permute-done | bytes 262176 | tf_op jit(solution)/shard_map/ppermute | solution.py:28
  184.0 4.5 %collective-permute-start.32 = (bf16[1024,256]{1,0:T(8,128)(2,1)S(1)}, bf16[1024,256]{1,0:T(8,128)(2,1)S(1)}, u32[]{:S(2)}, u32[]{:S(2)}) collective-permute-start(bf16[1024,256]{1,0:T(8,128)(2,1)S(1)} %pad_maximum_fusion.9), channel_id=1, source_target_pairs={{0,2},{2,0},{4,6},{6,4},{1,3},{3,1},{5,7},{7,5},{8,10},{10,8},{12,... | collective-permute-start | bytes 1572872 | tf_op jit(solution)/shard_map/ppermute | solution.py:28
  188.7 15.9 %collective-permute-done.34 = bf16[512,256]{1,0:T(8,128)(2,1)S(1)} collective-permute-done((bf16[512,256]{1,0:T(8,128)(2,1)S(1)}, bf16[512,256]{1,0:T(8,128)(2,1)S(1)}, u32[]{:S(2)}, u32[]{:S(2)}) %collective-permute-start.34) | collective-permute-done | bytes 262176 | tf_op jit(solution)/shard_map/ppermute | solution.py:28
  206.5 1.4 collective-permute-start.39
  207.9 2.8 collective-permute-start.35
  210.7 10.1 %collective-permute-done.35 = bf16[512,256]{1,0:T(8,128)(2,1)S(1)} collective-permute-done((bf16[512,256]{1,0:T(8,128)(2,1)S(1)}, bf16[512,256]{1,0:T(8,128)(2,1)S(1)}, u32[]{:S(2)}, u32[]{:S(2)}) %collective-permute-start.35) | collective-permute-done | bytes 262176 | tf_op jit(solution)/shard_map/ppermute | solution.py:28
  221.2 2.7 collective-permute-done.36
  223.9 6.6 %collective-permute-done.37 = bf16[512,256]{1,0:T(8,128)(2,1)S(1)} collective-permute-done((bf16[512,256]{1,0:T(8,128)(2,1)S(1)}, bf16[512,256]{1,0:T(8,128)(2,1)S(1)}, u32[]{:S(2)}, u32[]{:S(2)}) %collective-permute-start.37) | collective-permute-done | bytes 262176 | tf_op jit(solution)/shard_map/ppermute | solution.py:28
  233.4 3.0 collective-permute-done.45
  237.4 11.1 %project_products.2 = (f32[16,128,128]{2,1,0:T(8,128)}, bf16[16,128,128]{2,1,0:T(8,128)(2,1)}, f32[16,128,128]{2,1,0:T(8,128)}, bf16[16,128,128]{2,1,0:T(8,128)(2,1)}) custom-call(s32[10]{0:T(128)} %get-tuple-element.168.refs_0_, s32[544]{0:T(1024)} %get-tuple-element.169.refs_1_, s32[544]{0:T(1024)} %get-tuple-element.170.refs_2_, ...), custom_call_target="tpu_custom_call" | custom-call | flops 1073741824 | bytes 33554432 | tf_op jit(solution)/shard_map/project_products/pallas_call | solution.py:259
  249.7 1.2 copy-done.8
  250.9 1.2 copy-done.11
  252.1 1.2 copy-done.14
  253.4 1.9 gram_rows.2
  255.3 1.6 collective-permute-done.41.refs_5_
  258.3 1.7 collective-permute-start.48
  261.1 1.3 collective-permute-start.46
  263.3 11.3 %project_products.3 = (f32[16,128,128]{2,1,0:T(8,128)}, bf16[16,128,128]{2,1,0:T(8,128)(2,1)}, f32[16,128,128]{2,1,0:T(8,128)}, bf16[16,128,128]{2,1,0:T(8,128)(2,1)}) custom-call(s32[10]{0:T(128)} %get-tuple-element.168.refs_0_, s32[544]{0:T(1024)} %get-tuple-element.169.refs_1_, s32[544]{0:T(1024)} %get-tuple-element.170.refs_2_, ...), custom_call_target="tpu_custom_call" | custom-call | flops 1073741824 | bytes 33554432 | tf_op jit(solution)/shard_map/project_products/pallas_call | solution.py:259
  274.7 2.0 convert_add_fusion.2
  278.1 1.8 collective-permute-start.51
  281.0 3.9 %inverse_rows.4.refs_0_ = f32[128,512]{1,0:T(8,128)S(1)} custom-call(f32[256,256]{1,0:T(8,128)S(1)} %add.274.gram, f32[16,128,128]{2,1,0:T(8,128)S(1)} %copy-done.18), custom_call_target="tpu_custom_call" | custom-call | flops 67108864 | bytes 65536 | tf_op jit(solution)/shard_map/inverse_rows/pallas_call | solution.py:369
  285.0 3.7 %gram_rows.3 = f32[128,512]{1,0:T(8,128)S(1)} custom-call(s32[1]{0:T(128)} %bitcast.16.core_ref, bf16[2048,256]{1,0:T(8,128)(2,1)S(1)} %copy-done.4, bf16[2048,256]{1,0:T(8,128)(2,1)S(1)} %copy-done.9, bf16[2048,256]{1,0:T(8,128)(2,1)S(1)} %copy-done.12, bf16[2048,256]{1,0:T(8,128)(2,1)S(1)} %copy-done.15, bf16[2048,256]{1,0:T(8,128)(2,1)S(1)} %copy-done.6, ...), custom_call_target="tpu_custom_call" | custom-call | flops 2147483648 | bytes 8388608 | tf_op jit(solution)/shard_map/gram_rows/pallas_call | solution.py:332
  289.0 6.9 %collective-permute-done.51 = bf16[16,128,128]{2,1,0:T(8,128)(2,1)S(1)} collective-permute-done((bf16[16,128,128]{2,1,0:T(8,128)(2,1)S(1)}, bf16[16,128,128]{2,1,0:T(8,128)(2,1)S(1)}, u32[]{:S(2)}, u32[]{:S(2)}) %collective-permute-start.51) | collective-permute-done | bytes 524320 | tf_op jit(solution)/shard_map/ppermute | solution.py:23
  296.0 2.1 collective-permute-start.60
  298.4 1.8 collective-permute-start.55
  300.5 1.7 collective-permute-start.53
  302.2 4.9 %inverse_rows.5.refs_1_ = f32[128,512]{1,0:T(8,128)S(1)} custom-call(f32[256,256]{1,0:T(8,128)S(1)} %add.274.gram, f32[128,512]{1,0:T(8,128)S(1)} %inverse_rows.4.refs_0_, f32[2,4,256,128]{3,2,1,0:T(8,128)S(1)} %bitcast.71), custom_call_target="tpu_custom_call" | custom-call | flops 67108864 | bytes 65536 | tf_op jit(solution)/shard_map/inverse_rows/pallas_call | solution.py:369
  307.3 1.3 collective-permute-start.61
  308.5 3.0 collective-permute-done.53
  312.3 2.0 collective-permute-done.61
  314.6 5.6 %inverse_rows.6.refs_2_ = f32[128,512]{1,0:T(8,128)S(1)} custom-call(f32[256,512]{1,0:T(8,128)S(1)} %fusion.8.gram, f32[128,512]{1,0:T(8,128)S(1)} %inverse_rows.4.refs_0_, f32[128,512]{1,0:T(8,128)S(1)} %inverse_rows.5.refs_1_), custom_call_target="tpu_custom_call" | custom-call | flops 67108864 | bytes 65536 | tf_op jit(solution)/shard_map/inverse_rows/pallas_call | solution.py:369
  320.8 6.7 %inverse_rows.7 = f32[128,512]{1,0:T(8,128)S(1)} custom-call(f32[256,512]{1,0:T(8,128)S(1)} %fusion.8.gram, f32[128,512]{1,0:T(8,128)S(1)} %inverse_rows.4.refs_0_, f32[128,512]{1,0:T(8,128)S(1)} %inverse_rows.5.refs_1_, f32[128,512]{1,0:T(8,128)S(1)} %inverse_rows.6.refs_2_, f32[2,256,256]{2,1,0:T(8,128)S(1)} %convert_add_fusion.7.refs_3_), custom_call_target="tpu_custom_call" | custom-call | flops 67108864 | bytes 65536 | tf_op jit(solution)/shard_map/inverse_rows/pallas_call | solution.py:369
  327.5 1.7 collective-permute-start.62
  329.3 7.1 %collective-permute-done.62 = bf16[256,256]{1,0:T(8,128)(2,1)S(1)} collective-permute-done((bf16[256,256]{1,0:T(8,128)(2,1)S(1)}, bf16[256,256]{1,0:T(8,128)(2,1)S(1)}, u32[]{:S(2)}, u32[]{:S(2)}) %collective-permute-start.62) | collective-permute-done | bytes 131104 | tf_op jit(solution)/shard_map/ppermute | solution.py:28
  337.8 1.6 collective-permute-start.64
  340.1 2.7 convolution_convert_fusion
  342.8 2.2 collective-permute-done.64
  (247 shorter events, 40.2 us)
Async XLA Ops:
  0.6 34.7 %collective-permute-start.6 = (bf16[128,128,128]{2,1,0:T(8,128)(2,1)}, bf16[128,128,128]{2,1,0:T(8,128)(2,1)}, u32[]{:S(2)}, u32[]{:S(2)}) collective-permute-start(bf16[128,128,128]{2,1,0:T(8,128)(2,1)} %refs_4_.7), channel_id=1, source_target_pairs={{0,8},{8,0},{1,9},{9,1},{2,10},{10,2},{3,11},{11,3},{4,12},{12,4},... | collective-permute-start | bytes 12582920 | tf_op jit(solution)/shard_map/ppermute | solution.py:23
  1.9 8.5 %collective-permute-start.2 = (s32[128]{0:T(128)S(1)}, s32[128]{0:T(128)S(1)}, u32[]{:S(2)}, u32[]{:S(2)}) collective-permute-start(s32[128]{0:T(128)S(1)} %fusion.71), channel_id=1, source_target_pairs={{0,16},{16,0},{1,17},{17,1},{2,18},{18,2},{3,19},{19,3},{4,20},{20... | collective-permute-start | bytes 1544 | tf_op jit(solution)/shard_map/ppermute | solution.py:23
  4.4 6.5 %collective-permute-start.4 = (s32[128]{0:T(128)S(1)}, s32[128]{0:T(128)S(1)}, u32[]{:S(2)}, u32[]{:S(2)}) collective-permute-start(s32[128]{0:T(128)S(1)} %fusion.71), channel_id=1, source_target_pairs={{0,1},{1,0},{2,3},{3,2},{4,5},{5,4},{6,7},{7,6},{8,9},{9,8},{10,11... | collective-permute-start | bytes 1544 | tf_op jit(solution)/shard_map/ppermute | solution.py:23
  6.0 14.7 %collective-permute-start = (bf16[2,128,512]{2,1,0:T(8,128)(2,1)S(1)}, bf16[2,128,512]{2,1,0:T(8,128)(2,1)S(1)}, u32[]{:S(2)}, u32[]{:S(2)}) collective-permute-start(bf16[2,128,512]{2,1,0:T(8,128)(2,1)S(1)} %constant_dynamic-slice_fusion), channel_id=1, source_target_pairs={{0,4},{2,6},{4,0},{6,2},{1,5},{3,7},{5,1},{7,3},{8,12},{10,14},{12... | collective-permute-start | bytes 786440 | tf_op jit(solution)/shard_map/ppermute | solution.py:28
  10.3 24.7 %collective-permute-start.3 = (bf16[32,128,128]{2,1,0:T(8,128)(2,1)S(1)}, bf16[32,128,128]{2,1,0:T(8,128)(2,1)S(1)}, u32[]{:S(2)}, u32[]{:S(2)}) collective-permute-start(bf16[32,128,128]{2,1,0:T(8,128)(2,1)S(1)} %get-tuple-element.111), channel_id=1, source_target_pairs={{0,16},{16,0},{1,17},{17,1},{2,18},{18,2},{3,19},{19,3},{4,20},{20... | collective-permute-start | bytes 3145736 | tf_op jit(solution)/shard_map/ppermute | solution.py:23
  10.9 24.4 %collective-permute-start.5 = (bf16[32,128,128]{2,1,0:T(8,128)(2,1)S(1)}, bf16[32,128,128]{2,1,0:T(8,128)(2,1)S(1)}, u32[]{:S(2)}, u32[]{:S(2)}) collective-permute-start(bf16[32,128,128]{2,1,0:T(8,128)(2,1)S(1)} %get-tuple-element.112), channel_id=1, source_target_pairs={{0,1},{1,0},{2,3},{3,2},{4,5},{5,4},{6,7},{7,6},{8,9},{9,8},{10,11... | collective-permute-start | bytes 3145736 | tf_op jit(solution)/shard_map/ppermute | solution.py:23
  20.7 12.9 %collective-permute-start.1 = (bf16[4,128,512]{2,1,0:T(8,128)(2,1)S(1)}, bf16[4,128,512]{2,1,0:T(8,128)(2,1)S(1)}, u32[]{:S(2)}, u32[]{:S(2)}) collective-permute-start(bf16[4,128,512]{2,1,0:T(8,128)(2,1)S(1)} %pad_maximum_fusion.7), channel_id=1, source_target_pairs={{0,2},{2,0},{4,6},{6,4},{1,3},{3,1},{5,7},{7,5},{8,10},{10,8},{12,... | collective-permute-start | bytes 1572872 | tf_op jit(solution)/shard_map/ppermute | solution.py:28
  35.3 14.4 %collective-permute-start.8 = (bf16[2,128,512]{2,1,0:T(8,128)(2,1)S(1)}, bf16[2,128,512]{2,1,0:T(8,128)(2,1)S(1)}, u32[]{:S(2)}, u32[]{:S(2)}) collective-permute-start(bf16[2,128,512]{2,1,0:T(8,128)(2,1)S(1)} %slice.161), channel_id=1, source_target_pairs={{0,4},{2,6},{4,0},{6,2},{1,5},{3,7},{5,1},{7,3},{8,12},{10,14},{12... | collective-permute-start | bytes 786440 | tf_op jit(solution)/shard_map/ppermute | solution.py:28
  38.1 29.2 %collective-permute-start.12 = (bf16[32,128,128]{2,1,0:T(8,128)(2,1)S(1)}, bf16[32,128,128]{2,1,0:T(8,128)(2,1)S(1)}, u32[]{:S(2)}, u32[]{:S(2)}) collective-permute-start(bf16[32,128,128]{2,1,0:T(8,128)(2,1)S(1)} %collective-permute-done.3.refs_6_), channel_id=1, source_target_pairs={{0,8},{8,0},{1,9},{9,1},{2,10},{10,2},{3,11},{11,3},{4,12},{12,4},... | collective-permute-start | bytes 3145736 | tf_op jit(solution)/shard_map/ppermute | solution.py:23
  38.1 29.2 %collective-permute-start.13 = (bf16[32,128,128]{2,1,0:T(8,128)(2,1)S(1)}, bf16[32,128,128]{2,1,0:T(8,128)(2,1)}, u32[]{:S(2)}, u32[]{:S(2)}) collective-permute-start(bf16[32,128,128]{2,1,0:T(8,128)(2,1)S(1)} %collective-permute-done.5.refs_12_), channel_id=1, source_target_pairs={{0,8},{8,0},{1,9},{9,1},{2,10},{10,2},{3,11},{11,3},{4,12},{12,4},... | collective-permute-start | bytes 3145736 | tf_op jit(solution)/shard_map/ppermute | solution.py:23
  38.6 28.7 %collective-permute-start.10 = (bf16[8,128,512]{2,1,0:T(8,128)(2,1)}, bf16[8,128,512]{2,1,0:T(8,128)(2,1)}, u32[]{:S(2)}, u32[]{:S(2)}) collective-permute-start(bf16[8,128,512]{2,1,0:T(8,128)(2,1)} %pad_maximum_fusion.refs_14_), channel_id=1, source_target_pairs={{0,1},{1,0},{2,3},{3,2},{4,5},{5,4},{6,7},{7,6},{8,9},{9,8},{10,11... | collective-permute-start | bytes 3145736 | tf_op jit(solution)/shard_map/ppermute | solution.py:23
  39.1 28.2 %collective-permute-start.11 = (bf16[32,128,128]{2,1,0:T(8,128)(2,1)}, bf16[32,128,128]{2,1,0:T(8,128)(2,1)}, u32[]{:S(2)}, u32[]{:S(2)}) collective-permute-start(bf16[32,128,128]{2,1,0:T(8,128)(2,1)} %slice.160), channel_id=1, source_target_pairs={{0,16},{16,0},{1,17},{17,1},{2,18},{18,2},{3,19},{19,3},{4,20},{20... | collective-permute-start | bytes 3145736 | tf_op jit(solution)/shard_map/ppermute | solution.py:23
  51.3 14.0 %collective-permute-start.9 = (bf16[4,128,512]{2,1,0:T(8,128)(2,1)}, bf16[4,128,512]{2,1,0:T(8,128)(2,1)}, u32[]{:S(2)}, u32[]{:S(2)}) collective-permute-start(bf16[4,128,512]{2,1,0:T(8,128)(2,1)} %pad_maximum_fusion.8), channel_id=1, source_target_pairs={{0,2},{2,0},{4,6},{6,4},{1,3},{3,1},{5,7},{7,5},{8,10},{10,8},{12,... | collective-permute-start | bytes 1572872 | tf_op jit(solution)/shard_map/ppermute | solution.py:28
  65.2 2.1 collective-permute-start.15
  67.5 25.9 %collective-permute-start.16 = (bf16[8,128,512]{2,1,0:T(8,128)(2,1)}, bf16[8,128,512]{2,1,0:T(8,128)(2,1)}, u32[]{:S(2)}, u32[]{:S(2)}) collective-permute-start(bf16[8,128,512]{2,1,0:T(8,128)(2,1)} %pad_maximum_fusion.1.refs_18_), channel_id=1, source_target_pairs={{0,1},{1,0},{2,3},{3,2},{4,5},{5,4},{6,7},{7,6},{8,9},{9,8},{10,11... | collective-permute-start | bytes 3145736 | tf_op jit(solution)/shard_map/ppermute | solution.py:23
  68.1 25.4 %collective-permute-start.17 = (bf16[8,128,512]{2,1,0:T(8,128)(2,1)}, bf16[8,128,512]{2,1,0:T(8,128)(2,1)}, u32[]{:S(2)}, u32[]{:S(2)}) collective-permute-start(bf16[8,128,512]{2,1,0:T(8,128)(2,1)} %pad_maximum_fusion.refs_14_), channel_id=1, source_target_pairs={{0,8},{8,0},{1,9},{9,1},{2,10},{10,2},{3,11},{11,3},{4,12},{12,4},... | collective-permute-start | bytes 3145736 | tf_op jit(solution)/shard_map/ppermute | solution.py:23
  68.3 25.2 %collective-permute-start.18 = (bf16[8,128,512]{2,1,0:T(8,128)(2,1)}, bf16[8,128,512]{2,1,0:T(8,128)(2,1)}, u32[]{:S(2)}, u32[]{:S(2)}) collective-permute-start(bf16[8,128,512]{2,1,0:T(8,128)(2,1)} %collective-permute-done.10.refs_15_), channel_id=1, source_target_pairs={{0,8},{8,0},{1,9},{9,1},{2,10},{10,2},{3,11},{11,3},{4,12},{12,4},... | collective-permute-start | bytes 3145736 | tf_op jit(solution)/shard_map/ppermute | solution.py:23
  68.6 25.5 %collective-permute-start.19 = (bf16[32,128,128]{2,1,0:T(8,128)(2,1)}, bf16[32,128,128]{2,1,0:T(8,128)(2,1)S(1)}, u32[]{:S(2)}, u32[]{:S(2)}) collective-permute-start(bf16[32,128,128]{2,1,0:T(8,128)(2,1)} %slice.162), channel_id=1, source_target_pairs={{0,16},{16,0},{1,17},{17,1},{2,18},{18,2},{3,19},{19,3},{4,20},{20... | collective-permute-start | bytes 3145736 | tf_op jit(solution)/shard_map/ppermute | solution.py:23
  69.1 25.0 %collective-permute-start.20 = (bf16[32,128,128]{2,1,0:T(8,128)(2,1)}, bf16[32,128,128]{2,1,0:T(8,128)(2,1)S(1)}, u32[]{:S(2)}, u32[]{:S(2)}) collective-permute-start(bf16[32,128,128]{2,1,0:T(8,128)(2,1)} %collective-permute-done.11.refs_8_), channel_id=1, source_target_pairs={{0,8},{8,0},{1,9},{9,1},{2,10},{10,2},{3,11},{11,3},{4,12},{12,4},... | collective-permute-start | bytes 3145736 | tf_op jit(solution)/shard_map/ppermute | solution.py:23
  94.1 3.4 collective-permute-start.21
  94.1 4.5 %collective-permute-start.22 = (bf16[8,128,512]{2,1,0:T(8,128)(2,1)}, bf16[8,128,512]{2,1,0:T(8,128)(2,1)}, u32[]{:S(2)}, u32[]{:S(2)}) collective-permute-start(bf16[8,128,512]{2,1,0:T(8,128)(2,1)} %pad_maximum_fusion.1.refs_18_), channel_id=1, source_target_pairs={{0,8},{8,0},{1,9},{9,1},{2,10},{10,2},{3,11},{11,3},{4,12},{12,4},... | collective-permute-start | bytes 3145736 | tf_op jit(solution)/shard_map/ppermute | solution.py:23
  94.6 5.5 %collective-permute-start.23 = (bf16[8,128,512]{2,1,0:T(8,128)(2,1)}, bf16[8,128,512]{2,1,0:T(8,128)(2,1)}, u32[]{:S(2)}, u32[]{:S(2)}) collective-permute-start(bf16[8,128,512]{2,1,0:T(8,128)(2,1)} %collective-permute-done.16.refs_19_), channel_id=1, source_target_pairs={{0,8},{8,0},{1,9},{9,1},{2,10},{10,2},{3,11},{11,3},{4,12},{12,4},... | collective-permute-start | bytes 3145736 | tf_op jit(solution)/shard_map/ppermute | solution.py:23
  110.8 25.5 %collective-permute-start.24 = (bf16[16,128,256]{2,1,0:T(8,128)(2,1)}, bf16[16,128,256]{2,1,0:T(8,128)(2,1)S(1)}, u32[]{:S(2)}, u32[]{:S(2)}) collective-permute-start(bf16[16,128,256]{2,1,0:T(8,128)(2,1)} %get-tuple-element.152), channel_id=1, source_target_pairs={{0,1},{1,0},{2,3},{3,2},{4,5},{5,4},{6,7},{7,6},{8,9},{9,8},{10,11... | collective-permute-start | bytes 3145736 | tf_op jit(solution)/shard_map/ppermute | solution.py:23
  111.5 26.0 %collective-permute-start.25 = (bf16[16,128,256]{2,1,0:T(8,128)(2,1)}, bf16[16,128,256]{2,1,0:T(8,128)(2,1)}, u32[]{:S(2)}, u32[]{:S(2)}) collective-permute-start(bf16[16,128,256]{2,1,0:T(8,128)(2,1)} %get-tuple-element.153), channel_id=1, source_target_pairs={{0,16},{16,0},{1,17},{17,1},{2,18},{18,2},{3,19},{19,3},{4,20},{20... | collective-permute-start | bytes 3145736 | tf_op jit(solution)/shard_map/ppermute | solution.py:23
  137.5 25.1 %collective-permute-start.29 = (bf16[16,128,256]{2,1,0:T(8,128)(2,1)}, bf16[16,128,256]{2,1,0:T(8,128)(2,1)S(1)}, u32[]{:S(2)}, u32[]{:S(2)}) collective-permute-start(bf16[16,128,256]{2,1,0:T(8,128)(2,1)} %get-tuple-element.159), channel_id=1, source_target_pairs={{0,1},{1,0},{2,3},{3,2},{4,5},{5,4},{6,7},{7,6},{8,9},{9,8},{10,11... | collective-permute-start | bytes 3145736 | tf_op jit(solution)/shard_map/ppermute | solution.py:23
  138.1 24.7 %collective-permute-start.30 = (bf16[16,128,256]{2,1,0:T(8,128)(2,1)}, bf16[16,128,256]{2,1,0:T(8,128)(2,1)S(1)}, u32[]{:S(2)}, u32[]{:S(2)}) collective-permute-start(bf16[16,128,256]{2,1,0:T(8,128)(2,1)} %get-tuple-element.160), channel_id=1, source_target_pairs={{0,16},{16,0},{1,17},{17,1},{2,18},{18,2},{3,19},{19,3},{4,20},{20... | collective-permute-start | bytes 3145736 | tf_op jit(solution)/shard_map/ppermute | solution.py:23
  140.6 21.0 %collective-permute-start.26 = (bf16[512,256]{1,0:T(8,128)(2,1)S(1)}, bf16[512,256]{1,0:T(8,128)(2,1)S(1)}, u32[]{:S(2)}, u32[]{:S(2)}) collective-permute-start(bf16[512,256]{1,0:T(8,128)(2,1)S(1)} %bitcast.90), channel_id=1, source_target_pairs={{0,4},{2,6},{4,0},{6,2},{1,5},{3,7},{5,1},{7,3},{8,12},{10,14},{12... | collective-permute-start | bytes 786440 | tf_op jit(solution)/shard_map/ppermute | solution.py:28
  143.3 18.3 %collective-permute-start.27 = (bf16[512,256]{1,0:T(8,128)(2,1)S(1)}, bf16[512,256]{1,0:T(8,128)(2,1)S(1)}, u32[]{:S(2)}, u32[]{:S(2)}) collective-permute-start(bf16[512,256]{1,0:T(8,128)(2,1)S(1)} %bitcast.89), channel_id=1, source_target_pairs={{0,2},{2,0},{4,6},{6,4},{1,3},{3,1},{5,7},{7,5},{8,10},{10,8},{12,... | collective-permute-start | bytes 786440 | tf_op jit(solution)/shard_map/ppermute | solution.py:28
  145.0 16.6 %collective-permute-start.28 = (bf16[512,256]{1,0:T(8,128)(2,1)S(1)}, bf16[512,256]{1,0:T(8,128)(2,1)S(1)}, u32[]{:S(2)}, u32[]{:S(2)}) collective-permute-start(bf16[512,256]{1,0:T(8,128)(2,1)S(1)} %bitcast.88), channel_id=1, source_target_pairs={{0,6},{2,4},{4,2},{6,0},{1,7},{3,5},{5,3},{7,1},{8,14},{10,12},{12... | collective-permute-start | bytes 786440 | tf_op jit(solution)/shard_map/ppermute | solution.py:28
  163.3 25.1 %collective-permute-start.33 = (bf16[2,512,256]{2,1,0:T(8,128)(2,1)S(1)}, bf16[2,512,256]{2,1,0:T(8,128)(2,1)S(1)}, u32[]{:S(2)}, u32[]{:S(2)}) collective-permute-start(bf16[2,512,256]{2,1,0:T(8,128)(2,1)S(1)} %bitcast.83), channel_id=1, source_target_pairs={{0,2},{2,0},{4,6},{6,4},{1,3},{3,1},{5,7},{7,5},{8,10},{10,8},{12,... | collective-permute-start | bytes 1572872 | tf_op jit(solution)/shard_map/ppermute | solution.py:28
  167.3 16.6 %collective-permute-start.31 = (bf16[512,256]{1,0:T(8,128)(2,1)S(1)}, bf16[512,256]{1,0:T(8,128)(2,1)S(1)}, u32[]{:S(2)}, u32[]{:S(2)}) collective-permute-start(bf16[512,256]{1,0:T(8,128)(2,1)S(1)} %convert_element_type.126), channel_id=1, source_target_pairs={{0,4},{2,6},{4,0},{6,2},{1,5},{3,7},{5,1},{7,3},{8,12},{10,14},{12... | collective-permute-start | bytes 786440 | tf_op jit(solution)/shard_map/ppermute | solution.py:28
  184.0 21.3 %collective-permute-start.32 = (bf16[1024,256]{1,0:T(8,128)(2,1)S(1)}, bf16[1024,256]{1,0:T(8,128)(2,1)S(1)}, u32[]{:S(2)}, u32[]{:S(2)}) collective-permute-start(bf16[1024,256]{1,0:T(8,128)(2,1)S(1)} %pad_maximum_fusion.9), channel_id=1, source_target_pairs={{0,2},{2,0},{4,6},{6,4},{1,3},{3,1},{5,7},{7,5},{8,10},{10,8},{12,... | collective-permute-start | bytes 1572872 | tf_op jit(solution)/shard_map/ppermute | solution.py:28
  188.6 16.0 %collective-permute-start.34 = (bf16[512,256]{1,0:T(8,128)(2,1)S(1)}, bf16[512,256]{1,0:T(8,128)(2,1)S(1)}, u32[]{:S(2)}, u32[]{:S(2)}) collective-permute-start(bf16[512,256]{1,0:T(8,128)(2,1)S(1)} %fusion.12), channel_id=1, source_target_pairs={{0,4},{2,6},{4,0},{6,2},{1,5},{3,7},{5,1},{7,3},{8,12},{10,14},{12... | collective-permute-start | bytes 786440 | tf_op jit(solution)/shard_map/ppermute | solution.py:28
  205.4 25.2 %collective-permute-start.38 = (bf16[2048,256]{1,0:T(8,128)(2,1)S(1)}, bf16[2048,256]{1,0:T(8,128)(2,1)S(1)}, u32[]{:S(2)}, u32[]{:S(2)}) collective-permute-start(bf16[2048,256]{1,0:T(8,128)(2,1)S(1)} %pad_maximum_fusion.2.refs_0_), channel_id=1, source_target_pairs={{0,1},{1,0},{2,3},{3,2},{4,5},{5,4},{6,7},{7,6},{8,9},{9,8},{10,11... | collective-permute-start | bytes 3145736 | tf_op jit(solution)/shard_map/ppermute | solution.py:23
  206.5 24.2 %collective-permute-start.39 = (bf16[2048,256]{1,0:T(8,128)(2,1)S(1)}, bf16[2048,256]{1,0:T(8,128)(2,1)S(1)}, u32[]{:S(2)}, u32[]{:S(2)}) collective-permute-start(bf16[2048,256]{1,0:T(8,128)(2,1)S(1)} %pad_maximum_fusion.2.refs_0_), channel_id=1, source_target_pairs={{0,16},{16,0},{1,17},{17,1},{2,18},{18,2},{3,19},{19,3},{4,20},{20... | collective-permute-start | bytes 3145736 | tf_op jit(solution)/shard_map/ppermute | solution.py:23
  207.9 12.9 %collective-permute-start.35 = (bf16[512,256]{1,0:T(8,128)(2,1)S(1)}, bf16[512,256]{1,0:T(8,128)(2,1)S(1)}, u32[]{:S(2)}, u32[]{:S(2)}) collective-permute-start(bf16[512,256]{1,0:T(8,128)(2,1)S(1)} %convert_element_type.133), channel_id=1, source_target_pairs={{0,4},{2,6},{4,0},{6,2},{1,5},{3,7},{5,1},{7,3},{8,12},{10,14},{12... | collective-permute-start | bytes 786440 | tf_op jit(solution)/shard_map/ppermute | solution.py:28
  210.7 21.4 %collective-permute-start.43 = (bf16[2048,256]{1,0:T(8,128)(2,1)S(1)}, bf16[2048,256]{1,0:T(8,128)(2,1)S(1)}, u32[]{:S(2)}, u32[]{:S(2)}) collective-permute-start(bf16[2048,256]{1,0:T(8,128)(2,1)S(1)} %pad_maximum_fusion.2.refs_0_), channel_id=1, source_target_pairs={{0,8},{8,0},{1,9},{9,1},{2,10},{10,2},{3,11},{11,3},{4,12},{12,4},... | collective-permute-start | bytes 3145736 | tf_op jit(solution)/shard_map/ppermute | solution.py:23
  210.7 13.2 %collective-permute-start.36 = (bf16[512,256]{1,0:T(8,128)(2,1)S(1)}, bf16[512,256]{1,0:T(8,128)(2,1)S(1)}, u32[]{:S(2)}, u32[]{:S(2)}) collective-permute-start(bf16[512,256]{1,0:T(8,128)(2,1)S(1)} %convert_element_type.133), channel_id=1, source_target_pairs={{0,2},{2,0},{4,6},{6,4},{1,3},{3,1},{5,7},{7,5},{8,10},{10,8},{12,... | collective-permute-start | bytes 786440 | tf_op jit(solution)/shard_map/ppermute | solution.py:28
  220.8 9.7 %collective-permute-start.37 = (bf16[512,256]{1,0:T(8,128)(2,1)S(1)}, bf16[512,256]{1,0:T(8,128)(2,1)S(1)}, u32[]{:S(2)}, u32[]{:S(2)}) collective-permute-start(bf16[512,256]{1,0:T(8,128)(2,1)S(1)} %convert_element_type.133), channel_id=1, source_target_pairs={{0,6},{2,4},{4,2},{6,0},{1,7},{3,5},{5,3},{7,1},{8,14},{10,12},{12... | collective-permute-start | bytes 786440 | tf_op jit(solution)/shard_map/ppermute | solution.py:28
  230.7 2.7 collective-permute-start.44
  230.7 5.6 %collective-permute-start.45 = (bf16[2048,256]{1,0:T(8,128)(2,1)S(1)}, bf16[2048,256]{1,0:T(8,128)(2,1)S(1)}, u32[]{:S(2)}, u32[]{:S(2)}) collective-permute-start(bf16[2048,256]{1,0:T(8,128)(2,1)S(1)} %collective-permute-done.39), channel_id=1, source_target_pairs={{0,8},{8,0},{1,9},{9,1},{2,10},{10,2},{3,11},{11,3},{4,12},{12,4},... | collective-permute-start | bytes 3145736 | tf_op jit(solution)/shard_map/ppermute | solution.py:23
  231.2 24.1 %collective-permute-start.40 = (bf16[2048,256]{1,0:T(8,128)(2,1)S(1)}, bf16[2048,256]{1,0:T(8,128)(2,1)}, u32[]{:S(2)}, u32[]{:S(2)}) collective-permute-start(bf16[2048,256]{1,0:T(8,128)(2,1)S(1)} %pad_maximum_fusion.4.refs_4_), channel_id=1, source_target_pairs={{0,8},{8,0},{1,9},{9,1},{2,10},{10,2},{3,11},{11,3},{4,12},{12,4},... | collective-permute-start | bytes 3145736 | tf_op jit(solution)/shard_map/ppermute | solution.py:23
  231.3 25.6 %collective-permute-start.41 = (bf16[2048,256]{1,0:T(8,128)(2,1)S(1)}, bf16[2048,256]{1,0:T(8,128)(2,1)}, u32[]{:S(2)}, u32[]{:S(2)}) collective-permute-start(bf16[2048,256]{1,0:T(8,128)(2,1)S(1)} %pad_maximum_fusion.4.refs_4_), channel_id=1, source_target_pairs={{0,1},{1,0},{2,3},{3,2},{4,5},{5,4},{6,7},{7,6},{8,9},{9,8},{10,11... | collective-permute-start | bytes 3145736 | tf_op jit(solution)/shard_map/ppermute | solution.py:23
  232.2 25.3 %collective-permute-start.42 = (bf16[2048,256]{1,0:T(8,128)(2,1)S(1)}, bf16[2048,256]{1,0:T(8,128)(2,1)}, u32[]{:S(2)}, u32[]{:S(2)}) collective-permute-start(bf16[2048,256]{1,0:T(8,128)(2,1)S(1)} %pad_maximum_fusion.4.refs_4_), channel_id=1, source_target_pairs={{0,16},{16,0},{1,17},{17,1},{2,18},{18,2},{3,19},{19,3},{4,20},{20... | collective-permute-start | bytes 3145736 | tf_op jit(solution)/shard_map/ppermute | solution.py:23
  257.5 4.8 %collective-permute-start.49 = (bf16[2048,256]{1,0:T(8,128)(2,1)}, bf16[2048,256]{1,0:T(8,128)(2,1)S(1)}, u32[]{:S(2)}, u32[]{:S(2)}) collective-permute-start(bf16[2048,256]{1,0:T(8,128)(2,1)} %collective-permute-done.41.refs_5_), channel_id=1, source_target_pairs={{0,8},{8,0},{1,9},{9,1},{2,10},{10,2},{3,11},{11,3},{4,12},{12,4},... | collective-permute-start | bytes 3145736 | tf_op jit(solution)/shard_map/ppermute | solution.py:23
  257.5 4.8 %collective-permute-start.50 = (bf16[2048,256]{1,0:T(8,128)(2,1)}, bf16[2048,256]{1,0:T(8,128)(2,1)}, u32[]{:S(2)}, u32[]{:S(2)}) collective-permute-start(bf16[2048,256]{1,0:T(8,128)(2,1)} %collective-permute-done.42), channel_id=1, source_target_pairs={{0,8},{8,0},{1,9},{9,1},{2,10},{10,2},{3,11},{11,3},{4,12},{12,4},... | collective-permute-start | bytes 3145736 | tf_op jit(solution)/shard_map/ppermute | solution.py:23
  258.0 16.6 %collective-permute-start.47 = (bf16[16,128,128]{2,1,0:T(8,128)(2,1)}, bf16[16,128,128]{2,1,0:T(8,128)(2,1)}, u32[]{:S(2)}, u32[]{:S(2)}) collective-permute-start(bf16[16,128,128]{2,1,0:T(8,128)(2,1)} %get-tuple-element.185), channel_id=1, source_target_pairs={{0,16},{16,0},{1,17},{17,1},{2,18},{18,2},{3,19},{19,3},{4,20},{20... | collective-permute-start | bytes 1572872 | tf_op jit(solution)/shard_map/ppermute | solution.py:23
  258.3 16.3 %collective-permute-start.48 = (bf16[16,128,128]{2,1,0:T(8,128)(2,1)}, bf16[16,128,128]{2,1,0:T(8,128)(2,1)}, u32[]{:S(2)}, u32[]{:S(2)}) collective-permute-start(bf16[16,128,128]{2,1,0:T(8,128)(2,1)} %get-tuple-element.186), channel_id=1, source_target_pairs={{0,1},{1,0},{2,3},{3,2},{4,5},{5,4},{6,7},{7,6},{8,9},{9,8},{10,11... | collective-permute-start | bytes 1572872 | tf_op jit(solution)/shard_map/ppermute | solution.py:23
  261.1 19.9 %collective-permute-start.46 = (f32[256,256]{1,0:T(8,128)S(1)}, f32[256,256]{1,0:T(8,128)S(1)}, u32[]{:S(2)}, u32[]{:S(2)}) collective-permute-start(f32[256,256]{1,0:T(8,128)S(1)} %gram_rows.2), channel_id=1, source_target_pairs={{0,16},{16,0},{1,17},{17,1},{2,18},{18,2},{3,19},{19,3},{4,20},{20... | collective-permute-start | bytes 786440 | tf_op jit(solution)/shard_map/ppermute | solution.py:23
  276.8 12.1 %collective-permute-start.58 = (bf16[4,256,128]{2,1,0:T(8,128)(2,1)S(1)}, bf16[4,256,128]{2,1,0:T(8,128)(2,1)S(1)}, u32[]{:S(2)}, u32[]{:S(2)}) collective-permute-start(bf16[4,256,128]{2,1,0:T(8,128)(2,1)S(1)} %bitcast.87), channel_id=1, source_target_pairs={{0,1},{1,0},{2,3},{3,2},{4,5},{5,4},{6,7},{7,6},{8,9},{9,8},{10,11... | collective-permute-start | bytes 786440 | tf_op jit(solution)/shard_map/ppermute | solution.py:23
  277.8 11.1 %collective-permute-start.59 = (bf16[4,256,128]{2,1,0:T(8,128)(2,1)S(1)}, bf16[4,256,128]{2,1,0:T(8,128)(2,1)S(1)}, u32[]{:S(2)}, u32[]{:S(2)}) collective-permute-start(bf16[4,256,128]{2,1,0:T(8,128)(2,1)S(1)} %bitcast.86), channel_id=1, source_target_pairs={{0,16},{16,0},{1,17},{17,1},{2,18},{18,2},{3,19},{19,3},{4,20},{20... | collective-permute-start | bytes 786440 | tf_op jit(solution)/shard_map/ppermute | solution.py:23
  278.1 17.8 %collective-permute-start.51 = (bf16[16,128,128]{2,1,0:T(8,128)(2,1)S(1)}, bf16[16,128,128]{2,1,0:T(8,128)(2,1)S(1)}, u32[]{:S(2)}, u32[]{:S(2)}) collective-permute-start(bf16[16,128,128]{2,1,0:T(8,128)(2,1)S(1)} %copy-done.39), channel_id=1, source_target_pairs={{0,16},{16,0},{1,17},{17,1},{2,18},{18,2},{3,19},{19,3},{4,20},{20... | collective-permute-start | bytes 1572872 | tf_op jit(solution)/shard_map/ppermute | solution.py:23
  279.9 16.0 %collective-permute-start.52 = (bf16[16,128,128]{2,1,0:T(8,128)(2,1)S(1)}, bf16[16,128,128]{2,1,0:T(8,128)(2,1)S(1)}, u32[]{:S(2)}, u32[]{:S(2)}) collective-permute-start(bf16[16,128,128]{2,1,0:T(8,128)(2,1)S(1)} %copy-done.38), channel_id=1, source_target_pairs={{0,1},{1,0},{2,3},{3,2},{4,5},{5,4},{6,7},{7,6},{8,9},{9,8},{10,11... | collective-permute-start | bytes 1572872 | tf_op jit(solution)/shard_map/ppermute | solution.py:23
  296.0 11.1 %collective-permute-start.60 = (bf16[2,256,256]{2,1,0:T(8,128)(2,1)S(1)}, bf16[2,256,256]{2,1,0:T(8,128)(2,1)S(1)}, u32[]{:S(2)}, u32[]{:S(2)}) collective-permute-start(bf16[2,256,256]{2,1,0:T(8,128)(2,1)S(1)} %slice.247), channel_id=1, source_target_pairs={{0,2},{2,0},{4,6},{6,4},{1,3},{3,1},{5,7},{7,5},{8,10},{10,8},{12,... | collective-permute-start | bytes 786440 | tf_op jit(solution)/shard_map/ppermute | solution.py:28
  298.4 13.3 %collective-permute-start.55 = (bf16[4,256,128]{2,1,0:T(8,128)(2,1)S(1)}, bf16[4,256,128]{2,1,0:T(8,128)(2,1)S(1)}, u32[]{:S(2)}, u32[]{:S(2)}) collective-permute-start(bf16[4,256,128]{2,1,0:T(8,128)(2,1)S(1)} %bitcast.85), channel_id=1, source_target_pairs={{0,1},{1,0},{2,3},{3,2},{4,5},{5,4},{6,7},{7,6},{8,9},{9,8},{10,11... | collective-permute-start | bytes 786440 | tf_op jit(solution)/shard_map/ppermute | solution.py:23
  300.2 11.6 %collective-permute-start.56 = (bf16[4,256,128]{2,1,0:T(8,128)(2,1)S(1)}, bf16[4,256,128]{2,1,0:T(8,128)(2,1)S(1)}, u32[]{:S(2)}, u32[]{:S(2)}) collective-permute-start(bf16[4,256,128]{2,1,0:T(8,128)(2,1)S(1)} %bitcast.84), channel_id=1, source_target_pairs={{0,16},{16,0},{1,17},{17,1},{2,18},{18,2},{3,19},{19,3},{4,20},{20... | collective-permute-start | bytes 786440 | tf_op jit(solution)/shard_map/ppermute | solution.py:23
  300.5 11.1 %collective-permute-start.53 = (f32[128,512]{1,0:T(8,128)S(1)}, f32[128,512]{1,0:T(8,128)S(1)}, u32[]{:S(2)}, u32[]{:S(2)}) collective-permute-start(f32[128,512]{1,0:T(8,128)S(1)} %gram_rows.3), channel_id=1, source_target_pairs={{0,16},{16,0},{1,17},{17,1},{2,18},{18,2},{3,19},{19,3},{4,20},{20... | collective-permute-start | bytes 786440 | tf_op jit(solution)/shard_map/ppermute | solution.py:23
  307.3 7.1 %collective-permute-start.61 = (bf16[256,256]{1,0:T(8,128)(2,1)S(1)}, bf16[256,256]{1,0:T(8,128)(2,1)S(1)}, u32[]{:S(2)}, u32[]{:S(2)}) collective-permute-start(bf16[256,256]{1,0:T(8,128)(2,1)S(1)} %fusion.21), channel_id=1, source_target_pairs={{0,4},{2,6},{4,0},{6,2},{1,5},{3,7},{5,1},{7,3},{8,12},{10,14},{12... | collective-permute-start | bytes 393224 | tf_op jit(solution)/shard_map/ppermute | solution.py:28
  311.6 2.7 collective-permute-start.54
  311.9 8.8 %collective-permute-start.57 = (bf16[2,256,256]{2,1,0:T(8,128)(2,1)S(1)}, bf16[2,256,256]{2,1,0:T(8,128)(2,1)S(1)}, u32[]{:S(2)}, u32[]{:S(2)}) collective-permute-start(bf16[2,256,256]{2,1,0:T(8,128)(2,1)S(1)} %slice.250), channel_id=1, source_target_pairs={{0,2},{2,0},{4,6},{6,4},{1,3},{3,1},{5,7},{7,5},{8,10},{10,8},{12,... | collective-permute-start | bytes 786440 | tf_op jit(solution)/shard_map/ppermute | solution.py:28
  327.5 8.9 %collective-permute-start.62 = (bf16[256,256]{1,0:T(8,128)(2,1)S(1)}, bf16[256,256]{1,0:T(8,128)(2,1)S(1)}, u32[]{:S(2)}, u32[]{:S(2)}) collective-permute-start(bf16[256,256]{1,0:T(8,128)(2,1)S(1)} %fusion.22), channel_id=1, source_target_pairs={{0,4},{2,6},{4,0},{6,2},{1,5},{3,7},{5,1},{7,3},{8,12},{10,14},{12... | collective-permute-start | bytes 393224 | tf_op jit(solution)/shard_map/ppermute | solution.py:28
  337.1 5.7 %collective-permute-start.63 = (f32[128,256]{1,0:T(8,128)S(1)}, f32[128,256]{1,0:T(8,128)S(1)}, u32[]{:S(2)}, u32[]{:S(2)}) collective-permute-start(f32[128,256]{1,0:T(8,128)S(1)} %fusion.14), channel_id=1, source_target_pairs={{0,24},{8,0},{16,8},{24,16},{1,25},{9,1},{17,9},{25,17},{2,26},{10... | collective-permute-start | bytes 393224 | tf_op jit(solution)/shard_map/ppermute | solution.py:618
  337.8 7.2 %collective-permute-start.64 = (f32[128,256]{1,0:T(8,128)S(1)}, f32[128,256]{1,0:T(8,128)S(1)}, u32[]{:S(2)}, u32[]{:S(2)}) collective-permute-start(f32[128,256]{1,0:T(8,128)S(1)} %fusion.16), channel_id=1, source_target_pairs={{0,16},{8,24},{16,0},{24,8},{1,17},{9,25},{17,1},{25,9},{2,18},{10... | collective-permute-start | bytes 393224 | tf_op jit(solution)/shard_map/ppermute | solution.py:618
  340.0 5.8 %collective-permute-start.65 = (f32[128,256]{1,0:T(8,128)S(1)}, f32[128,256]{1,0:T(8,128)S(1)}, u32[]{:S(2)}, u32[]{:S(2)}) collective-permute-start(f32[128,256]{1,0:T(8,128)S(1)} %fusion.19), channel_id=1, source_target_pairs={{0,8},{8,16},{16,24},{24,0},{1,9},{9,17},{17,25},{25,1},{2,10},{10... | collective-permute-start | bytes 393224 | tf_op jit(solution)/shard_map/ppermute | solution.py:618
  (43 other events, 384.5 us)

commit v6 on v5

--- a/solution.py
+++ b/solution.py
@@ -10,6 +10,7 @@
 RB_DEV = 32
 UNROLL = 32
 AHEAD = 2
+WAITS = 16
 CHUNKS = 2
 LEAF = 128
 MOST_SLOTS = 512
@@ -147,6 +148,8 @@
         pltpu.make_async_copy(source, target, panel_sem.at[i])
         for i, (source, target) in enumerate(panel_copies)
     ]
+    for copy in copies:
+        copy.start()
 
     start = 0
     for turn, group in enumerate(passes_of(bounds)):
@@ -163,8 +166,6 @@
             lax.fori_loop(0, counts[s], take, 0)
             count = count + counts[s]
         if turn == 0:
-            for copy in copies:
-                copy.start()
 
             def clear(i, carry):
                 acc[i] = jnp.zeros(acc.shape[1:], acc.dtype)
@@ -172,11 +173,13 @@
 
             lax.fori_loop(0, acc.shape[0] - 1, clear, 0)
 
-        def settle(i, carry):
-            pltpu.make_async_copy(sources[0].at[0], slots.at[0], sem).wait()
+        def settle(i, carry, n=1):
+            some = pl.ds(0, n)
+            pltpu.make_async_copy(sources[0].at[some], slots.at[some], sem).wait()
             return carry
 
-        lax.fori_loop(0, count, settle, 0)
+        lax.fori_loop(0, count // WAITS, functools.partial(settle, n=WAITS), 0)
+        lax.fori_loop(0, count % WAITS, settle, 0)
         if turn == 0:
             for copy in copies:
                 copy.wait()
@@ -582,26 +585,26 @@
     got_gram = along_x(gram_a)
     spread_b = spread_b[0] + spread_b[1]
     all_b = together([line_b, *spread_b, *line_b_far, *across(spread_b)])[0]
-    first_a, zs_b = together(first_a, z_products(all_b))
+    gram_b = gram_rows(core, [near_a, same_x(all_b)], kc // 2)
+    got_b = along_x(gram_b)
+    first_a, zs_b, got_b = together(first_a, z_products(after(all_b, gram_b)), got_b)
     first_b = z_first(zs_b)
+    gram_b = sum(got_b, gram_b)
+    gram_b = absolute([gram_b, shift(gram_b, "core", 1)], "core")
+    gram_a = sum(after(got_gram, zs_b), gram_a)
     second_a = z_second(*z_summed(zs_a, first_a))
-    gram_a = sum(after(got_gram, zs_b), gram_a)
     more_rows(gram_a, zs_b[0])
-    gram_b = gram_rows(core, [near_a, same_x(after(all_b, zs_b))], kc // 2)
+    more_rows(gram_a)
     first_b, gram_b, _ = together(first_b, gram_b, inverse[-1])
-    got_gram = along_x(gram_b)
     summed_b = z_summed(zs_b, first_b)
     second_b = z_second(*summed_b)
     z_a = reduce_p(after(second_a, summed_b))
-    more_rows(gram_a, summed_b[0])
+    more_rows(gram_b, summed_b[0])
     second_b, _ = together(second_b, inverse[-1])
     half_b = reduce_half(second_b)
-    gram_b = sum(got_gram, gram_b)
-    gram_b = absolute([gram_b, shift(gram_b, "core", 1)], "core")
-    more_rows(gram_b)
+    more_rows(gram_b, second_b)
     half_b, _ = together(half_b, inverse[-1])
     z_b = reduce_rest(half_b)
-    more_rows(gram_b, half_b)
     inverse = jnp.concatenate(inverse, axis=0)
     own_rows = jnp.concatenate([own_a, own_b], axis=1)
 

time: 349 us -> 339 us (0.971)
  Pallas kernels: 85.8 us -> 81.4 us
    pallas_call x4, Pallas kernels: 43.7 us -> 39.3 us  [block_products(): pl.pallas_call(kernel, out_shape=outs, in_specs=[smem] * 4 + [anywhere] *...]
  transfers between devices with their start and end apart: 66 -> 66, of which waited for: 34 -> 34; matrix products, arithmetic and copies ran while one was open for 7% -> 6% of each run, Pallas kernels for 20% -> 21%
where the time goes in v6:
time: 339 us; the launch traced here: 338 us
  waiting for transfers between devices  164 us (48%)
  Pallas kernels  81.4 us (24%)
  starting transfers between devices  59.2 us (17%)
  local copies, waits for them, and re-layouts  14.5 us (4%)
  other arithmetic  12.3 us (4%)
  matrix products  5.32 us (2%)
    ppermute x18, waiting for transfers between devices, swap(): return lax.ppermute(value, 'p', [(i, i ^ bits) for i in range(size)])  115 us
    ppermute x45, waiting for transfers between devices, shift(): lax.ppermute(value, axis, [(i, (i + by) % size) for i in range(size)])  44.7 us
    pallas_call x4, Pallas kernels, block_products(): pl.pallas_call(kernel, out_shape=outs, in_specs=[smem] * 4 + [anywhere] *...  39.3 us
    ppermute x45, starting transfers between devices, shift(): lax.ppermute(value, axis, [(i, (i + by) % size) for i in range(size)])  29.6 us
    ppermute x18, starting transfers between devices, swap(): return lax.ppermute(value, 'p', [(i, i ^ bits) for i in range(size)])  28.1 us
    pallas_call x4, Pallas kernels, inverse_rows(): pl.pallas_call(functools.partial(inverse_kernel, scale, len(before), firs...  21.1 us
    pallas_call x2, Pallas kernels, block_lists(): pl.pallas_call(functools.partial(list_kernel, counts_in, bounds, spare),...  15.3 us
  transfers between devices with their start and end apart: 66, of which 34 were waited for; matrix products, arithmetic and copies ran while one was open for 6% of the time, Pallas kernels for 21%

profile of v6, /device:TPU:0, one launch (start us, length us, event | category | flops | bytes accessed | tf_op | source)
XLA Modules:
  0.0 338.3 jit_solution(11323890015094651356)
XLA Ops:
  1.9 2.6 collective-permute-start.2
  4.4 1.5 collective-permute-start.4
  6.0 2.7 collective-permute-start
  8.6 1.7 fusion.78
  11.4 9.2 %collective-permute-done = bf16[2,128,512]{2,1,0:T(8,128)(2,1)S(1)} collective-permute-done((bf16[2,128,512]{2,1,0:T(8,128)(2,1)S(1)}, bf16[2,128,512]{2,1,0:T(8,128)(2,1)S(1)}, u32[]{:S(2)}, u32[]{:S(2)}) %collective-permute-start) | collective-permute-done | bytes 262176 | tf_op jit(solution)/shard_map/ppermute | solution.py:29
  22.6 2.3 slice.160
  24.9 8.8 %collective-permute-done.1 = bf16[4,128,512]{2,1,0:T(8,128)(2,1)S(1)} collective-permute-done((bf16[4,128,512]{2,1,0:T(8,128)(2,1)S(1)}, bf16[4,128,512]{2,1,0:T(8,128)(2,1)S(1)}, u32[]{:S(2)}, u32[]{:S(2)}) %collective-permute-start.1) | collective-permute-done | bytes 524320 | tf_op jit(solution)/shard_map/ppermute | solution.py:29
  35.3 2.8 collective-permute-start.8
  39.7 10.0 %collective-permute-done.8 = bf16[2,128,512]{2,1,0:T(8,128)(2,1)S(1)} collective-permute-done((bf16[2,128,512]{2,1,0:T(8,128)(2,1)S(1)}, bf16[2,128,512]{2,1,0:T(8,128)(2,1)S(1)}, u32[]{:S(2)}, u32[]{:S(2)}) %collective-permute-start.8) | collective-permute-done | bytes 262176 | tf_op jit(solution)/shard_map/ppermute | solution.py:29
  52.2 2.3 slice.162
  54.5 10.7 %collective-permute-done.9 = bf16[4,128,512]{2,1,0:T(8,128)(2,1)} collective-permute-done((bf16[4,128,512]{2,1,0:T(8,128)(2,1)}, bf16[4,128,512]{2,1,0:T(8,128)(2,1)}, u32[]{:S(2)}, u32[]{:S(2)}) %collective-permute-start.9) | collective-permute-done | bytes 524320 | tf_op jit(solution)/shard_map/ppermute | solution.py:29
  65.2 2.1 pad_maximum_fusion.1.refs_18_
  70.5 7.6 %block_lists.2 = (s32[10]{0:T(128)}, s32[480]{0:T(512)}, s32[480]{0:T(512)}, s32[480]{0:T(512)}) custom-call(s32[512]{0:T(512)} %get-tuple-element.237.rows_ref, s32[512]{0:T(512)} %get-tuple-element.238.cols_ref), custom_call_target="tpu_custom_call" | custom-call | flops 4294967296 | bytes 16384 | tf_op jit(solution)/shard_map/block_lists/pallas_call | solution.py:134
  78.2 7.7 %block_lists.3 = (s32[10]{0:T(128)}, s32[544]{0:T(1024)}, s32[544]{0:T(1024)}, s32[544]{0:T(1024)}) custom-call(s32[512]{0:T(512)} %get-tuple-element.236.rows_ref, s32[512]{0:T(512)} %get-tuple-element.228.cols_ref), custom_call_target="tpu_custom_call" | custom-call | flops 4294967296 | bytes 16384 | tf_op jit(solution)/shard_map/block_lists/pallas_call | solution.py:134
  85.8 7.5 %collective-permute-done.16.refs_19_ = bf16[8,128,512]{2,1,0:T(8,128)(2,1)} collective-permute-done((bf16[8,128,512]{2,1,0:T(8,128)(2,1)}, bf16[8,128,512]{2,1,0:T(8,128)(2,1)}, u32[]{:S(2)}, u32[]{:S(2)}) %collective-permute-start.16) | collective-permute-done | bytes 1048608 | tf_op jit(solution)/shard_map/ppermute | solution.py:24
  94.6 2.8 collective-permute-done.21.refs_11_
  98.6 1.5 collective-permute-done.23.refs_21_
  100.1 9.6 %sketch_products.2 = (f32[16,128,256]{2,1,0:T(8,128)}, bf16[16,128,256]{2,1,0:T(8,128)(2,1)}, bf16[16,128,256]{2,1,0:T(8,128)(2,1)}) custom-call(s32[10]{0:T(128)} %get-tuple-element.141.refs_0_, s32[480]{0:T(512)} %get-tuple-element.142.refs_1_, s32[480]{0:T(512)} %get-tuple-element.143.refs_2_, s32[480]{0:T(512)} %get-tuple-element.144.refs_3_, ...), custom_call_target="tpu_custom_call" | custom-call | flops 1073741824 | bytes 33554432 | tf_op jit(solution)/shard_map/sketch_products/pallas_call | solution.py:262
  109.6 1.6 collective-permute-start.24
  111.2 1.5 collective-permute-start.25
  112.8 9.7 %sketch_products.3 = (f32[16,128,256]{2,1,0:T(8,128)}, bf16[16,128,256]{2,1,0:T(8,128)(2,1)}, bf16[16,128,256]{2,1,0:T(8,128)(2,1)}) custom-call(s32[10]{0:T(128)} %get-tuple-element.141.refs_0_, s32[480]{0:T(512)} %get-tuple-element.142.refs_1_, s32[480]{0:T(512)} %get-tuple-element.143.refs_2_, s32[480]{0:T(512)} %get-tuple-element.144.refs_3_, ...), custom_call_target="tpu_custom_call" | custom-call | flops 1073741824 | bytes 33554432 | tf_op jit(solution)/shard_map/sketch_products/pallas_call | solution.py:262
  122.5 12.6 %collective-permute-done.24 = bf16[16,128,256]{2,1,0:T(8,128)(2,1)S(1)} collective-permute-done((bf16[16,128,256]{2,1,0:T(8,128)(2,1)}, bf16[16,128,256]{2,1,0:T(8,128)(2,1)S(1)}, u32[]{:S(2)}, u32[]{:S(2)}) %collective-permute-start.24) | collective-permute-done | bytes 1048608 | tf_op jit(solution)/shard_map/ppermute | solution.py:24
  135.1 1.2 collective-permute-done.25
  137.5 1.7 fusion.77
  139.3 4.5 %collective-permute-start.28 = (bf16[512,256]{1,0:T(8,128)(2,1)S(1)}, bf16[512,256]{1,0:T(8,128)(2,1)S(1)}, u32[]{:S(2)}, u32[]{:S(2)}) collective-permute-start(bf16[512,256]{1,0:T(8,128)(2,1)S(1)} %bitcast.91), channel_id=1, source_target_pairs={{0,6},{2,4},{4,2},{6,0},{1,7},{3,5},{5,3},{7,1},{8,14},{10,12},{12... | collective-permute-start | bytes 786440 | tf_op jit(solution)/shard_map/ppermute | solution.py:29
  144.5 6.5 %collective-permute-done.28 = bf16[512,256]{1,0:T(8,128)(2,1)S(1)} collective-permute-done((bf16[512,256]{1,0:T(8,128)(2,1)S(1)}, bf16[512,256]{1,0:T(8,128)(2,1)S(1)}, u32[]{:S(2)}, u32[]{:S(2)}) %collective-permute-start.28) | collective-permute-done | bytes 262176 | tf_op jit(solution)/shard_map/ppermute | solution.py:29
  151.0 5.1 %collective-permute-done.27 = bf16[512,256]{1,0:T(8,128)(2,1)S(1)} collective-permute-done((bf16[512,256]{1,0:T(8,128)(2,1)S(1)}, bf16[512,256]{1,0:T(8,128)(2,1)S(1)}, u32[]{:S(2)}, u32[]{:S(2)}) %collective-permute-start.27) | collective-permute-done | bytes 262176 | tf_op jit(solution)/shard_map/ppermute | solution.py:29
  156.2 8.1 %collective-permute-done.26 = bf16[512,256]{1,0:T(8,128)(2,1)S(1)} collective-permute-done((bf16[512,256]{1,0:T(8,128)(2,1)S(1)}, bf16[512,256]{1,0:T(8,128)(2,1)S(1)}, u32[]{:S(2)}, u32[]{:S(2)}) %collective-permute-start.26) | collective-permute-done | bytes 262176 | tf_op jit(solution)/shard_map/ppermute | solution.py:29
  165.3 3.0 collective-permute-start.31
  168.4 12.8 %collective-permute-done.31 = bf16[512,256]{1,0:T(8,128)(2,1)S(1)} collective-permute-done((bf16[512,256]{1,0:T(8,128)(2,1)S(1)}, bf16[512,256]{1,0:T(8,128)(2,1)S(1)}, u32[]{:S(2)}, u32[]{:S(2)}) %collective-permute-start.31) | collective-permute-done | bytes 262176 | tf_op jit(solution)/shard_map/ppermute | solution.py:29
  181.3 2.8 collective-permute-start.32
  185.0 15.3 %collective-permute-done.32 = bf16[1024,256]{1,0:T(8,128)(2,1)S(1)} collective-permute-done((bf16[1024,256]{1,0:T(8,128)(2,1)S(1)}, bf16[1024,256]{1,0:T(8,128)(2,1)S(1)}, u32[]{:S(2)}, u32[]{:S(2)}) %collective-permute-start.32) | collective-permute-done | bytes 524320 | tf_op jit(solution)/shard_map/ppermute | solution.py:29
  200.9 1.8 collective-permute-start.37
  203.0 8.4 %collective-permute-done.37 = bf16[512,256]{1,0:T(8,128)(2,1)S(1)} collective-permute-done((bf16[512,256]{1,0:T(8,128)(2,1)S(1)}, bf16[512,256]{1,0:T(8,128)(2,1)S(1)}, u32[]{:S(2)}, u32[]{:S(2)}) %collective-permute-start.37) | collective-permute-done | bytes 262176 | tf_op jit(solution)/shard_map/ppermute | solution.py:29
  211.4 2.5 collective-permute-start.35
  213.8 3.3 collective-permute-done.36
  217.2 7.7 %collective-permute-done.35 = bf16[512,256]{1,0:T(8,128)(2,1)S(1)} collective-permute-done((bf16[512,256]{1,0:T(8,128)(2,1)S(1)}, bf16[512,256]{1,0:T(8,128)(2,1)S(1)}, u32[]{:S(2)}, u32[]{:S(2)}) %collective-permute-start.35) | collective-permute-done | bytes 262176 | tf_op jit(solution)/shard_map/ppermute | solution.py:29
  225.6 1.7 collective-permute-start.41
  227.3 1.7 collective-permute-start.42
  230.4 10.0 %project_products.2 = (f32[16,128,128]{2,1,0:T(8,128)}, bf16[16,128,128]{2,1,0:T(8,128)(2,1)}, f32[16,128,128]{2,1,0:T(8,128)}, bf16[16,128,128]{2,1,0:T(8,128)(2,1)}) custom-call(s32[10]{0:T(128)} %get-tuple-element.171.refs_0_, s32[544]{0:T(1024)} %get-tuple-element.172.refs_1_, s32[544]{0:T(1024)} %get-tuple-element.173.refs_2_, ...), custom_call_target="tpu_custom_call" | custom-call | flops 1073741824 | bytes 33554432 | tf_op jit(solution)/shard_map/project_products/pallas_call | solution.py:262
  244.1 2.0 gram_rows.2
  246.1 5.2 %collective-permute-done.41.refs_5_ = bf16[2048,256]{1,0:T(8,128)(2,1)} collective-permute-done((bf16[2048,256]{1,0:T(8,128)(2,1)S(1)}, bf16[2048,256]{1,0:T(8,128)(2,1)}, u32[]{:S(2)}, u32[]{:S(2)}) %collective-permute-start.41) | collective-permute-done | bytes 1048608 | tf_op jit(solution)/shard_map/ppermute | solution.py:24
  251.2 1.4 collective-permute-done.42
  253.1 1.7 collective-permute-start.47
  255.2 1.7 collective-permute-done.49.refs_7_
  257.1 3.7 %gram_rows.3 = f32[128,512]{1,0:T(8,128)S(1)} custom-call(s32[1]{0:T(128)} %bitcast.16.core_ref, bf16[2048,256]{1,0:T(8,128)(2,1)S(1)} %copy-done.4, bf16[2048,256]{1,0:T(8,128)(2,1)S(1)} %copy-done.9, bf16[2048,256]{1,0:T(8,128)(2,1)S(1)} %copy-done.11, bf16[2048,256]{1,0:T(8,128)(2,1)S(1)} %copy-done.13, bf16[2048,256]{1,0:T(8,128)(2,1)S(1)} %pad_maximum_fusion.4.refs_4_, ...), custom_call_target="tpu_custom_call" | custom-call | flops 2147483648 | bytes 8388608 | tf_op jit(solution)/shard_map/gram_rows/pallas_call | solution.py:335
  260.9 1.8 collective-permute-start.51
  262.9 10.1 %project_products.3 = (f32[16,128,128]{2,1,0:T(8,128)}, bf16[16,128,128]{2,1,0:T(8,128)(2,1)}, f32[16,128,128]{2,1,0:T(8,128)}, bf16[16,128,128]{2,1,0:T(8,128)(2,1)}) custom-call(s32[10]{0:T(128)} %get-tuple-element.171.refs_0_, s32[544]{0:T(1024)} %get-tuple-element.172.refs_1_, s32[544]{0:T(1024)} %get-tuple-element.173.refs_2_, ...), custom_call_target="tpu_custom_call" | custom-call | flops 1073741824 | bytes 33554432 | tf_op jit(solution)/shard_map/project_products/pallas_call | solution.py:262
  273.8 1.6 convert_add_fusion.2
  275.4 2.2 collective-permute-start.58
  280.1 1.7 collective-permute-start.57
  281.8 3.9 %inverse_rows.4.refs_0_ = f32[128,512]{1,0:T(8,128)S(1)} custom-call(f32[256,256]{1,0:T(8,128)S(1)} %add.274.gram, f32[16,128,128]{2,1,0:T(8,128)S(1)} %copy-done.14), custom_call_target="tpu_custom_call" | custom-call | flops 67108864 | bytes 65536 | tf_op jit(solution)/shard_map/inverse_rows/pallas_call | solution.py:372
  285.7 4.9 %inverse_rows.5.refs_1_ = f32[128,512]{1,0:T(8,128)S(1)} custom-call(f32[256,256]{1,0:T(8,128)S(1)} %add.274.gram, f32[128,512]{1,0:T(8,128)S(1)} %inverse_rows.4.refs_0_), custom_call_target="tpu_custom_call" | custom-call | flops 67108864 | bytes 65536 | tf_op jit(solution)/shard_map/inverse_rows/pallas_call | solution.py:372
  291.1 6.3 %collective-permute-done.57 = bf16[4,256,128]{2,1,0:T(8,128)(2,1)S(1)} collective-permute-done((bf16[4,256,128]{2,1,0:T(8,128)(2,1)S(1)}, bf16[4,256,128]{2,1,0:T(8,128)(2,1)S(1)}, u32[]{:S(2)}, u32[]{:S(2)}) %collective-permute-start.57) | collective-permute-done | bytes 262176 | tf_op jit(solution)/shard_map/ppermute | solution.py:24
  299.5 5.9 %inverse_rows.6.refs_2_ = f32[128,512]{1,0:T(8,128)S(1)} custom-call(f32[256,512]{1,0:T(8,128)S(1)} %fusion.8.gram, f32[128,512]{1,0:T(8,128)S(1)} %inverse_rows.4.refs_0_, f32[128,512]{1,0:T(8,128)S(1)} %inverse_rows.5.refs_1_, f32[2,4,256,128]{3,2,1,0:T(8,128)S(1)} %bitcast.71), custom_call_target="tpu_custom_call" | custom-call | flops 67108864 | bytes 65536 | tf_op jit(solution)/shard_map/inverse_rows/pallas_call | solution.py:372
  305.7 2.1 collective-permute-start.61
  307.7 6.4 %inverse_rows.7 = f32[128,512]{1,0:T(8,128)S(1)} custom-call(f32[256,512]{1,0:T(8,128)S(1)} %fusion.8.gram, f32[128,512]{1,0:T(8,128)S(1)} %inverse_rows.4.refs_0_, f32[128,512]{1,0:T(8,128)S(1)} %inverse_rows.5.refs_1_, f32[128,512]{1,0:T(8,128)S(1)} %inverse_rows.6.refs_2_, f32[4,256,256]{2,1,0:T(8,128)S(1)} %pad_maximum_fusion.5.refs_3_), custom_call_target="tpu_custom_call" | custom-call | flops 67108864 | bytes 65536 | tf_op jit(solution)/shard_map/inverse_rows/pallas_call | solution.py:372
  314.3 1.6 collective-permute-start.60
  316.1 1.5 collective-permute-start.62
  317.5 7.3 %collective-permute-done.60 = bf16[256,256]{1,0:T(8,128)(2,1)S(1)} collective-permute-done((bf16[256,256]{1,0:T(8,128)(2,1)S(1)}, bf16[256,256]{1,0:T(8,128)(2,1)S(1)}, u32[]{:S(2)}, u32[]{:S(2)}) %collective-permute-start.60) | collective-permute-done | bytes 131104 | tf_op jit(solution)/shard_map/ppermute | solution.py:29
  324.8 1.4 collective-permute-done.62
  328.3 1.3 collective-permute-start.64
  329.8 2.7 convolution_convert_fusion
  332.4 4.0 %collective-permute-done.64 = f32[128,256]{1,0:T(8,128)S(1)} collective-permute-done((f32[128,256]{1,0:T(8,128)S(1)}, f32[128,256]{1,0:T(8,128)S(1)}, u32[]{:S(2)}, u32[]{:S(2)}) %collective-permute-start.64) | collective-permute-done | bytes 131104 | tf_op jit(solution)/shard_map/ppermute | solution.py:621
  (246 shorter events, 37.5 us)
Async XLA Ops:
  0.6 34.7 %collective-permute-start.6 = (bf16[128,128,128]{2,1,0:T(8,128)(2,1)}, bf16[128,128,128]{2,1,0:T(8,128)(2,1)}, u32[]{:S(2)}, u32[]{:S(2)}) collective-permute-start(bf16[128,128,128]{2,1,0:T(8,128)(2,1)} %refs_4_.7), channel_id=1, source_target_pairs={{0,8},{8,0},{1,9},{9,1},{2,10},{10,2},{3,11},{11,3},{4,12},{12,4},... | collective-permute-start | bytes 12582920 | tf_op jit(solution)/shard_map/ppermute | solution.py:24
  1.9 8.5 %collective-permute-start.2 = (s32[128]{0:T(128)S(1)}, s32[128]{0:T(128)S(1)}, u32[]{:S(2)}, u32[]{:S(2)}) collective-permute-start(s32[128]{0:T(128)S(1)} %fusion.71), channel_id=1, source_target_pairs={{0,16},{16,0},{1,17},{17,1},{2,18},{18,2},{3,19},{19,3},{4,20},{20... | collective-permute-start | bytes 1544 | tf_op jit(solution)/shard_map/ppermute | solution.py:24
  4.4 6.5 %collective-permute-start.4 = (s32[128]{0:T(128)S(1)}, s32[128]{0:T(128)S(1)}, u32[]{:S(2)}, u32[]{:S(2)}) collective-permute-start(s32[128]{0:T(128)S(1)} %fusion.71), channel_id=1, source_target_pairs={{0,1},{1,0},{2,3},{3,2},{4,5},{5,4},{6,7},{7,6},{8,9},{9,8},{10,11... | collective-permute-start | bytes 1544 | tf_op jit(solution)/shard_map/ppermute | solution.py:24
  6.0 14.7 %collective-permute-start = (bf16[2,128,512]{2,1,0:T(8,128)(2,1)S(1)}, bf16[2,128,512]{2,1,0:T(8,128)(2,1)S(1)}, u32[]{:S(2)}, u32[]{:S(2)}) collective-permute-start(bf16[2,128,512]{2,1,0:T(8,128)(2,1)S(1)} %constant_dynamic-slice_fusion), channel_id=1, source_target_pairs={{0,4},{2,6},{4,0},{6,2},{1,5},{3,7},{5,1},{7,3},{8,12},{10,14},{12... | collective-permute-start | bytes 786440 | tf_op jit(solution)/shard_map/ppermute | solution.py:29
  10.3 24.7 %collective-permute-start.3 = (bf16[32,128,128]{2,1,0:T(8,128)(2,1)S(1)}, bf16[32,128,128]{2,1,0:T(8,128)(2,1)S(1)}, u32[]{:S(2)}, u32[]{:S(2)}) collective-permute-start(bf16[32,128,128]{2,1,0:T(8,128)(2,1)S(1)} %get-tuple-element.114), channel_id=1, source_target_pairs={{0,16},{16,0},{1,17},{17,1},{2,18},{18,2},{3,19},{19,3},{4,20},{20... | collective-permute-start | bytes 3145736 | tf_op jit(solution)/shard_map/ppermute | solution.py:24
  10.9 24.4 %collective-permute-start.5 = (bf16[32,128,128]{2,1,0:T(8,128)(2,1)S(1)}, bf16[32,128,128]{2,1,0:T(8,128)(2,1)S(1)}, u32[]{:S(2)}, u32[]{:S(2)}) collective-permute-start(bf16[32,128,128]{2,1,0:T(8,128)(2,1)S(1)} %get-tuple-element.115), channel_id=1, source_target_pairs={{0,1},{1,0},{2,3},{3,2},{4,5},{5,4},{6,7},{7,6},{8,9},{9,8},{10,11... | collective-permute-start | bytes 3145736 | tf_op jit(solution)/shard_map/ppermute | solution.py:24
  20.7 12.9 %collective-permute-start.1 = (bf16[4,128,512]{2,1,0:T(8,128)(2,1)S(1)}, bf16[4,128,512]{2,1,0:T(8,128)(2,1)S(1)}, u32[]{:S(2)}, u32[]{:S(2)}) collective-permute-start(bf16[4,128,512]{2,1,0:T(8,128)(2,1)S(1)} %pad_maximum_fusion.7), channel_id=1, source_target_pairs={{0,2},{2,0},{4,6},{6,4},{1,3},{3,1},{5,7},{7,5},{8,10},{10,8},{12,... | collective-permute-start | bytes 1572872 | tf_op jit(solution)/shard_map/ppermute | solution.py:29
  35.3 14.4 %collective-permute-start.8 = (bf16[2,128,512]{2,1,0:T(8,128)(2,1)S(1)}, bf16[2,128,512]{2,1,0:T(8,128)(2,1)S(1)}, u32[]{:S(2)}, u32[]{:S(2)}) collective-permute-start(bf16[2,128,512]{2,1,0:T(8,128)(2,1)S(1)} %slice.161), channel_id=1, source_target_pairs={{0,4},{2,6},{4,0},{6,2},{1,5},{3,7},{5,1},{7,3},{8,12},{10,14},{12... | collective-permute-start | bytes 786440 | tf_op jit(solution)/shard_map/ppermute | solution.py:29
  38.1 29.2 %collective-permute-start.10 = (bf16[8,128,512]{2,1,0:T(8,128)(2,1)}, bf16[8,128,512]{2,1,0:T(8,128)(2,1)}, u32[]{:S(2)}, u32[]{:S(2)}) collective-permute-start(bf16[8,128,512]{2,1,0:T(8,128)(2,1)} %pad_maximum_fusion.refs_14_), channel_id=1, source_target_pairs={{0,1},{1,0},{2,3},{3,2},{4,5},{5,4},{6,7},{7,6},{8,9},{9,8},{10,11... | collective-permute-start | bytes 3145736 | tf_op jit(solution)/shard_map/ppermute | solution.py:24
  38.6 28.7 %collective-permute-start.11 = (bf16[32,128,128]{2,1,0:T(8,128)(2,1)}, bf16[32,128,128]{2,1,0:T(8,128)(2,1)S(1)}, u32[]{:S(2)}, u32[]{:S(2)}) collective-permute-start(bf16[32,128,128]{2,1,0:T(8,128)(2,1)} %slice.160), channel_id=1, source_target_pairs={{0,16},{16,0},{1,17},{17,1},{2,18},{18,2},{3,19},{19,3},{4,20},{20... | collective-permute-start | bytes 3145736 | tf_op jit(solution)/shard_map/ppermute | solution.py:24
  39.2 28.2 %collective-permute-start.12 = (bf16[32,128,128]{2,1,0:T(8,128)(2,1)S(1)}, bf16[32,128,128]{2,1,0:T(8,128)(2,1)}, u32[]{:S(2)}, u32[]{:S(2)}) collective-permute-start(bf16[32,128,128]{2,1,0:T(8,128)(2,1)S(1)} %collective-permute-done.3.refs_6_), channel_id=1, source_target_pairs={{0,8},{8,0},{1,9},{9,1},{2,10},{10,2},{3,11},{11,3},{4,12},{12,4},... | collective-permute-start | bytes 3145736 | tf_op jit(solution)/shard_map/ppermute | solution.py:24
  39.2 28.2 %collective-permute-start.13 = (bf16[32,128,128]{2,1,0:T(8,128)(2,1)S(1)}, bf16[32,128,128]{2,1,0:T(8,128)(2,1)}, u32[]{:S(2)}, u32[]{:S(2)}) collective-permute-start(bf16[32,128,128]{2,1,0:T(8,128)(2,1)S(1)} %collective-permute-done.5.refs_12_), channel_id=1, source_target_pairs={{0,8},{8,0},{1,9},{9,1},{2,10},{10,2},{3,11},{11,3},{4,12},{12,4},... | collective-permute-start | bytes 3145736 | tf_op jit(solution)/shard_map/ppermute | solution.py:24
  51.2 14.0 %collective-permute-start.9 = (bf16[4,128,512]{2,1,0:T(8,128)(2,1)}, bf16[4,128,512]{2,1,0:T(8,128)(2,1)}, u32[]{:S(2)}, u32[]{:S(2)}) collective-permute-start(bf16[4,128,512]{2,1,0:T(8,128)(2,1)} %pad_maximum_fusion.8), channel_id=1, source_target_pairs={{0,2},{2,0},{4,6},{6,4},{1,3},{3,1},{5,7},{7,5},{8,10},{10,8},{12,... | collective-permute-start | bytes 1572872 | tf_op jit(solution)/shard_map/ppermute | solution.py:29
  65.2 2.1 collective-permute-start.15
  67.4 26.0 %collective-permute-start.16 = (bf16[8,128,512]{2,1,0:T(8,128)(2,1)}, bf16[8,128,512]{2,1,0:T(8,128)(2,1)}, u32[]{:S(2)}, u32[]{:S(2)}) collective-permute-start(bf16[8,128,512]{2,1,0:T(8,128)(2,1)} %pad_maximum_fusion.1.refs_18_), channel_id=1, source_target_pairs={{0,1},{1,0},{2,3},{3,2},{4,5},{5,4},{6,7},{7,6},{8,9},{9,8},{10,11... | collective-permute-start | bytes 3145736 | tf_op jit(solution)/shard_map/ppermute | solution.py:24
  68.0 25.4 %collective-permute-start.17 = (bf16[8,128,512]{2,1,0:T(8,128)(2,1)}, bf16[8,128,512]{2,1,0:T(8,128)(2,1)}, u32[]{:S(2)}, u32[]{:S(2)}) collective-permute-start(bf16[8,128,512]{2,1,0:T(8,128)(2,1)} %pad_maximum_fusion.refs_14_), channel_id=1, source_target_pairs={{0,8},{8,0},{1,9},{9,1},{2,10},{10,2},{3,11},{11,3},{4,12},{12,4},... | collective-permute-start | bytes 3145736 | tf_op jit(solution)/shard_map/ppermute | solution.py:24
  68.2 25.2 %collective-permute-start.18 = (bf16[8,128,512]{2,1,0:T(8,128)(2,1)}, bf16[8,128,512]{2,1,0:T(8,128)(2,1)}, u32[]{:S(2)}, u32[]{:S(2)}) collective-permute-start(bf16[8,128,512]{2,1,0:T(8,128)(2,1)} %collective-permute-done.10.refs_15_), channel_id=1, source_target_pairs={{0,8},{8,0},{1,9},{9,1},{2,10},{10,2},{3,11},{11,3},{4,12},{12,4},... | collective-permute-start | bytes 3145736 | tf_op jit(solution)/shard_map/ppermute | solution.py:24
  68.5 25.5 %collective-permute-start.19 = (bf16[32,128,128]{2,1,0:T(8,128)(2,1)}, bf16[32,128,128]{2,1,0:T(8,128)(2,1)S(1)}, u32[]{:S(2)}, u32[]{:S(2)}) collective-permute-start(bf16[32,128,128]{2,1,0:T(8,128)(2,1)} %slice.162), channel_id=1, source_target_pairs={{0,16},{16,0},{1,17},{17,1},{2,18},{18,2},{3,19},{19,3},{4,20},{20... | collective-permute-start | bytes 3145736 | tf_op jit(solution)/shard_map/ppermute | solution.py:24
  69.0 25.0 %collective-permute-start.20 = (bf16[32,128,128]{2,1,0:T(8,128)(2,1)S(1)}, bf16[32,128,128]{2,1,0:T(8,128)(2,1)S(1)}, u32[]{:S(2)}, u32[]{:S(2)}) collective-permute-start(bf16[32,128,128]{2,1,0:T(8,128)(2,1)S(1)} %collective-permute-done.11.refs_8_), channel_id=1, source_target_pairs={{0,8},{8,0},{1,9},{9,1},{2,10},{10,2},{3,11},{11,3},{4,12},{12,4},... | collective-permute-start | bytes 3145736 | tf_op jit(solution)/shard_map/ppermute | solution.py:24
  94.0 3.4 %collective-permute-start.21 = (bf16[32,128,128]{2,1,0:T(8,128)(2,1)S(1)}, bf16[32,128,128]{2,1,0:T(8,128)(2,1)S(1)}, u32[]{:S(2)}, u32[]{:S(2)}) collective-permute-start(bf16[32,128,128]{2,1,0:T(8,128)(2,1)S(1)} %collective-permute-done.19.refs_10_), channel_id=1, source_target_pairs={{0,8},{8,0},{1,9},{9,1},{2,10},{10,2},{3,11},{11,3},{4,12},{12,4},... | collective-permute-start | bytes 3145736 | tf_op jit(solution)/shard_map/ppermute | solution.py:24
  94.1 4.5 %collective-permute-start.22 = (bf16[8,128,512]{2,1,0:T(8,128)(2,1)}, bf16[8,128,512]{2,1,0:T(8,128)(2,1)}, u32[]{:S(2)}, u32[]{:S(2)}) collective-permute-start(bf16[8,128,512]{2,1,0:T(8,128)(2,1)} %pad_maximum_fusion.1.refs_18_), channel_id=1, source_target_pairs={{0,8},{8,0},{1,9},{9,1},{2,10},{10,2},{3,11},{11,3},{4,12},{12,4},... | collective-permute-start | bytes 3145736 | tf_op jit(solution)/shard_map/ppermute | solution.py:24
  94.6 5.5 %collective-permute-start.23 = (bf16[8,128,512]{2,1,0:T(8,128)(2,1)}, bf16[8,128,512]{2,1,0:T(8,128)(2,1)}, u32[]{:S(2)}, u32[]{:S(2)}) collective-permute-start(bf16[8,128,512]{2,1,0:T(8,128)(2,1)} %collective-permute-done.16.refs_19_), channel_id=1, source_target_pairs={{0,8},{8,0},{1,9},{9,1},{2,10},{10,2},{3,11},{11,3},{4,12},{12,4},... | collective-permute-start | bytes 3145736 | tf_op jit(solution)/shard_map/ppermute | solution.py:24
  109.6 25.5 %collective-permute-start.24 = (bf16[16,128,256]{2,1,0:T(8,128)(2,1)}, bf16[16,128,256]{2,1,0:T(8,128)(2,1)S(1)}, u32[]{:S(2)}, u32[]{:S(2)}) collective-permute-start(bf16[16,128,256]{2,1,0:T(8,128)(2,1)} %get-tuple-element.155), channel_id=1, source_target_pairs={{0,1},{1,0},{2,3},{3,2},{4,5},{5,4},{6,7},{7,6},{8,9},{9,8},{10,11... | collective-permute-start | bytes 3145736 | tf_op jit(solution)/shard_map/ppermute | solution.py:24
  111.2 25.1 %collective-permute-start.25 = (bf16[16,128,256]{2,1,0:T(8,128)(2,1)}, bf16[16,128,256]{2,1,0:T(8,128)(2,1)}, u32[]{:S(2)}, u32[]{:S(2)}) collective-permute-start(bf16[16,128,256]{2,1,0:T(8,128)(2,1)} %get-tuple-element.156), channel_id=1, source_target_pairs={{0,16},{16,0},{1,17},{17,1},{2,18},{18,2},{3,19},{19,3},{4,20},{20... | collective-permute-start | bytes 3145736 | tf_op jit(solution)/shard_map/ppermute | solution.py:24
  136.3 28.1 %collective-permute-start.29 = (bf16[16,128,256]{2,1,0:T(8,128)(2,1)}, bf16[16,128,256]{2,1,0:T(8,128)(2,1)S(1)}, u32[]{:S(2)}, u32[]{:S(2)}) collective-permute-start(bf16[16,128,256]{2,1,0:T(8,128)(2,1)} %get-tuple-element.162), channel_id=1, source_target_pairs={{0,1},{1,0},{2,3},{3,2},{4,5},{5,4},{6,7},{7,6},{8,9},{9,8},{10,11... | collective-permute-start | bytes 3145736 | tf_op jit(solution)/shard_map/ppermute | solution.py:24
  136.9 27.5 %collective-permute-start.30 = (bf16[16,128,256]{2,1,0:T(8,128)(2,1)}, bf16[16,128,256]{2,1,0:T(8,128)(2,1)S(1)}, u32[]{:S(2)}, u32[]{:S(2)}) collective-permute-start(bf16[16,128,256]{2,1,0:T(8,128)(2,1)} %get-tuple-element.163), channel_id=1, source_target_pairs={{0,16},{16,0},{1,17},{17,1},{2,18},{18,2},{3,19},{19,3},{4,20},{20... | collective-permute-start | bytes 3145736 | tf_op jit(solution)/shard_map/ppermute | solution.py:24
  139.3 11.7 %collective-permute-start.28 = (bf16[512,256]{1,0:T(8,128)(2,1)S(1)}, bf16[512,256]{1,0:T(8,128)(2,1)S(1)}, u32[]{:S(2)}, u32[]{:S(2)}) collective-permute-start(bf16[512,256]{1,0:T(8,128)(2,1)S(1)} %bitcast.91), channel_id=1, source_target_pairs={{0,6},{2,4},{4,2},{6,0},{1,7},{3,5},{5,3},{7,1},{8,14},{10,12},{12... | collective-permute-start | bytes 786440 | tf_op jit(solution)/shard_map/ppermute | solution.py:29
  143.8 12.4 %collective-permute-start.27 = (bf16[512,256]{1,0:T(8,128)(2,1)S(1)}, bf16[512,256]{1,0:T(8,128)(2,1)S(1)}, u32[]{:S(2)}, u32[]{:S(2)}) collective-permute-start(bf16[512,256]{1,0:T(8,128)(2,1)S(1)} %bitcast.90), channel_id=1, source_target_pairs={{0,2},{2,0},{4,6},{6,4},{1,3},{3,1},{5,7},{7,5},{8,10},{10,8},{12,... | collective-permute-start | bytes 786440 | tf_op jit(solution)/shard_map/ppermute | solution.py:29
  143.8 20.5 %collective-permute-start.26 = (bf16[512,256]{1,0:T(8,128)(2,1)S(1)}, bf16[512,256]{1,0:T(8,128)(2,1)S(1)}, u32[]{:S(2)}, u32[]{:S(2)}) collective-permute-start(bf16[512,256]{1,0:T(8,128)(2,1)S(1)} %bitcast.89), channel_id=1, source_target_pairs={{0,4},{2,6},{4,0},{6,2},{1,5},{3,7},{5,1},{7,3},{8,12},{10,14},{12... | collective-permute-start | bytes 786440 | tf_op jit(solution)/shard_map/ppermute | solution.py:29
  164.9 19.5 %collective-permute-start.33 = (bf16[2,512,256]{2,1,0:T(8,128)(2,1)S(1)}, bf16[2,512,256]{2,1,0:T(8,128)(2,1)S(1)}, u32[]{:S(2)}, u32[]{:S(2)}) collective-permute-start(bf16[2,512,256]{2,1,0:T(8,128)(2,1)S(1)} %bitcast.84), channel_id=1, source_target_pairs={{0,2},{2,0},{4,6},{6,4},{1,3},{3,1},{5,7},{7,5},{8,10},{10,8},{12,... | collective-permute-start | bytes 1572872 | tf_op jit(solution)/shard_map/ppermute | solution.py:29
  165.3 16.0 %collective-permute-start.31 = (bf16[512,256]{1,0:T(8,128)(2,1)S(1)}, bf16[512,256]{1,0:T(8,128)(2,1)S(1)}, u32[]{:S(2)}, u32[]{:S(2)}) collective-permute-start(bf16[512,256]{1,0:T(8,128)(2,1)S(1)} %convert_element_type.126), channel_id=1, source_target_pairs={{0,4},{2,6},{4,0},{6,2},{1,5},{3,7},{5,1},{7,3},{8,12},{10,14},{12... | collective-permute-start | bytes 786440 | tf_op jit(solution)/shard_map/ppermute | solution.py:29
  181.3 19.0 %collective-permute-start.32 = (bf16[1024,256]{1,0:T(8,128)(2,1)S(1)}, bf16[1024,256]{1,0:T(8,128)(2,1)S(1)}, u32[]{:S(2)}, u32[]{:S(2)}) collective-permute-start(bf16[1024,256]{1,0:T(8,128)(2,1)S(1)} %pad_maximum_fusion.9), channel_id=1, source_target_pairs={{0,2},{2,0},{4,6},{6,4},{1,3},{3,1},{5,7},{7,5},{8,10},{10,8},{12,... | collective-permute-start | bytes 1572872 | tf_op jit(solution)/shard_map/ppermute | solution.py:29
  184.5 15.8 %collective-permute-start.34 = (bf16[512,256]{1,0:T(8,128)(2,1)S(1)}, bf16[512,256]{1,0:T(8,128)(2,1)S(1)}, u32[]{:S(2)}, u32[]{:S(2)}) collective-permute-start(bf16[512,256]{1,0:T(8,128)(2,1)S(1)} %fusion.12), channel_id=1, source_target_pairs={{0,4},{2,6},{4,0},{6,2},{1,5},{3,7},{5,1},{7,3},{8,12},{10,14},{12... | collective-permute-start | bytes 786440 | tf_op jit(solution)/shard_map/ppermute | solution.py:29
  200.5 24.5 %collective-permute-start.38 = (bf16[2048,256]{1,0:T(8,128)(2,1)S(1)}, bf16[2048,256]{1,0:T(8,128)(2,1)S(1)}, u32[]{:S(2)}, u32[]{:S(2)}) collective-permute-start(bf16[2048,256]{1,0:T(8,128)(2,1)S(1)} %pad_maximum_fusion.2.refs_0_), channel_id=1, source_target_pairs={{0,1},{1,0},{2,3},{3,2},{4,5},{5,4},{6,7},{7,6},{8,9},{9,8},{10,11... | collective-permute-start | bytes 3145736 | tf_op jit(solution)/shard_map/ppermute | solution.py:24
  200.8 24.1 %collective-permute-start.39 = (bf16[2048,256]{1,0:T(8,128)(2,1)S(1)}, bf16[2048,256]{1,0:T(8,128)(2,1)S(1)}, u32[]{:S(2)}, u32[]{:S(2)}) collective-permute-start(bf16[2048,256]{1,0:T(8,128)(2,1)S(1)} %pad_maximum_fusion.2.refs_0_), channel_id=1, source_target_pairs={{0,16},{16,0},{1,17},{17,1},{2,18},{18,2},{3,19},{19,3},{4,20},{20... | collective-permute-start | bytes 3145736 | tf_op jit(solution)/shard_map/ppermute | solution.py:24
  200.9 10.5 %collective-permute-start.37 = (bf16[512,256]{1,0:T(8,128)(2,1)S(1)}, bf16[512,256]{1,0:T(8,128)(2,1)S(1)}, u32[]{:S(2)}, u32[]{:S(2)}) collective-permute-start(bf16[512,256]{1,0:T(8,128)(2,1)S(1)} %convert_element_type.133), channel_id=1, source_target_pairs={{0,6},{2,4},{4,2},{6,0},{1,7},{3,5},{5,3},{7,1},{8,14},{10,12},{12... | collective-permute-start | bytes 786440 | tf_op jit(solution)/shard_map/ppermute | solution.py:29
  202.7 24.6 %collective-permute-start.43 = (bf16[2048,256]{1,0:T(8,128)(2,1)S(1)}, bf16[2048,256]{1,0:T(8,128)(2,1)S(1)}, u32[]{:S(2)}, u32[]{:S(2)}) collective-permute-start(bf16[2048,256]{1,0:T(8,128)(2,1)S(1)} %pad_maximum_fusion.2.refs_0_), channel_id=1, source_target_pairs={{0,8},{8,0},{1,9},{9,1},{2,10},{10,2},{3,11},{11,3},{4,12},{12,4},... | collective-permute-start | bytes 3145736 | tf_op jit(solution)/shard_map/ppermute | solution.py:24
  202.7 14.5 %collective-permute-start.36 = (bf16[512,256]{1,0:T(8,128)(2,1)S(1)}, bf16[512,256]{1,0:T(8,128)(2,1)S(1)}, u32[]{:S(2)}, u32[]{:S(2)}) collective-permute-start(bf16[512,256]{1,0:T(8,128)(2,1)S(1)} %convert_element_type.133), channel_id=1, source_target_pairs={{0,2},{2,0},{4,6},{6,4},{1,3},{3,1},{5,7},{7,5},{8,10},{10,8},{12,... | collective-permute-start | bytes 786440 | tf_op jit(solution)/shard_map/ppermute | solution.py:29
  211.4 13.5 %collective-permute-start.35 = (bf16[512,256]{1,0:T(8,128)(2,1)S(1)}, bf16[512,256]{1,0:T(8,128)(2,1)S(1)}, u32[]{:S(2)}, u32[]{:S(2)}) collective-permute-start(bf16[512,256]{1,0:T(8,128)(2,1)S(1)} %convert_element_type.133), channel_id=1, source_target_pairs={{0,4},{2,6},{4,0},{6,2},{1,5},{3,7},{5,1},{7,3},{8,12},{10,14},{12... | collective-permute-start | bytes 786440 | tf_op jit(solution)/shard_map/ppermute | solution.py:29
  225.0 4.1 %collective-permute-start.44 = (bf16[2048,256]{1,0:T(8,128)(2,1)S(1)}, bf16[2048,256]{1,0:T(8,128)(2,1)S(1)}, u32[]{:S(2)}, u32[]{:S(2)}) collective-permute-start(bf16[2048,256]{1,0:T(8,128)(2,1)S(1)} %collective-permute-done.38.refs_1_), channel_id=1, source_target_pairs={{0,8},{8,0},{1,9},{9,1},{2,10},{10,2},{3,11},{11,3},{4,12},{12,4},... | collective-permute-start | bytes 3145736 | tf_op jit(solution)/shard_map/ppermute | solution.py:24
  225.1 4.1 %collective-permute-start.45 = (bf16[2048,256]{1,0:T(8,128)(2,1)S(1)}, bf16[2048,256]{1,0:T(8,128)(2,1)S(1)}, u32[]{:S(2)}, u32[]{:S(2)}) collective-permute-start(bf16[2048,256]{1,0:T(8,128)(2,1)S(1)} %collective-permute-done.39), channel_id=1, source_target_pairs={{0,8},{8,0},{1,9},{9,1},{2,10},{10,2},{3,11},{11,3},{4,12},{12,4},... | collective-permute-start | bytes 3145736 | tf_op jit(solution)/shard_map/ppermute | solution.py:24
  225.6 20.5 %collective-permute-start.40 = (bf16[2048,256]{1,0:T(8,128)(2,1)S(1)}, bf16[2048,256]{1,0:T(8,128)(2,1)S(1)}, u32[]{:S(2)}, u32[]{:S(2)}) collective-permute-start(bf16[2048,256]{1,0:T(8,128)(2,1)S(1)} %pad_maximum_fusion.4.refs_4_), channel_id=1, source_target_pairs={{0,8},{8,0},{1,9},{9,1},{2,10},{10,2},{3,11},{11,3},{4,12},{12,4},... | collective-permute-start | bytes 3145736 | tf_op jit(solution)/shard_map/ppermute | solution.py:24
  225.6 25.6 %collective-permute-start.41 = (bf16[2048,256]{1,0:T(8,128)(2,1)S(1)}, bf16[2048,256]{1,0:T(8,128)(2,1)}, u32[]{:S(2)}, u32[]{:S(2)}) collective-permute-start(bf16[2048,256]{1,0:T(8,128)(2,1)S(1)} %pad_maximum_fusion.4.refs_4_), channel_id=1, source_target_pairs={{0,1},{1,0},{2,3},{3,2},{4,5},{5,4},{6,7},{7,6},{8,9},{9,8},{10,11... | collective-permute-start | bytes 3145736 | tf_op jit(solution)/shard_map/ppermute | solution.py:24
  227.3 25.3 %collective-permute-start.42 = (bf16[2048,256]{1,0:T(8,128)(2,1)S(1)}, bf16[2048,256]{1,0:T(8,128)(2,1)}, u32[]{:S(2)}, u32[]{:S(2)}) collective-permute-start(bf16[2048,256]{1,0:T(8,128)(2,1)S(1)} %pad_maximum_fusion.4.refs_4_), channel_id=1, source_target_pairs={{0,16},{16,0},{1,17},{17,1},{2,18},{18,2},{3,19},{19,3},{4,20},{20... | collective-permute-start | bytes 3145736 | tf_op jit(solution)/shard_map/ppermute | solution.py:24
  252.6 4.3 %collective-permute-start.49 = (bf16[2048,256]{1,0:T(8,128)(2,1)}, bf16[2048,256]{1,0:T(8,128)(2,1)S(1)}, u32[]{:S(2)}, u32[]{:S(2)}) collective-permute-start(bf16[2048,256]{1,0:T(8,128)(2,1)} %collective-permute-done.41.refs_5_), channel_id=1, source_target_pairs={{0,8},{8,0},{1,9},{9,1},{2,10},{10,2},{3,11},{11,3},{4,12},{12,4},... | collective-permute-start | bytes 3145736 | tf_op jit(solution)/shard_map/ppermute | solution.py:24
  252.6 4.5 %collective-permute-start.50 = (bf16[2048,256]{1,0:T(8,128)(2,1)}, bf16[2048,256]{1,0:T(8,128)(2,1)}, u32[]{:S(2)}, u32[]{:S(2)}) collective-permute-start(bf16[2048,256]{1,0:T(8,128)(2,1)} %collective-permute-done.42), channel_id=1, source_target_pairs={{0,8},{8,0},{1,9},{9,1},{2,10},{10,2},{3,11},{11,3},{4,12},{12,4},... | collective-permute-start | bytes 3145736 | tf_op jit(solution)/shard_map/ppermute | solution.py:24
  253.1 19.9 %collective-permute-start.47 = (bf16[16,128,128]{2,1,0:T(8,128)(2,1)}, bf16[16,128,128]{2,1,0:T(8,128)(2,1)}, u32[]{:S(2)}, u32[]{:S(2)}) collective-permute-start(bf16[16,128,128]{2,1,0:T(8,128)(2,1)} %get-tuple-element.188), channel_id=1, source_target_pairs={{0,16},{16,0},{1,17},{17,1},{2,18},{18,2},{3,19},{19,3},{4,20},{20... | collective-permute-start | bytes 1572872 | tf_op jit(solution)/shard_map/ppermute | solution.py:24
  254.9 18.2 %collective-permute-start.48 = (bf16[16,128,128]{2,1,0:T(8,128)(2,1)}, bf16[16,128,128]{2,1,0:T(8,128)(2,1)}, u32[]{:S(2)}, u32[]{:S(2)}) collective-permute-start(bf16[16,128,128]{2,1,0:T(8,128)(2,1)} %get-tuple-element.189), channel_id=1, source_target_pairs={{0,1},{1,0},{2,3},{3,2},{4,5},{5,4},{6,7},{7,6},{8,9},{9,8},{10,11... | collective-permute-start | bytes 1572872 | tf_op jit(solution)/shard_map/ppermute | solution.py:24
  260.9 12.9 %collective-permute-start.51 = (f32[128,512]{1,0:T(8,128)S(1)}, f32[128,512]{1,0:T(8,128)S(1)}, u32[]{:S(2)}, u32[]{:S(2)}) collective-permute-start(f32[128,512]{1,0:T(8,128)S(1)} %gram_rows.3), channel_id=1, source_target_pairs={{0,16},{16,0},{1,17},{17,1},{2,18},{18,2},{3,19},{19,3},{4,20},{20... | collective-permute-start | bytes 786440 | tf_op jit(solution)/shard_map/ppermute | solution.py:24
  262.7 16.3 %collective-permute-start.46 = (f32[256,256]{1,0:T(8,128)}, f32[256,256]{1,0:T(8,128)}, u32[]{:S(2)}, u32[]{:S(2)}) collective-permute-start(f32[256,256]{1,0:T(8,128)} %copy-done.15), channel_id=1, source_target_pairs={{0,16},{16,0},{1,17},{17,1},{2,18},{18,2},{3,19},{19,3},{4,20},{20... | collective-permute-start | bytes 786440 | tf_op jit(solution)/shard_map/ppermute | solution.py:24
  275.4 15.3 %collective-permute-start.58 = (bf16[4,256,128]{2,1,0:T(8,128)(2,1)S(1)}, bf16[4,256,128]{2,1,0:T(8,128)(2,1)S(1)}, u32[]{:S(2)}, u32[]{:S(2)}) collective-permute-start(bf16[4,256,128]{2,1,0:T(8,128)(2,1)S(1)} %bitcast.85), channel_id=1, source_target_pairs={{0,16},{16,0},{1,17},{17,1},{2,18},{18,2},{3,19},{19,3},{4,20},{20... | collective-permute-start | bytes 786440 | tf_op jit(solution)/shard_map/ppermute | solution.py:24
  277.8 19.7 %collective-permute-start.52 = (bf16[16,128,128]{2,1,0:T(8,128)(2,1)S(1)}, bf16[16,128,128]{2,1,0:T(8,128)(2,1)S(1)}, u32[]{:S(2)}, u32[]{:S(2)}) collective-permute-start(bf16[16,128,128]{2,1,0:T(8,128)(2,1)S(1)} %copy-done.39), channel_id=1, source_target_pairs={{0,16},{16,0},{1,17},{17,1},{2,18},{18,2},{3,19},{19,3},{4,20},{20... | collective-permute-start | bytes 1572872 | tf_op jit(solution)/shard_map/ppermute | solution.py:24
  278.5 19.0 %collective-permute-start.53 = (bf16[16,128,128]{2,1,0:T(8,128)(2,1)S(1)}, bf16[16,128,128]{2,1,0:T(8,128)(2,1)S(1)}, u32[]{:S(2)}, u32[]{:S(2)}) collective-permute-start(bf16[16,128,128]{2,1,0:T(8,128)(2,1)S(1)} %copy-done.38), channel_id=1, source_target_pairs={{0,1},{1,0},{2,3},{3,2},{4,5},{5,4},{6,7},{7,6},{8,9},{9,8},{10,11... | collective-permute-start | bytes 1572872 | tf_op jit(solution)/shard_map/ppermute | solution.py:24
  280.0 10.9 %collective-permute-start.54 = (f32[128,512]{1,0:T(8,128)S(1)}, f32[128,512]{1,0:T(8,128)S(1)}, u32[]{:S(2)}, u32[]{:S(2)}) collective-permute-start(f32[128,512]{1,0:T(8,128)S(1)} %add.275), channel_id=1, source_target_pairs={{0,8},{8,0},{1,9},{9,1},{2,10},{10,2},{3,11},{11,3},{4,12},{12,4},... | collective-permute-start | bytes 786440 | tf_op jit(solution)/shard_map/ppermute | solution.py:24
  280.1 17.3 %collective-permute-start.57 = (bf16[4,256,128]{2,1,0:T(8,128)(2,1)S(1)}, bf16[4,256,128]{2,1,0:T(8,128)(2,1)S(1)}, u32[]{:S(2)}, u32[]{:S(2)}) collective-permute-start(bf16[4,256,128]{2,1,0:T(8,128)(2,1)S(1)} %bitcast.86), channel_id=1, source_target_pairs={{0,1},{1,0},{2,3},{3,2},{4,5},{5,4},{6,7},{7,6},{8,9},{9,8},{10,11... | collective-permute-start | bytes 786440 | tf_op jit(solution)/shard_map/ppermute | solution.py:24
  297.7 7.7 %collective-permute-start.56 = (bf16[4,256,128]{2,1,0:T(8,128)(2,1)S(1)}, bf16[4,256,128]{2,1,0:T(8,128)(2,1)S(1)}, u32[]{:S(2)}, u32[]{:S(2)}) collective-permute-start(bf16[4,256,128]{2,1,0:T(8,128)(2,1)S(1)} %bitcast.87), channel_id=1, source_target_pairs={{0,16},{16,0},{1,17},{17,1},{2,18},{18,2},{3,19},{19,3},{4,20},{20... | collective-permute-start | bytes 786440 | tf_op jit(solution)/shard_map/ppermute | solution.py:24
  299.0 6.5 %collective-permute-start.55 = (bf16[4,256,128]{2,1,0:T(8,128)(2,1)S(1)}, bf16[4,256,128]{2,1,0:T(8,128)(2,1)S(1)}, u32[]{:S(2)}, u32[]{:S(2)}) collective-permute-start(bf16[4,256,128]{2,1,0:T(8,128)(2,1)S(1)} %bitcast.88), channel_id=1, source_target_pairs={{0,1},{1,0},{2,3},{3,2},{4,5},{5,4},{6,7},{7,6},{8,9},{9,8},{10,11... | collective-permute-start | bytes 786440 | tf_op jit(solution)/shard_map/ppermute | solution.py:24
  299.4 14.8 %collective-permute-start.59 = (bf16[2,256,256]{2,1,0:T(8,128)(2,1)S(1)}, bf16[2,256,256]{2,1,0:T(8,128)(2,1)S(1)}, u32[]{:S(2)}, u32[]{:S(2)}) collective-permute-start(bf16[2,256,256]{2,1,0:T(8,128)(2,1)S(1)} %slice.248), channel_id=1, source_target_pairs={{0,2},{2,0},{4,6},{6,4},{1,3},{3,1},{5,7},{7,5},{8,10},{10,8},{12,... | collective-permute-start | bytes 786440 | tf_op jit(solution)/shard_map/ppermute | solution.py:29
  305.7 10.3 %collective-permute-start.61 = (bf16[2,256,256]{2,1,0:T(8,128)(2,1)S(1)}, bf16[2,256,256]{2,1,0:T(8,128)(2,1)S(1)}, u32[]{:S(2)}, u32[]{:S(2)}) collective-permute-start(bf16[2,256,256]{2,1,0:T(8,128)(2,1)S(1)} %slice.247), channel_id=1, source_target_pairs={{0,2},{2,0},{4,6},{6,4},{1,3},{3,1},{5,7},{7,5},{8,10},{10,8},{12,... | collective-permute-start | bytes 786440 | tf_op jit(solution)/shard_map/ppermute | solution.py:29
  314.3 10.5 %collective-permute-start.60 = (bf16[256,256]{1,0:T(8,128)(2,1)S(1)}, bf16[256,256]{1,0:T(8,128)(2,1)S(1)}, u32[]{:S(2)}, u32[]{:S(2)}) collective-permute-start(bf16[256,256]{1,0:T(8,128)(2,1)S(1)} %fusion.21), channel_id=1, source_target_pairs={{0,4},{2,6},{4,0},{6,2},{1,5},{3,7},{5,1},{7,3},{8,12},{10,14},{12... | collective-permute-start | bytes 393224 | tf_op jit(solution)/shard_map/ppermute | solution.py:29
  316.1 10.1 %collective-permute-start.62 = (bf16[256,256]{1,0:T(8,128)(2,1)S(1)}, bf16[256,256]{1,0:T(8,128)(2,1)S(1)}, u32[]{:S(2)}, u32[]{:S(2)}) collective-permute-start(bf16[256,256]{1,0:T(8,128)(2,1)S(1)} %fusion.22), channel_id=1, source_target_pairs={{0,4},{2,6},{4,0},{6,2},{1,5},{3,7},{5,1},{7,3},{8,12},{10,14},{12... | collective-permute-start | bytes 393224 | tf_op jit(solution)/shard_map/ppermute | solution.py:29
  328.2 4.2 %collective-permute-start.63 = (f32[128,256]{1,0:T(8,128)S(1)}, f32[128,256]{1,0:T(8,128)S(1)}, u32[]{:S(2)}, u32[]{:S(2)}) collective-permute-start(f32[128,256]{1,0:T(8,128)S(1)} %fusion.14), channel_id=1, source_target_pairs={{0,24},{8,0},{16,8},{24,16},{1,25},{9,1},{17,9},{25,17},{2,26},{10... | collective-permute-start | bytes 393224 | tf_op jit(solution)/shard_map/ppermute | solution.py:621
  328.3 8.1 %collective-permute-start.64 = (f32[128,256]{1,0:T(8,128)S(1)}, f32[128,256]{1,0:T(8,128)S(1)}, u32[]{:S(2)}, u32[]{:S(2)}) collective-permute-start(f32[128,256]{1,0:T(8,128)S(1)} %fusion.16), channel_id=1, source_target_pairs={{0,16},{8,24},{16,0},{24,8},{1,17},{9,25},{17,1},{25,9},{2,18},{10... | collective-permute-start | bytes 393224 | tf_op jit(solution)/shard_map/ppermute | solution.py:621
  329.6 7.1 %collective-permute-start.65 = (f32[128,256]{1,0:T(8,128)S(1)}, f32[128,256]{1,0:T(8,128)S(1)}, u32[]{:S(2)}, u32[]{:S(2)}) collective-permute-start(f32[128,256]{1,0:T(8,128)S(1)} %fusion.19), channel_id=1, source_target_pairs={{0,8},{8,16},{16,24},{24,0},{1,9},{9,17},{17,25},{25,1},{2,10},{10... | collective-permute-start | bytes 393224 | tf_op jit(solution)/shard_map/ppermute | solution.py:621
  (42 other events, 374.9 us)

commit v7 on v6

--- a/solution.py
+++ b/solution.py
@@ -616,9 +616,10 @@
     kept, *sent = [
         dot32(turned[k * rows_n : (k + 1) * rows_n], z_rows, ((1,), (1,))) for k in range(obs_n)
     ]
+    sent = [part.astype(bf16) for part in sent]
     basis = dot32(after(own_rows, sent), inverse, ((1,), (1,))).astype(bf16)
     got = [
-        lax.ppermute(part, ("x", "core"), [(i, (i + k) % obs_n) for i in range(obs_n)])
+        lax.ppermute(part, ("x", "core"), [(i, (i + k) % obs_n) for i in range(obs_n)]).astype(f32)
         for k, part in enumerate(sent, 1)
     ]
     laid = jnp.concatenate(got[::-1] + [kept] + got[::-1], axis=1)

time: 339 us -> 337 us (level)
  Pallas kernels: 81.4 us -> 85 us
  starting transfers between devices: 59.2 us -> 55.8 us
    pallas_call x4, Pallas kernels: 39.3 us -> 43 us  [block_products(): pl.pallas_call(kernel, out_shape=outs, in_specs=[smem] * 4 + [anywhere] *...]
  transfers between devices with their start and end apart: 66 -> 66, of which waited for: 34 -> 32; matrix products, arithmetic and copies ran while one was open for 6% -> 7% of each run, Pallas kernels for 21% -> 22%
where the time goes in v7:
time: 337 us; the launch traced here: 335 us
  waiting for transfers between devices  161 us (48%)
  Pallas kernels  85 us (25%)
  starting transfers between devices  55.8 us (17%)
  local copies, waits for them, and re-layouts  14.3 us (4%)
  other arithmetic  12.4 us (4%)
  matrix products  5.31 us (2%)
    ppermute x18, waiting for transfers between devices, swap(): return lax.ppermute(value, 'p', [(i, i ^ bits) for i in range(size)])  115 us
    ppermute x45, waiting for transfers between devices, shift(): lax.ppermute(value, axis, [(i, (i + by) % size) for i in range(size)])  44.5 us
    pallas_call x4, Pallas kernels, block_products(): pl.pallas_call(kernel, out_shape=outs, in_specs=[smem] * 4 + [anywhere] *...  43 us
    ppermute x45, starting transfers between devices, shift(): lax.ppermute(value, axis, [(i, (i + by) % size) for i in range(size)])  28.8 us
    ppermute x18, starting transfers between devices, swap(): return lax.ppermute(value, 'p', [(i, i ^ bits) for i in range(size)])  25.9 us
    pallas_call x4, Pallas kernels, inverse_rows(): pl.pallas_call(functools.partial(inverse_kernel, scale, len(before), firs...  21.1 us
    pallas_call x2, Pallas kernels, block_lists(): pl.pallas_call(functools.partial(list_kernel, counts_in, bounds, spare),...  15.3 us
  transfers between devices with their start and end apart: 66, of which 32 were waited for; matrix products, arithmetic and copies ran while one was open for 7% of the time, Pallas kernels for 22%

profile of v7, /device:TPU:0, one launch (start us, length us, event | category | flops | bytes accessed | tf_op | source)
XLA Modules:
  0.0 335.2 jit_solution(15426400667256791761)
XLA Ops:
  1.9 2.6 collective-permute-start.2
  4.4 1.5 collective-permute-start.4
  6.0 2.7 collective-permute-start
  8.6 1.7 fusion.75
  11.4 9.2 %collective-permute-done = bf16[2,128,512]{2,1,0:T(8,128)(2,1)S(1)} collective-permute-done((bf16[2,128,512]{2,1,0:T(8,128)(2,1)S(1)}, bf16[2,128,512]{2,1,0:T(8,128)(2,1)S(1)}, u32[]{:S(2)}, u32[]{:S(2)}) %collective-permute-start) | collective-permute-done | bytes 262176 | tf_op jit(solution)/shard_map/ppermute | solution.py:29
  22.6 2.3 slice.160
  24.9 8.8 %collective-permute-done.1 = bf16[4,128,512]{2,1,0:T(8,128)(2,1)S(1)} collective-permute-done((bf16[4,128,512]{2,1,0:T(8,128)(2,1)S(1)}, bf16[4,128,512]{2,1,0:T(8,128)(2,1)S(1)}, u32[]{:S(2)}, u32[]{:S(2)}) %collective-permute-start.1) | collective-permute-done | bytes 524320 | tf_op jit(solution)/shard_map/ppermute | solution.py:29
  35.3 2.8 collective-permute-start.8
  39.7 10.0 %collective-permute-done.8 = bf16[2,128,512]{2,1,0:T(8,128)(2,1)S(1)} collective-permute-done((bf16[2,128,512]{2,1,0:T(8,128)(2,1)S(1)}, bf16[2,128,512]{2,1,0:T(8,128)(2,1)S(1)}, u32[]{:S(2)}, u32[]{:S(2)}) %collective-permute-start.8) | collective-permute-done | bytes 262176 | tf_op jit(solution)/shard_map/ppermute | solution.py:29
  52.2 2.3 slice.162
  54.5 10.7 %collective-permute-done.9 = bf16[4,128,512]{2,1,0:T(8,128)(2,1)} collective-permute-done((bf16[4,128,512]{2,1,0:T(8,128)(2,1)}, bf16[4,128,512]{2,1,0:T(8,128)(2,1)}, u32[]{:S(2)}, u32[]{:S(2)}) %collective-permute-start.9) | collective-permute-done | bytes 524320 | tf_op jit(solution)/shard_map/ppermute | solution.py:29
  65.2 2.1 pad_maximum_fusion.1.refs_18_
  70.5 7.6 %block_lists.2 = (s32[10]{0:T(128)}, s32[480]{0:T(512)}, s32[480]{0:T(512)}, s32[480]{0:T(512)}) custom-call(s32[512]{0:T(512)} %get-tuple-element.237.rows_ref, s32[512]{0:T(512)} %get-tuple-element.238.cols_ref), custom_call_target="tpu_custom_call" | custom-call | flops 4294967296 | bytes 16384 | tf_op jit(solution)/shard_map/block_lists/pallas_call | solution.py:134
  78.2 7.7 %block_lists.3 = (s32[10]{0:T(128)}, s32[544]{0:T(1024)}, s32[544]{0:T(1024)}, s32[544]{0:T(1024)}) custom-call(s32[512]{0:T(512)} %get-tuple-element.236.rows_ref, s32[512]{0:T(512)} %get-tuple-element.228.cols_ref), custom_call_target="tpu_custom_call" | custom-call | flops 4294967296 | bytes 16384 | tf_op jit(solution)/shard_map/block_lists/pallas_call | solution.py:134
  85.8 7.5 %collective-permute-done.16.refs_19_ = bf16[8,128,512]{2,1,0:T(8,128)(2,1)} collective-permute-done((bf16[8,128,512]{2,1,0:T(8,128)(2,1)}, bf16[8,128,512]{2,1,0:T(8,128)(2,1)}, u32[]{:S(2)}, u32[]{:S(2)}) %collective-permute-start.16) | collective-permute-done | bytes 1048608 | tf_op jit(solution)/shard_map/ppermute | solution.py:24
  94.6 2.8 collective-permute-done.21.refs_11_
  97.4 1.1 collective-permute-done.22.refs_20_
  98.6 1.5 collective-permute-done.23.refs_21_
  100.1 10.4 %sketch_products.2 = (f32[16,128,256]{2,1,0:T(8,128)}, bf16[16,128,256]{2,1,0:T(8,128)(2,1)}, bf16[16,128,256]{2,1,0:T(8,128)(2,1)}) custom-call(s32[10]{0:T(128)} %get-tuple-element.141.refs_0_, s32[480]{0:T(512)} %get-tuple-element.142.refs_1_, s32[480]{0:T(512)} %get-tuple-element.143.refs_2_, s32[480]{0:T(512)} %get-tuple-element.144.refs_3_, ...), custom_call_target="tpu_custom_call" | custom-call | flops 1073741824 | bytes 33554432 | tf_op jit(solution)/shard_map/sketch_products/pallas_call | solution.py:262
  110.4 1.6 collective-permute-start.24
  112.1 10.4 %sketch_products.3 = (f32[16,128,256]{2,1,0:T(8,128)}, bf16[16,128,256]{2,1,0:T(8,128)(2,1)}, bf16[16,128,256]{2,1,0:T(8,128)(2,1)}) custom-call(s32[10]{0:T(128)} %get-tuple-element.141.refs_0_, s32[480]{0:T(512)} %get-tuple-element.142.refs_1_, s32[480]{0:T(512)} %get-tuple-element.143.refs_2_, s32[480]{0:T(512)} %get-tuple-element.144.refs_3_, ...), custom_call_target="tpu_custom_call" | custom-call | flops 1073741824 | bytes 33554432 | tf_op jit(solution)/shard_map/sketch_products/pallas_call | solution.py:262
  122.5 13.6 %collective-permute-done.24 = bf16[16,128,256]{2,1,0:T(8,128)(2,1)S(1)} collective-permute-done((bf16[16,128,256]{2,1,0:T(8,128)(2,1)}, bf16[16,128,256]{2,1,0:T(8,128)(2,1)S(1)}, u32[]{:S(2)}, u32[]{:S(2)}) %collective-permute-start.24) | collective-permute-done | bytes 1048608 | tf_op jit(solution)/shard_map/ppermute | solution.py:24
  136.1 1.1 collective-permute-done.25
  138.3 1.7 fusion.74
  140.1 3.6 %collective-permute-start.28 = (bf16[512,256]{1,0:T(8,128)(2,1)S(1)}, bf16[512,256]{1,0:T(8,128)(2,1)S(1)}, u32[]{:S(2)}, u32[]{:S(2)}) collective-permute-start(bf16[512,256]{1,0:T(8,128)(2,1)S(1)} %bitcast.91), channel_id=1, source_target_pairs={{0,6},{2,4},{4,2},{6,0},{1,7},{3,5},{5,3},{7,1},{8,14},{10,12},{12... | collective-permute-start | bytes 786440 | tf_op jit(solution)/shard_map/ppermute | solution.py:29
  144.6 6.6 %collective-permute-done.28 = bf16[512,256]{1,0:T(8,128)(2,1)S(1)} collective-permute-done((bf16[512,256]{1,0:T(8,128)(2,1)S(1)}, bf16[512,256]{1,0:T(8,128)(2,1)S(1)}, u32[]{:S(2)}, u32[]{:S(2)}) %collective-permute-start.28) | collective-permute-done | bytes 262176 | tf_op jit(solution)/shard_map/ppermute | solution.py:29
  151.2 5.1 %collective-permute-done.27 = bf16[512,256]{1,0:T(8,128)(2,1)S(1)} collective-permute-done((bf16[512,256]{1,0:T(8,128)(2,1)S(1)}, bf16[512,256]{1,0:T(8,128)(2,1)S(1)}, u32[]{:S(2)}, u32[]{:S(2)}) %collective-permute-start.27) | collective-permute-done | bytes 262176 | tf_op jit(solution)/shard_map/ppermute | solution.py:29
  156.3 8.8 %collective-permute-done.26 = bf16[512,256]{1,0:T(8,128)(2,1)S(1)} collective-permute-done((bf16[512,256]{1,0:T(8,128)(2,1)S(1)}, bf16[512,256]{1,0:T(8,128)(2,1)S(1)}, u32[]{:S(2)}, u32[]{:S(2)}) %collective-permute-start.26) | collective-permute-done | bytes 262176 | tf_op jit(solution)/shard_map/ppermute | solution.py:29
  166.0 3.0 collective-permute-start.31
  169.2 12.6 %collective-permute-done.31 = bf16[512,256]{1,0:T(8,128)(2,1)S(1)} collective-permute-done((bf16[512,256]{1,0:T(8,128)(2,1)S(1)}, bf16[512,256]{1,0:T(8,128)(2,1)S(1)}, u32[]{:S(2)}, u32[]{:S(2)}) %collective-permute-start.31) | collective-permute-done | bytes 262176 | tf_op jit(solution)/shard_map/ppermute | solution.py:29
  181.8 3.1 collective-permute-start.32
  185.5 15.3 %collective-permute-done.32 = bf16[1024,256]{1,0:T(8,128)(2,1)S(1)} collective-permute-done((bf16[1024,256]{1,0:T(8,128)(2,1)S(1)}, bf16[1024,256]{1,0:T(8,128)(2,1)S(1)}, u32[]{:S(2)}, u32[]{:S(2)}) %collective-permute-start.32) | collective-permute-done | bytes 524320 | tf_op jit(solution)/shard_map/ppermute | solution.py:29
  201.0 1.1 collective-permute-start.38
  202.1 1.7 collective-permute-start.39
  203.9 1.5 collective-permute-start.37
  205.7 9.0 %collective-permute-done.37 = bf16[512,256]{1,0:T(8,128)(2,1)S(1)} collective-permute-done((bf16[512,256]{1,0:T(8,128)(2,1)S(1)}, bf16[512,256]{1,0:T(8,128)(2,1)S(1)}, u32[]{:S(2)}, u32[]{:S(2)}) %collective-permute-start.37) | collective-permute-done | bytes 262176 | tf_op jit(solution)/shard_map/ppermute | solution.py:29
  215.7 4.5 %collective-permute-done.36 = bf16[512,256]{1,0:T(8,128)(2,1)S(1)} collective-permute-done((bf16[512,256]{1,0:T(8,128)(2,1)S(1)}, bf16[512,256]{1,0:T(8,128)(2,1)S(1)}, u32[]{:S(2)}, u32[]{:S(2)}) %collective-permute-start.36) | collective-permute-done | bytes 262176 | tf_op jit(solution)/shard_map/ppermute | solution.py:29
  220.2 5.4 %collective-permute-done.35 = bf16[512,256]{1,0:T(8,128)(2,1)S(1)} collective-permute-done((bf16[512,256]{1,0:T(8,128)(2,1)S(1)}, bf16[512,256]{1,0:T(8,128)(2,1)S(1)}, u32[]{:S(2)}, u32[]{:S(2)}) %collective-permute-start.35) | collective-permute-done | bytes 262176 | tf_op jit(solution)/shard_map/ppermute | solution.py:29
  227.4 1.4 collective-permute-start.42
  228.7 1.2 collective-permute-done.45
  231.0 11.0 %project_products.2 = (f32[16,128,128]{2,1,0:T(8,128)}, bf16[16,128,128]{2,1,0:T(8,128)(2,1)}, f32[16,128,128]{2,1,0:T(8,128)}, bf16[16,128,128]{2,1,0:T(8,128)(2,1)}) custom-call(s32[10]{0:T(128)} %get-tuple-element.171.refs_0_, s32[544]{0:T(1024)} %get-tuple-element.172.refs_1_, s32[544]{0:T(1024)} %get-tuple-element.173.refs_2_, ...), custom_call_target="tpu_custom_call" | custom-call | flops 1073741824 | bytes 33554432 | tf_op jit(solution)/shard_map/project_products/pallas_call | solution.py:262
  242.0 1.2 copy-done.8
  243.2 1.2 copy-done.11
  244.5 1.2 copy-done.13
  245.7 2.0 gram_rows.2
  247.7 4.3 %collective-permute-done.41.refs_5_ = bf16[2048,256]{1,0:T(8,128)(2,1)} collective-permute-done((bf16[2048,256]{1,0:T(8,128)(2,1)S(1)}, bf16[2048,256]{1,0:T(8,128)(2,1)}, u32[]{:S(2)}, u32[]{:S(2)}) %collective-permute-start.41) | collective-permute-done | bytes 1048608 | tf_op jit(solution)/shard_map/ppermute | solution.py:24
  253.2 1.4 collective-permute-start.47
  255.0 2.0 collective-permute-done.49.refs_7_
  257.2 3.7 %gram_rows.3 = f32[128,512]{1,0:T(8,128)S(1)} custom-call(s32[1]{0:T(128)} %bitcast.16.core_ref, bf16[2048,256]{1,0:T(8,128)(2,1)S(1)} %copy-done.4, bf16[2048,256]{1,0:T(8,128)(2,1)S(1)} %copy-done.9, bf16[2048,256]{1,0:T(8,128)(2,1)S(1)} %copy-done.11, bf16[2048,256]{1,0:T(8,128)(2,1)S(1)} %copy-done.13, bf16[2048,256]{1,0:T(8,128)(2,1)S(1)} %pad_maximum_fusion.4.refs_4_, ...), custom_call_target="tpu_custom_call" | custom-call | flops 2147483648 | bytes 8388608 | tf_op jit(solution)/shard_map/gram_rows/pallas_call | solution.py:335
  260.9 1.4 collective-permute-start.51
  263.0 11.2 %project_products.3 = (f32[16,128,128]{2,1,0:T(8,128)}, bf16[16,128,128]{2,1,0:T(8,128)(2,1)}, f32[16,128,128]{2,1,0:T(8,128)}, bf16[16,128,128]{2,1,0:T(8,128)(2,1)}) custom-call(s32[10]{0:T(128)} %get-tuple-element.171.refs_0_, s32[544]{0:T(1024)} %get-tuple-element.172.refs_1_, s32[544]{0:T(1024)} %get-tuple-element.173.refs_2_, ...), custom_call_target="tpu_custom_call" | custom-call | flops 1073741824 | bytes 33554432 | tf_op jit(solution)/shard_map/project_products/pallas_call | solution.py:262
  274.3 1.5 convert_add_fusion.2
  277.1 1.1 collective-permute-start.52
  281.5 3.9 %inverse_rows.4.refs_0_ = f32[128,512]{1,0:T(8,128)S(1)} custom-call(f32[256,256]{1,0:T(8,128)S(1)} %add.274.gram, f32[16,128,128]{2,1,0:T(8,128)S(1)} %copy-done.14), custom_call_target="tpu_custom_call" | custom-call | flops 67108864 | bytes 65536 | tf_op jit(solution)/shard_map/inverse_rows/pallas_call | solution.py:372
  285.4 4.9 %inverse_rows.5.refs_1_ = f32[128,512]{1,0:T(8,128)S(1)} custom-call(f32[256,256]{1,0:T(8,128)S(1)} %add.274.gram, f32[128,512]{1,0:T(8,128)S(1)} %inverse_rows.4.refs_0_), custom_call_target="tpu_custom_call" | custom-call | flops 67108864 | bytes 65536 | tf_op jit(solution)/shard_map/inverse_rows/pallas_call | solution.py:372
  290.8 6.0 %collective-permute-done.57 = bf16[4,256,128]{2,1,0:T(8,128)(2,1)S(1)} collective-permute-done((bf16[4,256,128]{2,1,0:T(8,128)(2,1)S(1)}, bf16[4,256,128]{2,1,0:T(8,128)(2,1)S(1)}, u32[]{:S(2)}, u32[]{:S(2)}) %collective-permute-start.57) | collective-permute-done | bytes 262176 | tf_op jit(solution)/shard_map/ppermute | solution.py:24
  299.4 5.9 %inverse_rows.6.refs_2_ = f32[128,512]{1,0:T(8,128)S(1)} custom-call(f32[256,512]{1,0:T(8,128)S(1)} %fusion.8.gram, f32[128,512]{1,0:T(8,128)S(1)} %inverse_rows.4.refs_0_, f32[128,512]{1,0:T(8,128)S(1)} %inverse_rows.5.refs_1_, f32[2,4,256,128]{3,2,1,0:T(8,128)S(1)} %bitcast.71), custom_call_target="tpu_custom_call" | custom-call | flops 67108864 | bytes 65536 | tf_op jit(solution)/shard_map/inverse_rows/pallas_call | solution.py:372
  305.7 2.1 collective-permute-start.61
  307.7 6.4 %inverse_rows.7 = f32[128,512]{1,0:T(8,128)S(1)} custom-call(f32[256,512]{1,0:T(8,128)S(1)} %fusion.8.gram, f32[128,512]{1,0:T(8,128)S(1)} %inverse_rows.4.refs_0_, f32[128,512]{1,0:T(8,128)S(1)} %inverse_rows.5.refs_1_, f32[128,512]{1,0:T(8,128)S(1)} %inverse_rows.6.refs_2_, f32[4,256,256]{2,1,0:T(8,128)S(1)} %pad_maximum_fusion.5.refs_3_), custom_call_target="tpu_custom_call" | custom-call | flops 67108864 | bytes 65536 | tf_op jit(solution)/shard_map/inverse_rows/pallas_call | solution.py:372
  314.6 3.0 collective-permute-start.62
  317.5 6.6 %collective-permute-done.60 = bf16[256,256]{1,0:T(8,128)(2,1)S(1)} collective-permute-done((bf16[256,256]{1,0:T(8,128)(2,1)S(1)}, bf16[256,256]{1,0:T(8,128)(2,1)S(1)}, u32[]{:S(2)}, u32[]{:S(2)}) %collective-permute-start.60) | collective-permute-done | bytes 131104 | tf_op jit(solution)/shard_map/ppermute | solution.py:29
  324.1 2.0 collective-permute-done.62
  329.3 2.7 convolution_convert_fusion
  332.0 1.3 collective-permute-done.64
  (246 shorter events, 37.7 us)
Async XLA Ops:
  0.6 34.7 %collective-permute-start.6 = (bf16[128,128,128]{2,1,0:T(8,128)(2,1)}, bf16[128,128,128]{2,1,0:T(8,128)(2,1)}, u32[]{:S(2)}, u32[]{:S(2)}) collective-permute-start(bf16[128,128,128]{2,1,0:T(8,128)(2,1)} %refs_4_.7), channel_id=1, source_target_pairs={{0,8},{8,0},{1,9},{9,1},{2,10},{10,2},{3,11},{11,3},{4,12},{12,4},... | collective-permute-start | bytes 12582920 | tf_op jit(solution)/shard_map/ppermute | solution.py:24
  1.9 8.5 %collective-permute-start.2 = (s32[128]{0:T(128)S(1)}, s32[128]{0:T(128)S(1)}, u32[]{:S(2)}, u32[]{:S(2)}) collective-permute-start(s32[128]{0:T(128)S(1)} %fusion.68), channel_id=1, source_target_pairs={{0,16},{16,0},{1,17},{17,1},{2,18},{18,2},{3,19},{19,3},{4,20},{20... | collective-permute-start | bytes 1544 | tf_op jit(solution)/shard_map/ppermute | solution.py:24
  4.4 6.5 %collective-permute-start.4 = (s32[128]{0:T(128)S(1)}, s32[128]{0:T(128)S(1)}, u32[]{:S(2)}, u32[]{:S(2)}) collective-permute-start(s32[128]{0:T(128)S(1)} %fusion.68), channel_id=1, source_target_pairs={{0,1},{1,0},{2,3},{3,2},{4,5},{5,4},{6,7},{7,6},{8,9},{9,8},{10,11... | collective-permute-start | bytes 1544 | tf_op jit(solution)/shard_map/ppermute | solution.py:24
  6.0 14.7 %collective-permute-start = (bf16[2,128,512]{2,1,0:T(8,128)(2,1)S(1)}, bf16[2,128,512]{2,1,0:T(8,128)(2,1)S(1)}, u32[]{:S(2)}, u32[]{:S(2)}) collective-permute-start(bf16[2,128,512]{2,1,0:T(8,128)(2,1)S(1)} %constant_dynamic-slice_fusion), channel_id=1, source_target_pairs={{0,4},{2,6},{4,0},{6,2},{1,5},{3,7},{5,1},{7,3},{8,12},{10,14},{12... | collective-permute-start | bytes 786440 | tf_op jit(solution)/shard_map/ppermute | solution.py:29
  10.3 24.7 %collective-permute-start.3 = (bf16[32,128,128]{2,1,0:T(8,128)(2,1)S(1)}, bf16[32,128,128]{2,1,0:T(8,128)(2,1)S(1)}, u32[]{:S(2)}, u32[]{:S(2)}) collective-permute-start(bf16[32,128,128]{2,1,0:T(8,128)(2,1)S(1)} %get-tuple-element.114), channel_id=1, source_target_pairs={{0,16},{16,0},{1,17},{17,1},{2,18},{18,2},{3,19},{19,3},{4,20},{20... | collective-permute-start | bytes 3145736 | tf_op jit(solution)/shard_map/ppermute | solution.py:24
  10.9 24.4 %collective-permute-start.5 = (bf16[32,128,128]{2,1,0:T(8,128)(2,1)S(1)}, bf16[32,128,128]{2,1,0:T(8,128)(2,1)S(1)}, u32[]{:S(2)}, u32[]{:S(2)}) collective-permute-start(bf16[32,128,128]{2,1,0:T(8,128)(2,1)S(1)} %get-tuple-element.115), channel_id=1, source_target_pairs={{0,1},{1,0},{2,3},{3,2},{4,5},{5,4},{6,7},{7,6},{8,9},{9,8},{10,11... | collective-permute-start | bytes 3145736 | tf_op jit(solution)/shard_map/ppermute | solution.py:24
  20.7 12.9 %collective-permute-start.1 = (bf16[4,128,512]{2,1,0:T(8,128)(2,1)S(1)}, bf16[4,128,512]{2,1,0:T(8,128)(2,1)S(1)}, u32[]{:S(2)}, u32[]{:S(2)}) collective-permute-start(bf16[4,128,512]{2,1,0:T(8,128)(2,1)S(1)} %pad_maximum_fusion.7), channel_id=1, source_target_pairs={{0,2},{2,0},{4,6},{6,4},{1,3},{3,1},{5,7},{7,5},{8,10},{10,8},{12,... | collective-permute-start | bytes 1572872 | tf_op jit(solution)/shard_map/ppermute | solution.py:29
  35.3 14.4 %collective-permute-start.8 = (bf16[2,128,512]{2,1,0:T(8,128)(2,1)S(1)}, bf16[2,128,512]{2,1,0:T(8,128)(2,1)S(1)}, u32[]{:S(2)}, u32[]{:S(2)}) collective-permute-start(bf16[2,128,512]{2,1,0:T(8,128)(2,1)S(1)} %slice.161), channel_id=1, source_target_pairs={{0,4},{2,6},{4,0},{6,2},{1,5},{3,7},{5,1},{7,3},{8,12},{10,14},{12... | collective-permute-start | bytes 786440 | tf_op jit(solution)/shard_map/ppermute | solution.py:29
  38.1 29.2 %collective-permute-start.10 = (bf16[8,128,512]{2,1,0:T(8,128)(2,1)}, bf16[8,128,512]{2,1,0:T(8,128)(2,1)}, u32[]{:S(2)}, u32[]{:S(2)}) collective-permute-start(bf16[8,128,512]{2,1,0:T(8,128)(2,1)} %pad_maximum_fusion.refs_14_), channel_id=1, source_target_pairs={{0,1},{1,0},{2,3},{3,2},{4,5},{5,4},{6,7},{7,6},{8,9},{9,8},{10,11... | collective-permute-start | bytes 3145736 | tf_op jit(solution)/shard_map/ppermute | solution.py:24
  38.6 28.7 %collective-permute-start.11 = (bf16[32,128,128]{2,1,0:T(8,128)(2,1)}, bf16[32,128,128]{2,1,0:T(8,128)(2,1)S(1)}, u32[]{:S(2)}, u32[]{:S(2)}) collective-permute-start(bf16[32,128,128]{2,1,0:T(8,128)(2,1)} %slice.160), channel_id=1, source_target_pairs={{0,16},{16,0},{1,17},{17,1},{2,18},{18,2},{3,19},{19,3},{4,20},{20... | collective-permute-start | bytes 3145736 | tf_op jit(solution)/shard_map/ppermute | solution.py:24
  39.2 28.2 %collective-permute-start.12 = (bf16[32,128,128]{2,1,0:T(8,128)(2,1)S(1)}, bf16[32,128,128]{2,1,0:T(8,128)(2,1)}, u32[]{:S(2)}, u32[]{:S(2)}) collective-permute-start(bf16[32,128,128]{2,1,0:T(8,128)(2,1)S(1)} %collective-permute-done.3.refs_6_), channel_id=1, source_target_pairs={{0,8},{8,0},{1,9},{9,1},{2,10},{10,2},{3,11},{11,3},{4,12},{12,4},... | collective-permute-start | bytes 3145736 | tf_op jit(solution)/shard_map/ppermute | solution.py:24
  39.2 28.2 %collective-permute-start.13 = (bf16[32,128,128]{2,1,0:T(8,128)(2,1)S(1)}, bf16[32,128,128]{2,1,0:T(8,128)(2,1)}, u32[]{:S(2)}, u32[]{:S(2)}) collective-permute-start(bf16[32,128,128]{2,1,0:T(8,128)(2,1)S(1)} %collective-permute-done.5.refs_12_), channel_id=1, source_target_pairs={{0,8},{8,0},{1,9},{9,1},{2,10},{10,2},{3,11},{11,3},{4,12},{12,4},... | collective-permute-start | bytes 3145736 | tf_op jit(solution)/shard_map/ppermute | solution.py:24
  51.2 14.0 %collective-permute-start.9 = (bf16[4,128,512]{2,1,0:T(8,128)(2,1)}, bf16[4,128,512]{2,1,0:T(8,128)(2,1)}, u32[]{:S(2)}, u32[]{:S(2)}) collective-permute-start(bf16[4,128,512]{2,1,0:T(8,128)(2,1)} %pad_maximum_fusion.8), channel_id=1, source_target_pairs={{0,2},{2,0},{4,6},{6,4},{1,3},{3,1},{5,7},{7,5},{8,10},{10,8},{12,... | collective-permute-start | bytes 1572872 | tf_op jit(solution)/shard_map/ppermute | solution.py:29
  65.2 2.1 collective-permute-start.15
  67.4 26.0 %collective-permute-start.16 = (bf16[8,128,512]{2,1,0:T(8,128)(2,1)}, bf16[8,128,512]{2,1,0:T(8,128)(2,1)}, u32[]{:S(2)}, u32[]{:S(2)}) collective-permute-start(bf16[8,128,512]{2,1,0:T(8,128)(2,1)} %pad_maximum_fusion.1.refs_18_), channel_id=1, source_target_pairs={{0,1},{1,0},{2,3},{3,2},{4,5},{5,4},{6,7},{7,6},{8,9},{9,8},{10,11... | collective-permute-start | bytes 3145736 | tf_op jit(solution)/shard_map/ppermute | solution.py:24
  68.0 25.4 %collective-permute-start.17 = (bf16[8,128,512]{2,1,0:T(8,128)(2,1)}, bf16[8,128,512]{2,1,0:T(8,128)(2,1)}, u32[]{:S(2)}, u32[]{:S(2)}) collective-permute-start(bf16[8,128,512]{2,1,0:T(8,128)(2,1)} %pad_maximum_fusion.refs_14_), channel_id=1, source_target_pairs={{0,8},{8,0},{1,9},{9,1},{2,10},{10,2},{3,11},{11,3},{4,12},{12,4},... | collective-permute-start | bytes 3145736 | tf_op jit(solution)/shard_map/ppermute | solution.py:24
  68.2 25.2 %collective-permute-start.18 = (bf16[8,128,512]{2,1,0:T(8,128)(2,1)}, bf16[8,128,512]{2,1,0:T(8,128)(2,1)}, u32[]{:S(2)}, u32[]{:S(2)}) collective-permute-start(bf16[8,128,512]{2,1,0:T(8,128)(2,1)} %collective-permute-done.10.refs_15_), channel_id=1, source_target_pairs={{0,8},{8,0},{1,9},{9,1},{2,10},{10,2},{3,11},{11,3},{4,12},{12,4},... | collective-permute-start | bytes 3145736 | tf_op jit(solution)/shard_map/ppermute | solution.py:24
  68.5 25.5 %collective-permute-start.19 = (bf16[32,128,128]{2,1,0:T(8,128)(2,1)}, bf16[32,128,128]{2,1,0:T(8,128)(2,1)S(1)}, u32[]{:S(2)}, u32[]{:S(2)}) collective-permute-start(bf16[32,128,128]{2,1,0:T(8,128)(2,1)} %slice.162), channel_id=1, source_target_pairs={{0,16},{16,0},{1,17},{17,1},{2,18},{18,2},{3,19},{19,3},{4,20},{20... | collective-permute-start | bytes 3145736 | tf_op jit(solution)/shard_map/ppermute | solution.py:24
  69.0 25.0 %collective-permute-start.20 = (bf16[32,128,128]{2,1,0:T(8,128)(2,1)S(1)}, bf16[32,128,128]{2,1,0:T(8,128)(2,1)S(1)}, u32[]{:S(2)}, u32[]{:S(2)}) collective-permute-start(bf16[32,128,128]{2,1,0:T(8,128)(2,1)S(1)} %collective-permute-done.11.refs_8_), channel_id=1, source_target_pairs={{0,8},{8,0},{1,9},{9,1},{2,10},{10,2},{3,11},{11,3},{4,12},{12,4},... | collective-permute-start | bytes 3145736 | tf_op jit(solution)/shard_map/ppermute | solution.py:24
  94.0 3.4 %collective-permute-start.21 = (bf16[32,128,128]{2,1,0:T(8,128)(2,1)S(1)}, bf16[32,128,128]{2,1,0:T(8,128)(2,1)S(1)}, u32[]{:S(2)}, u32[]{:S(2)}) collective-permute-start(bf16[32,128,128]{2,1,0:T(8,128)(2,1)S(1)} %collective-permute-done.19.refs_10_), channel_id=1, source_target_pairs={{0,8},{8,0},{1,9},{9,1},{2,10},{10,2},{3,11},{11,3},{4,12},{12,4},... | collective-permute-start | bytes 3145736 | tf_op jit(solution)/shard_map/ppermute | solution.py:24
  94.1 4.5 %collective-permute-start.22 = (bf16[8,128,512]{2,1,0:T(8,128)(2,1)}, bf16[8,128,512]{2,1,0:T(8,128)(2,1)}, u32[]{:S(2)}, u32[]{:S(2)}) collective-permute-start(bf16[8,128,512]{2,1,0:T(8,128)(2,1)} %pad_maximum_fusion.1.refs_18_), channel_id=1, source_target_pairs={{0,8},{8,0},{1,9},{9,1},{2,10},{10,2},{3,11},{11,3},{4,12},{12,4},... | collective-permute-start | bytes 3145736 | tf_op jit(solution)/shard_map/ppermute | solution.py:24
  94.6 5.5 %collective-permute-start.23 = (bf16[8,128,512]{2,1,0:T(8,128)(2,1)}, bf16[8,128,512]{2,1,0:T(8,128)(2,1)}, u32[]{:S(2)}, u32[]{:S(2)}) collective-permute-start(bf16[8,128,512]{2,1,0:T(8,128)(2,1)} %collective-permute-done.16.refs_19_), channel_id=1, source_target_pairs={{0,8},{8,0},{1,9},{9,1},{2,10},{10,2},{3,11},{11,3},{4,12},{12,4},... | collective-permute-start | bytes 3145736 | tf_op jit(solution)/shard_map/ppermute | solution.py:24
  110.4 25.7 %collective-permute-start.24 = (bf16[16,128,256]{2,1,0:T(8,128)(2,1)}, bf16[16,128,256]{2,1,0:T(8,128)(2,1)S(1)}, u32[]{:S(2)}, u32[]{:S(2)}) collective-permute-start(bf16[16,128,256]{2,1,0:T(8,128)(2,1)} %get-tuple-element.155), channel_id=1, source_target_pairs={{0,1},{1,0},{2,3},{3,2},{4,5},{5,4},{6,7},{7,6},{8,9},{9,8},{10,11... | collective-permute-start | bytes 3145736 | tf_op jit(solution)/shard_map/ppermute | solution.py:24
  112.1 25.2 %collective-permute-start.25 = (bf16[16,128,256]{2,1,0:T(8,128)(2,1)}, bf16[16,128,256]{2,1,0:T(8,128)(2,1)}, u32[]{:S(2)}, u32[]{:S(2)}) collective-permute-start(bf16[16,128,256]{2,1,0:T(8,128)(2,1)} %get-tuple-element.156), channel_id=1, source_target_pairs={{0,16},{16,0},{1,17},{17,1},{2,18},{18,2},{3,19},{19,3},{4,20},{20... | collective-permute-start | bytes 3145736 | tf_op jit(solution)/shard_map/ppermute | solution.py:24
  137.3 27.9 %collective-permute-start.29 = (bf16[16,128,256]{2,1,0:T(8,128)(2,1)}, bf16[16,128,256]{2,1,0:T(8,128)(2,1)S(1)}, u32[]{:S(2)}, u32[]{:S(2)}) collective-permute-start(bf16[16,128,256]{2,1,0:T(8,128)(2,1)} %get-tuple-element.162), channel_id=1, source_target_pairs={{0,1},{1,0},{2,3},{3,2},{4,5},{5,4},{6,7},{7,6},{8,9},{9,8},{10,11... | collective-permute-start | bytes 3145736 | tf_op jit(solution)/shard_map/ppermute | solution.py:24
  138.0 27.2 %collective-permute-start.30 = (bf16[16,128,256]{2,1,0:T(8,128)(2,1)}, bf16[16,128,256]{2,1,0:T(8,128)(2,1)S(1)}, u32[]{:S(2)}, u32[]{:S(2)}) collective-permute-start(bf16[16,128,256]{2,1,0:T(8,128)(2,1)} %get-tuple-element.163), channel_id=1, source_target_pairs={{0,16},{16,0},{1,17},{17,1},{2,18},{18,2},{3,19},{19,3},{4,20},{20... | collective-permute-start | bytes 3145736 | tf_op jit(solution)/shard_map/ppermute | solution.py:24
  140.1 11.1 %collective-permute-start.28 = (bf16[512,256]{1,0:T(8,128)(2,1)S(1)}, bf16[512,256]{1,0:T(8,128)(2,1)S(1)}, u32[]{:S(2)}, u32[]{:S(2)}) collective-permute-start(bf16[512,256]{1,0:T(8,128)(2,1)S(1)} %bitcast.91), channel_id=1, source_target_pairs={{0,6},{2,4},{4,2},{6,0},{1,7},{3,5},{5,3},{7,1},{8,14},{10,12},{12... | collective-permute-start | bytes 786440 | tf_op jit(solution)/shard_map/ppermute | solution.py:29
  143.7 12.6 %collective-permute-start.27 = (bf16[512,256]{1,0:T(8,128)(2,1)S(1)}, bf16[512,256]{1,0:T(8,128)(2,1)S(1)}, u32[]{:S(2)}, u32[]{:S(2)}) collective-permute-start(bf16[512,256]{1,0:T(8,128)(2,1)S(1)} %bitcast.90), channel_id=1, source_target_pairs={{0,2},{2,0},{4,6},{6,4},{1,3},{3,1},{5,7},{7,5},{8,10},{10,8},{12,... | collective-permute-start | bytes 786440 | tf_op jit(solution)/shard_map/ppermute | solution.py:29
  143.7 21.3 %collective-permute-start.26 = (bf16[512,256]{1,0:T(8,128)(2,1)S(1)}, bf16[512,256]{1,0:T(8,128)(2,1)S(1)}, u32[]{:S(2)}, u32[]{:S(2)}) collective-permute-start(bf16[512,256]{1,0:T(8,128)(2,1)S(1)} %bitcast.89), channel_id=1, source_target_pairs={{0,4},{2,6},{4,0},{6,2},{1,5},{3,7},{5,1},{7,3},{8,12},{10,14},{12... | collective-permute-start | bytes 786440 | tf_op jit(solution)/shard_map/ppermute | solution.py:29
  165.7 19.2 %collective-permute-start.33 = (bf16[2,512,256]{2,1,0:T(8,128)(2,1)S(1)}, bf16[2,512,256]{2,1,0:T(8,128)(2,1)S(1)}, u32[]{:S(2)}, u32[]{:S(2)}) collective-permute-start(bf16[2,512,256]{2,1,0:T(8,128)(2,1)S(1)} %bitcast.84), channel_id=1, source_target_pairs={{0,2},{2,0},{4,6},{6,4},{1,3},{3,1},{5,7},{7,5},{8,10},{10,8},{12,... | collective-permute-start | bytes 1572872 | tf_op jit(solution)/shard_map/ppermute | solution.py:29
  166.0 15.7 %collective-permute-start.31 = (bf16[512,256]{1,0:T(8,128)(2,1)S(1)}, bf16[512,256]{1,0:T(8,128)(2,1)S(1)}, u32[]{:S(2)}, u32[]{:S(2)}) collective-permute-start(bf16[512,256]{1,0:T(8,128)(2,1)S(1)} %convert_element_type.144), channel_id=1, source_target_pairs={{0,4},{2,6},{4,0},{6,2},{1,5},{3,7},{5,1},{7,3},{8,12},{10,14},{12... | collective-permute-start | bytes 786440 | tf_op jit(solution)/shard_map/ppermute | solution.py:29
  181.8 19.0 %collective-permute-start.32 = (bf16[1024,256]{1,0:T(8,128)(2,1)S(1)}, bf16[1024,256]{1,0:T(8,128)(2,1)S(1)}, u32[]{:S(2)}, u32[]{:S(2)}) collective-permute-start(bf16[1024,256]{1,0:T(8,128)(2,1)S(1)} %pad_maximum_fusion.9), channel_id=1, source_target_pairs={{0,2},{2,0},{4,6},{6,4},{1,3},{3,1},{5,7},{7,5},{8,10},{10,8},{12,... | collective-permute-start | bytes 1572872 | tf_op jit(solution)/shard_map/ppermute | solution.py:29
  185.1 15.8 %collective-permute-start.34 = (bf16[512,256]{1,0:T(8,128)(2,1)S(1)}, bf16[512,256]{1,0:T(8,128)(2,1)S(1)}, u32[]{:S(2)}, u32[]{:S(2)}) collective-permute-start(bf16[512,256]{1,0:T(8,128)(2,1)S(1)} %fusion.12), channel_id=1, source_target_pairs={{0,4},{2,6},{4,0},{6,2},{1,5},{3,7},{5,1},{7,3},{8,12},{10,14},{12... | collective-permute-start | bytes 786440 | tf_op jit(solution)/shard_map/ppermute | solution.py:29
  201.0 24.7 %collective-permute-start.38 = (bf16[2048,256]{1,0:T(8,128)(2,1)S(1)}, bf16[2048,256]{1,0:T(8,128)(2,1)S(1)}, u32[]{:S(2)}, u32[]{:S(2)}) collective-permute-start(bf16[2048,256]{1,0:T(8,128)(2,1)S(1)} %pad_maximum_fusion.2.refs_0_), channel_id=1, source_target_pairs={{0,1},{1,0},{2,3},{3,2},{4,5},{5,4},{6,7},{7,6},{8,9},{9,8},{10,11... | collective-permute-start | bytes 3145736 | tf_op jit(solution)/shard_map/ppermute | solution.py:24
  202.1 23.6 %collective-permute-start.39 = (bf16[2048,256]{1,0:T(8,128)(2,1)S(1)}, bf16[2048,256]{1,0:T(8,128)(2,1)S(1)}, u32[]{:S(2)}, u32[]{:S(2)}) collective-permute-start(bf16[2048,256]{1,0:T(8,128)(2,1)S(1)} %pad_maximum_fusion.2.refs_0_), channel_id=1, source_target_pairs={{0,16},{16,0},{1,17},{17,1},{2,18},{18,2},{3,19},{19,3},{4,20},{20... | collective-permute-start | bytes 3145736 | tf_op jit(solution)/shard_map/ppermute | solution.py:24
  203.9 10.8 %collective-permute-start.37 = (bf16[512,256]{1,0:T(8,128)(2,1)S(1)}, bf16[512,256]{1,0:T(8,128)(2,1)S(1)}, u32[]{:S(2)}, u32[]{:S(2)}) collective-permute-start(bf16[512,256]{1,0:T(8,128)(2,1)S(1)} %convert_element_type.151), channel_id=1, source_target_pairs={{0,6},{2,4},{4,2},{6,0},{1,7},{3,5},{5,3},{7,1},{8,14},{10,12},{12... | collective-permute-start | bytes 786440 | tf_op jit(solution)/shard_map/ppermute | solution.py:29
  205.3 22.0 %collective-permute-start.43 = (bf16[2048,256]{1,0:T(8,128)(2,1)S(1)}, bf16[2048,256]{1,0:T(8,128)(2,1)S(1)}, u32[]{:S(2)}, u32[]{:S(2)}) collective-permute-start(bf16[2048,256]{1,0:T(8,128)(2,1)S(1)} %pad_maximum_fusion.2.refs_0_), channel_id=1, source_target_pairs={{0,8},{8,0},{1,9},{9,1},{2,10},{10,2},{3,11},{11,3},{4,12},{12,4},... | collective-permute-start | bytes 3145736 | tf_op jit(solution)/shard_map/ppermute | solution.py:24
  205.3 14.9 %collective-permute-start.36 = (bf16[512,256]{1,0:T(8,128)(2,1)S(1)}, bf16[512,256]{1,0:T(8,128)(2,1)S(1)}, u32[]{:S(2)}, u32[]{:S(2)}) collective-permute-start(bf16[512,256]{1,0:T(8,128)(2,1)S(1)} %convert_element_type.151), channel_id=1, source_target_pairs={{0,2},{2,0},{4,6},{6,4},{1,3},{3,1},{5,7},{7,5},{8,10},{10,8},{12,... | collective-permute-start | bytes 786440 | tf_op jit(solution)/shard_map/ppermute | solution.py:29
  214.7 10.9 %collective-permute-start.35 = (bf16[512,256]{1,0:T(8,128)(2,1)S(1)}, bf16[512,256]{1,0:T(8,128)(2,1)S(1)}, u32[]{:S(2)}, u32[]{:S(2)}) collective-permute-start(bf16[512,256]{1,0:T(8,128)(2,1)S(1)} %convert_element_type.151), channel_id=1, source_target_pairs={{0,4},{2,6},{4,0},{6,2},{1,5},{3,7},{5,1},{7,3},{8,12},{10,14},{12... | collective-permute-start | bytes 786440 | tf_op jit(solution)/shard_map/ppermute | solution.py:29
  225.7 3.0 collective-permute-start.44
  225.8 4.1 %collective-permute-start.45 = (bf16[2048,256]{1,0:T(8,128)(2,1)S(1)}, bf16[2048,256]{1,0:T(8,128)(2,1)S(1)}, u32[]{:S(2)}, u32[]{:S(2)}) collective-permute-start(bf16[2048,256]{1,0:T(8,128)(2,1)S(1)} %collective-permute-done.39), channel_id=1, source_target_pairs={{0,8},{8,0},{1,9},{9,1},{2,10},{10,2},{3,11},{11,3},{4,12},{12,4},... | collective-permute-start | bytes 3145736 | tf_op jit(solution)/shard_map/ppermute | solution.py:24
  226.3 21.4 %collective-permute-start.40 = (bf16[2048,256]{1,0:T(8,128)(2,1)S(1)}, bf16[2048,256]{1,0:T(8,128)(2,1)S(1)}, u32[]{:S(2)}, u32[]{:S(2)}) collective-permute-start(bf16[2048,256]{1,0:T(8,128)(2,1)S(1)} %pad_maximum_fusion.4.refs_4_), channel_id=1, source_target_pairs={{0,8},{8,0},{1,9},{9,1},{2,10},{10,2},{3,11},{11,3},{4,12},{12,4},... | collective-permute-start | bytes 3145736 | tf_op jit(solution)/shard_map/ppermute | solution.py:24
  226.4 25.6 %collective-permute-start.41 = (bf16[2048,256]{1,0:T(8,128)(2,1)S(1)}, bf16[2048,256]{1,0:T(8,128)(2,1)}, u32[]{:S(2)}, u32[]{:S(2)}) collective-permute-start(bf16[2048,256]{1,0:T(8,128)(2,1)S(1)} %pad_maximum_fusion.4.refs_4_), channel_id=1, source_target_pairs={{0,1},{1,0},{2,3},{3,2},{4,5},{5,4},{6,7},{7,6},{8,9},{9,8},{10,11... | collective-permute-start | bytes 3145736 | tf_op jit(solution)/shard_map/ppermute | solution.py:24
  227.4 25.3 %collective-permute-start.42 = (bf16[2048,256]{1,0:T(8,128)(2,1)S(1)}, bf16[2048,256]{1,0:T(8,128)(2,1)}, u32[]{:S(2)}, u32[]{:S(2)}) collective-permute-start(bf16[2048,256]{1,0:T(8,128)(2,1)S(1)} %pad_maximum_fusion.4.refs_4_), channel_id=1, source_target_pairs={{0,16},{16,0},{1,17},{17,1},{2,18},{18,2},{3,19},{19,3},{4,20},{20... | collective-permute-start | bytes 3145736 | tf_op jit(solution)/shard_map/ppermute | solution.py:24
  252.7 4.3 %collective-permute-start.49 = (bf16[2048,256]{1,0:T(8,128)(2,1)}, bf16[2048,256]{1,0:T(8,128)(2,1)S(1)}, u32[]{:S(2)}, u32[]{:S(2)}) collective-permute-start(bf16[2048,256]{1,0:T(8,128)(2,1)} %collective-permute-done.41.refs_5_), channel_id=1, source_target_pairs={{0,8},{8,0},{1,9},{9,1},{2,10},{10,2},{3,11},{11,3},{4,12},{12,4},... | collective-permute-start | bytes 3145736 | tf_op jit(solution)/shard_map/ppermute | solution.py:24
  252.7 4.5 %collective-permute-start.50 = (bf16[2048,256]{1,0:T(8,128)(2,1)}, bf16[2048,256]{1,0:T(8,128)(2,1)}, u32[]{:S(2)}, u32[]{:S(2)}) collective-permute-start(bf16[2048,256]{1,0:T(8,128)(2,1)} %collective-permute-done.42), channel_id=1, source_target_pairs={{0,8},{8,0},{1,9},{9,1},{2,10},{10,2},{3,11},{11,3},{4,12},{12,4},... | collective-permute-start | bytes 3145736 | tf_op jit(solution)/shard_map/ppermute | solution.py:24
  253.2 21.0 %collective-permute-start.47 = (bf16[16,128,128]{2,1,0:T(8,128)(2,1)}, bf16[16,128,128]{2,1,0:T(8,128)(2,1)}, u32[]{:S(2)}, u32[]{:S(2)}) collective-permute-start(bf16[16,128,128]{2,1,0:T(8,128)(2,1)} %get-tuple-element.188), channel_id=1, source_target_pairs={{0,16},{16,0},{1,17},{17,1},{2,18},{18,2},{3,19},{19,3},{4,20},{20... | collective-permute-start | bytes 1572872 | tf_op jit(solution)/shard_map/ppermute | solution.py:24
  254.6 19.6 %collective-permute-start.48 = (bf16[16,128,128]{2,1,0:T(8,128)(2,1)}, bf16[16,128,128]{2,1,0:T(8,128)(2,1)}, u32[]{:S(2)}, u32[]{:S(2)}) collective-permute-start(bf16[16,128,128]{2,1,0:T(8,128)(2,1)} %get-tuple-element.189), channel_id=1, source_target_pairs={{0,1},{1,0},{2,3},{3,2},{4,5},{5,4},{6,7},{7,6},{8,9},{9,8},{10,11... | collective-permute-start | bytes 1572872 | tf_op jit(solution)/shard_map/ppermute | solution.py:24
  260.9 13.3 %collective-permute-start.51 = (f32[128,512]{1,0:T(8,128)S(1)}, f32[128,512]{1,0:T(8,128)S(1)}, u32[]{:S(2)}, u32[]{:S(2)}) collective-permute-start(f32[128,512]{1,0:T(8,128)S(1)} %gram_rows.3), channel_id=1, source_target_pairs={{0,16},{16,0},{1,17},{17,1},{2,18},{18,2},{3,19},{19,3},{4,20},{20... | collective-permute-start | bytes 786440 | tf_op jit(solution)/shard_map/ppermute | solution.py:24
  262.3 16.9 %collective-permute-start.46 = (f32[256,256]{1,0:T(8,128)}, f32[256,256]{1,0:T(8,128)}, u32[]{:S(2)}, u32[]{:S(2)}) collective-permute-start(f32[256,256]{1,0:T(8,128)} %copy-done.15), channel_id=1, source_target_pairs={{0,16},{16,0},{1,17},{17,1},{2,18},{18,2},{3,19},{19,3},{4,20},{20... | collective-permute-start | bytes 786440 | tf_op jit(solution)/shard_map/ppermute | solution.py:24
  275.9 14.6 %collective-permute-start.58 = (bf16[4,256,128]{2,1,0:T(8,128)(2,1)S(1)}, bf16[4,256,128]{2,1,0:T(8,128)(2,1)S(1)}, u32[]{:S(2)}, u32[]{:S(2)}) collective-permute-start(bf16[4,256,128]{2,1,0:T(8,128)(2,1)S(1)} %bitcast.85), channel_id=1, source_target_pairs={{0,16},{16,0},{1,17},{17,1},{2,18},{18,2},{3,19},{19,3},{4,20},{20... | collective-permute-start | bytes 786440 | tf_op jit(solution)/shard_map/ppermute | solution.py:24
  277.1 19.8 %collective-permute-start.52 = (bf16[16,128,128]{2,1,0:T(8,128)(2,1)S(1)}, bf16[16,128,128]{2,1,0:T(8,128)(2,1)S(1)}, u32[]{:S(2)}, u32[]{:S(2)}) collective-permute-start(bf16[16,128,128]{2,1,0:T(8,128)(2,1)S(1)} %copy-done.39), channel_id=1, source_target_pairs={{0,16},{16,0},{1,17},{17,1},{2,18},{18,2},{3,19},{19,3},{4,20},{20... | collective-permute-start | bytes 1572872 | tf_op jit(solution)/shard_map/ppermute | solution.py:24
  278.3 18.7 %collective-permute-start.53 = (bf16[16,128,128]{2,1,0:T(8,128)(2,1)S(1)}, bf16[16,128,128]{2,1,0:T(8,128)(2,1)S(1)}, u32[]{:S(2)}, u32[]{:S(2)}) collective-permute-start(bf16[16,128,128]{2,1,0:T(8,128)(2,1)S(1)} %copy-done.38), channel_id=1, source_target_pairs={{0,1},{1,0},{2,3},{3,2},{4,5},{5,4},{6,7},{7,6},{8,9},{9,8},{10,11... | collective-permute-start | bytes 1572872 | tf_op jit(solution)/shard_map/ppermute | solution.py:24
  280.3 10.3 %collective-permute-start.54 = (f32[128,512]{1,0:T(8,128)S(1)}, f32[128,512]{1,0:T(8,128)S(1)}, u32[]{:S(2)}, u32[]{:S(2)}) collective-permute-start(f32[128,512]{1,0:T(8,128)S(1)} %add.275), channel_id=1, source_target_pairs={{0,8},{8,0},{1,9},{9,1},{2,10},{10,2},{3,11},{11,3},{4,12},{12,4},... | collective-permute-start | bytes 786440 | tf_op jit(solution)/shard_map/ppermute | solution.py:24
  280.4 16.3 %collective-permute-start.57 = (bf16[4,256,128]{2,1,0:T(8,128)(2,1)S(1)}, bf16[4,256,128]{2,1,0:T(8,128)(2,1)S(1)}, u32[]{:S(2)}, u32[]{:S(2)}) collective-permute-start(bf16[4,256,128]{2,1,0:T(8,128)(2,1)S(1)} %bitcast.86), channel_id=1, source_target_pairs={{0,1},{1,0},{2,3},{3,2},{4,5},{5,4},{6,7},{7,6},{8,9},{9,8},{10,11... | collective-permute-start | bytes 786440 | tf_op jit(solution)/shard_map/ppermute | solution.py:24
  297.1 8.3 %collective-permute-start.56 = (bf16[4,256,128]{2,1,0:T(8,128)(2,1)S(1)}, bf16[4,256,128]{2,1,0:T(8,128)(2,1)S(1)}, u32[]{:S(2)}, u32[]{:S(2)}) collective-permute-start(bf16[4,256,128]{2,1,0:T(8,128)(2,1)S(1)} %bitcast.87), channel_id=1, source_target_pairs={{0,16},{16,0},{1,17},{17,1},{2,18},{18,2},{3,19},{19,3},{4,20},{20... | collective-permute-start | bytes 786440 | tf_op jit(solution)/shard_map/ppermute | solution.py:24
  298.3 7.2 %collective-permute-start.55 = (bf16[4,256,128]{2,1,0:T(8,128)(2,1)S(1)}, bf16[4,256,128]{2,1,0:T(8,128)(2,1)S(1)}, u32[]{:S(2)}, u32[]{:S(2)}) collective-permute-start(bf16[4,256,128]{2,1,0:T(8,128)(2,1)S(1)} %bitcast.88), channel_id=1, source_target_pairs={{0,1},{1,0},{2,3},{3,2},{4,5},{5,4},{6,7},{7,6},{8,9},{9,8},{10,11... | collective-permute-start | bytes 786440 | tf_op jit(solution)/shard_map/ppermute | solution.py:24
  299.4 14.8 %collective-permute-start.59 = (bf16[2,256,256]{2,1,0:T(8,128)(2,1)S(1)}, bf16[2,256,256]{2,1,0:T(8,128)(2,1)S(1)}, u32[]{:S(2)}, u32[]{:S(2)}) collective-permute-start(bf16[2,256,256]{2,1,0:T(8,128)(2,1)S(1)} %slice.248), channel_id=1, source_target_pairs={{0,2},{2,0},{4,6},{6,4},{1,3},{3,1},{5,7},{7,5},{8,10},{10,8},{12,... | collective-permute-start | bytes 786440 | tf_op jit(solution)/shard_map/ppermute | solution.py:29
  305.7 8.8 %collective-permute-start.61 = (bf16[2,256,256]{2,1,0:T(8,128)(2,1)S(1)}, bf16[2,256,256]{2,1,0:T(8,128)(2,1)S(1)}, u32[]{:S(2)}, u32[]{:S(2)}) collective-permute-start(bf16[2,256,256]{2,1,0:T(8,128)(2,1)S(1)} %slice.247), channel_id=1, source_target_pairs={{0,2},{2,0},{4,6},{6,4},{1,3},{3,1},{5,7},{7,5},{8,10},{10,8},{12,... | collective-permute-start | bytes 786440 | tf_op jit(solution)/shard_map/ppermute | solution.py:29
  314.3 9.8 %collective-permute-start.60 = (bf16[256,256]{1,0:T(8,128)(2,1)S(1)}, bf16[256,256]{1,0:T(8,128)(2,1)S(1)}, u32[]{:S(2)}, u32[]{:S(2)}) collective-permute-start(bf16[256,256]{1,0:T(8,128)(2,1)S(1)} %fusion.18), channel_id=1, source_target_pairs={{0,4},{2,6},{4,0},{6,2},{1,5},{3,7},{5,1},{7,3},{8,12},{10,14},{12... | collective-permute-start | bytes 393224 | tf_op jit(solution)/shard_map/ppermute | solution.py:29
  314.6 11.6 %collective-permute-start.62 = (bf16[256,256]{1,0:T(8,128)(2,1)S(1)}, bf16[256,256]{1,0:T(8,128)(2,1)S(1)}, u32[]{:S(2)}, u32[]{:S(2)}) collective-permute-start(bf16[256,256]{1,0:T(8,128)(2,1)S(1)} %fusion.19), channel_id=1, source_target_pairs={{0,4},{2,6},{4,0},{6,2},{1,5},{3,7},{5,1},{7,3},{8,12},{10,14},{12... | collective-permute-start | bytes 393224 | tf_op jit(solution)/shard_map/ppermute | solution.py:29
  328.2 3.7 %collective-permute-start.63 = (bf16[128,256]{1,0:T(8,128)(2,1)S(1)}, bf16[128,256]{1,0:T(8,128)(2,1)S(1)}, u32[]{:S(2)}, u32[]{:S(2)}) collective-permute-start(bf16[128,256]{1,0:T(8,128)(2,1)S(1)} %convolution_convert_fusion.1), channel_id=1, source_target_pairs={{0,24},{8,0},{16,8},{24,16},{1,25},{9,1},{17,9},{25,17},{2,26},{10... | collective-permute-start | bytes 196616 | tf_op jit(solution)/shard_map/ppermute | solution.py:622
  328.3 5.0 %collective-permute-start.64 = (bf16[128,256]{1,0:T(8,128)(2,1)S(1)}, bf16[128,256]{1,0:T(8,128)(2,1)S(1)}, u32[]{:S(2)}, u32[]{:S(2)}) collective-permute-start(bf16[128,256]{1,0:T(8,128)(2,1)S(1)} %convolution_convert_fusion.2), channel_id=1, source_target_pairs={{0,16},{8,24},{16,0},{24,8},{1,17},{9,25},{17,1},{25,9},{2,18},{10... | collective-permute-start | bytes 196616 | tf_op jit(solution)/shard_map/ppermute | solution.py:622
  329.2 4.3 %collective-permute-start.65 = (bf16[128,256]{1,0:T(8,128)(2,1)S(1)}, bf16[128,256]{1,0:T(8,128)(2,1)S(1)}, u32[]{:S(2)}, u32[]{:S(2)}) collective-permute-start(bf16[128,256]{1,0:T(8,128)(2,1)S(1)} %convolution_convert_fusion.3), channel_id=1, source_target_pairs={{0,8},{8,16},{16,24},{24,0},{1,9},{9,17},{17,25},{25,1},{2,10},{10... | collective-permute-start | bytes 196616 | tf_op jit(solution)/shard_map/ppermute | solution.py:622
  (42 other events, 368.2 us)
